TPU v7x, 32 devices: a whole 2x2x4 slice. The times are simulated.
32 devices in a mesh: pipe: 8 (over z, core), seq: 4 (over y, x).
Axes of the slice: x: 2, y: 2, z: 4, core: 2. Of those that a mesh axis runs over, the one named last changes fastest.
Arguments:
- x_fwd: float32 [8, 512, 2048], P('pipe', 'seq'), may hold values from -12 to 12
- x_bwd: float32 [8, 512, 2048], P('pipe', 'seq'), may hold values from -12 to 12
- grad_in: float32 [8, 512, 2048], P('pipe', 'seq'), may hold values from -6 to 6
- gain: float32 [8, 2048], P('pipe'), may hold values from 0.25 to 1.75
- w_query: bfloat16 [8, 2048, 2048], P('pipe', None, 'seq'), may hold values from -2 to 2
- w_key: bfloat16 [8, 2048, 2048], P('pipe', None, 'seq'), may hold values from -2 to 2
- w_value: bfloat16 [8, 2048, 2048], P('pipe', None, 'seq'), may hold values from -0.125 to 0.125
- w_out: bfloat16 [8, 2048, 2048], P('pipe', None, 'seq'), may hold values from -0.125 to 0.125
Outputs:
- act_next: float32 [8, 512, 2048], P('pipe', 'seq')
- grad_prev: float32 [8, 512, 2048], P('pipe', 'seq')
All inputs are finite; a program needn't handle non-finite values.
Results may differ from a plain program's by a relative error of at most 0.012.
The roundings to bfloat16 on the way count: a program that leaves them out, or rounds other values in their place, can miss the bound.
Values may be sent and summed in bfloat16 or wider, within the bound.
No kernel may reach another device: no remote copies, remote signals or barrier semaphores. Data moves between devices by JAX's collectives and lax.ppermute only.
A program may use at most 192 MiB of HBM per device.

v0:
```python
import functools
import math

import jax
import jax.numpy as jnp
from jax import lax
from jax.experimental import pallas as pl
from jax.experimental.pallas import tpu as pltpu
from jax.sharding import PartitionSpec as P

HD = 128
LANES = 128
CHUNK = 256
EXP2_SCALE = HD ** (-0.5) * math.log2(math.e)
NT = (((1,), (1,)), ((), ()))
TN = (((0,), (0,)), ((), ()))
VMEM_LIMIT = 50 * 1024 * 1024


def bits_of(number):
    return [bit for bit in range(number.bit_length()) if (number >> bit) & 1]


def by_distance(count):
    return sorted(range(1, count), key=lambda rel: (len(bits_of(rel)), rel))


def part_bounds(width, count):
    parts = max(count.bit_length() - 1, 1)
    tiles = width // LANES
    return [(tiles * i // parts * LANES, tiles * (i + 1) // parts * LANES) for i in range(parts)]


def last_bit(rel, part):
    bits = bits_of(rel)
    return bits[part % len(bits)]


def across(value, bit):
    count = lax.axis_size("seq")
    return lax.ppermute(value, "seq", [(i, i ^ (1 << bit)) for i in range(count)])


def across_and_on(value, flip):
    count, sections = lax.axis_size("seq"), lax.axis_size("pipe")
    pairs = [
        (p * count + i, (p + 1) % sections * count + (i ^ flip))
        for p in range(sections)
        for i in range(count)
    ]
    return lax.ppermute(value, ("pipe", "seq"), pairs)


def passed_along(value, axis, steps):
    count = lax.axis_size(axis)
    pairs = [(source, (source + steps) % count) for source in range(count)]
    return lax.ppermute(value, axis, pairs)


def gather_blocks(own_parts):
    count = lax.axis_size("seq")
    blocks = {(0, part): value for part, value in enumerate(own_parts)}
    for rel in by_distance(count):
        for part in range(len(own_parts)):
            bit = last_bit(rel, part)
            blocks[rel, part] = across(blocks[rel ^ (1 << bit), part], bit)
    return blocks


def summed_on_the_way(count, parts):
    return {
        (rel ^ (1 << last_bit(rel, part)), part)
        for rel in range(1, count)
        for part in range(parts)
        if len(bits_of(rel)) > 1
    }


def scatter_blocks(terms, send_last):
    count = lax.axis_size("seq")
    arrived, final = {}, {}
    for rel in reversed(by_distance(count)):
        for part in sorted({key[1] for key in terms}):
            total = terms[rel, part]
            for piece in arrived.get((rel, part), []):
                total = total + piece.astype(jnp.float32)
            bit = last_bit(rel, part)
            target = rel ^ (1 << bit)
            if target:
                piece = across(total.astype(jnp.bfloat16), bit)
                arrived.setdefault((target, part), []).append(piece)
            else:
                final[rel, part] = send_last(total.astype(jnp.bfloat16), bit)
    return final


def call(kernel, out_shapes, operands, in_specs, scratch=(), flops=0, name=None):
    moved = sum(math.prod(x.shape) * x.dtype.itemsize for x in list(operands) + list(out_shapes))
    return pl.pallas_call(
        kernel,
        out_shape=out_shapes,
        in_specs=in_specs,
        out_specs=[pl.BlockSpec(memory_space=pltpu.VMEM)] * len(out_shapes),
        scratch_shapes=list(scratch),
        compiler_params=pltpu.CompilerParams(vmem_limit_bytes=VMEM_LIMIT),
        cost_estimate=pl.CostEstimate(flops=int(flops), bytes_accessed=int(moved), transcendentals=0),
        name=name,
    )(*operands)


ANY = pl.BlockSpec(memory_space=pl.ANY)
VMEM = pl.BlockSpec(memory_space=pltpu.VMEM)


def norm_parts(inputs, gain, count, after=()):
    rows, width = inputs.shape
    bounds = part_bounds(width, count)

    def kernel(x_ref, gain_ref, *refs):
        refs = refs[len(after) :]
        x = x_ref[...]
        inv = lax.rsqrt(jnp.mean(x * x, -1, keepdims=True) + 1e-05)
        for ref, (low, high) in zip(refs, bounds):
            ref[...] = (x_ref[:, low:high] * inv * gain_ref[:, low:high]).astype(jnp.bfloat16)
        refs[-1][...] = inv

    outs = [jax.ShapeDtypeStruct((rows, high - low), jnp.bfloat16) for low, high in bounds]
    outs.append(jax.ShapeDtypeStruct((rows, 1), jnp.float32))
    *parts, inv = call(
        kernel, outs, (inputs, gain, *after), [VMEM, VMEM] + [ANY] * len(after), name="norm"
    )
    return parts, inv


def cast_parts(inputs, count, after=()):
    rows, width = inputs.shape
    bounds = part_bounds(width, count)

    def kernel(x_ref, *refs):
        for ref, (low, high) in zip(refs[len(after) :], bounds):
            ref[...] = x_ref[:, low:high].astype(jnp.bfloat16)

    outs = [jax.ShapeDtypeStruct((rows, high - low), jnp.bfloat16) for low, high in bounds]
    return call(kernel, outs, (inputs, *after), [VMEM] + [ANY] * len(after), name="cast")


def block_copies(block_refs, keys, rows, bounds, all_rows, sems):
    return [
        pltpu.make_async_copy(
            ref,
            all_rows.at[pl.ds(rel * rows, rows), pl.ds(bounds[part][0], ref.shape[1])],
            sems.at[i],
        )
        for i, (ref, (rel, part)) in enumerate(zip(block_refs, keys))
    ]


def turned(values, cosine, sine):
    return values * cosine + pltpu.roll(values, HD // 2, 1) * sine


def project_into(rows_ref, weight_ref, out_ref, cos_ref=None, sin_ref=None):
    features = out_ref.shape[1]
    for low in range(0, features, CHUNK):
        high = min(low + CHUNK, features)
        values = jnp.dot(
            rows_ref[...], weight_ref[:, low:high], preferred_element_type=jnp.float32
        )
        for head in range(0, high - low, HD):
            piece = values[:, head : head + HD]
            if cos_ref is not None:
                piece = turned(piece, cos_ref[...], sin_ref[...])
            out_ref[:, low + head : low + head + HD] = piece.astype(jnp.bfloat16)


def project(blocks, weights, cosine, sine, rows, bounds):
    keys = sorted(blocks)
    length, width = cosine.shape[0], bounds[-1][1]
    features = weights[0].shape[1]
    n = len(keys)

    def kernel(*refs):
        block_refs, weight_refs = refs[:n], refs[n : n + 3]
        cos_ref, sin_ref = refs[n + 3 : n + 5]
        outs = refs[n + 5 : n + 8]
        all_rows, held, sems = refs[n + 8 :]
        copies = block_copies(block_refs, keys, rows, bounds, all_rows, sems)
        loads = [
            pltpu.make_async_copy(weight_refs[i], held.at[i], sems.at[n + i]) for i in range(3)
        ]
        for copy in copies + loads:
            copy.start()
        for copy in copies:
            copy.wait()
        for i in range(3):
            loads[i].wait()
            tables = (cos_ref, sin_ref) if i < 2 else ()
            project_into(all_rows, held.at[i], outs[i], *tables)

    return call(
        kernel,
        [jax.ShapeDtypeStruct((length, features), jnp.bfloat16)] * 3,
        [blocks[key] for key in keys] + list(weights) + [cosine, sine],
        [ANY] * (n + 3) + [VMEM, VMEM],
        [
            pltpu.VMEM((length, width), jnp.bfloat16),
            pltpu.VMEM((3, width, features), jnp.bfloat16),
            pltpu.SemaphoreType.DMA((n + 3,)),
        ],
        flops=6 * length * width * features,
        name="project",
    )


def term_outs(rows, bounds, count):
    later = summed_on_the_way(count, len(bounds))
    keys = [(rel, part) for rel in reversed(by_distance(count)) for part in range(len(bounds))]
    shapes = [
        jax.ShapeDtypeStruct(
            (rows, bounds[part][1] - bounds[part][0]),
            jnp.float32 if (rel, part) in later else jnp.bfloat16,
        )
        for rel, part in keys
    ]
    return keys, shapes


def store_terms(values, low, refs, keys, rows, bounds):
    high = low + values.shape[1]
    for ref, (rel, part) in zip(refs, keys):
        first, last = bounds[part]
        start, stop = max(first, low), min(last, high)
        if start < stop:
            piece = values[rel * rows : (rel + 1) * rows, start - low : stop - low]
            ref[:, start - first : stop - first] = piece.astype(ref.dtype)


def backward_terms(blocks, qkv, weights, cosine, sine, rows, bounds, count):
    in_keys = sorted(blocks)
    length, width = cosine.shape[0], bounds[-1][1]
    features = qkv[0].shape[1]
    n = len(in_keys)
    keys, shapes = term_outs(rows, bounds, count)
    step = min(length, 512)

    def kernel(*refs):
        block_refs, weight_refs = refs[:n], refs[n : n + 4]
        q_ref, k_ref, v_ref, cos_ref, sin_ref = refs[n + 4 : n + 9]
        own_ref = refs[n + 9]
        outs = refs[n + 10 : n + 10 + len(keys)]
        all_rows, held, d_attn, d_qkv, sems = refs[n + 10 + len(keys) :]
        copies = block_copies(block_refs, in_keys, rows, bounds, all_rows, sems)
        loads = [
            pltpu.make_async_copy(weight_refs[i], held.at[i], sems.at[n + i]) for i in range(4)
        ]
        for copy in copies + loads:
            copy.start()
        for copy in copies:
            copy.wait()
        loads[0].wait()
        project_into(all_rows, held.at[0], d_attn)

        for head in range(features // HD):
            cols = slice(head * HD, (head + 1) * HD)
            key, value = k_ref[:, cols], v_ref[:, cols]
            d_key, d_value = 0.0, 0.0
            for low in range(0, length, step):
                part = slice(low, low + step)
                query, grad = q_ref[part, cols], d_attn[part, cols]
                scores = lax.dot_general(key, query, NT, preferred_element_type=jnp.float32)
                top = jnp.max(scores, 0, keepdims=True)
                raised = jnp.exp2((scores - top) * EXP2_SCALE)
                probs = raised * (1.0 / jnp.sum(raised, 0, keepdims=True))
                d_value += jnp.dot(
                    probs.astype(jnp.bfloat16), grad, preferred_element_type=jnp.float32
                )
                d_probs = lax.dot_general(value, grad, NT, preferred_element_type=jnp.float32)
                delta = jnp.sum(probs * d_probs, 0, keepdims=True)
                d_scores = (probs * (d_probs - delta) * HD ** (-0.5)).astype(jnp.bfloat16)
                d_key += jnp.dot(d_scores, query, preferred_element_type=jnp.float32)
                d_query = lax.dot_general(
                    key, d_scores, TN, preferred_element_type=jnp.float32
                ).T
                d_qkv[0, part, cols] = turned(
                    d_query, cos_ref[part, :], -sin_ref[part, :]
                ).astype(jnp.bfloat16)
            d_qkv[1, :, cols] = turned(d_key, cos_ref[...], -sin_ref[...]).astype(jnp.bfloat16)
            d_qkv[2, :, cols] = d_value.astype(jnp.bfloat16)

        for i in range(1, 4):
            loads[i].wait()
        for low in range(0, width, CHUNK):
            total = 0.0
            for i in range(3):
                total += lax.dot_general(
                    d_qkv[i],
                    held[i + 1, low : low + CHUNK, :],
                    NT,
                    preferred_element_type=jnp.float32,
                )
            own_ref[:, low : low + CHUNK] = total[:rows]
            store_terms(total, low, outs, keys, rows, bounds)

    own, *terms = call(
        kernel,
        [jax.ShapeDtypeStruct((rows, width), jnp.float32)] + shapes,
        [blocks[key] for key in in_keys] + list(weights) + list(qkv) + [cosine, sine],
        [ANY] * (n + 4) + [VMEM] * 5,
        [
            pltpu.VMEM((length, width), jnp.bfloat16),
            pltpu.VMEM((4, width, features), jnp.bfloat16),
            pltpu.VMEM((length, features), jnp.bfloat16),
            pltpu.VMEM((3, length, features), jnp.bfloat16),
            pltpu.SemaphoreType.DMA((n + 4,)),
        ],
        flops=8 * length * width * features + 10 * length * length * features,
        name="backward",
    )
    return own, dict(zip(keys, terms))


def forward_terms(blocks, act_in, weights, cosine, sine, rows, bounds, count):
    in_keys = sorted(blocks)
    length, width = cosine.shape[0], bounds[-1][1]
    features = weights[0].shape[1]
    n = len(in_keys)
    keys, shapes = term_outs(rows, bounds, count)
    step = min(length, 512)

    def kernel(*refs):
        block_refs, weight_refs = refs[:n], refs[n : n + 4]
        act_ref, cos_ref, sin_ref = refs[n + 4 : n + 7]
        own_ref = refs[n + 7]
        outs = refs[n + 8 : n + 8 + len(keys)]
        all_rows, held, qkv, attn, sems = refs[n + 8 + len(keys) :]
        copies = block_copies(block_refs, in_keys, rows, bounds, all_rows, sems)
        loads = [
            pltpu.make_async_copy(weight_refs[i], held.at[i], sems.at[n + i]) for i in range(4)
        ]
        for copy in copies + loads:
            copy.start()
        for copy in copies:
            copy.wait()
        for i in range(3):
            loads[i].wait()
            tables = (cos_ref, sin_ref) if i < 2 else ()
            project_into(all_rows, held.at[i], qkv.at[i], *tables)

        for head in range(features // HD):
            cols = slice(head * HD, (head + 1) * HD)
            for low in range(0, length, step):
                part = slice(low, low + step)
                scores = lax.dot_general(
                    qkv[0, part, cols], qkv[1, :, cols], NT, preferred_element_type=jnp.float32
                )
                top = jnp.max(scores, 1, keepdims=True)
                raised = jnp.exp2((scores - top) * EXP2_SCALE)
                total = jnp.sum(raised, 1, keepdims=True)
                mixed = jnp.dot(
                    raised.astype(jnp.bfloat16), qkv[2, :, cols], preferred_element_type=jnp.float32
                )
                attn[part, cols] = (mixed * (1.0 / total)).astype(jnp.bfloat16)

        loads[3].wait()
        for low in range(0, width, CHUNK):
            total = lax.dot_general(
                attn[...], held[3, low : low + CHUNK, :], NT, preferred_element_type=jnp.float32
            )
            own = total[:rows] + act_ref[:, low : low + CHUNK]
            own_ref[:, low : low + CHUNK] = own.astype(jnp.bfloat16)
            store_terms(total, low, outs, keys, rows, bounds)

    own, *terms = call(
        kernel,
        [jax.ShapeDtypeStruct((rows, width), jnp.bfloat16)] + shapes,
        [blocks[key] for key in in_keys] + list(weights) + [act_in, cosine, sine],
        [ANY] * (n + 4) + [VMEM] * 3,
        [
            pltpu.VMEM((length, width), jnp.bfloat16),
            pltpu.VMEM((4, width, features), jnp.bfloat16),
            pltpu.VMEM((3, length, features), jnp.bfloat16),
            pltpu.VMEM((length, features), jnp.bfloat16),
            pltpu.SemaphoreType.DMA((n + 4,)),
        ],
        flops=8 * length * width * features + 4 * length * length * features,
        name="forward",
    )
    return own, dict(zip(keys, terms))


def input_grad(own, pieces, saved, grad, inv, gain, bounds):
    keys = sorted(pieces)

    def kernel(own_ref, saved_ref, grad_ref, inv_ref, gain_ref, *refs):
        out_ref, scaled = refs[len(keys) :]
        inv_rows = inv_ref[...]
        product = 0.0
        for part, (low, high) in enumerate(bounds):
            total = own_ref[:, low:high]
            for ref, key in zip(refs, keys):
                if key[1] == part:
                    total = total + ref[...].astype(jnp.float32)
            total = total * gain_ref[:, low:high]
            scaled[:, low:high] = total
            product += jnp.sum(saved_ref[:, low:high] * total, -1, keepdims=True)
        mean = product / own_ref.shape[1]
        factor = inv_rows * inv_rows * inv_rows * mean
        out_ref[...] = (
            grad_ref[...] + inv_rows * scaled[...] - saved_ref[...] * factor
        ).astype(jnp.bfloat16)

    return call(
        kernel,
        [jax.ShapeDtypeStruct(own.shape, jnp.bfloat16)],
        [own, saved, grad, inv, gain] + [pieces[key] for key in keys],
        [VMEM] * (5 + len(keys)),
        [pltpu.VMEM(own.shape, jnp.float32)],
        name="input_grad",
    )[0]


def activation_sum(own, pieces, bounds):
    keys = sorted(pieces)

    def kernel(own_ref, *refs):
        out_ref = refs[len(keys)]
        for part, (low, high) in enumerate(bounds):
            total = own_ref[:, low:high].astype(jnp.float32)
            for ref, key in zip(refs, keys):
                if key[1] == part:
                    total = total + ref[...].astype(jnp.float32)
            out_ref[0, :, low:high] = total

    return call(
        kernel,
        [jax.ShapeDtypeStruct((1, *own.shape), jnp.float32)],
        [own] + [pieces[key] for key in keys],
        [VMEM] * (1 + len(keys)),
        name="activation_sum",
    )[0]


def rope_tables(positions):
    half_dim = HD // 2
    inverse = 10000.0 ** (-(jnp.arange(half_dim).astype(jnp.float32) * 2.0 / HD))
    angles = positions.astype(jnp.float32)[:, None] * inverse[None, :]
    cosine, sine = jnp.cos(angles), jnp.sin(angles)
    return jnp.concatenate([cosine, cosine], 1), jnp.concatenate([-sine, sine], 1)


def shards(x_fwd, x_bwd, grad_in, gain, w_query, w_key, w_value, w_out):
    act_in, saved_in, grad = x_fwd[0], x_bwd[0], grad_in[0]
    rows, width = act_in.shape
    count = lax.axis_size("seq")
    bounds = part_bounds(width, count)
    own_query, own_key, own_value, own_out = w_query[0], w_key[0], w_value[0], w_out[0]

    block_of = lax.axis_index("seq") ^ jnp.arange(count)
    positions = (block_of[:, None] * rows + jnp.arange(rows)[None, :]).reshape(-1)
    cosine, sine = rope_tables(positions)

    def first_arrivals(blocks):
        return [blocks[1 << last_bit(count - 1, part), part] for part in range(len(bounds))]

    parts_bwd, inv_bwd = norm_parts(saved_in, gain, count)
    all_bwd = gather_blocks(parts_bwd)
    all_grad = gather_blocks(cast_parts(grad, count, first_arrivals(all_bwd)))
    parts_fwd, _ = norm_parts(act_in, gain, count, first_arrivals(all_grad))
    all_fwd = gather_blocks(parts_fwd)

    qkv = project(all_bwd, (own_query, own_key, own_value), cosine, sine, rows, bounds)
    d_own, d_terms = backward_terms(
        all_grad, qkv, (own_out, own_query, own_key, own_value), cosine, sine, rows, bounds, count
    )
    d_pieces = scatter_blocks(d_terms, across)

    own, terms = forward_terms(
        all_fwd, act_in, (own_query, own_key, own_value, own_out), cosine, sine, rows, bounds, count
    )
    own = across_and_on(own, 0)
    pieces = scatter_blocks(terms, lambda value, bit: across_and_on(value, 1 << bit))

    d_input = input_grad(d_own, d_pieces, saved_in, grad, inv_bwd, gain, bounds)
    sent_backward = passed_along(d_input, "pipe", -1).astype(jnp.float32)
    return (activation_sum(own, pieces, bounds), sent_backward[None])


def solution(mesh):
    placed = (
        P("pipe", "seq", None),
        P("pipe", "seq", None),
        P("pipe", "seq", None),
        P("pipe", None),
        P("pipe", None, "seq"),
        P("pipe", None, "seq"),
        P("pipe", None, "seq"),
        P("pipe", None, "seq"),
    )
    return jax.shard_map(
        shards,
        mesh=mesh,
        in_specs=placed,
        out_specs=(P("pipe", "seq", None), P("pipe", "seq", None)),
        check_vma=False,
    )
```

profile of v0, /device:TPU:0, one launch (start us, length us, event | category | flops | bytes accessed | tf_op | source)
XLA Modules:
  0.0 126.6 jit_solution(1864317739745530551)
XLA Ops:
  0.6 1.2 copy-done.1
  1.9 0.7 copy-done.5
  2.8 3.0 %collective-permute-start = (bf16[128,1024]{1,0:T(8,128)(2,1)S(1)}, bf16[128,1024]{1,0:T(8,128)(2,1)S(1)}, u32[]{:S(2)}, u32[]{:S(2)}) collective-permute-start(bf16[128,1024]{1,0:T(8,128)(2,1)S(1)} %get-tuple-element.26.refs_0_), channel_id=1, source_target_pairs={{0,1},{1,0},{2,3},{3,2},{4,5},{5,4},{6,7},{7,6},{8,9},{9,8},{10,11... | collective-permute-start | bytes 786440 | tf_op jit(solution)/shard_map/ppermute | solution.py:41
  5.8 1.5 %collective-permute-start.1 = (bf16[128,1024]{1,0:T(8,128)(2,1)S(1)}, bf16[128,1024]{1,0:T(8,128)(2,1)S(1)}, u32[]{:S(2)}, u32[]{:S(2)}) collective-permute-start(bf16[128,1024]{1,0:T(8,128)(2,1)S(1)} %get-tuple-element.27.refs_1_), channel_id=1, source_target_pairs={{0,2},{1,3},{2,0},{3,1},{4,6},{5,7},{6,4},{7,5},{8,10},{9,11},{10,... | collective-permute-start | bytes 786440 | tf_op jit(solution)/shard_map/ppermute | solution.py:41
  7.9 5.0 %collective-permute-done.refs_0_.refs_2_ = bf16[128,1024]{1,0:T(8,128)(2,1)S(1)} collective-permute-done((bf16[128,1024]{1,0:T(8,128)(2,1)S(1)}, bf16[128,1024]{1,0:T(8,128)(2,1)S(1)}, u32[]{:S(2)}, u32[]{:S(2)}) %collective-permute-start) | collective-permute-done | bytes 262176 | tf_op jit(solution)/shard_map/ppermute | solution.py:41
  12.9 2.1 %collective-permute-done.1.refs_1_.refs_5_ = bf16[128,1024]{1,0:T(8,128)(2,1)S(1)} collective-permute-done((bf16[128,1024]{1,0:T(8,128)(2,1)S(1)}, bf16[128,1024]{1,0:T(8,128)(2,1)S(1)}, u32[]{:S(2)}, u32[]{:S(2)}) %collective-permute-start.1) | collective-permute-done | bytes 262176 | tf_op jit(solution)/shard_map/ppermute | solution.py:41
  15.0 1.2 copy-done
  16.5 2.0 %collective-permute-start.18 = (bf16[128,1024]{1,0:T(8,128)(2,1)S(1)}, bf16[128,1024]{1,0:T(8,128)(2,1)S(1)}, u32[]{:S(2)}, u32[]{:S(2)}) collective-permute-start(bf16[128,1024]{1,0:T(8,128)(2,1)S(1)} %get-tuple-element.28.refs_0_), channel_id=1, source_target_pairs={{0,2},{1,3},{2,0},{3,1},{4,6},{5,7},{6,4},{7,5},{8,10},{9,11},{10,... | collective-permute-start | bytes 786440 | tf_op jit(solution)/shard_map/ppermute | solution.py:41
  18.5 1.5 %collective-permute-start.17 = (bf16[128,1024]{1,0:T(8,128)(2,1)S(1)}, bf16[128,1024]{1,0:T(8,128)(2,1)S(1)}, u32[]{:S(2)}, u32[]{:S(2)}) collective-permute-start(bf16[128,1024]{1,0:T(8,128)(2,1)S(1)} %get-tuple-element.29.refs_1_), channel_id=1, source_target_pairs={{0,1},{1,0},{2,3},{3,2},{4,5},{5,4},{6,7},{7,6},{8,9},{9,8},{10,11... | collective-permute-start | bytes 786440 | tf_op jit(solution)/shard_map/ppermute | solution.py:41
  20.0 0.6 collective-permute-done.22.refs_4_
  20.6 1.5 %collective-permute-start.3 = (bf16[128,1024]{1,0:T(8,128)(2,1)S(1)}, bf16[128,1024]{1,0:T(8,128)(2,1)S(1)}, u32[]{:S(2)}, u32[]{:S(2)}) collective-permute-start(bf16[128,1024]{1,0:T(8,128)(2,1)S(1)} %get-tuple-element.29.refs_1_), channel_id=1, source_target_pairs={{0,2},{1,3},{2,0},{3,1},{4,6},{5,7},{6,4},{7,5},{8,10},{9,11},{10,... | collective-permute-start | bytes 786440 | tf_op jit(solution)/shard_map/ppermute | solution.py:41
  22.2 0.5 collective-permute-start.23
  22.7 2.9 %collective-permute-done.2.refs_0_.refs_2_ = bf16[128,1024]{1,0:T(8,128)(2,1)S(1)} collective-permute-done((bf16[128,1024]{1,0:T(8,128)(2,1)S(1)}, bf16[128,1024]{1,0:T(8,128)(2,1)S(1)}, u32[]{:S(2)}, u32[]{:S(2)}) %collective-permute-start.2) | collective-permute-done | bytes 262176 | tf_op jit(solution)/shard_map/ppermute | solution.py:41
  25.6 1.5 %collective-permute-start.24 = (bf16[128,1024]{1,0:T(8,128)(2,1)S(1)}, bf16[128,1024]{1,0:T(8,128)(2,1)S(1)}, u32[]{:S(2)}, u32[]{:S(2)}) collective-permute-start(bf16[128,1024]{1,0:T(8,128)(2,1)S(1)} %collective-permute-done.21.refs_3_), channel_id=1, source_target_pairs={{0,2},{1,3},{2,0},{3,1},{4,6},{5,7},{6,4},{7,5},{8,10},{9,11},{10,... | collective-permute-start | bytes 786440 | tf_op jit(solution)/shard_map/ppermute | solution.py:41
  27.1 1.0 fusion
  28.3 3.5 %collective-permute-done.3.refs_1_.refs_5_ = bf16[128,1024]{1,0:T(8,128)(2,1)S(1)} collective-permute-done((bf16[128,1024]{1,0:T(8,128)(2,1)S(1)}, bf16[128,1024]{1,0:T(8,128)(2,1)S(1)}, u32[]{:S(2)}, u32[]{:S(2)}) %collective-permute-start.3) | collective-permute-done | bytes 262176 | tf_op jit(solution)/shard_map/ppermute | solution.py:41
  31.9 0.8 norm.3
  32.7 1.5 %collective-permute-start.6 = (bf16[128,1024]{1,0:T(8,128)(2,1)S(1)}, bf16[128,1024]{1,0:T(8,128)(2,1)S(1)}, u32[]{:S(2)}, u32[]{:S(2)}) collective-permute-start(bf16[128,1024]{1,0:T(8,128)(2,1)S(1)} %get-tuple-element.30.refs_0_), channel_id=1, source_target_pairs={{0,2},{1,3},{2,0},{3,1},{4,6},{5,7},{6,4},{7,5},{8,10},{9,11},{10,... | collective-permute-start | bytes 786440 | tf_op jit(solution)/shard_map/ppermute | solution.py:41
  34.6 1.7 %collective-permute-start.5 = (bf16[128,1024]{1,0:T(8,128)(2,1)S(1)}, bf16[128,1024]{1,0:T(8,128)(2,1)S(1)}, u32[]{:S(2)}, u32[]{:S(2)}) collective-permute-start(bf16[128,1024]{1,0:T(8,128)(2,1)S(1)} %get-tuple-element.31.refs_1_), channel_id=1, source_target_pairs={{0,1},{1,0},{2,3},{3,2},{4,5},{5,4},{6,7},{7,6},{8,9},{9,8},{10,11... | collective-permute-start | bytes 786440 | tf_op jit(solution)/shard_map/ppermute | solution.py:41
  36.6 1.8 %collective-permute-start.20 = (bf16[128,1024]{1,0:T(8,128)(2,1)S(1)}, bf16[128,1024]{1,0:T(8,128)(2,1)S(1)}, u32[]{:S(2)}, u32[]{:S(2)}) collective-permute-start(bf16[128,1024]{1,0:T(8,128)(2,1)S(1)} %collective-permute-done.17.refs_3_), channel_id=1, source_target_pairs={{0,2},{1,3},{2,0},{3,1},{4,6},{5,7},{6,4},{7,5},{8,10},{9,11},{10,... | collective-permute-start | bytes 786440 | tf_op jit(solution)/shard_map/ppermute | solution.py:41
  38.4 6.8 %project.1 = (bf16[512,512]{1,0:T(8,128)(2,1)S(1)}, bf16[512,512]{1,0:T(8,128)(2,1)S(1)}, bf16[512,512]{1,0:T(8,128)(2,1)}) custom-call(bf16[128,1024]{1,0:T(8,128)(2,1)S(1)} %get-tuple-element.26.refs_0_, bf16[128,1024]{1,0:T(8,128)(2,1)S(1)} %get-tuple-element.27.refs_1_, bf16[128,1024]{1,0:T(8,128)(2,1)S(1)} %collective-permute-done.refs_0_.refs_2_, ...), custom_call_target="tpu_custom_call" | custom-call | flops 3221225472 | bytes 10485760 | tf_op jit(solution)/shard_map/project/pallas_call | solution.py:99
  45.2 0.8 copy-done.7
  46.0 0.8 copy-done.8
  46.8 0.6 collective-permute-done.19.refs_6_
  47.4 13.1 %backward.1 = (f32[128,2048]{1,0:T(8,128)}, bf16[128,1024]{1,0:T(8,128)(2,1)S(1)}, bf16[128,1024]{1,0:T(8,128)(2,1)S(1)}, f32[128,1024]{1,0:T(8,128)}, bf16[128,...) custom-call(bf16[128,1024]{1,0:T(8,128)(2,1)S(1)} %get-tuple-element.28.refs_0_, ...), custom_call_target="tpu_custom_call" | custom-call | flops 5637144576 | bytes 15728640 | tf_op jit(solution)/shard_map/backward/pallas_call | solution.py:99
  60.4 1.8 %collective-permute-start.28 = (bf16[128,1024]{1,0:T(8,128)(2,1)S(1)}, bf16[128,1024]{1,0:T(8,128)(2,1)S(1)}, u32[]{:S(2)}, u32[]{:S(2)}) collective-permute-start(bf16[128,1024]{1,0:T(8,128)(2,1)S(1)} %get-tuple-element.48), channel_id=1, source_target_pairs={{0,1},{1,0},{2,3},{3,2},{4,5},{5,4},{6,7},{7,6},{8,9},{9,8},{10,11... | collective-permute-start | bytes 786440 | tf_op jit(solution)/shard_map/ppermute | solution.py:41
  62.3 1.5 %collective-permute-start.26 = (bf16[128,1024]{1,0:T(8,128)(2,1)S(1)}, bf16[128,1024]{1,0:T(8,128)(2,1)S(1)}, u32[]{:S(2)}, u32[]{:S(2)}) collective-permute-start(bf16[128,1024]{1,0:T(8,128)(2,1)S(1)} %get-tuple-element.46), channel_id=1, source_target_pairs={{0,2},{1,3},{2,0},{3,1},{4,6},{5,7},{6,4},{7,5},{8,10},{9,11},{10,... | collective-permute-start | bytes 786440 | tf_op jit(solution)/shard_map/ppermute | solution.py:41
  64.6 1.7 %collective-permute-start.8 = (bf16[128,1024]{1,0:T(8,128)(2,1)S(1)}, bf16[128,1024]{1,0:T(8,128)(2,1)S(1)}, u32[]{:S(2)}, u32[]{:S(2)}) collective-permute-start(bf16[128,1024]{1,0:T(8,128)(2,1)S(1)} %collective-permute-done.6.refs_4_), channel_id=1, source_target_pairs={{0,1},{1,0},{2,3},{3,2},{4,5},{5,4},{6,7},{7,6},{8,9},{9,8},{10,11... | collective-permute-start | bytes 786440 | tf_op jit(solution)/shard_map/ppermute | solution.py:41
  66.3 3.4 %collective-permute-done.28 = bf16[128,1024]{1,0:T(8,128)(2,1)S(1)} collective-permute-done((bf16[128,1024]{1,0:T(8,128)(2,1)S(1)}, bf16[128,1024]{1,0:T(8,128)(2,1)S(1)}, u32[]{:S(2)}, u32[]{:S(2)}) %collective-permute-start.28) | collective-permute-done | bytes 262176 | tf_op jit(solution)/shard_map/ppermute | solution.py:41
  69.8 1.5 %collective-permute-start.9 = (bf16[128,1024]{1,0:T(8,128)(2,1)S(1)}, bf16[128,1024]{1,0:T(8,128)(2,1)S(1)}, u32[]{:S(2)}, u32[]{:S(2)}) collective-permute-start(bf16[128,1024]{1,0:T(8,128)(2,1)S(1)} %collective-permute-done.5.refs_3_), channel_id=1, source_target_pairs={{0,2},{1,3},{2,0},{3,1},{4,6},{5,7},{6,4},{7,5},{8,10},{9,11},{10,... | collective-permute-start | bytes 786440 | tf_op jit(solution)/shard_map/ppermute | solution.py:41
  71.3 1.1 add_convert_fusion
  72.4 1.8 %collective-permute-start.25 = (bf16[128,1024]{1,0:T(8,128)(2,1)S(1)}, bf16[128,1024]{1,0:T(8,128)(2,1)S(1)}, u32[]{:S(2)}, u32[]{:S(2)}) collective-permute-start(bf16[128,1024]{1,0:T(8,128)(2,1)S(1)} %get-tuple-element.44), channel_id=1, source_target_pairs={{0,1},{1,0},{2,3},{3,2},{4,5},{5,4},{6,7},{7,6},{8,9},{9,8},{10,11... | collective-permute-start | bytes 786440 | tf_op jit(solution)/shard_map/ppermute | solution.py:41
  74.2 1.1 add_convert_fusion.1
  75.4 1.5 %collective-permute-start.30 = (bf16[128,1024]{1,0:T(8,128)(2,1)S(1)}, bf16[128,1024]{1,0:T(8,128)(2,1)S(1)}, u32[]{:S(2)}, u32[]{:S(2)}) collective-permute-start(bf16[128,1024]{1,0:T(8,128)(2,1)S(1)} %get-tuple-element.49), channel_id=1, source_target_pairs={{0,2},{1,3},{2,0},{3,1},{4,6},{5,7},{6,4},{7,5},{8,10},{9,11},{10,... | collective-permute-start | bytes 786440 | tf_op jit(solution)/shard_map/ppermute | solution.py:41
  77.1 1.5 %collective-permute-start.29 = (bf16[128,1024]{1,0:T(8,128)(2,1)S(1)}, bf16[128,1024]{1,0:T(8,128)(2,1)S(1)}, u32[]{:S(2)}, u32[]{:S(2)}) collective-permute-start(bf16[128,1024]{1,0:T(8,128)(2,1)S(1)} %add_convert_fusion), channel_id=1, source_target_pairs={{0,2},{1,3},{2,0},{3,1},{4,6},{5,7},{6,4},{7,5},{8,10},{9,11},{10,... | collective-permute-start | bytes 786440 | tf_op jit(solution)/shard_map/ppermute | solution.py:41
  78.6 2.4 %collective-permute-done.8.refs_6_ = bf16[128,1024]{1,0:T(8,128)(2,1)S(1)} collective-permute-done((bf16[128,1024]{1,0:T(8,128)(2,1)S(1)}, bf16[128,1024]{1,0:T(8,128)(2,1)S(1)}, u32[]{:S(2)}, u32[]{:S(2)}) %collective-permute-start.8) | collective-permute-done | bytes 262176 | tf_op jit(solution)/shard_map/ppermute | solution.py:41
  81.0 1.7 %collective-permute-start.27 = (bf16[128,1024]{1,0:T(8,128)(2,1)S(1)}, bf16[128,1024]{1,0:T(8,128)(2,1)S(1)}, u32[]{:S(2)}, u32[]{:S(2)}) collective-permute-start(bf16[128,1024]{1,0:T(8,128)(2,1)S(1)} %add_convert_fusion.1), channel_id=1, source_target_pairs={{0,1},{1,0},{2,3},{3,2},{4,5},{5,4},{6,7},{7,6},{8,9},{9,8},{10,11... | collective-permute-start | bytes 786440 | tf_op jit(solution)/shard_map/ppermute | solution.py:41
  82.7 11.0 %forward.1 = (bf16[128,2048]{1,0:T(8,128)(2,1)}, bf16[128,1024]{1,0:T(8,128)(2,1)S(1)}, bf16[128,1024]{1,0:T(8,128)(2,1)S(1)}, f32[128,1024]{1,0:T(8,128)}, bf16...) custom-call(bf16[128,1024]{1,0:T(8,128)(2,1)S(1)} %get-tuple-element.30.refs_0_, ...), custom_call_target="tpu_custom_call" | custom-call | flops 4831838208 | bytes 14680064 | tf_op jit(solution)/shard_map/forward/pallas_call | solution.py:99
  94.1 1.5 %collective-permute-start.12 = (bf16[128,1024]{1,0:T(8,128)(2,1)S(1)}, bf16[128,1024]{1,0:T(8,128)(2,1)S(1)}, u32[]{:S(2)}, u32[]{:S(2)}) collective-permute-start(bf16[128,1024]{1,0:T(8,128)(2,1)S(1)} %get-tuple-element.35), channel_id=1, source_target_pairs={{0,2},{1,3},{2,0},{3,1},{4,6},{5,7},{6,4},{7,5},{8,10},{9,11},{10,... | collective-permute-start | bytes 786440 | tf_op jit(solution)/shard_map/ppermute | solution.py:41
  95.7 3.0 %collective-permute-start.11 = (bf16[128,1024]{1,0:T(8,128)(2,1)S(1)}, bf16[128,1024]{1,0:T(8,128)(2,1)S(1)}, u32[]{:S(2)}, u32[]{:S(2)}) collective-permute-start(bf16[128,1024]{1,0:T(8,128)(2,1)S(1)} %get-tuple-element.33), channel_id=1, source_target_pairs={{0,5},{1,4},{2,7},{3,6},{4,9},{5,8},{6,11},{7,10},{8,13},{9,12},{1... | collective-permute-start | bytes 786440 | tf_op jit(solution)/shard_map/ppermute | solution.py:51
  98.7 1.9 %input_grad.1 = bf16[128,2048]{1,0:T(8,128)(2,1)S(1)} custom-call(f32[128,2048]{1,0:T(8,128)S(1)} %copy-done.4, f32[128,2048]{1,0:T(8,128)S(1)} %bitcast.15, f32[128,2048]{1,0:T(8,128)} %bitcast.12, f32[128,1]{1,0:T(8,128)S(1)} %get-tuple-element.43.inv_ref, f32[1,2048]{1,0:T(1,128)S(1)} %copy-done.6, bf16[128,1024]{1,0:T(8,128)(2,1)S(1)} %collective-permute-done.25.refs_0_, ...), custom_call_target="tpu_custom_call" | custom-call | bytes 4727296 | tf_op jit(solution)/shard_map/input_grad/pallas_call | solution.py:99
  100.6 3.5 %collective-permute-start.31 = (bf16[128,2048]{1,0:T(8,128)(2,1)S(1)}, bf16[128,2048]{1,0:T(8,128)(2,1)S(1)}, u32[]{:S(2)}, u32[]{:S(2)}) collective-permute-start(bf16[128,2048]{1,0:T(8,128)(2,1)S(1)} %input_grad.1), channel_id=1, source_target_pairs={{0,28},{4,0},{8,4},{12,8},{16,12},{20,16},{24,20},{28,24},{1,29},{... | collective-permute-start | bytes 1572872 | tf_op jit(solution)/shard_map/ppermute | solution.py:57
  104.4 10.3 %collective-permute-done.11.refs_0_ = bf16[128,1024]{1,0:T(8,128)(2,1)S(1)} collective-permute-done((bf16[128,1024]{1,0:T(8,128)(2,1)S(1)}, bf16[128,1024]{1,0:T(8,128)(2,1)S(1)}, u32[]{:S(2)}, u32[]{:S(2)}) %collective-permute-start.11) | collective-permute-done | bytes 262176 | tf_op jit(solution)/shard_map/ppermute | solution.py:51
  114.6 1.9 %collective-permute-done.16.refs_3_ = bf16[128,1024]{1,0:T(8,128)(2,1)S(1)} collective-permute-done((bf16[128,1024]{1,0:T(8,128)(2,1)S(1)}, bf16[128,1024]{1,0:T(8,128)(2,1)S(1)}, u32[]{:S(2)}, u32[]{:S(2)}) %collective-permute-start.16) | collective-permute-done | bytes 262176 | tf_op jit(solution)/shard_map/ppermute | solution.py:51
  116.5 3.8 %collective-permute-done.15.refs_2_ = bf16[128,1024]{1,0:T(8,128)(2,1)S(1)} collective-permute-done((bf16[128,1024]{1,0:T(8,128)(2,1)S(1)}, bf16[128,1024]{1,0:T(8,128)(2,1)S(1)}, u32[]{:S(2)}, u32[]{:S(2)}) %collective-permute-start.15) | collective-permute-done | bytes 262176 | tf_op jit(solution)/shard_map/ppermute | solution.py:51
  120.3 4.0 %collective-permute-done.13.refs_1_ = bf16[128,1024]{1,0:T(8,128)(2,1)S(1)} collective-permute-done((bf16[128,1024]{1,0:T(8,128)(2,1)S(1)}, bf16[128,1024]{1,0:T(8,128)(2,1)S(1)}, u32[]{:S(2)}, u32[]{:S(2)}) %collective-permute-start.13) | collective-permute-done | bytes 262176 | tf_op jit(solution)/shard_map/ppermute | solution.py:51
  124.4 1.1 activation_sum.1
  125.5 1.1 bitcast_convert_fusion
  (56 shorter events, 3.6 us)
Async XLA Ops:
  0.6 1.2 copy-start.1
  1.9 0.7 copy-start.5
  2.6 29.3 %copy-start.3 = (f32[1,128,2048]{2,1,0:T(8,128)S(1)}, f32[1,128,2048]{2,1,0:T(8,128)}, u32[]{:S(2)}) copy-start(f32[1,128,2048]{2,1,0:T(8,128)} %param.8) | copy-start | bytes 3145732
  2.8 29.1 %copy-start.6 = (f32[1,2048]{1,0:T(1,128)S(1)}, f32[1,2048]{1,0:T(1,128)}, u32[]{:S(2)}) copy-start(f32[1,2048]{1,0:T(1,128)} %gain_ref.5) | copy-start | bytes 24580
  2.8 10.1 %collective-permute-start = (bf16[128,1024]{1,0:T(8,128)(2,1)S(1)}, bf16[128,1024]{1,0:T(8,128)(2,1)S(1)}, u32[]{:S(2)}, u32[]{:S(2)}) collective-permute-start(bf16[128,1024]{1,0:T(8,128)(2,1)S(1)} %get-tuple-element.26.refs_0_), channel_id=1, source_target_pairs={{0,1},{1,0},{2,3},{3,2},{4,5},{5,4},{6,7},{7,6},{8,9},{9,8},{10,11... | collective-permute-start | bytes 786440 | tf_op jit(solution)/shard_map/ppermute | solution.py:41
  5.8 9.2 %collective-permute-start.1 = (bf16[128,1024]{1,0:T(8,128)(2,1)S(1)}, bf16[128,1024]{1,0:T(8,128)(2,1)S(1)}, u32[]{:S(2)}, u32[]{:S(2)}) collective-permute-start(bf16[128,1024]{1,0:T(8,128)(2,1)S(1)} %get-tuple-element.27.refs_1_), channel_id=1, source_target_pairs={{0,2},{1,3},{2,0},{3,1},{4,6},{5,7},{6,4},{7,5},{8,10},{9,11},{10,... | collective-permute-start | bytes 786440 | tf_op jit(solution)/shard_map/ppermute | solution.py:41
  7.3 13.3 %collective-permute-start.22 = (bf16[128,1024]{1,0:T(8,128)(2,1)S(1)}, bf16[128,1024]{1,0:T(8,128)(2,1)S(1)}, u32[]{:S(2)}, u32[]{:S(2)}) collective-permute-start(bf16[128,1024]{1,0:T(8,128)(2,1)S(1)} %get-tuple-element.26.refs_0_), channel_id=1, source_target_pairs={{0,2},{1,3},{2,0},{3,1},{4,6},{5,7},{6,4},{7,5},{8,10},{9,11},{10,... | collective-permute-start | bytes 786440 | tf_op jit(solution)/shard_map/ppermute | solution.py:41
  7.8 14.3 %collective-permute-start.21 = (bf16[128,1024]{1,0:T(8,128)(2,1)S(1)}, bf16[128,1024]{1,0:T(8,128)(2,1)S(1)}, u32[]{:S(2)}, u32[]{:S(2)}) collective-permute-start(bf16[128,1024]{1,0:T(8,128)(2,1)S(1)} %get-tuple-element.27.refs_1_), channel_id=1, source_target_pairs={{0,1},{1,0},{2,3},{3,2},{4,5},{5,4},{6,7},{7,6},{8,9},{9,8},{10,11... | collective-permute-start | bytes 786440 | tf_op jit(solution)/shard_map/ppermute | solution.py:41
  15.0 1.2 copy-start
  16.3 9.3 %collective-permute-start.2 = (bf16[128,1024]{1,0:T(8,128)(2,1)S(1)}, bf16[128,1024]{1,0:T(8,128)(2,1)S(1)}, u32[]{:S(2)}, u32[]{:S(2)}) collective-permute-start(bf16[128,1024]{1,0:T(8,128)(2,1)S(1)} %get-tuple-element.28.refs_0_), channel_id=1, source_target_pairs={{0,1},{1,0},{2,3},{3,2},{4,5},{5,4},{6,7},{7,6},{8,9},{9,8},{10,11... | collective-permute-start | bytes 786440 | tf_op jit(solution)/shard_map/ppermute | solution.py:41
  16.5 19.8 %collective-permute-start.18 = (bf16[128,1024]{1,0:T(8,128)(2,1)S(1)}, bf16[128,1024]{1,0:T(8,128)(2,1)S(1)}, u32[]{:S(2)}, u32[]{:S(2)}) collective-permute-start(bf16[128,1024]{1,0:T(8,128)(2,1)S(1)} %get-tuple-element.28.refs_0_), channel_id=1, source_target_pairs={{0,2},{1,3},{2,0},{3,1},{4,6},{5,7},{6,4},{7,5},{8,10},{9,11},{10,... | collective-permute-start | bytes 786440 | tf_op jit(solution)/shard_map/ppermute | solution.py:41
  18.5 18.1 %collective-permute-start.17 = (bf16[128,1024]{1,0:T(8,128)(2,1)S(1)}, bf16[128,1024]{1,0:T(8,128)(2,1)S(1)}, u32[]{:S(2)}, u32[]{:S(2)}) collective-permute-start(bf16[128,1024]{1,0:T(8,128)(2,1)S(1)} %get-tuple-element.29.refs_1_), channel_id=1, source_target_pairs={{0,1},{1,0},{2,3},{3,2},{4,5},{5,4},{6,7},{7,6},{8,9},{9,8},{10,11... | collective-permute-start | bytes 786440 | tf_op jit(solution)/shard_map/ppermute | solution.py:41
  20.6 11.2 %collective-permute-start.3 = (bf16[128,1024]{1,0:T(8,128)(2,1)S(1)}, bf16[128,1024]{1,0:T(8,128)(2,1)S(1)}, u32[]{:S(2)}, u32[]{:S(2)}) collective-permute-start(bf16[128,1024]{1,0:T(8,128)(2,1)S(1)} %get-tuple-element.29.refs_1_), channel_id=1, source_target_pairs={{0,2},{1,3},{2,0},{3,1},{4,6},{5,7},{6,4},{7,5},{8,10},{9,11},{10,... | collective-permute-start | bytes 786440 | tf_op jit(solution)/shard_map/ppermute | solution.py:41
  22.2 12.4 %collective-permute-start.23 = (bf16[128,1024]{1,0:T(8,128)(2,1)S(1)}, bf16[128,1024]{1,0:T(8,128)(2,1)S(1)}, u32[]{:S(2)}, u32[]{:S(2)}) collective-permute-start(bf16[128,1024]{1,0:T(8,128)(2,1)S(1)} %collective-permute-done.22.refs_4_), channel_id=1, source_target_pairs={{0,1},{1,0},{2,3},{3,2},{4,5},{5,4},{6,7},{7,6},{8,9},{9,8},{10,11... | collective-permute-start | bytes 786440 | tf_op jit(solution)/shard_map/ppermute | solution.py:41
  25.6 12.8 %collective-permute-start.24 = (bf16[128,1024]{1,0:T(8,128)(2,1)S(1)}, bf16[128,1024]{1,0:T(8,128)(2,1)S(1)}, u32[]{:S(2)}, u32[]{:S(2)}) collective-permute-start(bf16[128,1024]{1,0:T(8,128)(2,1)S(1)} %collective-permute-done.21.refs_3_), channel_id=1, source_target_pairs={{0,2},{1,3},{2,0},{3,1},{4,6},{5,7},{6,4},{7,5},{8,10},{9,11},{10,... | collective-permute-start | bytes 786440 | tf_op jit(solution)/shard_map/ppermute | solution.py:41
  32.7 31.4 %collective-permute-start.6 = (bf16[128,1024]{1,0:T(8,128)(2,1)S(1)}, bf16[128,1024]{1,0:T(8,128)(2,1)S(1)}, u32[]{:S(2)}, u32[]{:S(2)}) collective-permute-start(bf16[128,1024]{1,0:T(8,128)(2,1)S(1)} %get-tuple-element.30.refs_0_), channel_id=1, source_target_pairs={{0,2},{1,3},{2,0},{3,1},{4,6},{5,7},{6,4},{7,5},{8,10},{9,11},{10,... | collective-permute-start | bytes 786440 | tf_op jit(solution)/shard_map/ppermute | solution.py:41
  34.6 30.0 %collective-permute-start.5 = (bf16[128,1024]{1,0:T(8,128)(2,1)S(1)}, bf16[128,1024]{1,0:T(8,128)(2,1)S(1)}, u32[]{:S(2)}, u32[]{:S(2)}) collective-permute-start(bf16[128,1024]{1,0:T(8,128)(2,1)S(1)} %get-tuple-element.31.refs_1_), channel_id=1, source_target_pairs={{0,1},{1,0},{2,3},{3,2},{4,5},{5,4},{6,7},{7,6},{8,9},{9,8},{10,11... | collective-permute-start | bytes 786440 | tf_op jit(solution)/shard_map/ppermute | solution.py:41
  36.3 11.0 %collective-permute-start.19 = (bf16[128,1024]{1,0:T(8,128)(2,1)S(1)}, bf16[128,1024]{1,0:T(8,128)(2,1)S(1)}, u32[]{:S(2)}, u32[]{:S(2)}) collective-permute-start(bf16[128,1024]{1,0:T(8,128)(2,1)S(1)} %collective-permute-done.18.refs_4_), channel_id=1, source_target_pairs={{0,1},{1,0},{2,3},{3,2},{4,5},{5,4},{6,7},{7,6},{8,9},{9,8},{10,11... | collective-permute-start | bytes 786440 | tf_op jit(solution)/shard_map/ppermute | solution.py:41
  36.6 10.8 %collective-permute-start.20 = (bf16[128,1024]{1,0:T(8,128)(2,1)S(1)}, bf16[128,1024]{1,0:T(8,128)(2,1)S(1)}, u32[]{:S(2)}, u32[]{:S(2)}) collective-permute-start(bf16[128,1024]{1,0:T(8,128)(2,1)S(1)} %collective-permute-done.17.refs_3_), channel_id=1, source_target_pairs={{0,2},{1,3},{2,0},{3,1},{4,6},{5,7},{6,4},{7,5},{8,10},{9,11},{10,... | collective-permute-start | bytes 786440 | tf_op jit(solution)/shard_map/ppermute | solution.py:41
  45.2 0.8 copy-start.7
  46.0 0.8 copy-start.8
  60.4 9.3 %collective-permute-start.28 = (bf16[128,1024]{1,0:T(8,128)(2,1)S(1)}, bf16[128,1024]{1,0:T(8,128)(2,1)S(1)}, u32[]{:S(2)}, u32[]{:S(2)}) collective-permute-start(bf16[128,1024]{1,0:T(8,128)(2,1)S(1)} %get-tuple-element.48), channel_id=1, source_target_pairs={{0,1},{1,0},{2,3},{3,2},{4,5},{5,4},{6,7},{7,6},{8,9},{9,8},{10,11... | collective-permute-start | bytes 786440 | tf_op jit(solution)/shard_map/ppermute | solution.py:41
  62.3 10.1 %collective-permute-start.26 = (bf16[128,1024]{1,0:T(8,128)(2,1)S(1)}, bf16[128,1024]{1,0:T(8,128)(2,1)S(1)}, u32[]{:S(2)}, u32[]{:S(2)}) collective-permute-start(bf16[128,1024]{1,0:T(8,128)(2,1)S(1)} %get-tuple-element.46), channel_id=1, source_target_pairs={{0,2},{1,3},{2,0},{3,1},{4,6},{5,7},{6,4},{7,5},{8,10},{9,11},{10,... | collective-permute-start | bytes 786440 | tf_op jit(solution)/shard_map/ppermute | solution.py:41
  63.8 11.6 %collective-permute-start.4 = (bf16[128,1024]{1,0:T(8,128)(2,1)S(1)}, bf16[128,1024]{1,0:T(8,128)(2,1)S(1)}, u32[]{:S(2)}, u32[]{:S(2)}) collective-permute-start(bf16[128,1024]{1,0:T(8,128)(2,1)S(1)} %get-tuple-element.30.refs_0_), channel_id=1, source_target_pairs={{0,1},{1,0},{2,3},{3,2},{4,5},{5,4},{6,7},{7,6},{8,9},{9,8},{10,11... | collective-permute-start | bytes 786440 | tf_op jit(solution)/shard_map/ppermute | solution.py:41
  64.1 13.1 %collective-permute-start.7 = (bf16[128,1024]{1,0:T(8,128)(2,1)S(1)}, bf16[128,1024]{1,0:T(8,128)(2,1)S(1)}, u32[]{:S(2)}, u32[]{:S(2)}) collective-permute-start(bf16[128,1024]{1,0:T(8,128)(2,1)S(1)} %get-tuple-element.31.refs_1_), channel_id=1, source_target_pairs={{0,2},{1,3},{2,0},{3,1},{4,6},{5,7},{6,4},{7,5},{8,10},{9,11},{10,... | collective-permute-start | bytes 786440 | tf_op jit(solution)/shard_map/ppermute | solution.py:41
  64.6 16.4 %collective-permute-start.8 = (bf16[128,1024]{1,0:T(8,128)(2,1)S(1)}, bf16[128,1024]{1,0:T(8,128)(2,1)S(1)}, u32[]{:S(2)}, u32[]{:S(2)}) collective-permute-start(bf16[128,1024]{1,0:T(8,128)(2,1)S(1)} %collective-permute-done.6.refs_4_), channel_id=1, source_target_pairs={{0,1},{1,0},{2,3},{3,2},{4,5},{5,4},{6,7},{7,6},{8,9},{9,8},{10,11... | collective-permute-start | bytes 786440 | tf_op jit(solution)/shard_map/ppermute | solution.py:41
  69.8 13.0 %collective-permute-start.9 = (bf16[128,1024]{1,0:T(8,128)(2,1)S(1)}, bf16[128,1024]{1,0:T(8,128)(2,1)S(1)}, u32[]{:S(2)}, u32[]{:S(2)}) collective-permute-start(bf16[128,1024]{1,0:T(8,128)(2,1)S(1)} %collective-permute-done.5.refs_3_), channel_id=1, source_target_pairs={{0,2},{1,3},{2,0},{3,1},{4,6},{5,7},{6,4},{7,5},{8,10},{9,11},{10,... | collective-permute-start | bytes 786440 | tf_op jit(solution)/shard_map/ppermute | solution.py:41
  72.4 21.7 %collective-permute-start.25 = (bf16[128,1024]{1,0:T(8,128)(2,1)S(1)}, bf16[128,1024]{1,0:T(8,128)(2,1)S(1)}, u32[]{:S(2)}, u32[]{:S(2)}) collective-permute-start(bf16[128,1024]{1,0:T(8,128)(2,1)S(1)} %get-tuple-element.44), channel_id=1, source_target_pairs={{0,1},{1,0},{2,3},{3,2},{4,5},{5,4},{6,7},{7,6},{8,9},{9,8},{10,11... | collective-permute-start | bytes 786440 | tf_op jit(solution)/shard_map/ppermute | solution.py:41
  75.4 23.3 %copy-start.2 = (f32[1,128,2048]{2,1,0:T(8,128)S(1)}, f32[1,128,2048]{2,1,0:T(8,128)}, u32[]{:S(2)}) copy-start(f32[1,128,2048]{2,1,0:T(8,128)} %param.9) | copy-start | bytes 3145732
  75.4 23.3 %copy-start.4 = (f32[128,2048]{1,0:T(8,128)S(1)}, f32[128,2048]{1,0:T(8,128)}, u32[]{:S(2)}) copy-start(f32[128,2048]{1,0:T(8,128)} %get-tuple-element.42.own_ref) | copy-start | bytes 3145732
  75.4 20.3 %collective-permute-start.30 = (bf16[128,1024]{1,0:T(8,128)(2,1)S(1)}, bf16[128,1024]{1,0:T(8,128)(2,1)S(1)}, u32[]{:S(2)}, u32[]{:S(2)}) collective-permute-start(bf16[128,1024]{1,0:T(8,128)(2,1)S(1)} %get-tuple-element.49), channel_id=1, source_target_pairs={{0,2},{1,3},{2,0},{3,1},{4,6},{5,7},{6,4},{7,5},{8,10},{9,11},{10,... | collective-permute-start | bytes 786440 | tf_op jit(solution)/shard_map/ppermute | solution.py:41
  77.1 18.5 %collective-permute-start.29 = (bf16[128,1024]{1,0:T(8,128)(2,1)S(1)}, bf16[128,1024]{1,0:T(8,128)(2,1)S(1)}, u32[]{:S(2)}, u32[]{:S(2)}) collective-permute-start(bf16[128,1024]{1,0:T(8,128)(2,1)S(1)} %add_convert_fusion), channel_id=1, source_target_pairs={{0,2},{1,3},{2,0},{3,1},{4,6},{5,7},{6,4},{7,5},{8,10},{9,11},{10,... | collective-permute-start | bytes 786440 | tf_op jit(solution)/shard_map/ppermute | solution.py:41
  81.0 17.7 %collective-permute-start.27 = (bf16[128,1024]{1,0:T(8,128)(2,1)S(1)}, bf16[128,1024]{1,0:T(8,128)(2,1)S(1)}, u32[]{:S(2)}, u32[]{:S(2)}) collective-permute-start(bf16[128,1024]{1,0:T(8,128)(2,1)S(1)} %add_convert_fusion.1), channel_id=1, source_target_pairs={{0,1},{1,0},{2,3},{3,2},{4,5},{5,4},{6,7},{7,6},{8,9},{9,8},{10,11... | collective-permute-start | bytes 786440 | tf_op jit(solution)/shard_map/ppermute | solution.py:41
  93.8 6.8 %collective-permute-start.14 = (bf16[128,1024]{1,0:T(8,128)(2,1)S(1)}, bf16[128,1024]{1,0:T(8,128)(2,1)S(1)}, u32[]{:S(2)}, u32[]{:S(2)}) collective-permute-start(bf16[128,1024]{1,0:T(8,128)(2,1)S(1)} %get-tuple-element.37), channel_id=1, source_target_pairs={{0,1},{1,0},{2,3},{3,2},{4,5},{5,4},{6,7},{7,6},{8,9},{9,8},{10,11... | collective-permute-start | bytes 786440 | tf_op jit(solution)/shard_map/ppermute | solution.py:41
  94.1 10.1 %collective-permute-start.12 = (bf16[128,1024]{1,0:T(8,128)(2,1)S(1)}, bf16[128,1024]{1,0:T(8,128)(2,1)S(1)}, u32[]{:S(2)}, u32[]{:S(2)}) collective-permute-start(bf16[128,1024]{1,0:T(8,128)(2,1)S(1)} %get-tuple-element.35), channel_id=1, source_target_pairs={{0,2},{1,3},{2,0},{3,1},{4,6},{5,7},{6,4},{7,5},{8,10},{9,11},{10,... | collective-permute-start | bytes 786440 | tf_op jit(solution)/shard_map/ppermute | solution.py:41
  95.6 20.9 %collective-permute-start.10 = (bf16[128,2048]{1,0:T(8,128)(2,1)}, bf16[128,2048]{1,0:T(8,128)(2,1)S(1)}, u32[]{:S(2)}, u32[]{:S(2)}) collective-permute-start(bf16[128,2048]{1,0:T(8,128)(2,1)} %get-tuple-element.32), channel_id=1, source_target_pairs={{0,4},{1,5},{2,6},{3,7},{4,8},{5,9},{6,10},{7,11},{8,12},{9,13},{1... | collective-permute-start | bytes 1572872 | tf_op jit(solution)/shard_map/ppermute | solution.py:51
  95.7 19.0 %collective-permute-start.11 = (bf16[128,1024]{1,0:T(8,128)(2,1)S(1)}, bf16[128,1024]{1,0:T(8,128)(2,1)S(1)}, u32[]{:S(2)}, u32[]{:S(2)}) collective-permute-start(bf16[128,1024]{1,0:T(8,128)(2,1)S(1)} %get-tuple-element.33), channel_id=1, source_target_pairs={{0,5},{1,4},{2,7},{3,6},{4,9},{5,8},{6,11},{7,10},{8,13},{9,12},{1... | collective-permute-start | bytes 786440 | tf_op jit(solution)/shard_map/ppermute | solution.py:51
  98.7 17.8 %collective-permute-start.16 = (bf16[128,1024]{1,0:T(8,128)(2,1)S(1)}, bf16[128,1024]{1,0:T(8,128)(2,1)S(1)}, u32[]{:S(2)}, u32[]{:S(2)}) collective-permute-start(bf16[128,1024]{1,0:T(8,128)(2,1)S(1)} %get-tuple-element.38), channel_id=1, source_target_pairs={{0,6},{1,7},{2,4},{3,5},{4,10},{5,11},{6,8},{7,9},{8,14},{9,15},{1... | collective-permute-start | bytes 786440 | tf_op jit(solution)/shard_map/ppermute | solution.py:51
  98.7 5.4 %copy-start.10 = (f32[128,1024]{1,0:T(8,128)S(1)}, f32[128,1024]{1,0:T(8,128)}, u32[]{:S(2)}) copy-start(f32[128,1024]{1,0:T(8,128)} %get-tuple-element.36) | copy-start | bytes 1572868
  98.7 5.5 %copy-start.9 = (f32[128,1024]{1,0:T(8,128)S(1)}, f32[128,1024]{1,0:T(8,128)}, u32[]{:S(2)}) copy-start(f32[128,1024]{1,0:T(8,128)} %get-tuple-element.34) | copy-start | bytes 1572868
  100.6 24.9 %collective-permute-start.31 = (bf16[128,2048]{1,0:T(8,128)(2,1)S(1)}, bf16[128,2048]{1,0:T(8,128)(2,1)S(1)}, u32[]{:S(2)}, u32[]{:S(2)}) collective-permute-start(bf16[128,2048]{1,0:T(8,128)(2,1)S(1)} %input_grad.1), channel_id=1, source_target_pairs={{0,28},{4,0},{8,4},{12,8},{16,12},{20,16},{24,20},{28,24},{1,29},{... | collective-permute-start | bytes 1572872 | tf_op jit(solution)/shard_map/ppermute | solution.py:57
  104.2 16.1 %collective-permute-start.15 = (bf16[128,1024]{1,0:T(8,128)(2,1)S(1)}, bf16[128,1024]{1,0:T(8,128)(2,1)S(1)}, u32[]{:S(2)}, u32[]{:S(2)}) collective-permute-start(bf16[128,1024]{1,0:T(8,128)(2,1)S(1)} %add_convert_fusion.2), channel_id=1, source_target_pairs={{0,6},{1,7},{2,4},{3,5},{4,10},{5,11},{6,8},{7,9},{8,14},{9,15},{1... | collective-permute-start | bytes 786440 | tf_op jit(solution)/shard_map/ppermute | solution.py:51
  114.6 9.8 %collective-permute-start.13 = (bf16[128,1024]{1,0:T(8,128)(2,1)S(1)}, bf16[128,1024]{1,0:T(8,128)(2,1)S(1)}, u32[]{:S(2)}, u32[]{:S(2)}) collective-permute-start(bf16[128,1024]{1,0:T(8,128)(2,1)S(1)} %add_convert_fusion.3), channel_id=1, source_target_pairs={{0,5},{1,4},{2,7},{3,6},{4,9},{5,8},{6,11},{7,10},{8,13},{9,12},{1... | collective-permute-start | bytes 786440 | tf_op jit(solution)/shard_map/ppermute | solution.py:51
where the time goes:
time: 127 us
  waiting for transfers between devices  41.3 us (33%)
  starting transfers between devices  40.1 us (32%)
  Pallas kernels  35 us (28%)
  local copies, waits for them, and re-layouts  4.78 us (4%)
  other arithmetic  4.7 us (4%)
    pallas_call x8, Pallas kernels, call(): pl.pallas_call(kernel, out_shape=out_shapes, in_specs=in_specs, out_specs...  35 us
    ppermute x26, starting transfers between devices, across(): return lax.ppermute(value, 'seq', [(i, i ^ 1 << bit) for i in range(count)])  33.5 us
    ppermute x26, waiting for transfers between devices, across(): return lax.ppermute(value, 'seq', [(i, i ^ 1 << bit) for i in range(count)])  21.2 us
    ppermute x5, waiting for transfers between devices, across_and_on(): return lax.ppermute(value, ('pipe', 'seq'), pairs)  20 us
    unnamed x22, local copies, waits for them, and re-layouts  4.78 us
    ppermute x1, starting transfers between devices, passed_along(): return lax.ppermute(value, axis, pairs)  3.51 us
    ppermute x5, starting transfers between devices, across_and_on(): return lax.ppermute(value, ('pipe', 'seq'), pairs)  3.1 us
  transfers between devices with their start and end apart: 32, of which 15 were waited for; matrix products, arithmetic and copies ran while one was open for 3% of the time, Pallas kernels for 27%

commit v1 on v0

v1 whole, which is shorter than its diff:
```python
import functools
import math

import jax
import jax.numpy as jnp
from jax import lax
from jax.experimental import pallas as pl
from jax.experimental.pallas import tpu as pltpu
from jax.sharding import PartitionSpec as P

HD = 128
LANES = 128
CHUNK = 256
EXP2_SCALE = HD ** (-0.5) * math.log2(math.e)
NT = (((1,), (1,)), ((), ()))
TN = (((0,), (0,)), ((), ()))
HEADS_WEIGHT = 8_000_000_000
TERMS_WEIGHT = 3_000_000_000
INPUT_GRAD_WEIGHT = 8_000_000_000
LAST_SUM_WEIGHT = 8_000_000_000
VMEM_LIMIT = 50 * 1024 * 1024


def bits_of(number):
    return [bit for bit in range(number.bit_length()) if (number >> bit) & 1]


def by_distance(count):
    return sorted(range(1, count), key=lambda rel: (len(bits_of(rel)), rel))


def part_bounds(rows, count):
    parts = 2 if count > 2 else 1
    return [(rows * i // parts, rows * (i + 1) // parts) for i in range(parts)]


def last_bit(rel, part):
    bits = bits_of(rel)
    return bits[part % len(bits)]


def ways_to(rel, bounds):
    ways = {}
    for part, (low, high) in enumerate(bounds):
        bit = last_bit(rel, part)
        ways[bit] = (min(low, ways.get(bit, (low, high))[0]), high)
    return [(bit, low, high) for bit, (low, high) in ways.items()]


def across(value, bit):
    count = lax.axis_size("seq")
    return lax.ppermute(value, "seq", [(i, i ^ (1 << bit)) for i in range(count)])


def across_and_on(value, flip):
    count, sections = lax.axis_size("seq"), lax.axis_size("pipe")
    pairs = [
        (p * count + i, (p + 1) % sections * count + (i ^ flip))
        for p in range(sections)
        for i in range(count)
    ]
    return lax.ppermute(value, ("pipe", "seq"), pairs)


def passed_along(value, axis, steps):
    count = lax.axis_size(axis)
    pairs = [(source, (source + steps) % count) for source in range(count)]
    return lax.ppermute(value, axis, pairs)


def onward_rows(count, bounds):
    return [
        (rel ^ (1 << bit), bit, low, high)
        for rel in by_distance(count)
        for bit, low, high in ways_to(rel, bounds)
    ]


def gather_first(own, what):
    count = lax.axis_size("seq")
    blocks = {(0, 0): own}
    for rel in by_distance(count):
        if len(bits_of(rel)) == 1:
            with jax.named_scope(f"gather_{what}_block{rel}"):
                blocks[rel, 0] = across(own, bits_of(rel)[0])
    return blocks


def second_hops(blocks, rows):
    count = lax.axis_size("seq")
    return [
        (blocks[rel, 0], low, high)
        for rel, bit, low, high in onward_rows(count, part_bounds(rows, count))
        if len(bits_of(rel)) == 1
    ]


def gather_rest(blocks, picked, what):
    count = lax.axis_size("seq")
    rows = blocks[0, 0].shape[0]
    picked = list(picked)
    for rel, bit, low, high in onward_rows(count, part_bounds(rows, count)):
        if rel == 0:
            continue
        value = picked.pop(0) if len(bits_of(rel)) == 1 else blocks[rel, low]
        if value.shape[0] > high - low:
            value = value[: high - low]
        with jax.named_scope(f"gather_{what}_block{rel ^ (1 << bit)}_row{low}"):
            blocks[rel ^ (1 << bit), low] = across(value, bit)
    return blocks


def messages_of(rows, count):
    bounds = part_bounds(rows, count)
    parts = range(len(bounds))
    later = {
        (rel ^ (1 << last_bit(rel, part)), part)
        for rel in range(1, count)
        for part in parts
        if len(bits_of(rel)) > 1
    }
    keys = [(rel, part) for rel in reversed(by_distance(count)) for part in parts]
    groups = {}
    for key in keys:
        if key not in later:
            groups.setdefault(last_bit(*key), []).append(key)
    return list(groups.values()), [key for key in keys if key in later]


def scatter_blocks(own, terms, rows, send_last, what, after=(), close=False):
    count = lax.axis_size("seq")
    bounds = part_bounds(rows, count)
    groups, later = messages_of(rows, count)
    arrived, near, last, sums = {}, {}, {}, []

    def send(value, keys):
        bit = last_bit(*keys[0])
        targets = [(rel ^ (1 << bit), part) for rel, part in keys]
        onward = any(rel for rel, _ in targets)
        with jax.named_scope(f"scatter_{what}_block{keys[0][0]}_part{keys[0][1]}"):
            moved = (across if onward else send_last)(value, bit)
        first = 0
        for key, target in zip(keys, targets):
            if target[0]:
                arrived.setdefault(target, []).append((moved, first))
            else:
                (near if onward else last)[key] = (moved, first)
            first += bounds[key[1]][1] - bounds[key[1]][0]

    for value, keys in zip(terms, groups):
        send(value, keys)
    values = dict(zip(later, terms[len(groups) :]))
    for level in sorted({len(bits_of(rel)) for rel, _ in later}, reverse=True):
        keys = [key for key in later if len(bits_of(key[0])) == level]
        totals = [(values[key], [(0, *piece) for piece in arrived[key]]) for key in keys]
        if close and level == 1:
            totals.append((own, [(bounds[key[1]][0], *near[key]) for key in sorted(near)]))
        results = sum_rows(totals, bounds, after)
        if close and level == 1:
            own = results[-1]
        sums += results[: len(keys)]
        for key, value in zip(keys, results):
            send(value, [key])
    if not close:
        last.update(near)
    elif not later:
        own = own.astype(jnp.bfloat16)
    return own, last, sums


def call(kernel, out_shapes, operands, in_specs, scratch=(), flops=1, name=None):
    return pl.pallas_call(
        kernel,
        out_shape=out_shapes,
        in_specs=in_specs,
        out_specs=[pl.BlockSpec(memory_space=pltpu.VMEM)] * len(out_shapes),
        scratch_shapes=list(scratch),
        compiler_params=pltpu.CompilerParams(vmem_limit_bytes=VMEM_LIMIT),
        cost_estimate=pl.CostEstimate(flops=int(flops), bytes_accessed=1, transcendentals=0),
        name=name,
    )(*operands)


ANY = pl.BlockSpec(memory_space=pl.ANY)
VMEM = pl.BlockSpec(memory_space=pltpu.VMEM)


def picked_shapes(pieces):
    return [
        jax.ShapeDtypeStruct((high - low, value.shape[1]), value.dtype)
        for value, low, high in pieces
    ]


def pick(pieces, in_refs, out_refs):
    for (_, low, high), in_ref, out_ref in zip(pieces, in_refs, out_refs):
        out_ref[...] = in_ref[low:high, :]


def normed_rows(inputs, gain, pieces=(), after=()):
    rows, width = inputs.shape
    n = len(pieces)

    def kernel(x_ref, gain_ref, *refs):
        refs = refs[:n] + refs[n + len(after) :]
        out_ref, inv_ref = refs[n : n + 2]
        x = x_ref[...]
        inv = lax.rsqrt(jnp.mean(x * x, -1, keepdims=True) + 1e-05)
        out_ref[...] = (x * inv * gain_ref[...]).astype(jnp.bfloat16)
        inv_ref[...] = inv
        pick(pieces, refs[:n], refs[n + 2 :])

    return call(
        kernel,
        [
            jax.ShapeDtypeStruct((rows, width), jnp.bfloat16),
            jax.ShapeDtypeStruct((rows, 1), jnp.float32),
        ]
        + picked_shapes(pieces),
        [inputs, gain] + [value for value, _, _ in pieces] + list(after),
        [VMEM] * (2 + n) + [ANY] * len(after),
        name="norm",
    )


def picked_rows(pieces, after=()):
    n = len(pieces)

    def kernel(*refs):
        pick(pieces, refs[:n], refs[n + len(after) :])

    return call(
        kernel,
        picked_shapes(pieces),
        [value for value, _, _ in pieces] + list(after),
        [VMEM] * n + [ANY] * len(after),
        name="pick",
    )


def cast_rows(inputs, after=()):
    def kernel(x_ref, *refs):
        refs[len(after)][...] = x_ref[...].astype(jnp.bfloat16)

    return call(
        kernel,
        [jax.ShapeDtypeStruct(inputs.shape, jnp.bfloat16)],
        (inputs, *after),
        [VMEM] + [ANY] * len(after),
        name="cast",
    )[0]


def sum_rows(totals, bounds, after=()):
    height = bounds[0][1] - bounds[0][0]
    pieces = [piece for _, pieces in totals for piece in pieces]
    n, m = len(totals), len(pieces)

    def kernel(*refs):
        terms, arrivals, outs = refs[:n], list(refs[n : n + m]), refs[-n:]
        for (term, moved), term_ref, out_ref in zip(totals, terms, outs):
            found = [(row, first, arrivals.pop(0)) for row, _, first in moved]
            for low in range(0, term.shape[0], height):
                total = term_ref[low : low + height, :]
                for row, first, ref in found:
                    if row == low:
                        total = total + ref[first : first + height, :].astype(jnp.float32)
                out_ref[low : low + height, :] = total.astype(jnp.bfloat16)

    return call(
        kernel,
        [jax.ShapeDtypeStruct(term.shape, jnp.bfloat16) for term, _ in totals],
        [term for term, _ in totals] + [value for _, value, _ in pieces] + list(after),
        [VMEM] * (n + m) + [ANY] * len(after),
        name="sum_rows",
    )


def block_copies(block_refs, keys, rows, all_rows, sems):
    return [
        pltpu.make_async_copy(
            ref, all_rows.at[pl.ds(rel * rows + low, ref.shape[0]), :], sems.at[i]
        )
        for i, (ref, (rel, low)) in enumerate(zip(block_refs, keys))
    ]


def turned(values, cosine, sine):
    return values * cosine + pltpu.roll(values, HD // 2, 1) * sine


def project_into(rows_ref, weight_ref, out_ref, cos_ref=None, sin_ref=None):
    features = out_ref.shape[1]
    for low in range(0, features, CHUNK):
        high = min(low + CHUNK, features)
        values = jnp.dot(
            rows_ref[...], weight_ref[:, low:high], preferred_element_type=jnp.float32
        )
        for head in range(0, high - low, HD):
            piece = values[:, head : head + HD]
            if cos_ref is not None:
                piece = turned(piece, cos_ref[...], sin_ref[...])
            out_ref[:, low + head : low + head + HD] = piece.astype(jnp.bfloat16)


def project(blocks, weights, cosine, sine, rows):
    keys = sorted(blocks)
    length, width = cosine.shape[0], blocks[0, 0].shape[1]
    features = weights[0].shape[1]
    n = len(keys)

    def kernel(*refs):
        block_refs, weight_refs = refs[:n], refs[n : n + 3]
        cos_ref, sin_ref = refs[n + 3 : n + 5]
        outs = refs[n + 5 : n + 8]
        all_rows, held, sems = refs[n + 8 :]
        copies = block_copies(block_refs, keys, rows, all_rows, sems)
        loads = [
            pltpu.make_async_copy(weight_refs[i], held.at[i], sems.at[n + i]) for i in range(3)
        ]
        for copy in copies + loads:
            copy.start()
        for copy in copies:
            copy.wait()
        for i in range(3):
            loads[i].wait()
            tables = (cos_ref, sin_ref) if i < 2 else ()
            project_into(all_rows, held.at[i], outs[i], *tables)

    return call(
        kernel,
        [jax.ShapeDtypeStruct((length, features), jnp.bfloat16)] * 3,
        [blocks[key] for key in keys] + list(weights) + [cosine, sine],
        [ANY] * (n + 3) + [VMEM, VMEM],
        [
            pltpu.VMEM((length, width), jnp.bfloat16),
            pltpu.VMEM((3, width, features), jnp.bfloat16),
            pltpu.SemaphoreType.DMA((n + 3,)),
        ],
        name="project",
    )


def term_outs(rows, width, count):
    bounds = part_bounds(rows, count)
    groups, later = messages_of(rows, count)

    def shape(keys, dtype):
        height = sum(bounds[part][1] - bounds[part][0] for _, part in keys)
        return jax.ShapeDtypeStruct((height, width), dtype)

    return [shape(keys, jnp.bfloat16) for keys in groups] + [
        shape([key], jnp.float32) for key in later
    ]


def store_terms(values, low, refs, rows, count):
    bounds = part_bounds(rows, count)
    groups, later = messages_of(rows, count)
    for ref, keys in zip(refs, groups + [[key] for key in later]):
        at = 0
        for rel, part in keys:
            first, last = bounds[part]
            piece = values[rel * rows + first : rel * rows + last]
            ref[at : at + last - first, low : low + values.shape[1]] = piece.astype(ref.dtype)
            at += last - first


def backward_heads(blocks, qkv, weight, cosine, sine, rows):
    in_keys = sorted(blocks)
    length, width = cosine.shape[0], blocks[0, 0].shape[1]
    features = qkv[0].shape[1]
    n = len(in_keys)
    step = min(length, 512)

    def kernel(*refs):
        block_refs, weight_ref = refs[:n], refs[n]
        q_ref, k_ref, v_ref, cos_ref, sin_ref = refs[n + 1 : n + 6]
        d_qkv = refs[n + 6 : n + 9]
        all_rows, held, d_attn, sems = refs[n + 9 :]
        copies = block_copies(block_refs, in_keys, rows, all_rows, sems)
        copies.append(pltpu.make_async_copy(weight_ref, held, sems.at[n]))
        for copy in copies:
            copy.start()
        for copy in copies:
            copy.wait()
        project_into(all_rows, held, d_attn)

        for head in range(features // HD):
            cols = slice(head * HD, (head + 1) * HD)
            key, value = k_ref[:, cols], v_ref[:, cols]
            d_key, d_value = 0.0, 0.0
            for low in range(0, length, step):
                part = slice(low, low + step)
                query, grad = q_ref[part, cols], d_attn[part, cols]
                scores = lax.dot_general(key, query, NT, preferred_element_type=jnp.float32)
                top = jnp.max(scores, 0, keepdims=True)
                raised = jnp.exp2((scores - top) * EXP2_SCALE)
                probs = raised * (1.0 / jnp.sum(raised, 0, keepdims=True))
                d_value += jnp.dot(
                    probs.astype(jnp.bfloat16), grad, preferred_element_type=jnp.float32
                )
                d_probs = lax.dot_general(value, grad, NT, preferred_element_type=jnp.float32)
                delta = jnp.sum(probs * d_probs, 0, keepdims=True)
                d_scores = (probs * (d_probs - delta) * HD ** (-0.5)).astype(jnp.bfloat16)
                d_key += jnp.dot(d_scores, query, preferred_element_type=jnp.float32)
                d_query = lax.dot_general(
                    key, d_scores, TN, preferred_element_type=jnp.float32
                ).T
                d_qkv[0][part, cols] = turned(
                    d_query, cos_ref[part, :], -sin_ref[part, :]
                ).astype(jnp.bfloat16)
            d_qkv[1][:, cols] = turned(d_key, cos_ref[...], -sin_ref[...]).astype(jnp.bfloat16)
            d_qkv[2][:, cols] = d_value.astype(jnp.bfloat16)

    return call(
        kernel,
        [jax.ShapeDtypeStruct((length, features), jnp.bfloat16)] * 3,
        [blocks[key] for key in in_keys] + [weight] + list(qkv) + [cosine, sine],
        [ANY] * (n + 1) + [VMEM] * 5,
        [
            pltpu.VMEM((length, width), jnp.bfloat16),
            pltpu.VMEM((width, features), jnp.bfloat16),
            pltpu.VMEM((length, features), jnp.bfloat16),
            pltpu.SemaphoreType.DMA((n + 1,)),
        ],
        flops=HEADS_WEIGHT,
        name="backward_heads",
    )


def backward_terms(d_qkv, weights, rows, count, after=()):
    length, features = d_qkv[0].shape
    width = weights[0].shape[0]
    shapes = term_outs(rows, width, count)

    def kernel(*refs):
        grads, weight_refs = refs[:3], refs[3:6]
        own_ref, *outs = refs[6 + len(after) : -2]
        held, sems = refs[-2:]
        loads = [pltpu.make_async_copy(weight_refs[i], held.at[i], sems.at[i]) for i in range(3)]
        for load in loads:
            load.start()
        for load in loads:
            load.wait()
        for low in range(0, width, CHUNK):
            total = 0.0
            for i in range(3):
                total += lax.dot_general(
                    grads[i][...],
                    held[i, low : low + CHUNK, :],
                    NT,
                    preferred_element_type=jnp.float32,
                )
            own_ref[:, low : low + CHUNK] = total[:rows]
            store_terms(total, low, outs, rows, count)

    own, *terms = call(
        kernel,
        [jax.ShapeDtypeStruct((rows, width), jnp.float32)] + shapes,
        list(d_qkv) + list(weights) + list(after),
        [VMEM] * 3 + [ANY] * (3 + len(after)),
        [pltpu.VMEM((3, width, features), jnp.bfloat16), pltpu.SemaphoreType.DMA((3,))],
        flops=TERMS_WEIGHT,
        name="backward_terms",
    )
    return own, terms


def forward_terms(qkv, act_in, weight, rows, count, after=()):
    length, features = qkv[0].shape
    width = weight.shape[0]
    shapes = term_outs(rows, width, count)
    step = min(length, 512)

    def kernel(*refs):
        q_ref, k_ref, v_ref, act_ref, weight_ref = refs[:5]
        own_ref, *outs = refs[5 + len(after) : -3]
        held, attn, sem = refs[-3:]
        load = pltpu.make_async_copy(weight_ref, held, sem)
        load.start()
        for head in range(features // HD):
            cols = slice(head * HD, (head + 1) * HD)
            for low in range(0, length, step):
                part = slice(low, low + step)
                scores = lax.dot_general(
                    q_ref[part, cols], k_ref[:, cols], NT, preferred_element_type=jnp.float32
                )
                top = jnp.max(scores, 1, keepdims=True)
                raised = jnp.exp2((scores - top) * EXP2_SCALE)
                total = jnp.sum(raised, 1, keepdims=True)
                mixed = jnp.dot(
                    raised.astype(jnp.bfloat16), v_ref[:, cols], preferred_element_type=jnp.float32
                )
                attn[part, cols] = (mixed * (1.0 / total)).astype(jnp.bfloat16)

        load.wait()
        for low in range(0, width, CHUNK):
            total = lax.dot_general(
                attn[...], held[low : low + CHUNK, :], NT, preferred_element_type=jnp.float32
            )
            own_ref[:, low : low + CHUNK] = total[:rows] + act_ref[:, low : low + CHUNK]
            store_terms(total, low, outs, rows, count)

    own, *terms = call(
        kernel,
        [jax.ShapeDtypeStruct((rows, width), jnp.float32)] + shapes,
        list(qkv) + [act_in, weight, *after],
        [VMEM] * 4 + [ANY] * (1 + len(after)),
        [
            pltpu.VMEM((width, features), jnp.bfloat16),
            pltpu.VMEM((length, features), jnp.bfloat16),
            pltpu.SemaphoreType.DMA,
        ],
        name="forward_terms",
    )
    return own, terms


def input_grad(own, pieces, saved, grad, inv, gain, bounds, after=()):
    keys = sorted(pieces)

    def kernel(own_ref, saved_ref, grad_ref, inv_ref, gain_ref, *refs):
        out_ref = refs[-1]
        for part, (low, high) in enumerate(bounds):
            total = own_ref[low:high, :]
            for ref, key in zip(refs, keys):
                if key[1] == part:
                    first = pieces[key][1]
                    total = total + ref[first : first + high - low, :].astype(jnp.float32)
            total = total * gain_ref[...]
            saved_rows = saved_ref[low:high, :]
            mean = jnp.mean(saved_rows * total, -1, keepdims=True)
            inv_rows = inv_ref[low:high, :]
            out_ref[low:high, :] = (
                grad_ref[low:high, :]
                + inv_rows * total
                - saved_rows * (inv_rows * inv_rows * inv_rows * mean)
            ).astype(jnp.bfloat16)

    return call(
        kernel,
        [jax.ShapeDtypeStruct(own.shape, jnp.bfloat16)],
        [own, saved, grad, inv, gain] + [pieces[key][0] for key in keys] + list(after),
        [VMEM] * (5 + len(keys)) + [ANY] * len(after),
        flops=INPUT_GRAD_WEIGHT,
        name="input_grad",
    )[0]


def activation_sum(own, pieces, bounds):
    keys = sorted(pieces)

    def kernel(own_ref, *refs):
        out_ref = refs[len(keys)]
        for part, (low, high) in enumerate(bounds):
            total = own_ref[low:high, :].astype(jnp.float32)
            for ref, key in zip(refs, keys):
                if key[1] == part:
                    first = pieces[key][1]
                    total = total + ref[first : first + high - low, :].astype(jnp.float32)
            out_ref[0, low:high, :] = total

    return call(
        kernel,
        [jax.ShapeDtypeStruct((1, *own.shape), jnp.float32)],
        [own] + [pieces[key][0] for key in keys],
        [VMEM] * (1 + len(keys)),
        flops=LAST_SUM_WEIGHT,
        name="activation_sum",
    )[0]


def widened(values, after=()):
    def kernel(in_ref, *refs):
        refs[len(after)][0] = in_ref[...].astype(jnp.float32)

    return call(
        kernel,
        [jax.ShapeDtypeStruct((1, *values.shape), jnp.float32)],
        (values, *after),
        [VMEM] + [ANY] * len(after),
        name="widen",
    )[0]


def rope_tables(positions):
    half_dim = HD // 2
    inverse = 10000.0 ** (-(jnp.arange(half_dim).astype(jnp.float32) * 2.0 / HD))
    angles = positions.astype(jnp.float32)[:, None] * inverse[None, :]
    cosine, sine = jnp.cos(angles), jnp.sin(angles)
    return jnp.concatenate([cosine, cosine], 1), jnp.concatenate([-sine, sine], 1)


def shards(x_fwd, x_bwd, grad_in, gain, w_query, w_key, w_value, w_out):
    act_in, saved_in, grad = x_fwd[0], x_bwd[0], grad_in[0]
    rows = act_in.shape[0]
    count = lax.axis_size("seq")
    bounds = part_bounds(rows, count)
    own_query, own_key, own_value, own_out = w_query[0], w_key[0], w_value[0], w_out[0]

    block_of = lax.axis_index("seq") ^ jnp.arange(count)
    positions = (block_of[:, None] * rows + jnp.arange(rows)[None, :]).reshape(-1)
    cosine, sine = rope_tables(positions)

    def last_arrivals(blocks):
        return [value for (rel, _), value in blocks.items() if rel == count - 1]

    projections = (own_query, own_key, own_value)
    normed_bwd, inv_bwd = normed_rows(saved_in, gain)
    grad_low = cast_rows(grad, [normed_bwd])
    all_bwd = gather_first(normed_bwd, "saved")
    all_grad = gather_first(grad_low, "grad")
    picked = picked_rows(second_hops(all_bwd, rows), [grad_low])
    all_bwd = gather_rest(all_bwd, picked, "saved")
    picked = picked_rows(second_hops(all_grad, rows), picked)
    all_grad = gather_rest(all_grad, picked, "grad")
    normed_fwd, _ = normed_rows(act_in, gain, after=picked)
    all_fwd = gather_first(normed_fwd, "input")

    qkv = project(all_bwd, projections, cosine, sine, rows)
    d_qkv = backward_heads(all_grad, qkv, own_out, cosine, sine, rows)
    picked = picked_rows(second_hops(all_fwd, rows), d_qkv[:1])
    all_fwd = gather_rest(all_fwd, picked, "input")
    d_own, d_terms = backward_terms(d_qkv, projections, rows, count, picked)
    qkv = project(all_fwd, projections, cosine, sine, rows)
    own, terms = forward_terms(qkv, act_in, own_out, rows, count)

    d_own, d_pieces, d_sums = scatter_blocks(d_own, d_terms, rows, across, "grad", [own])
    own, pieces, sums = scatter_blocks(
        own,
        terms,
        rows,
        lambda value, bit: across_and_on(value, 1 << bit),
        "branch",
        d_sums,
        close=True,
    )
    own = across_and_on(own, 0)
    d_input = input_grad(d_own, d_pieces, saved_in, grad, inv_bwd, gain, bounds, sums)
    act_next = activation_sum(own, pieces, bounds)
    return (act_next, widened(passed_along(d_input, "pipe", -1), [act_next]))


def solution(mesh):
    placed = (
        P("pipe", "seq", None),
        P("pipe", "seq", None),
        P("pipe", "seq", None),
        P("pipe", None),
        P("pipe", None, "seq"),
        P("pipe", None, "seq"),
        P("pipe", None, "seq"),
        P("pipe", None, "seq"),
    )
    return jax.shard_map(
        shards,
        mesh=mesh,
        in_specs=placed,
        out_specs=(P("pipe", "seq", None), P("pipe", "seq", None)),
        check_vma=False,
    )
```

time: 127 us -> 121 us (0.953)
  starting transfers between devices: 40.1 us -> 27 us
  Pallas kernels: 35 us -> 42.3 us
  other arithmetic: 4.7 us -> 1.28 us
  local copies, waits for them, and re-layouts: 4.78 us -> 8.03 us
    ppermute x26 -> x18, starting transfers between devices: 33.5 us -> 19.8 us  [across(): return lax.ppermute(value, 'seq', [(i, i ^ 1 << bit) for i in range(count)])]
    pallas_call x8 -> x16, Pallas kernels: 35 us -> 42.3 us  [call(): pl.pallas_call(kernel, out_shape=out_shapes, in_specs=in_specs, out_specs...]
    ppermute x5 -> x3, waiting for transfers between devices: 20 us -> 13 us  [across_and_on(): return lax.ppermute(value, ('pipe', 'seq'), pairs)]
    ppermute x26 -> x18, waiting for transfers between devices: 21.2 us -> 27.8 us  [across(): return lax.ppermute(value, 'seq', [(i, i ^ 1 << bit) for i in range(count)])]
    unnamed x22 -> x30, local copies, waits for them, and re-layouts: 4.78 us -> 8.03 us
    convert_element_type x4 -> x0, other arithmetic: 2.35 us -> none  [scatter_blocks(): final[rel, part] = send_last(total.astype(jnp.bfloat16), bit)]
    ppermute x5 -> x3, starting transfers between devices: 3.1 us -> 3.63 us  [across_and_on(): return lax.ppermute(value, ('pipe', 'seq'), pairs)]
  transfers between devices with their start and end apart: 32 -> 22, of which waited for: 15 -> 8; matrix products, arithmetic and copies ran while one was open for 3% -> 1% of each run, Pallas kernels for 27% -> 34%
where the time goes in v1:
time: 121 us; the launch traced here: 120 us
  Pallas kernels  42.3 us (35%)
  waiting for transfers between devices  40.8 us (34%)
  starting transfers between devices  27 us (22%)
  local copies, waits for them, and re-layouts  8.03 us (7%)
  other arithmetic  1.28 us (1%)
    pallas_call x16, Pallas kernels, call(): pl.pallas_call(kernel, out_shape=out_shapes, in_specs=in_specs, out_specs...  42.3 us
    ppermute x18, waiting for transfers between devices, across(): return lax.ppermute(value, 'seq', [(i, i ^ 1 << bit) for i in range(count)])  27.8 us
    ppermute x18, starting transfers between devices, across(): return lax.ppermute(value, 'seq', [(i, i ^ 1 << bit) for i in range(count)])  19.8 us
    ppermute x3, waiting for transfers between devices, across_and_on(): return lax.ppermute(value, ('pipe', 'seq'), pairs)  13 us
    unnamed x30, local copies, waits for them, and re-layouts  8.03 us
    ppermute x3, starting transfers between devices, across_and_on(): return lax.ppermute(value, ('pipe', 'seq'), pairs)  3.63 us
    ppermute x1, starting transfers between devices, passed_along(): return lax.ppermute(value, axis, pairs)  3.59 us
  transfers between devices with their start and end apart: 22, of which 8 were waited for; matrix products, arithmetic and copies ran while one was open for 1% of the time, Pallas kernels for 34%

profile of v1, /device:TPU:0, one launch (start us, length us, event | category | flops | bytes accessed | tf_op | source)
XLA Modules:
  0.0 120.3 jit_solution(378082233521884710)
XLA Ops:
  0.6 1.2 %copy-done.5 = f32[1,128,2048]{2,1,0:T(8,128)S(1)} copy-done((f32[1,128,2048]{2,1,0:T(8,128)S(1)}, f32[1,128,2048]{2,1,0:T(8,128)}, u32[]{:S(2)}) %copy-start.5) | copy-done | bytes 1048600
  1.9 0.7 copy-done.8
  2.6 0.2 norm.2
  2.8 3.0 %collective-permute-start.3 = (bf16[128,2048]{1,0:T(8,128)(2,1)S(1)}, bf16[128,2048]{1,0:T(8,128)(2,1)S(1)}, u32[]{:S(2)}, u32[]{:S(2)}) collective-permute-start(bf16[128,2048]{1,0:T(8,128)(2,1)S(1)} %get-tuple-element.35.refs_0_), channel_id=1, source_target_pairs={{0,1},{1,0},{2,3},{3,2},{4,5},{5,4},{6,7},{7,6},{8,9},{9,8},{10,11... | collective-permute-start | bytes 1572872 | tf_op jit(solution)/shard_map/gather_saved_block1/ppermute | solution.py:52
  5.8 1.5 %collective-permute-start.2 = (bf16[128,2048]{1,0:T(8,128)(2,1)S(1)}, bf16[128,2048]{1,0:T(8,128)(2,1)S(1)}, u32[]{:S(2)}, u32[]{:S(2)}) collective-permute-start(bf16[128,2048]{1,0:T(8,128)(2,1)S(1)} %get-tuple-element.35.refs_0_), channel_id=1, source_target_pairs={{0,2},{1,3},{2,0},{3,1},{4,6},{5,7},{6,4},{7,5},{8,10},{9,11},{10,... | collective-permute-start | bytes 1572872 | tf_op jit(solution)/shard_map/gather_saved_block2/ppermute | solution.py:52
  7.3 1.2 %copy-done.4 = f32[1,128,2048]{2,1,0:T(8,128)S(1)} copy-done((f32[1,128,2048]{2,1,0:T(8,128)S(1)}, f32[1,128,2048]{2,1,0:T(8,128)}, u32[]{:S(2)}) %copy-start.4) | copy-done | bytes 1048600
  8.6 0.6 collective-permute-start.1
  9.3 9.2 %collective-permute-done.3.refs_1_ = bf16[128,2048]{1,0:T(8,128)(2,1)S(1)} collective-permute-done((bf16[128,2048]{1,0:T(8,128)(2,1)S(1)}, bf16[128,2048]{1,0:T(8,128)(2,1)S(1)}, u32[]{:S(2)}, u32[]{:S(2)}) %collective-permute-start.3) | collective-permute-done | bytes 524320 | tf_op jit(solution)/shard_map/gather_saved_block1/ppermute | solution.py:52
  18.5 2.1 %collective-permute-done.2.refs_0_.refs_2_ = bf16[128,2048]{1,0:T(8,128)(2,1)S(1)} collective-permute-done((bf16[128,2048]{1,0:T(8,128)(2,1)S(1)}, bf16[128,2048]{1,0:T(8,128)(2,1)S(1)}, u32[]{:S(2)}, u32[]{:S(2)}) %collective-permute-start.2) | collective-permute-done | bytes 524320 | tf_op jit(solution)/shard_map/gather_saved_block2/ppermute | solution.py:52
  20.7 0.1 collective-permute-start.8
  20.8 2.0 %collective-permute-start.9 = (bf16[64,2048]{1,0:T(8,128)(2,1)S(1)}, bf16[64,2048]{1,0:T(8,128)(2,1)S(1)}, u32[]{:S(2)}, u32[]{:S(2)}) collective-permute-start(bf16[64,2048]{1,0:T(8,128)(2,1)S(1)} %get-tuple-element.37.refs_3_), channel_id=1, source_target_pairs={{0,2},{1,3},{2,0},{3,1},{4,6},{5,7},{6,4},{7,5},{8,10},{9,11},{10,... | collective-permute-start | bytes 786440 | tf_op jit(solution)/shard_map/gather_saved_block3_row64/ppermute | solution.py:52
  22.8 7.0 %collective-permute-done.1.refs_1_ = bf16[128,2048]{1,0:T(8,128)(2,1)S(1)} collective-permute-done((bf16[128,2048]{1,0:T(8,128)(2,1)S(1)}, bf16[128,2048]{1,0:T(8,128)(2,1)S(1)}, u32[]{:S(2)}, u32[]{:S(2)}) %collective-permute-start.1) | collective-permute-done | bytes 524320 | tf_op jit(solution)/shard_map/gather_grad_block1/ppermute | solution.py:52
  29.8 2.1 %collective-permute-done.refs_0_.refs_2_ = bf16[128,2048]{1,0:T(8,128)(2,1)S(1)} collective-permute-done((bf16[128,2048]{1,0:T(8,128)(2,1)S(1)}, bf16[128,2048]{1,0:T(8,128)(2,1)S(1)}, u32[]{:S(2)}, u32[]{:S(2)}) %collective-permute-start) | collective-permute-done | bytes 524320 | tf_op jit(solution)/shard_map/gather_grad_block2/ppermute | solution.py:52
  31.9 0.1 collective-permute-start.6
  32.0 2.0 %collective-permute-start.7 = (bf16[64,2048]{1,0:T(8,128)(2,1)S(1)}, bf16[64,2048]{1,0:T(8,128)(2,1)S(1)}, u32[]{:S(2)}, u32[]{:S(2)}) collective-permute-start(bf16[64,2048]{1,0:T(8,128)(2,1)S(1)} %get-tuple-element.39.refs_1_), channel_id=1, source_target_pairs={{0,2},{1,3},{2,0},{3,1},{4,6},{5,7},{6,4},{7,5},{8,10},{9,11},{10,... | collective-permute-start | bytes 786440 | tf_op jit(solution)/shard_map/gather_grad_block3_row64/ppermute | solution.py:52
  34.0 1.0 fusion
  35.0 0.2 pad_maximum_fusion
  35.2 0.8 norm.3
  36.1 1.9 %collective-permute-start.4 = (bf16[128,2048]{1,0:T(8,128)(2,1)S(1)}, bf16[128,2048]{1,0:T(8,128)(2,1)S(1)}, u32[]{:S(2)}, u32[]{:S(2)}) collective-permute-start(bf16[128,2048]{1,0:T(8,128)(2,1)S(1)} %get-tuple-element.40.refs_0_), channel_id=1, source_target_pairs={{0,1},{1,0},{2,3},{3,2},{4,5},{5,4},{6,7},{7,6},{8,9},{9,8},{10,11... | collective-permute-start | bytes 1572872 | tf_op jit(solution)/shard_map/gather_input_block1/ppermute | solution.py:52
  38.1 6.1 %project.2 = (bf16[512,512]{1,0:T(8,128)(2,1)S(1)}, bf16[512,512]{1,0:T(8,128)(2,1)S(1)}, bf16[512,512]{1,0:T(8,128)(2,1)S(1)}) custom-call(bf16[128,2048]{1,0:T(8,128)(2,1)S(1)} %get-tuple-element.35.refs_0_, bf16[128,2048]{1,0:T(8,128)(2,1)S(1)} %collective-permute-done.3.refs_1_, bf16[128,2048]{1,0:T(8,128)(2,1)} %copy-done.2, ...), custom_call_target="tpu_custom_call" | custom-call | flops 1 | bytes 1 | tf_op jit(solution)/shard_map/project/pallas_call | solution.py:172
  44.2 0.8 copy-done.10
  45.0 0.8 copy-done.11
  45.8 0.8 copy-done.12
  46.6 8.6 %backward_heads.1 = (bf16[512,512]{1,0:T(8,128)(2,1)S(1)}, bf16[512,512]{1,0:T(8,128)(2,1)S(1)}, bf16[512,512]{1,0:T(8,128)(2,1)S(1)}) custom-call(bf16[128,2048]{1,0:T(8,128)(2,1)S(1)} %cast.1.refs_2_.refs_0_, bf16[128,2048]{1,0:T(8,128)(2,1)S(1)} %collective-permute-done.1.refs_1_, bf16[128,2048]{1,0:T(8,128)(2,1)} %copy-done.7, ...), custom_call_target="tpu_custom_call" | custom-call | flops 8000000000 | bytes 1 | tf_op jit(solution)/shard_map/backward_heads/pallas_call | solution.py:172
  55.3 0.3 collective-permute-start.10
  55.6 1.9 %collective-permute-start.11 = (bf16[64,2048]{1,0:T(8,128)(2,1)S(1)}, bf16[64,2048]{1,0:T(8,128)(2,1)S(1)}, u32[]{:S(2)}, u32[]{:S(2)}) collective-permute-start(bf16[64,2048]{1,0:T(8,128)(2,1)S(1)} %get-tuple-element.46.refs_7_), channel_id=1, source_target_pairs={{0,2},{1,3},{2,0},{3,1},{4,6},{5,7},{6,4},{7,5},{8,10},{9,11},{10,... | collective-permute-start | bytes 786440 | tf_op jit(solution)/shard_map/gather_input_block3_row64/ppermute | solution.py:52
  57.4 8.2 %backward_terms.1 = (f32[128,2048]{1,0:T(8,128)}, bf16[128,2048]{1,0:T(8,128)(2,1)S(1)}, bf16[128,2048]{1,0:T(8,128)(2,1)S(1)}, f32[64,2048]{1,0:T(8,128)S(1)}, f32[64,2048]{1,0:T(8,128)S(1)}) custom-call(bf16[512,512]{1,0:T(8,128)(2,1)S(1)} %get-tuple-element.44.refs_2_.refs_0_, bf16[512,512]{1,0:T(8,128)(2,1)S(1)} %get-tuple-element.55.refs_1_, ...), custom_call_target="tpu_custom_call" | custom-call | flops 3000000000 | bytes 1 | tf_op jit(solution)/shard_map/backward_terms/pallas_call | solution.py:172
  65.7 1.6 %collective-permute-start.14 = (bf16[128,2048]{1,0:T(8,128)(2,1)S(1)}, bf16[128,2048]{1,0:T(8,128)(2,1)S(1)}, u32[]{:S(2)}, u32[]{:S(2)}) collective-permute-start(bf16[128,2048]{1,0:T(8,128)(2,1)S(1)} %get-tuple-element.59), channel_id=1, source_target_pairs={{0,1},{1,0},{2,3},{3,2},{4,5},{5,4},{6,7},{7,6},{8,9},{9,8},{10,11... | collective-permute-start | bytes 1572872 | tf_op jit(solution)/shard_map/scatter_grad_block3_part0/ppermute | solution.py:52
  67.2 0.5 collective-permute-start.15
  67.7 6.2 %project.3 = (bf16[512,512]{1,0:T(8,128)(2,1)S(1)}, bf16[512,512]{1,0:T(8,128)(2,1)S(1)}, bf16[512,512]{1,0:T(8,128)(2,1)S(1)}) custom-call(bf16[128,2048]{1,0:T(8,128)(2,1)S(1)} %get-tuple-element.40.refs_0_, bf16[128,2048]{1,0:T(8,128)(2,1)S(1)} %collective-permute-done.4.refs_1_, bf16[128,2048]{1,0:T(8,128)(2,1)} %copy-done.3, ...), custom_call_target="tpu_custom_call" | custom-call | flops 1 | bytes 1 | tf_op jit(solution)/shard_map/project/pallas_call | solution.py:172
  73.9 6.3 %forward_terms.1 = (f32[128,2048]{1,0:T(8,128)}, bf16[128,2048]{1,0:T(8,128)(2,1)S(1)}, bf16[128,2048]{1,0:T(8,128)(2,1)S(1)}, f32[64,2048]{1,0:T(8,128)S(1)}, f32[64,2048]{1,0:T(8,128)S(1)}) custom-call(bf16[512,512]{1,0:T(8,128)(2,1)S(1)} %get-tuple-element.47.refs_0_, bf16[512,512]{1,0:T(8,128)(2,1)S(1)} %get-tuple-element.48.refs_1_, ...), custom_call_target="tpu_custom_call" | custom-call | flops 1 | bytes 1 | tf_op jit(solution)/shard_map/forward_terms/pallas_call | solution.py:172
  80.2 0.2 collective-permute-start.12
  80.5 1.9 %collective-permute-start.13 = (bf16[128,2048]{1,0:T(8,128)(2,1)S(1)}, bf16[128,2048]{1,0:T(8,128)(2,1)S(1)}, u32[]{:S(2)}, u32[]{:S(2)}) collective-permute-start(bf16[128,2048]{1,0:T(8,128)(2,1)S(1)} %get-tuple-element.54), channel_id=1, source_target_pairs={{0,2},{1,3},{2,0},{3,1},{4,6},{5,7},{6,4},{7,5},{8,10},{9,11},{10,... | collective-permute-start | bytes 1572872 | tf_op jit(solution)/shard_map/scatter_branch_block3_part1/ppermute | solution.py:52
  82.4 1.2 %copy-done = f32[128,2048]{1,0:T(8,128)S(1)} copy-done((f32[128,2048]{1,0:T(8,128)S(1)}, f32[128,2048]{1,0:T(8,128)}, u32[]{:S(2)}) %copy-start) | copy-done | bytes 1048600
  83.6 0.1 sum_rows.2
  83.7 0.2 collective-permute-start.20
  83.9 1.8 %collective-permute-start.19 = (bf16[64,2048]{1,0:T(8,128)(2,1)S(1)}, bf16[64,2048]{1,0:T(8,128)(2,1)S(1)}, u32[]{:S(2)}, u32[]{:S(2)}) collective-permute-start(bf16[64,2048]{1,0:T(8,128)(2,1)S(1)} %get-tuple-element.62.refs_8_), channel_id=1, source_target_pairs={{0,1},{1,0},{2,3},{3,2},{4,5},{5,4},{6,7},{7,6},{8,9},{9,8},{10,11... | collective-permute-start | bytes 786440 | tf_op jit(solution)/shard_map/scatter_grad_block1_part1/ppermute | solution.py:52
  85.7 7.0 %collective-permute-done.12.refs_3_.refs_5_ = bf16[128,2048]{1,0:T(8,128)(2,1)S(1)} collective-permute-done((bf16[128,2048]{1,0:T(8,128)(2,1)S(1)}, bf16[128,2048]{1,0:T(8,128)(2,1)S(1)}, u32[]{:S(2)}, u32[]{:S(2)}) %collective-permute-start.12) | collective-permute-done | bytes 524320 | tf_op jit(solution)/shard_map/scatter_branch_block3_part0/ppermute | solution.py:52
  92.7 0.4 collective-permute-done.13.refs_4_.refs_6_
  93.1 1.5 %sum_rows.3 = (bf16[64,2048]{1,0:T(8,128)(2,1)S(1)}, bf16[64,2048]{1,0:T(8,128)(2,1)S(1)}, bf16[128,2048]{1,0:T(8,128)(2,1)S(1)}) custom-call(f32[64,2048]{1,0:T(8,128)S(1)} %get-tuple-element.50.refs_0_, f32[64,2048]{1,0:T(8,128)S(1)} %get-tuple-element.51.refs_1_, f32[128,2048]{1,0:T(8,128)} %get-tuple-element.52.refs_4_.refs_2_, ...), custom_call_target="tpu_custom_call" | custom-call | flops 1 | bytes 1 | tf_op jit(solution)/shard_map/sum_rows/pallas_call | solution.py:172
  94.7 3.6 %collective-permute-start.18 = (bf16[64,2048]{1,0:T(8,128)(2,1)S(1)}, bf16[64,2048]{1,0:T(8,128)(2,1)S(1)}, u32[]{:S(2)}, u32[]{:S(2)}) collective-permute-start(bf16[64,2048]{1,0:T(8,128)(2,1)S(1)} %get-tuple-element.65.refs_4_), channel_id=1, source_target_pairs={{0,6},{1,7},{2,4},{3,5},{4,10},{5,11},{6,8},{7,9},{8,14},{9,15},{1... | collective-permute-start | bytes 786440 | tf_op jit(solution)/shard_map/scatter_branch_block2_part0/ppermute | solution.py:62
  98.3 2.0 %input_grad.1 = bf16[128,2048]{1,0:T(8,128)(2,1)S(1)} custom-call(f32[128,2048]{1,0:T(8,128)S(1)} %copy-done.13, f32[128,2048]{1,0:T(8,128)} %bitcast.13, f32[128,2048]{1,0:T(8,128)} %bitcast.11, f32[128,1]{1,0:T(8,128)S(1)} %get-tuple-element.67.inv_ref, f32[1,2048]{1,0:T(1,128)S(1)} %copy-done.9, ...), custom_call_target="tpu_custom_call" | custom-call | flops 8000000000 | bytes 1 | tf_op jit(solution)/shard_map/input_grad/pallas_call | solution.py:172
  100.3 3.6 %collective-permute-start.21 = (bf16[128,2048]{1,0:T(8,128)(2,1)S(1)}, bf16[128,2048]{1,0:T(8,128)(2,1)S(1)}, u32[]{:S(2)}, u32[]{:S(2)}) collective-permute-start(bf16[128,2048]{1,0:T(8,128)(2,1)S(1)} %input_grad.1), channel_id=1, source_target_pairs={{0,28},{4,0},{8,4},{12,8},{16,12},{20,16},{24,20},{28,24},{1,29},{... | collective-permute-start | bytes 1572872 | tf_op jit(solution)/shard_map/ppermute | solution.py:68
  103.9 3.8 %collective-permute-done.18.refs_1_ = bf16[64,2048]{1,0:T(8,128)(2,1)S(1)} collective-permute-done((bf16[64,2048]{1,0:T(8,128)(2,1)S(1)}, bf16[64,2048]{1,0:T(8,128)(2,1)S(1)}, u32[]{:S(2)}, u32[]{:S(2)}) %collective-permute-start.18) | collective-permute-done | bytes 262176 | tf_op jit(solution)/shard_map/scatter_branch_block2_part0/ppermute | solution.py:62
  107.7 9.3 %collective-permute-done.16.own_ref = bf16[128,2048]{1,0:T(8,128)(2,1)S(1)} collective-permute-done((bf16[128,2048]{1,0:T(8,128)(2,1)S(1)}, bf16[128,2048]{1,0:T(8,128)(2,1)S(1)}, u32[]{:S(2)}, u32[]{:S(2)}) %collective-permute-start.16) | collective-permute-done | bytes 524320 | tf_op jit(solution)/shard_map/ppermute | solution.py:62
  116.9 1.1 activation_sum.1.refs_0_
  118.0 1.2 %copy-done.6 = f32[1,128,2048]{2,1,0:T(8,128)S(1)} copy-done((f32[1,128,2048]{2,1,0:T(8,128)S(1)}, f32[1,128,2048]{2,1,0:T(8,128)}, u32[]{:S(2)}) %copy-start.6) | copy-done | bytes 1048600
  119.2 1.0 widen.1
  (47 shorter events, 0.5 us)
Async XLA Ops:
  0.6 1.2 %copy-start.5 = (f32[1,128,2048]{2,1,0:T(8,128)S(1)}, f32[1,128,2048]{2,1,0:T(8,128)}, u32[]{:S(2)}) copy-start(f32[1,128,2048]{2,1,0:T(8,128)} %param.9) | copy-start | bytes 3145732
  1.9 0.7 copy-start.8
  2.8 15.8 %collective-permute-start.3 = (bf16[128,2048]{1,0:T(8,128)(2,1)S(1)}, bf16[128,2048]{1,0:T(8,128)(2,1)S(1)}, u32[]{:S(2)}, u32[]{:S(2)}) collective-permute-start(bf16[128,2048]{1,0:T(8,128)(2,1)S(1)} %get-tuple-element.35.refs_0_), channel_id=1, source_target_pairs={{0,1},{1,0},{2,3},{3,2},{4,5},{5,4},{6,7},{7,6},{8,9},{9,8},{10,11... | collective-permute-start | bytes 1572872 | tf_op jit(solution)/shard_map/gather_saved_block1/ppermute | solution.py:52
  5.8 14.8 %collective-permute-start.2 = (bf16[128,2048]{1,0:T(8,128)(2,1)S(1)}, bf16[128,2048]{1,0:T(8,128)(2,1)S(1)}, u32[]{:S(2)}, u32[]{:S(2)}) collective-permute-start(bf16[128,2048]{1,0:T(8,128)(2,1)S(1)} %get-tuple-element.35.refs_0_), channel_id=1, source_target_pairs={{0,2},{1,3},{2,0},{3,1},{4,6},{5,7},{6,4},{7,5},{8,10},{9,11},{10,... | collective-permute-start | bytes 1572872 | tf_op jit(solution)/shard_map/gather_saved_block2/ppermute | solution.py:52
  7.3 1.2 %copy-start.4 = (f32[1,128,2048]{2,1,0:T(8,128)S(1)}, f32[1,128,2048]{2,1,0:T(8,128)}, u32[]{:S(2)}) copy-start(f32[1,128,2048]{2,1,0:T(8,128)} %param.10) | copy-start | bytes 3145732
  8.6 21.2 %collective-permute-start.1 = (bf16[128,2048]{1,0:T(8,128)(2,1)S(1)}, bf16[128,2048]{1,0:T(8,128)(2,1)S(1)}, u32[]{:S(2)}, u32[]{:S(2)}) collective-permute-start(bf16[128,2048]{1,0:T(8,128)(2,1)S(1)} %cast.1.refs_2_.refs_0_), channel_id=1, source_target_pairs={{0,1},{1,0},{2,3},{3,2},{4,5},{5,4},{6,7},{7,6},{8,9},{9,8},{10,11... | collective-permute-start | bytes 1572872 | tf_op jit(solution)/shard_map/gather_grad_block1/ppermute | solution.py:52
  9.2 22.7 %collective-permute-start = (bf16[128,2048]{1,0:T(8,128)(2,1)S(1)}, bf16[128,2048]{1,0:T(8,128)(2,1)S(1)}, u32[]{:S(2)}, u32[]{:S(2)}) collective-permute-start(bf16[128,2048]{1,0:T(8,128)(2,1)S(1)} %cast.1.refs_2_.refs_0_), channel_id=1, source_target_pairs={{0,2},{1,3},{2,0},{3,1},{4,6},{5,7},{6,4},{7,5},{8,10},{9,11},{10,... | collective-permute-start | bytes 1572872 | tf_op jit(solution)/shard_map/gather_grad_block2/ppermute | solution.py:52
  20.6 14.6 %copy-start.2 = (bf16[128,2048]{1,0:T(8,128)(2,1)}, bf16[128,2048]{1,0:T(8,128)(2,1)S(1)}, u32[]{:S(2)}) copy-start(bf16[128,2048]{1,0:T(8,128)(2,1)S(1)} %collective-permute-done.2.refs_0_.refs_2_) | copy-start | bytes 1572868
  20.7 14.6 %copy-start.1 = (f32[1,128,2048]{2,1,0:T(8,128)S(1)}, f32[1,128,2048]{2,1,0:T(8,128)}, u32[]{:S(2)}) copy-start(f32[1,128,2048]{2,1,0:T(8,128)} %param.8) | copy-start | bytes 3145732
  20.7 14.6 %copy-start.9 = (f32[1,2048]{1,0:T(1,128)S(1)}, f32[1,2048]{1,0:T(1,128)}, u32[]{:S(2)}) copy-start(f32[1,2048]{1,0:T(1,128)} %gain_ref.5) | copy-start | bytes 24580
  20.7 15.4 %collective-permute-start.8 = (bf16[64,2048]{1,0:T(8,128)(2,1)S(1)}, bf16[64,2048]{1,0:T(8,128)(2,1)S(1)}, u32[]{:S(2)}, u32[]{:S(2)}) collective-permute-start(bf16[64,2048]{1,0:T(8,128)(2,1)S(1)} %get-tuple-element.36.refs_2_), channel_id=1, source_target_pairs={{0,1},{1,0},{2,3},{3,2},{4,5},{5,4},{6,7},{7,6},{8,9},{9,8},{10,11... | collective-permute-start | bytes 786440 | tf_op jit(solution)/shard_map/gather_saved_block3_row0/ppermute | solution.py:52
  20.8 17.3 %collective-permute-start.9 = (bf16[64,2048]{1,0:T(8,128)(2,1)S(1)}, bf16[64,2048]{1,0:T(8,128)(2,1)S(1)}, u32[]{:S(2)}, u32[]{:S(2)}) collective-permute-start(bf16[64,2048]{1,0:T(8,128)(2,1)S(1)} %get-tuple-element.37.refs_3_), channel_id=1, source_target_pairs={{0,2},{1,3},{2,0},{3,1},{4,6},{5,7},{6,4},{7,5},{8,10},{9,11},{10,... | collective-permute-start | bytes 786440 | tf_op jit(solution)/shard_map/gather_saved_block3_row64/ppermute | solution.py:52
  31.9 4.2 %copy-start.7 = (bf16[128,2048]{1,0:T(8,128)(2,1)}, bf16[128,2048]{1,0:T(8,128)(2,1)S(1)}, u32[]{:S(2)}) copy-start(bf16[128,2048]{1,0:T(8,128)(2,1)S(1)} %collective-permute-done.refs_0_.refs_2_) | copy-start | bytes 1572868
  31.9 14.7 %collective-permute-start.6 = (bf16[64,2048]{1,0:T(8,128)(2,1)S(1)}, bf16[64,2048]{1,0:T(8,128)(2,1)S(1)}, u32[]{:S(2)}, u32[]{:S(2)}) collective-permute-start(bf16[64,2048]{1,0:T(8,128)(2,1)S(1)} %get-tuple-element.38.refs_0_), channel_id=1, source_target_pairs={{0,1},{1,0},{2,3},{3,2},{4,5},{5,4},{6,7},{7,6},{8,9},{9,8},{10,11... | collective-permute-start | bytes 786440 | tf_op jit(solution)/shard_map/gather_grad_block3_row0/ppermute | solution.py:52
  32.0 14.6 %collective-permute-start.7 = (bf16[64,2048]{1,0:T(8,128)(2,1)S(1)}, bf16[64,2048]{1,0:T(8,128)(2,1)S(1)}, u32[]{:S(2)}, u32[]{:S(2)}) collective-permute-start(bf16[64,2048]{1,0:T(8,128)(2,1)S(1)} %get-tuple-element.39.refs_1_), channel_id=1, source_target_pairs={{0,2},{1,3},{2,0},{3,1},{4,6},{5,7},{6,4},{7,5},{8,10},{9,11},{10,... | collective-permute-start | bytes 786440 | tf_op jit(solution)/shard_map/gather_grad_block3_row64/ppermute | solution.py:52
  36.1 19.1 %collective-permute-start.5 = (bf16[128,2048]{1,0:T(8,128)(2,1)S(1)}, bf16[128,2048]{1,0:T(8,128)(2,1)S(1)}, u32[]{:S(2)}, u32[]{:S(2)}) collective-permute-start(bf16[128,2048]{1,0:T(8,128)(2,1)S(1)} %get-tuple-element.40.refs_0_), channel_id=1, source_target_pairs={{0,2},{1,3},{2,0},{3,1},{4,6},{5,7},{6,4},{7,5},{8,10},{9,11},{10,... | collective-permute-start | bytes 1572872 | tf_op jit(solution)/shard_map/gather_input_block2/ppermute | solution.py:52
  36.1 19.1 %collective-permute-start.4 = (bf16[128,2048]{1,0:T(8,128)(2,1)S(1)}, bf16[128,2048]{1,0:T(8,128)(2,1)S(1)}, u32[]{:S(2)}, u32[]{:S(2)}) collective-permute-start(bf16[128,2048]{1,0:T(8,128)(2,1)S(1)} %get-tuple-element.40.refs_0_), channel_id=1, source_target_pairs={{0,1},{1,0},{2,3},{3,2},{4,5},{5,4},{6,7},{7,6},{8,9},{9,8},{10,11... | collective-permute-start | bytes 1572872 | tf_op jit(solution)/shard_map/gather_input_block1/ppermute | solution.py:52
  44.2 0.8 copy-start.10
  45.0 0.8 copy-start.11
  45.8 0.8 copy-start.12
  55.2 2.2 %copy-start.14 = (bf16[512,512]{1,0:T(8,128)(2,1)}, bf16[512,512]{1,0:T(8,128)(2,1)S(1)}, u32[]{:S(2)}) copy-start(bf16[512,512]{1,0:T(8,128)(2,1)S(1)} %get-tuple-element.56.refs_2_) | copy-start | bytes 1572868
  55.2 10.4 %copy-start.3 = (bf16[128,2048]{1,0:T(8,128)(2,1)}, bf16[128,2048]{1,0:T(8,128)(2,1)S(1)}, u32[]{:S(2)}) copy-start(bf16[128,2048]{1,0:T(8,128)(2,1)S(1)} %collective-permute-done.5.refs_0_.refs_2_) | copy-start | bytes 1572868
  55.3 12.4 %collective-permute-start.10 = (bf16[64,2048]{1,0:T(8,128)(2,1)S(1)}, bf16[64,2048]{1,0:T(8,128)(2,1)S(1)}, u32[]{:S(2)}, u32[]{:S(2)}) collective-permute-start(bf16[64,2048]{1,0:T(8,128)(2,1)S(1)} %get-tuple-element.45.refs_6_), channel_id=1, source_target_pairs={{0,1},{1,0},{2,3},{3,2},{4,5},{5,4},{6,7},{7,6},{8,9},{9,8},{10,11... | collective-permute-start | bytes 786440 | tf_op jit(solution)/shard_map/gather_input_block3_row0/ppermute | solution.py:52
  55.6 12.2 %collective-permute-start.11 = (bf16[64,2048]{1,0:T(8,128)(2,1)S(1)}, bf16[64,2048]{1,0:T(8,128)(2,1)S(1)}, u32[]{:S(2)}, u32[]{:S(2)}) collective-permute-start(bf16[64,2048]{1,0:T(8,128)(2,1)S(1)} %get-tuple-element.46.refs_7_), channel_id=1, source_target_pairs={{0,2},{1,3},{2,0},{3,1},{4,6},{5,7},{6,4},{7,5},{8,10},{9,11},{10,... | collective-permute-start | bytes 786440 | tf_op jit(solution)/shard_map/gather_input_block3_row64/ppermute | solution.py:52
  65.7 16.7 %collective-permute-start.14 = (bf16[128,2048]{1,0:T(8,128)(2,1)S(1)}, bf16[128,2048]{1,0:T(8,128)(2,1)S(1)}, u32[]{:S(2)}, u32[]{:S(2)}) collective-permute-start(bf16[128,2048]{1,0:T(8,128)(2,1)S(1)} %get-tuple-element.59), channel_id=1, source_target_pairs={{0,1},{1,0},{2,3},{3,2},{4,5},{5,4},{6,7},{7,6},{8,9},{9,8},{10,11... | collective-permute-start | bytes 1572872 | tf_op jit(solution)/shard_map/scatter_grad_block3_part0/ppermute | solution.py:52
  67.2 15.1 %collective-permute-start.15 = (bf16[128,2048]{1,0:T(8,128)(2,1)S(1)}, bf16[128,2048]{1,0:T(8,128)(2,1)S(1)}, u32[]{:S(2)}, u32[]{:S(2)}) collective-permute-start(bf16[128,2048]{1,0:T(8,128)(2,1)S(1)} %get-tuple-element.60), channel_id=1, source_target_pairs={{0,2},{1,3},{2,0},{3,1},{4,6},{5,7},{6,4},{7,5},{8,10},{9,11},{10,... | collective-permute-start | bytes 1572872 | tf_op jit(solution)/shard_map/scatter_grad_block3_part1/ppermute | solution.py:52
  80.2 12.5 %collective-permute-start.12 = (bf16[128,2048]{1,0:T(8,128)(2,1)S(1)}, bf16[128,2048]{1,0:T(8,128)(2,1)S(1)}, u32[]{:S(2)}, u32[]{:S(2)}) collective-permute-start(bf16[128,2048]{1,0:T(8,128)(2,1)S(1)} %get-tuple-element.53), channel_id=1, source_target_pairs={{0,1},{1,0},{2,3},{3,2},{4,5},{5,4},{6,7},{7,6},{8,9},{9,8},{10,11... | collective-permute-start | bytes 1572872 | tf_op jit(solution)/shard_map/scatter_branch_block3_part0/ppermute | solution.py:52
  80.5 12.6 %collective-permute-start.13 = (bf16[128,2048]{1,0:T(8,128)(2,1)S(1)}, bf16[128,2048]{1,0:T(8,128)(2,1)S(1)}, u32[]{:S(2)}, u32[]{:S(2)}) collective-permute-start(bf16[128,2048]{1,0:T(8,128)(2,1)S(1)} %get-tuple-element.54), channel_id=1, source_target_pairs={{0,2},{1,3},{2,0},{3,1},{4,6},{5,7},{6,4},{7,5},{8,10},{9,11},{10,... | collective-permute-start | bytes 1572872 | tf_op jit(solution)/shard_map/scatter_branch_block3_part1/ppermute | solution.py:52
  82.4 1.2 %copy-start = (f32[128,2048]{1,0:T(8,128)S(1)}, f32[128,2048]{1,0:T(8,128)}, u32[]{:S(2)}) copy-start(f32[128,2048]{1,0:T(8,128)} %get-tuple-element.52.refs_4_.refs_2_) | copy-start | bytes 3145732
  83.7 14.6 %collective-permute-start.20 = (bf16[64,2048]{1,0:T(8,128)(2,1)S(1)}, bf16[64,2048]{1,0:T(8,128)(2,1)S(1)}, u32[]{:S(2)}, u32[]{:S(2)}) collective-permute-start(bf16[64,2048]{1,0:T(8,128)(2,1)S(1)} %get-tuple-element.61.refs_7_), channel_id=1, source_target_pairs={{0,2},{1,3},{2,0},{3,1},{4,6},{5,7},{6,4},{7,5},{8,10},{9,11},{10,... | collective-permute-start | bytes 786440 | tf_op jit(solution)/shard_map/scatter_grad_block2_part0/ppermute | solution.py:52
  83.9 14.4 %collective-permute-start.19 = (bf16[64,2048]{1,0:T(8,128)(2,1)S(1)}, bf16[64,2048]{1,0:T(8,128)(2,1)S(1)}, u32[]{:S(2)}, u32[]{:S(2)}) collective-permute-start(bf16[64,2048]{1,0:T(8,128)(2,1)S(1)} %get-tuple-element.62.refs_8_), channel_id=1, source_target_pairs={{0,1},{1,0},{2,3},{3,2},{4,5},{5,4},{6,7},{7,6},{8,9},{9,8},{10,11... | collective-permute-start | bytes 786440 | tf_op jit(solution)/shard_map/scatter_grad_block1_part1/ppermute | solution.py:52
  93.1 5.1 %copy-start.13 = (f32[128,2048]{1,0:T(8,128)S(1)}, f32[128,2048]{1,0:T(8,128)}, u32[]{:S(2)}) copy-start(f32[128,2048]{1,0:T(8,128)} %get-tuple-element.66.own_ref) | copy-start | bytes 3145732
  94.6 9.3 %collective-permute-start.17 = (bf16[64,2048]{1,0:T(8,128)(2,1)S(1)}, bf16[64,2048]{1,0:T(8,128)(2,1)S(1)}, u32[]{:S(2)}, u32[]{:S(2)}) collective-permute-start(bf16[64,2048]{1,0:T(8,128)(2,1)S(1)} %get-tuple-element.64.refs_5_), channel_id=1, source_target_pairs={{0,5},{1,4},{2,7},{3,6},{4,9},{5,8},{6,11},{7,10},{8,13},{9,12},{1... | collective-permute-start | bytes 786440 | tf_op jit(solution)/shard_map/scatter_branch_block1_part1/ppermute | solution.py:62
  94.7 13.0 %collective-permute-start.18 = (bf16[64,2048]{1,0:T(8,128)(2,1)S(1)}, bf16[64,2048]{1,0:T(8,128)(2,1)S(1)}, u32[]{:S(2)}, u32[]{:S(2)}) collective-permute-start(bf16[64,2048]{1,0:T(8,128)(2,1)S(1)} %get-tuple-element.65.refs_4_), channel_id=1, source_target_pairs={{0,6},{1,7},{2,4},{3,5},{4,10},{5,11},{6,8},{7,9},{8,14},{9,15},{1... | collective-permute-start | bytes 786440 | tf_op jit(solution)/shard_map/scatter_branch_block2_part0/ppermute | solution.py:62
  98.2 18.7 %collective-permute-start.16 = (bf16[128,2048]{1,0:T(8,128)(2,1)S(1)}, bf16[128,2048]{1,0:T(8,128)(2,1)S(1)}, u32[]{:S(2)}, u32[]{:S(2)}) collective-permute-start(bf16[128,2048]{1,0:T(8,128)(2,1)S(1)} %get-tuple-element.63), channel_id=1, source_target_pairs={{0,4},{1,5},{2,6},{3,7},{4,8},{5,9},{6,10},{7,11},{8,12},{9,13},{1... | collective-permute-start | bytes 1572872 | tf_op jit(solution)/shard_map/ppermute | solution.py:62
  100.3 17.7 %collective-permute-start.21 = (bf16[128,2048]{1,0:T(8,128)(2,1)S(1)}, bf16[128,2048]{1,0:T(8,128)(2,1)S(1)}, u32[]{:S(2)}, u32[]{:S(2)}) collective-permute-start(bf16[128,2048]{1,0:T(8,128)(2,1)S(1)} %input_grad.1), channel_id=1, source_target_pairs={{0,28},{4,0},{8,4},{12,8},{16,12},{20,16},{24,20},{28,24},{1,29},{... | collective-permute-start | bytes 1572872 | tf_op jit(solution)/shard_map/ppermute | solution.py:68
  118.0 1.2 %copy-start.6 = (f32[1,128,2048]{2,1,0:T(8,128)S(1)}, f32[1,128,2048]{2,1,0:T(8,128)}, u32[]{:S(2)}) copy-start(f32[1,128,2048]{2,1,0:T(8,128)} %activation_sum.1.refs_0_) | copy-start | bytes 3145732

commit v2 on v1

--- a/solution.py
+++ b/solution.py
@@ -18,7 +18,8 @@
 TERMS_WEIGHT = 3_000_000_000
 INPUT_GRAD_WEIGHT = 8_000_000_000
 LAST_SUM_WEIGHT = 8_000_000_000
-VMEM_LIMIT = 50 * 1024 * 1024
+FORWARD_WEIGHT = 5_000_000_000
+MIB = 1024 * 1024
 
 
 def bits_of(number):
@@ -110,72 +111,84 @@
     return blocks
 
 
-def messages_of(rows, count):
-    bounds = part_bounds(rows, count)
-    parts = range(len(bounds))
+def messages_of(rows, count, whole):
+    parts = range(len(part_bounds(rows, count)))
     later = {
         (rel ^ (1 << last_bit(rel, part)), part)
         for rel in range(1, count)
         for part in parts
         if len(bits_of(rel)) > 1
     }
-    keys = [(rel, part) for rel in reversed(by_distance(count)) for part in parts]
-    groups = {}
-    for key in keys:
-        if key not in later:
-            groups.setdefault(last_bit(*key), []).append(key)
-    return list(groups.values()), [key for key in keys if key in later]
-
-
-def scatter_blocks(own, terms, rows, send_last, what, after=(), close=False):
+    groups, waiting = {}, {}
+    for rel in reversed(by_distance(count)):
+        for part in parts:
+            key = (rel, part)
+            if whole and len(bits_of(rel)) == 1:
+                waiting.setdefault(rel, []).append(key)
+            elif key in later:
+                waiting[key] = [key]
+            else:
+                groups.setdefault(key if whole else last_bit(*key), []).append(key)
+    return list(groups.values()), list(waiting.values())
+
+
+def row_of(keys, key, bounds):
+    before = keys[: keys.index(key)]
+    return sum(bounds[part][1] - bounds[part][0] for _, part in before)
+
+
+def scatter_blocks(terms, rows, whole, send_last, what, after=()):
     count = lax.axis_size("seq")
     bounds = part_bounds(rows, count)
-    groups, later = messages_of(rows, count)
-    arrived, near, last, sums = {}, {}, {}, []
+    groups, waiting = messages_of(rows, count, whole)
+    arrived, final, sums = {}, {}, []
 
     def send(value, keys):
         bit = last_bit(*keys[0])
         targets = [(rel ^ (1 << bit), part) for rel, part in keys]
-        onward = any(rel for rel, _ in targets)
         with jax.named_scope(f"scatter_{what}_block{keys[0][0]}_part{keys[0][1]}"):
-            moved = (across if onward else send_last)(value, bit)
-        first = 0
+            moved = (across if any(rel for rel, _ in targets) else send_last)(value, bit)
         for key, target in zip(keys, targets):
+            piece = (moved, row_of(keys, key, bounds))
             if target[0]:
-                arrived.setdefault(target, []).append((moved, first))
+                arrived.setdefault(target, []).append(piece)
             else:
-                (near if onward else last)[key] = (moved, first)
-            first += bounds[key[1]][1] - bounds[key[1]][0]
+                final[key] = piece
 
     for value, keys in zip(terms, groups):
         send(value, keys)
-    values = dict(zip(later, terms[len(groups) :]))
-    for level in sorted({len(bits_of(rel)) for rel, _ in later}, reverse=True):
-        keys = [key for key in later if len(bits_of(key[0])) == level]
-        totals = [(values[key], [(0, *piece) for piece in arrived[key]]) for key in keys]
-        if close and level == 1:
-            totals.append((own, [(bounds[key[1]][0], *near[key]) for key in sorted(near)]))
-        results = sum_rows(totals, bounds, after)
-        if close and level == 1:
-            own = results[-1]
-        sums += results[: len(keys)]
-        for key, value in zip(keys, results):
-            send(value, [key])
-    if not close:
-        last.update(near)
-    elif not later:
-        own = own.astype(jnp.bfloat16)
-    return own, last, sums
-
-
-def call(kernel, out_shapes, operands, in_specs, scratch=(), flops=1, name=None):
+    values = terms[len(groups) :]
+    for level in sorted({len(bits_of(keys[0][0])) for keys in waiting}, reverse=True):
+        found = [i for i, keys in enumerate(waiting) if len(bits_of(keys[0][0])) == level]
+        results = sum_rows(
+            [
+                (
+                    values[i],
+                    [
+                        (row_of(waiting[i], key, bounds), *piece)
+                        for key in waiting[i]
+                        for piece in arrived.get(key, [])
+                    ],
+                )
+                for i in found
+            ],
+            bounds,
+            after,
+        )
+        sums += results
+        for i, value in zip(found, results):
+            send(value, waiting[i])
+    return final, sums
+
+
+def call(kernel, out_shapes, operands, in_specs, scratch=(), flops=1, vmem=10, name=None):
     return pl.pallas_call(
         kernel,
         out_shape=out_shapes,
         in_specs=in_specs,
         out_specs=[pl.BlockSpec(memory_space=pltpu.VMEM)] * len(out_shapes),
         scratch_shapes=list(scratch),
-        compiler_params=pltpu.CompilerParams(vmem_limit_bytes=VMEM_LIMIT),
+        compiler_params=pltpu.CompilerParams(vmem_limit_bytes=vmem * MIB),
         cost_estimate=pl.CostEstimate(flops=int(flops), bytes_accessed=1, transcendentals=0),
         name=name,
     )(*operands)
@@ -303,7 +316,7 @@
             out_ref[:, low + head : low + head + HD] = piece.astype(jnp.bfloat16)
 
 
-def project(blocks, weights, cosine, sine, rows):
+def project(blocks, weights, cosine, sine, rows, weight=1):
     keys = sorted(blocks)
     length, width = cosine.shape[0], blocks[0, 0].shape[1]
     features = weights[0].shape[1]
@@ -313,51 +326,45 @@
         block_refs, weight_refs = refs[:n], refs[n : n + 3]
         cos_ref, sin_ref = refs[n + 3 : n + 5]
         outs = refs[n + 5 : n + 8]
-        all_rows, held, sems = refs[n + 8 :]
+        all_rows, sems = refs[n + 8 :]
         copies = block_copies(block_refs, keys, rows, all_rows, sems)
-        loads = [
-            pltpu.make_async_copy(weight_refs[i], held.at[i], sems.at[n + i]) for i in range(3)
-        ]
-        for copy in copies + loads:
+        for copy in copies:
             copy.start()
         for copy in copies:
             copy.wait()
         for i in range(3):
-            loads[i].wait()
             tables = (cos_ref, sin_ref) if i < 2 else ()
-            project_into(all_rows, held.at[i], outs[i], *tables)
+            project_into(all_rows, weight_refs[i], outs[i], *tables)
 
     return call(
         kernel,
         [jax.ShapeDtypeStruct((length, features), jnp.bfloat16)] * 3,
         [blocks[key] for key in keys] + list(weights) + [cosine, sine],
-        [ANY] * (n + 3) + [VMEM, VMEM],
-        [
-            pltpu.VMEM((length, width), jnp.bfloat16),
-            pltpu.VMEM((3, width, features), jnp.bfloat16),
-            pltpu.SemaphoreType.DMA((n + 3,)),
-        ],
+        [ANY] * n + [VMEM] * 5,
+        [pltpu.VMEM((length, width), jnp.bfloat16), pltpu.SemaphoreType.DMA((n,))],
+        flops=weight,
+        vmem=20,
         name="project",
     )
 
 
-def term_outs(rows, width, count):
+def term_outs(rows, width, count, whole):
     bounds = part_bounds(rows, count)
-    groups, later = messages_of(rows, count)
+    groups, waiting = messages_of(rows, count, whole)
 
     def shape(keys, dtype):
         height = sum(bounds[part][1] - bounds[part][0] for _, part in keys)
         return jax.ShapeDtypeStruct((height, width), dtype)
 
     return [shape(keys, jnp.bfloat16) for keys in groups] + [
-        shape([key], jnp.float32) for key in later
+        shape(keys, jnp.float32) for keys in waiting
     ]
 
 
-def store_terms(values, low, refs, rows, count):
+def store_terms(values, low, refs, rows, count, whole):
     bounds = part_bounds(rows, count)
-    groups, later = messages_of(rows, count)
-    for ref, keys in zip(refs, groups + [[key] for key in later]):
+    groups, waiting = messages_of(rows, count, whole)
+    for ref, keys in zip(refs, groups + waiting):
         at = 0
         for rel, part in keys:
             first, last = bounds[part]
@@ -377,14 +384,13 @@
         block_refs, weight_ref = refs[:n], refs[n]
         q_ref, k_ref, v_ref, cos_ref, sin_ref = refs[n + 1 : n + 6]
         d_qkv = refs[n + 6 : n + 9]
-        all_rows, held, d_attn, sems = refs[n + 9 :]
+        all_rows, d_attn, sems = refs[n + 9 :]
         copies = block_copies(block_refs, in_keys, rows, all_rows, sems)
-        copies.append(pltpu.make_async_copy(weight_ref, held, sems.at[n]))
         for copy in copies:
             copy.start()
         for copy in copies:
             copy.wait()
-        project_into(all_rows, held, d_attn)
+        project_into(all_rows, weight_ref, d_attn)
 
         for head in range(features // HD):
             cols = slice(head * HD, (head + 1) * HD)
@@ -417,68 +423,60 @@
         kernel,
         [jax.ShapeDtypeStruct((length, features), jnp.bfloat16)] * 3,
         [blocks[key] for key in in_keys] + [weight] + list(qkv) + [cosine, sine],
-        [ANY] * (n + 1) + [VMEM] * 5,
+        [ANY] * n + [VMEM] * 6,
         [
             pltpu.VMEM((length, width), jnp.bfloat16),
-            pltpu.VMEM((width, features), jnp.bfloat16),
             pltpu.VMEM((length, features), jnp.bfloat16),
-            pltpu.SemaphoreType.DMA((n + 1,)),
+            pltpu.SemaphoreType.DMA((n,)),
         ],
+        vmem=28,
         flops=HEADS_WEIGHT,
         name="backward_heads",
     )
 
 
-def backward_terms(d_qkv, weights, rows, count, after=()):
+def backward_terms(d_qkv, weights, rows, count, whole, after=()):
     length, features = d_qkv[0].shape
     width = weights[0].shape[0]
-    shapes = term_outs(rows, width, count)
+    shapes = term_outs(rows, width, count, whole)
 
     def kernel(*refs):
         grads, weight_refs = refs[:3], refs[3:6]
-        own_ref, *outs = refs[6 + len(after) : -2]
-        held, sems = refs[-2:]
-        loads = [pltpu.make_async_copy(weight_refs[i], held.at[i], sems.at[i]) for i in range(3)]
-        for load in loads:
-            load.start()
-        for load in loads:
-            load.wait()
+        own_ref, *outs = refs[6 + len(after) :]
         for low in range(0, width, CHUNK):
             total = 0.0
             for i in range(3):
                 total += lax.dot_general(
                     grads[i][...],
-                    held[i, low : low + CHUNK, :],
+                    weight_refs[i][low : low + CHUNK, :],
                     NT,
                     preferred_element_type=jnp.float32,
                 )
             own_ref[:, low : low + CHUNK] = total[:rows]
-            store_terms(total, low, outs, rows, count)
+            store_terms(total, low, outs, rows, count, whole)
 
     own, *terms = call(
         kernel,
         [jax.ShapeDtypeStruct((rows, width), jnp.float32)] + shapes,
         list(d_qkv) + list(weights) + list(after),
-        [VMEM] * 3 + [ANY] * (3 + len(after)),
-        [pltpu.VMEM((3, width, features), jnp.bfloat16), pltpu.SemaphoreType.DMA((3,))],
+        [VMEM] * 6 + [ANY] * len(after),
+        vmem=24,
         flops=TERMS_WEIGHT,
         name="backward_terms",
     )
     return own, terms
 
 
-def forward_terms(qkv, act_in, weight, rows, count, after=()):
+def forward_terms(qkv, act_in, weight, rows, count, whole, after=()):
     length, features = qkv[0].shape
     width = weight.shape[0]
-    shapes = term_outs(rows, width, count)
+    shapes = term_outs(rows, width, count, whole)
     step = min(length, 512)
 
     def kernel(*refs):
         q_ref, k_ref, v_ref, act_ref, weight_ref = refs[:5]
-        own_ref, *outs = refs[5 + len(after) : -3]
-        held, attn, sem = refs[-3:]
-        load = pltpu.make_async_copy(weight_ref, held, sem)
-        load.start()
+        own_ref, *outs = refs[5 + len(after) : -1]
+        attn = refs[-1]
         for head in range(features // HD):
             cols = slice(head * HD, (head + 1) * HD)
             for low in range(0, length, step):
@@ -494,24 +492,22 @@
                 )
                 attn[part, cols] = (mixed * (1.0 / total)).astype(jnp.bfloat16)
 
-        load.wait()
         for low in range(0, width, CHUNK):
             total = lax.dot_general(
-                attn[...], held[low : low + CHUNK, :], NT, preferred_element_type=jnp.float32
+                attn[...], weight_ref[low : low + CHUNK, :], NT, preferred_element_type=jnp.float32
             )
-            own_ref[:, low : low + CHUNK] = total[:rows] + act_ref[:, low : low + CHUNK]
-            store_terms(total, low, outs, rows, count)
+            own = total[:rows] + act_ref[:, low : low + CHUNK]
+            own_ref[:, low : low + CHUNK] = own.astype(jnp.bfloat16)
+            store_terms(total, low, outs, rows, count, whole)
 
     own, *terms = call(
         kernel,
-        [jax.ShapeDtypeStruct((rows, width), jnp.float32)] + shapes,
+        [jax.ShapeDtypeStruct((rows, width), jnp.bfloat16)] + shapes,
         list(qkv) + [act_in, weight, *after],
-        [VMEM] * 4 + [ANY] * (1 + len(after)),
-        [
-            pltpu.VMEM((width, features), jnp.bfloat16),
-            pltpu.VMEM((length, features), jnp.bfloat16),
-            pltpu.SemaphoreType.DMA,
-        ],
+        [VMEM] * 5 + [ANY] * len(after),
+        [pltpu.VMEM((length, features), jnp.bfloat16)],
+        vmem=24,
+        flops=FORWARD_WEIGHT,
         name="forward_terms",
     )
     return own, terms
@@ -622,19 +618,13 @@
     d_qkv = backward_heads(all_grad, qkv, own_out, cosine, sine, rows)
     picked = picked_rows(second_hops(all_fwd, rows), d_qkv[:1])
     all_fwd = gather_rest(all_fwd, picked, "input")
-    d_own, d_terms = backward_terms(d_qkv, projections, rows, count, picked)
-    qkv = project(all_fwd, projections, cosine, sine, rows)
-    own, terms = forward_terms(qkv, act_in, own_out, rows, count)
-
-    d_own, d_pieces, d_sums = scatter_blocks(d_own, d_terms, rows, across, "grad", [own])
-    own, pieces, sums = scatter_blocks(
-        own,
-        terms,
-        rows,
-        lambda value, bit: across_and_on(value, 1 << bit),
-        "branch",
-        d_sums,
-        close=True,
+    d_own, d_terms = backward_terms(d_qkv, projections, rows, count, False, picked)
+    qkv = project(all_fwd, projections, cosine, sine, rows, FORWARD_WEIGHT)
+    own, terms = forward_terms(qkv, act_in, own_out, rows, count, True)
+
+    d_pieces, d_sums = scatter_blocks(d_terms, rows, False, across, "grad", [own])
+    pieces, sums = scatter_blocks(
+        terms, rows, True, lambda value, bit: across_and_on(value, 1 << bit), "branch", d_sums
     )
     own = across_and_on(own, 0)
     d_input = input_grad(d_own, d_pieces, saved_in, grad, inv_bwd, gain, bounds, sums)

time: 121 us -> 108 us (0.89)
  Pallas kernels: 42.3 us -> 26 us
  waiting for transfers between devices: 40.8 us -> 50.8 us
  local copies, waits for them, and re-layouts: 8.03 us -> 4.41 us
  starting transfers between devices: 27 us -> 24.4 us
    pallas_call x16, Pallas kernels: 42.3 us -> 26 us  [call(): pl.pallas_call(kernel, out_shape=out_shapes, in_specs=in_specs, out_specs...]
    ppermute x3, waiting for transfers between devices: 13 us -> 19.4 us  [across_and_on(): return lax.ppermute(value, ('pipe', 'seq'), pairs)]
    unnamed x30 -> x24, local copies, waits for them, and re-layouts: 8.03 us -> 4.41 us
    ppermute x18, waiting for transfers between devices: 27.8 us -> 31.4 us  [across(): return lax.ppermute(value, 'seq', [(i, i ^ 1 << bit) for i in range(count)])]
    ppermute x1, starting transfers between devices: 3.59 us -> 1.53 us  [passed_along(): return lax.ppermute(value, axis, pairs)]
    ppermute x3, starting transfers between devices: 3.63 us -> 2.36 us  [across_and_on(): return lax.ppermute(value, ('pipe', 'seq'), pairs)]
  transfers between devices with their start and end apart: 22 -> 22, of which waited for: 8 -> 13; matrix products, arithmetic and copies ran while one was open for 1% -> 1% of each run, Pallas kernels for 34% -> 23%
where the time goes in v2:
time: 108 us
  waiting for transfers between devices  50.8 us (47%)
  Pallas kernels  26 us (24%)
  starting transfers between devices  24.4 us (23%)
  local copies, waits for them, and re-layouts  4.41 us (4%)
  other arithmetic  1.28 us (1%)
    ppermute x18, waiting for transfers between devices, across(): return lax.ppermute(value, 'seq', [(i, i ^ 1 << bit) for i in range(count)])  31.4 us
    pallas_call x16, Pallas kernels, call(): pl.pallas_call(kernel, out_shape=out_shapes, in_specs=in_specs, out_specs...  26 us
    ppermute x18, starting transfers between devices, across(): return lax.ppermute(value, 'seq', [(i, i ^ 1 << bit) for i in range(count)])  20.5 us
    ppermute x3, waiting for transfers between devices, across_and_on(): return lax.ppermute(value, ('pipe', 'seq'), pairs)  19.4 us
    unnamed x24, local copies, waits for them, and re-layouts  4.41 us
    ppermute x3, starting transfers between devices, across_and_on(): return lax.ppermute(value, ('pipe', 'seq'), pairs)  2.36 us
  transfers between devices with their start and end apart: 22, of which 13 were waited for; matrix products, arithmetic and copies ran while one was open for 1% of the time, Pallas kernels for 23%

profile of v2, /device:TPU:0, one launch (start us, length us, event | category | flops | bytes accessed | tf_op | source)
XLA Modules:
  0.0 107.7 jit_solution(11799857209826545102)
XLA Ops:
  0.6 1.2 %copy-done.6 = f32[1,128,2048]{2,1,0:T(8,128)S(1)} copy-done((f32[1,128,2048]{2,1,0:T(8,128)S(1)}, f32[1,128,2048]{2,1,0:T(8,128)}, u32[]{:S(2)}) %copy-start.6) | copy-done | bytes 1048600
  1.9 0.7 copy-done.9
  2.6 0.2 norm.2
  2.8 3.0 %collective-permute-start.3 = (bf16[128,2048]{1,0:T(8,128)(2,1)S(1)}, bf16[128,2048]{1,0:T(8,128)(2,1)S(1)}, u32[]{:S(2)}, u32[]{:S(2)}) collective-permute-start(bf16[128,2048]{1,0:T(8,128)(2,1)S(1)} %get-tuple-element.34.refs_0_), channel_id=1, source_target_pairs={{0,1},{1,0},{2,3},{3,2},{4,5},{5,4},{6,7},{7,6},{8,9},{9,8},{10,11... | collective-permute-start | bytes 1572872 | tf_op jit(solution)/shard_map/gather_saved_block1/ppermute | solution.py:53
  5.8 1.5 %collective-permute-start.2 = (bf16[128,2048]{1,0:T(8,128)(2,1)S(1)}, bf16[128,2048]{1,0:T(8,128)(2,1)S(1)}, u32[]{:S(2)}, u32[]{:S(2)}) collective-permute-start(bf16[128,2048]{1,0:T(8,128)(2,1)S(1)} %get-tuple-element.34.refs_0_), channel_id=1, source_target_pairs={{0,2},{1,3},{2,0},{3,1},{4,6},{5,7},{6,4},{7,5},{8,10},{9,11},{10,... | collective-permute-start | bytes 1572872 | tf_op jit(solution)/shard_map/gather_saved_block2/ppermute | solution.py:53
  7.3 1.2 %copy-done.4 = f32[1,128,2048]{2,1,0:T(8,128)S(1)} copy-done((f32[1,128,2048]{2,1,0:T(8,128)S(1)}, f32[1,128,2048]{2,1,0:T(8,128)}, u32[]{:S(2)}) %copy-start.4) | copy-done | bytes 1048600
  8.6 0.6 collective-permute-start.1
  9.3 9.2 %collective-permute-done.3.refs_1_ = bf16[128,2048]{1,0:T(8,128)(2,1)S(1)} collective-permute-done((bf16[128,2048]{1,0:T(8,128)(2,1)S(1)}, bf16[128,2048]{1,0:T(8,128)(2,1)S(1)}, u32[]{:S(2)}, u32[]{:S(2)}) %collective-permute-start.3) | collective-permute-done | bytes 524320 | tf_op jit(solution)/shard_map/gather_saved_block1/ppermute | solution.py:53
  18.5 2.1 %collective-permute-done.2.refs_0_.refs_2_ = bf16[128,2048]{1,0:T(8,128)(2,1)S(1)} collective-permute-done((bf16[128,2048]{1,0:T(8,128)(2,1)S(1)}, bf16[128,2048]{1,0:T(8,128)(2,1)S(1)}, u32[]{:S(2)}, u32[]{:S(2)}) %collective-permute-start.2) | collective-permute-done | bytes 524320 | tf_op jit(solution)/shard_map/gather_saved_block2/ppermute | solution.py:53
  20.7 0.1 collective-permute-start.8
  20.8 2.0 %collective-permute-start.9 = (bf16[64,2048]{1,0:T(8,128)(2,1)S(1)}, bf16[64,2048]{1,0:T(8,128)(2,1)S(1)}, u32[]{:S(2)}, u32[]{:S(2)}) collective-permute-start(bf16[64,2048]{1,0:T(8,128)(2,1)S(1)} %get-tuple-element.36.refs_3_), channel_id=1, source_target_pairs={{0,2},{1,3},{2,0},{3,1},{4,6},{5,7},{6,4},{7,5},{8,10},{9,11},{10,... | collective-permute-start | bytes 786440 | tf_op jit(solution)/shard_map/gather_saved_block3_row64/ppermute | solution.py:53
  22.8 7.1 %collective-permute-done.1.refs_1_ = bf16[128,2048]{1,0:T(8,128)(2,1)} collective-permute-done((bf16[128,2048]{1,0:T(8,128)(2,1)S(1)}, bf16[128,2048]{1,0:T(8,128)(2,1)}, u32[]{:S(2)}, u32[]{:S(2)}) %collective-permute-start.1) | collective-permute-done | bytes 524320 | tf_op jit(solution)/shard_map/gather_grad_block1/ppermute | solution.py:53
  29.9 2.1 %collective-permute-done.refs_0_.refs_2_ = bf16[128,2048]{1,0:T(8,128)(2,1)} collective-permute-done((bf16[128,2048]{1,0:T(8,128)(2,1)S(1)}, bf16[128,2048]{1,0:T(8,128)(2,1)}, u32[]{:S(2)}, u32[]{:S(2)}) %collective-permute-start) | collective-permute-done | bytes 524320 | tf_op jit(solution)/shard_map/gather_grad_block2/ppermute | solution.py:53
  32.0 1.4 %pick.4 = (bf16[64,2048]{1,0:T(8,128)(2,1)S(1)}, bf16[64,2048]{1,0:T(8,128)(2,1)S(1)}) custom-call(bf16[128,2048]{1,0:T(8,128)(2,1)} %collective-permute-done.refs_0_.refs_2_, bf16[128,2048]{1,0:T(8,128)(2,1)} %collective-permute-done.1.refs_1_, bf16[64,2048]{1,0:T(8,128)(2,1)S(1)} %get-tuple-element.35.refs_2_, bf16[64,2048]{1,0:T(8,128)(2,1)S(1)} %get-tuple-element.36.refs_3_), custom_call_target="tpu_custom_call" | custom-call | flops 1 | bytes 1 | tf_op jit(solution)/shard_map/pick/pallas_call | solution.py:185
  33.5 2.0 %collective-permute-start.7 = (bf16[64,2048]{1,0:T(8,128)(2,1)S(1)}, bf16[64,2048]{1,0:T(8,128)(2,1)S(1)}, u32[]{:S(2)}, u32[]{:S(2)}) collective-permute-start(bf16[64,2048]{1,0:T(8,128)(2,1)S(1)} %get-tuple-element.38.refs_1_), channel_id=1, source_target_pairs={{0,2},{1,3},{2,0},{3,1},{4,6},{5,7},{6,4},{7,5},{8,10},{9,11},{10,... | collective-permute-start | bytes 786440 | tf_op jit(solution)/shard_map/gather_grad_block3_row64/ppermute | solution.py:53
  35.5 1.0 fusion
  36.5 0.2 pad_maximum_fusion
  36.7 0.8 norm.3
  37.6 1.9 %collective-permute-start.4 = (bf16[128,2048]{1,0:T(8,128)(2,1)S(1)}, bf16[128,2048]{1,0:T(8,128)(2,1)S(1)}, u32[]{:S(2)}, u32[]{:S(2)}) collective-permute-start(bf16[128,2048]{1,0:T(8,128)(2,1)S(1)} %get-tuple-element.39.refs_0_), channel_id=1, source_target_pairs={{0,1},{1,0},{2,3},{3,2},{4,5},{5,4},{6,7},{7,6},{8,9},{9,8},{10,11... | collective-permute-start | bytes 1572872 | tf_op jit(solution)/shard_map/gather_input_block1/ppermute | solution.py:53
  39.6 3.8 %project.2 = (bf16[512,512]{1,0:T(8,128)(2,1)S(1)}, bf16[512,512]{1,0:T(8,128)(2,1)S(1)}, bf16[512,512]{1,0:T(8,128)(2,1)S(1)}) custom-call(bf16[128,2048]{1,0:T(8,128)(2,1)S(1)} %get-tuple-element.34.refs_0_, bf16[128,2048]{1,0:T(8,128)(2,1)S(1)} %collective-permute-done.3.refs_1_, bf16[128,2048]{1,0:T(8,128)(2,1)S(1)} %collective-permute-done.2.refs_0_.refs_2_, ...), custom_call_target="tpu_custom_call" | custom-call | flops 1 | bytes 1 | tf_op jit(solution)/shard_map/project/pallas_call | solution.py:185
  43.4 6.6 %backward_heads.1 = (bf16[512,512]{1,0:T(8,128)(2,1)S(1)}, bf16[512,512]{1,0:T(8,128)(2,1)S(1)}, bf16[512,512]{1,0:T(8,128)(2,1)S(1)}) custom-call(bf16[128,2048]{1,0:T(8,128)(2,1)S(1)} %cast.1.refs_2_.refs_0_, bf16[128,2048]{1,0:T(8,128)(2,1)} %collective-permute-done.1.refs_1_, bf16[128,2048]{1,0:T(8,128)(2,1)} %collective-permute-done.refs_0_.refs_2_, ...), custom_call_target="tpu_custom_call" | custom-call | flops 8000000000 | bytes 1 | tf_op jit(solution)/shard_map/backward_heads/pallas_call | solution.py:185
  50.0 2.8 %collective-permute-done.5.refs_0_.refs_2_ = bf16[128,2048]{1,0:T(8,128)(2,1)S(1)} collective-permute-done((bf16[128,2048]{1,0:T(8,128)(2,1)S(1)}, bf16[128,2048]{1,0:T(8,128)(2,1)S(1)}, u32[]{:S(2)}, u32[]{:S(2)}) %collective-permute-start.5) | collective-permute-done | bytes 524320 | tf_op jit(solution)/shard_map/gather_input_block2/ppermute | solution.py:53
  52.9 0.4 collective-permute-start.10
  53.3 1.7 %collective-permute-start.11 = (bf16[64,2048]{1,0:T(8,128)(2,1)S(1)}, bf16[64,2048]{1,0:T(8,128)(2,1)S(1)}, u32[]{:S(2)}, u32[]{:S(2)}) collective-permute-start(bf16[64,2048]{1,0:T(8,128)(2,1)S(1)} %get-tuple-element.45.refs_7_), channel_id=1, source_target_pairs={{0,2},{1,3},{2,0},{3,1},{4,6},{5,7},{6,4},{7,5},{8,10},{9,11},{10,... | collective-permute-start | bytes 786440 | tf_op jit(solution)/shard_map/gather_input_block3_row64/ppermute | solution.py:53
  55.0 3.4 %backward_terms.1 = (f32[128,2048]{1,0:T(8,128)S(1)}, bf16[128,2048]{1,0:T(8,128)(2,1)S(1)}, bf16[128,2048]{1,0:T(8,128)(2,1)S(1)}, f32[64,2048]{1,0:T(8,128)S(1)}, f32[64,2048]{1,0:T(8,128)S(1)}) custom-call(bf16[512,512]{1,0:T(8,128)(2,1)S(1)} %get-tuple-element.43.refs_2_.refs_0_, bf16[512,512]{1,0:T(8,128)(2,1)S(1)} %get-tuple-element.54.refs_1_, ...), custom_call_target="tpu_custom_call" | custom-call | flops 3000000000 | bytes 1 | tf_op jit(solution)/shard_map/backward_terms/pallas_call | solution.py:185
  58.5 1.6 %collective-permute-start.15 = (bf16[128,2048]{1,0:T(8,128)(2,1)S(1)}, bf16[128,2048]{1,0:T(8,128)(2,1)S(1)}, u32[]{:S(2)}, u32[]{:S(2)}) collective-permute-start(bf16[128,2048]{1,0:T(8,128)(2,1)S(1)} %get-tuple-element.58), channel_id=1, source_target_pairs={{0,1},{1,0},{2,3},{3,2},{4,5},{5,4},{6,7},{7,6},{8,9},{9,8},{10,11... | collective-permute-start | bytes 1572872 | tf_op jit(solution)/shard_map/scatter_grad_block3_part0/ppermute | solution.py:53
  60.0 0.5 collective-permute-start.16
  60.5 3.8 %project.3 = (bf16[512,512]{1,0:T(8,128)(2,1)S(1)}, bf16[512,512]{1,0:T(8,128)(2,1)S(1)}, bf16[512,512]{1,0:T(8,128)(2,1)S(1)}) custom-call(bf16[128,2048]{1,0:T(8,128)(2,1)S(1)} %get-tuple-element.39.refs_0_, bf16[128,2048]{1,0:T(8,128)(2,1)S(1)} %collective-permute-done.4.refs_1_, bf16[128,2048]{1,0:T(8,128)(2,1)S(1)} %collective-permute-done.5.refs_0_.refs_2_, ...), custom_call_target="tpu_custom_call" | custom-call | flops 5000000000 | bytes 1 | tf_op jit(solution)/shard_map/project/pallas_call | solution.py:185
  64.4 2.8 %forward_terms.1 = (bf16[128,2048]{1,0:T(8,128)(2,1)S(1)}, bf16[64,2048]{1,0:T(8,128)(2,1)S(1)}, bf16[64,2048]{1,0:T(8,128)(2,1)S(1)}, f32[128,2048]{1,0:T(8,128)S(1)}, f32[128,2048]{1,0:T(8,128)S(1)}) custom-call(bf16[512,512]{1,0:T(8,128)(2,1)S(1)} %get-tuple-element.46.refs_0_, bf16[512,512]{1,0:T(8,128)(2,1)S(1)} %get-tuple-element.47.refs_1_, ...), custom_call_target="tpu_custom_call" | custom-call | flops 5000000000 | bytes 1 | tf_op jit(solution)/shard_map/forward_terms/pallas_call | solution.py:185
  67.2 1.7 %collective-permute-start.13 = (bf16[64,2048]{1,0:T(8,128)(2,1)S(1)}, bf16[64,2048]{1,0:T(8,128)(2,1)S(1)}, u32[]{:S(2)}, u32[]{:S(2)}) collective-permute-start(bf16[64,2048]{1,0:T(8,128)(2,1)S(1)} %get-tuple-element.52), channel_id=1, source_target_pairs={{0,1},{1,0},{2,3},{3,2},{4,5},{5,4},{6,7},{7,6},{8,9},{9,8},{10,11... | collective-permute-start | bytes 786440 | tf_op jit(solution)/shard_map/scatter_branch_block3_part0/ppermute | solution.py:53
  68.9 2.3 %collective-permute-start.14 = (bf16[64,2048]{1,0:T(8,128)(2,1)S(1)}, bf16[64,2048]{1,0:T(8,128)(2,1)S(1)}, u32[]{:S(2)}, u32[]{:S(2)}) collective-permute-start(bf16[64,2048]{1,0:T(8,128)(2,1)S(1)} %get-tuple-element.53), channel_id=1, source_target_pairs={{0,2},{1,3},{2,0},{3,1},{4,6},{5,7},{6,4},{7,5},{8,10},{9,11},{10,... | collective-permute-start | bytes 786440 | tf_op jit(solution)/shard_map/scatter_branch_block3_part1/ppermute | solution.py:53
  71.2 2.2 %collective-permute-done.15.refs_2_.refs_0_ = bf16[128,2048]{1,0:T(8,128)(2,1)S(1)} collective-permute-done((bf16[128,2048]{1,0:T(8,128)(2,1)S(1)}, bf16[128,2048]{1,0:T(8,128)(2,1)S(1)}, u32[]{:S(2)}, u32[]{:S(2)}) %collective-permute-start.15) | collective-permute-done | bytes 524320 | tf_op jit(solution)/shard_map/scatter_grad_block3_part0/ppermute | solution.py:53
  73.4 1.5 %collective-permute-done.16.refs_3_ = bf16[128,2048]{1,0:T(8,128)(2,1)S(1)} collective-permute-done((bf16[128,2048]{1,0:T(8,128)(2,1)S(1)}, bf16[128,2048]{1,0:T(8,128)(2,1)S(1)}, u32[]{:S(2)}, u32[]{:S(2)}) %collective-permute-start.16) | collective-permute-done | bytes 524320 | tf_op jit(solution)/shard_map/scatter_grad_block3_part1/ppermute | solution.py:53
  75.0 0.6 collective-permute-start.20
  75.6 0.3 collective-permute-start.19
  75.9 3.1 %collective-permute-done.13.refs_2_ = bf16[64,2048]{1,0:T(8,128)(2,1)S(1)} collective-permute-done((bf16[64,2048]{1,0:T(8,128)(2,1)S(1)}, bf16[64,2048]{1,0:T(8,128)(2,1)S(1)}, u32[]{:S(2)}, u32[]{:S(2)}) %collective-permute-start.13) | collective-permute-done | bytes 262176 | tf_op jit(solution)/shard_map/scatter_branch_block3_part0/ppermute | solution.py:53
  79.0 1.0 collective-permute-done.14.refs_3_
  80.0 0.1 sum_rows.3
  80.2 2.3 %collective-permute-start.18 = (bf16[128,2048]{1,0:T(8,128)(2,1)S(1)}, bf16[128,2048]{1,0:T(8,128)(2,1)S(1)}, u32[]{:S(2)}, u32[]{:S(2)}) collective-permute-start(bf16[128,2048]{1,0:T(8,128)(2,1)S(1)} %get-tuple-element.63.refs_4_), channel_id=1, source_target_pairs={{0,6},{1,7},{2,4},{3,5},{4,10},{5,11},{6,8},{7,9},{8,14},{9,15},{1... | collective-permute-start | bytes 1572872 | tf_op jit(solution)/shard_map/scatter_branch_block2_part0/ppermute | solution.py:63
  82.5 0.3 collective-permute-done.20.refs_2_
  82.8 0.5 input_grad.1
  83.3 1.5 %collective-permute-start.21 = (bf16[128,2048]{1,0:T(8,128)(2,1)S(1)}, bf16[128,2048]{1,0:T(8,128)(2,1)S(1)}, u32[]{:S(2)}, u32[]{:S(2)}) collective-permute-start(bf16[128,2048]{1,0:T(8,128)(2,1)S(1)} %input_grad.1), channel_id=1, source_target_pairs={{0,28},{4,0},{8,4},{12,8},{16,12},{20,16},{24,20},{28,24},{1,29},{... | collective-permute-start | bytes 1572872 | tf_op jit(solution)/shard_map/ppermute | solution.py:69
  84.9 1.4 %collective-permute-done.12.own_ref = bf16[128,2048]{1,0:T(8,128)(2,1)S(1)} collective-permute-done((bf16[128,2048]{1,0:T(8,128)(2,1)S(1)}, bf16[128,2048]{1,0:T(8,128)(2,1)S(1)}, u32[]{:S(2)}, u32[]{:S(2)}) %collective-permute-start.12) | collective-permute-done | bytes 524320 | tf_op jit(solution)/shard_map/ppermute | solution.py:63
  86.3 10.6 %collective-permute-done.17.refs_0_.refs_1_ = bf16[128,2048]{1,0:T(8,128)(2,1)S(1)} collective-permute-done((bf16[128,2048]{1,0:T(8,128)(2,1)S(1)}, bf16[128,2048]{1,0:T(8,128)(2,1)S(1)}, u32[]{:S(2)}, u32[]{:S(2)}) %collective-permute-start.17) | collective-permute-done | bytes 524320 | tf_op jit(solution)/shard_map/scatter_branch_block1_part0/ppermute | solution.py:63
  96.9 7.4 %collective-permute-done.18.refs_2_.refs_3_ = bf16[128,2048]{1,0:T(8,128)(2,1)S(1)} collective-permute-done((bf16[128,2048]{1,0:T(8,128)(2,1)S(1)}, bf16[128,2048]{1,0:T(8,128)(2,1)S(1)}, u32[]{:S(2)}, u32[]{:S(2)}) %collective-permute-start.18) | collective-permute-done | bytes 524320 | tf_op jit(solution)/shard_map/scatter_branch_block2_part0/ppermute | solution.py:63
  104.3 1.1 %activation_sum.1.refs_0_ = f32[1,128,2048]{2,1,0:T(8,128)} custom-call(bf16[128,2048]{1,0:T(8,128)(2,1)S(1)} %collective-permute-done.12.own_ref, bf16[128,2048]{1,0:T(8,128)(2,1)S(1)} %collective-permute-done.17.refs_0_.refs_1_, bf16[128,2048]{1,0:T(8,128)(2,1)S(1)} %collective-permute-done.17.refs_0_.refs_1_, ...), custom_call_target="tpu_custom_call" | custom-call | flops 8000000000 | bytes 1 | tf_op jit(solution)/shard_map/activation_sum/pallas_call | solution.py:185
  105.5 1.2 %copy-done.8 = f32[1,128,2048]{2,1,0:T(8,128)S(1)} copy-done((f32[1,128,2048]{2,1,0:T(8,128)S(1)}, f32[1,128,2048]{2,1,0:T(8,128)}, u32[]{:S(2)}) %copy-start.8) | copy-done | bytes 1048600
  106.7 1.0 widen.1
  (41 shorter events, 0.6 us)
Async XLA Ops:
  0.6 1.2 %copy-start.6 = (f32[1,128,2048]{2,1,0:T(8,128)S(1)}, f32[1,128,2048]{2,1,0:T(8,128)}, u32[]{:S(2)}) copy-start(f32[1,128,2048]{2,1,0:T(8,128)} %param.9) | copy-start | bytes 3145732
  1.9 0.7 copy-start.9
  2.8 15.8 %collective-permute-start.3 = (bf16[128,2048]{1,0:T(8,128)(2,1)S(1)}, bf16[128,2048]{1,0:T(8,128)(2,1)S(1)}, u32[]{:S(2)}, u32[]{:S(2)}) collective-permute-start(bf16[128,2048]{1,0:T(8,128)(2,1)S(1)} %get-tuple-element.34.refs_0_), channel_id=1, source_target_pairs={{0,1},{1,0},{2,3},{3,2},{4,5},{5,4},{6,7},{7,6},{8,9},{9,8},{10,11... | collective-permute-start | bytes 1572872 | tf_op jit(solution)/shard_map/gather_saved_block1/ppermute | solution.py:53
  5.8 14.8 %collective-permute-start.2 = (bf16[128,2048]{1,0:T(8,128)(2,1)S(1)}, bf16[128,2048]{1,0:T(8,128)(2,1)S(1)}, u32[]{:S(2)}, u32[]{:S(2)}) collective-permute-start(bf16[128,2048]{1,0:T(8,128)(2,1)S(1)} %get-tuple-element.34.refs_0_), channel_id=1, source_target_pairs={{0,2},{1,3},{2,0},{3,1},{4,6},{5,7},{6,4},{7,5},{8,10},{9,11},{10,... | collective-permute-start | bytes 1572872 | tf_op jit(solution)/shard_map/gather_saved_block2/ppermute | solution.py:53
  7.3 1.2 %copy-start.4 = (f32[1,128,2048]{2,1,0:T(8,128)S(1)}, f32[1,128,2048]{2,1,0:T(8,128)}, u32[]{:S(2)}) copy-start(f32[1,128,2048]{2,1,0:T(8,128)} %param.10) | copy-start | bytes 3145732
  8.5 28.2 %copy-start.3 = (f32[1,128,2048]{2,1,0:T(8,128)S(1)}, f32[1,128,2048]{2,1,0:T(8,128)}, u32[]{:S(2)}) copy-start(f32[1,128,2048]{2,1,0:T(8,128)} %param.8) | copy-start | bytes 3145732
  8.6 21.3 %collective-permute-start.1 = (bf16[128,2048]{1,0:T(8,128)(2,1)S(1)}, bf16[128,2048]{1,0:T(8,128)(2,1)}, u32[]{:S(2)}, u32[]{:S(2)}) collective-permute-start(bf16[128,2048]{1,0:T(8,128)(2,1)S(1)} %cast.1.refs_2_.refs_0_), channel_id=1, source_target_pairs={{0,1},{1,0},{2,3},{3,2},{4,5},{5,4},{6,7},{7,6},{8,9},{9,8},{10,11... | collective-permute-start | bytes 1572872 | tf_op jit(solution)/shard_map/gather_grad_block1/ppermute | solution.py:53
  9.2 22.8 %collective-permute-start = (bf16[128,2048]{1,0:T(8,128)(2,1)S(1)}, bf16[128,2048]{1,0:T(8,128)(2,1)}, u32[]{:S(2)}, u32[]{:S(2)}) collective-permute-start(bf16[128,2048]{1,0:T(8,128)(2,1)S(1)} %cast.1.refs_2_.refs_0_), channel_id=1, source_target_pairs={{0,2},{1,3},{2,0},{3,1},{4,6},{5,7},{6,4},{7,5},{8,10},{9,11},{10,... | collective-permute-start | bytes 1572872 | tf_op jit(solution)/shard_map/gather_grad_block2/ppermute | solution.py:53
  20.6 18.9 %copy-start.2 = (bf16[1,2048,512]{2,1,0:T(8,128)(2,1)S(1)}, bf16[1,2048,512]{2,1,0:T(8,128)(2,1)}, u32[]{:S(2)}) copy-start(bf16[1,2048,512]{2,1,0:T(8,128)(2,1)} %param.14) | copy-start | bytes 6291460
  20.7 16.0 %copy-start.10 = (f32[1,2048]{1,0:T(1,128)S(1)}, f32[1,2048]{1,0:T(1,128)}, u32[]{:S(2)}) copy-start(f32[1,2048]{1,0:T(1,128)} %gain_ref.5) | copy-start | bytes 24580
  20.7 16.9 %collective-permute-start.8 = (bf16[64,2048]{1,0:T(8,128)(2,1)S(1)}, bf16[64,2048]{1,0:T(8,128)(2,1)S(1)}, u32[]{:S(2)}, u32[]{:S(2)}) collective-permute-start(bf16[64,2048]{1,0:T(8,128)(2,1)S(1)} %get-tuple-element.35.refs_2_), channel_id=1, source_target_pairs={{0,1},{1,0},{2,3},{3,2},{4,5},{5,4},{6,7},{7,6},{8,9},{9,8},{10,11... | collective-permute-start | bytes 786440 | tf_op jit(solution)/shard_map/gather_saved_block3_row0/ppermute | solution.py:53
  20.8 18.8 %collective-permute-start.9 = (bf16[64,2048]{1,0:T(8,128)(2,1)S(1)}, bf16[64,2048]{1,0:T(8,128)(2,1)S(1)}, u32[]{:S(2)}, u32[]{:S(2)}) collective-permute-start(bf16[64,2048]{1,0:T(8,128)(2,1)S(1)} %get-tuple-element.36.refs_3_), channel_id=1, source_target_pairs={{0,2},{1,3},{2,0},{3,1},{4,6},{5,7},{6,4},{7,5},{8,10},{9,11},{10,... | collective-permute-start | bytes 786440 | tf_op jit(solution)/shard_map/gather_saved_block3_row64/ppermute | solution.py:53
  32.0 7.6 %copy-start.1 = (bf16[1,2048,512]{2,1,0:T(8,128)(2,1)S(1)}, bf16[1,2048,512]{2,1,0:T(8,128)(2,1)}, u32[]{:S(2)}) copy-start(bf16[1,2048,512]{2,1,0:T(8,128)(2,1)} %param.13) | copy-start | bytes 6291460
  33.3 6.2 %copy-start = (bf16[1,2048,512]{2,1,0:T(8,128)(2,1)S(1)}, bf16[1,2048,512]{2,1,0:T(8,128)(2,1)}, u32[]{:S(2)}) copy-start(bf16[1,2048,512]{2,1,0:T(8,128)(2,1)} %param.12) | copy-start | bytes 6291460
  33.4 10.0 %collective-permute-start.6 = (bf16[64,2048]{1,0:T(8,128)(2,1)S(1)}, bf16[64,2048]{1,0:T(8,128)(2,1)S(1)}, u32[]{:S(2)}, u32[]{:S(2)}) collective-permute-start(bf16[64,2048]{1,0:T(8,128)(2,1)S(1)} %get-tuple-element.37.refs_0_), channel_id=1, source_target_pairs={{0,1},{1,0},{2,3},{3,2},{4,5},{5,4},{6,7},{7,6},{8,9},{9,8},{10,11... | collective-permute-start | bytes 786440 | tf_op jit(solution)/shard_map/gather_grad_block3_row0/ppermute | solution.py:53
  33.5 9.9 %collective-permute-start.7 = (bf16[64,2048]{1,0:T(8,128)(2,1)S(1)}, bf16[64,2048]{1,0:T(8,128)(2,1)S(1)}, u32[]{:S(2)}, u32[]{:S(2)}) collective-permute-start(bf16[64,2048]{1,0:T(8,128)(2,1)S(1)} %get-tuple-element.38.refs_1_), channel_id=1, source_target_pairs={{0,2},{1,3},{2,0},{3,1},{4,6},{5,7},{6,4},{7,5},{8,10},{9,11},{10,... | collective-permute-start | bytes 786440 | tf_op jit(solution)/shard_map/gather_grad_block3_row64/ppermute | solution.py:53
  37.5 15.3 %collective-permute-start.5 = (bf16[128,2048]{1,0:T(8,128)(2,1)S(1)}, bf16[128,2048]{1,0:T(8,128)(2,1)S(1)}, u32[]{:S(2)}, u32[]{:S(2)}) collective-permute-start(bf16[128,2048]{1,0:T(8,128)(2,1)S(1)} %get-tuple-element.39.refs_0_), channel_id=1, source_target_pairs={{0,2},{1,3},{2,0},{3,1},{4,6},{5,7},{6,4},{7,5},{8,10},{9,11},{10,... | collective-permute-start | bytes 1572872 | tf_op jit(solution)/shard_map/gather_input_block2/ppermute | solution.py:53
  37.6 15.3 %collective-permute-start.4 = (bf16[128,2048]{1,0:T(8,128)(2,1)S(1)}, bf16[128,2048]{1,0:T(8,128)(2,1)S(1)}, u32[]{:S(2)}, u32[]{:S(2)}) collective-permute-start(bf16[128,2048]{1,0:T(8,128)(2,1)S(1)} %get-tuple-element.39.refs_0_), channel_id=1, source_target_pairs={{0,1},{1,0},{2,3},{3,2},{4,5},{5,4},{6,7},{7,6},{8,9},{9,8},{10,11... | collective-permute-start | bytes 1572872 | tf_op jit(solution)/shard_map/gather_input_block1/ppermute | solution.py:53
  39.6 3.8 %copy-start.11 = (bf16[1,2048,512]{2,1,0:T(8,128)(2,1)S(1)}, bf16[1,2048,512]{2,1,0:T(8,128)(2,1)}, u32[]{:S(2)}) copy-start(bf16[1,2048,512]{2,1,0:T(8,128)(2,1)} %param.15) | copy-start | bytes 6291460
  52.9 7.6 %collective-permute-start.10 = (bf16[64,2048]{1,0:T(8,128)(2,1)S(1)}, bf16[64,2048]{1,0:T(8,128)(2,1)S(1)}, u32[]{:S(2)}, u32[]{:S(2)}) collective-permute-start(bf16[64,2048]{1,0:T(8,128)(2,1)S(1)} %get-tuple-element.44.refs_6_), channel_id=1, source_target_pairs={{0,1},{1,0},{2,3},{3,2},{4,5},{5,4},{6,7},{7,6},{8,9},{9,8},{10,11... | collective-permute-start | bytes 786440 | tf_op jit(solution)/shard_map/gather_input_block3_row0/ppermute | solution.py:53
  53.3 7.2 %collective-permute-start.11 = (bf16[64,2048]{1,0:T(8,128)(2,1)S(1)}, bf16[64,2048]{1,0:T(8,128)(2,1)S(1)}, u32[]{:S(2)}, u32[]{:S(2)}) collective-permute-start(bf16[64,2048]{1,0:T(8,128)(2,1)S(1)} %get-tuple-element.45.refs_7_), channel_id=1, source_target_pairs={{0,2},{1,3},{2,0},{3,1},{4,6},{5,7},{6,4},{7,5},{8,10},{9,11},{10,... | collective-permute-start | bytes 786440 | tf_op jit(solution)/shard_map/gather_input_block3_row64/ppermute | solution.py:53
  58.5 14.9 %collective-permute-start.15 = (bf16[128,2048]{1,0:T(8,128)(2,1)S(1)}, bf16[128,2048]{1,0:T(8,128)(2,1)S(1)}, u32[]{:S(2)}, u32[]{:S(2)}) collective-permute-start(bf16[128,2048]{1,0:T(8,128)(2,1)S(1)} %get-tuple-element.58), channel_id=1, source_target_pairs={{0,1},{1,0},{2,3},{3,2},{4,5},{5,4},{6,7},{7,6},{8,9},{9,8},{10,11... | collective-permute-start | bytes 1572872 | tf_op jit(solution)/shard_map/scatter_grad_block3_part0/ppermute | solution.py:53
  60.0 14.9 %collective-permute-start.16 = (bf16[128,2048]{1,0:T(8,128)(2,1)S(1)}, bf16[128,2048]{1,0:T(8,128)(2,1)S(1)}, u32[]{:S(2)}, u32[]{:S(2)}) collective-permute-start(bf16[128,2048]{1,0:T(8,128)(2,1)S(1)} %get-tuple-element.59), channel_id=1, source_target_pairs={{0,2},{1,3},{2,0},{3,1},{4,6},{5,7},{6,4},{7,5},{8,10},{9,11},{10,... | collective-permute-start | bytes 1572872 | tf_op jit(solution)/shard_map/scatter_grad_block3_part1/ppermute | solution.py:53
  67.2 11.8 %collective-permute-start.13 = (bf16[64,2048]{1,0:T(8,128)(2,1)S(1)}, bf16[64,2048]{1,0:T(8,128)(2,1)S(1)}, u32[]{:S(2)}, u32[]{:S(2)}) collective-permute-start(bf16[64,2048]{1,0:T(8,128)(2,1)S(1)} %get-tuple-element.52), channel_id=1, source_target_pairs={{0,1},{1,0},{2,3},{3,2},{4,5},{5,4},{6,7},{7,6},{8,9},{9,8},{10,11... | collective-permute-start | bytes 786440 | tf_op jit(solution)/shard_map/scatter_branch_block3_part0/ppermute | solution.py:53
  68.9 11.1 %collective-permute-start.14 = (bf16[64,2048]{1,0:T(8,128)(2,1)S(1)}, bf16[64,2048]{1,0:T(8,128)(2,1)S(1)}, u32[]{:S(2)}, u32[]{:S(2)}) collective-permute-start(bf16[64,2048]{1,0:T(8,128)(2,1)S(1)} %get-tuple-element.53), channel_id=1, source_target_pairs={{0,2},{1,3},{2,0},{3,1},{4,6},{5,7},{6,4},{7,5},{8,10},{9,11},{10,... | collective-permute-start | bytes 786440 | tf_op jit(solution)/shard_map/scatter_branch_block3_part1/ppermute | solution.py:53
  75.0 7.8 %copy-start.5 = (f32[1,128,2048]{2,1,0:T(8,128)S(1)}, f32[1,128,2048]{2,1,0:T(8,128)}, u32[]{:S(2)}) copy-start(f32[1,128,2048]{2,1,0:T(8,128)} %param.10) | copy-start | bytes 3145732
  75.0 7.8 %copy-start.7 = (f32[1,128,2048]{2,1,0:T(8,128)S(1)}, f32[1,128,2048]{2,1,0:T(8,128)}, u32[]{:S(2)}) copy-start(f32[1,128,2048]{2,1,0:T(8,128)} %param.9) | copy-start | bytes 3145732
  75.0 7.8 %collective-permute-start.20 = (bf16[64,2048]{1,0:T(8,128)(2,1)S(1)}, bf16[64,2048]{1,0:T(8,128)(2,1)S(1)}, u32[]{:S(2)}, u32[]{:S(2)}) collective-permute-start(bf16[64,2048]{1,0:T(8,128)(2,1)S(1)} %get-tuple-element.60.refs_4_), channel_id=1, source_target_pairs={{0,2},{1,3},{2,0},{3,1},{4,6},{5,7},{6,4},{7,5},{8,10},{9,11},{10,... | collective-permute-start | bytes 786440 | tf_op jit(solution)/shard_map/scatter_grad_block2_part0/ppermute | solution.py:53
  75.6 7.2 %collective-permute-start.19 = (bf16[64,2048]{1,0:T(8,128)(2,1)S(1)}, bf16[64,2048]{1,0:T(8,128)(2,1)S(1)}, u32[]{:S(2)}, u32[]{:S(2)}) collective-permute-start(bf16[64,2048]{1,0:T(8,128)(2,1)S(1)} %get-tuple-element.61.refs_5_), channel_id=1, source_target_pairs={{0,1},{1,0},{2,3},{3,2},{4,5},{5,4},{6,7},{7,6},{8,9},{9,8},{10,11... | collective-permute-start | bytes 786440 | tf_op jit(solution)/shard_map/scatter_grad_block1_part1/ppermute | solution.py:53
  75.9 10.4 %collective-permute-start.12 = (bf16[128,2048]{1,0:T(8,128)(2,1)S(1)}, bf16[128,2048]{1,0:T(8,128)(2,1)S(1)}, u32[]{:S(2)}, u32[]{:S(2)}) collective-permute-start(bf16[128,2048]{1,0:T(8,128)(2,1)S(1)} %get-tuple-element.49.refs_4_), channel_id=1, source_target_pairs={{0,4},{1,5},{2,6},{3,7},{4,8},{5,9},{6,10},{7,11},{8,12},{9,13},{1... | collective-permute-start | bytes 1572872 | tf_op jit(solution)/shard_map/ppermute | solution.py:63
  80.1 16.8 %collective-permute-start.17 = (bf16[128,2048]{1,0:T(8,128)(2,1)S(1)}, bf16[128,2048]{1,0:T(8,128)(2,1)S(1)}, u32[]{:S(2)}, u32[]{:S(2)}) collective-permute-start(bf16[128,2048]{1,0:T(8,128)(2,1)S(1)} %get-tuple-element.62.refs_5_), channel_id=1, source_target_pairs={{0,5},{1,4},{2,7},{3,6},{4,9},{5,8},{6,11},{7,10},{8,13},{9,12},{1... | collective-permute-start | bytes 1572872 | tf_op jit(solution)/shard_map/scatter_branch_block1_part0/ppermute | solution.py:63
  80.2 24.1 %collective-permute-start.18 = (bf16[128,2048]{1,0:T(8,128)(2,1)S(1)}, bf16[128,2048]{1,0:T(8,128)(2,1)S(1)}, u32[]{:S(2)}, u32[]{:S(2)}) collective-permute-start(bf16[128,2048]{1,0:T(8,128)(2,1)S(1)} %get-tuple-element.63.refs_4_), channel_id=1, source_target_pairs={{0,6},{1,7},{2,4},{3,5},{4,10},{5,11},{6,8},{7,9},{8,14},{9,15},{1... | collective-permute-start | bytes 1572872 | tf_op jit(solution)/shard_map/scatter_branch_block2_part0/ppermute | solution.py:63
  83.3 22.1 %collective-permute-start.21 = (bf16[128,2048]{1,0:T(8,128)(2,1)S(1)}, bf16[128,2048]{1,0:T(8,128)(2,1)S(1)}, u32[]{:S(2)}, u32[]{:S(2)}) collective-permute-start(bf16[128,2048]{1,0:T(8,128)(2,1)S(1)} %input_grad.1), channel_id=1, source_target_pairs={{0,28},{4,0},{8,4},{12,8},{16,12},{20,16},{24,20},{28,24},{1,29},{... | collective-permute-start | bytes 1572872 | tf_op jit(solution)/shard_map/ppermute | solution.py:69
  105.5 1.2 %copy-start.8 = (f32[1,128,2048]{2,1,0:T(8,128)S(1)}, f32[1,128,2048]{2,1,0:T(8,128)}, u32[]{:S(2)}) copy-start(f32[1,128,2048]{2,1,0:T(8,128)} %activation_sum.1.refs_0_) | copy-start | bytes 3145732

commit v3 on v2

--- a/solution.py
+++ b/solution.py
@@ -111,7 +111,7 @@
     return blocks
 
 
-def messages_of(rows, count, whole):
+def messages_of(rows, count, joined):
     parts = range(len(part_bounds(rows, count)))
     later = {
         (rel ^ (1 << last_bit(rel, part)), part)
@@ -119,66 +119,55 @@
         for part in parts
         if len(bits_of(rel)) > 1
     }
-    groups, waiting = {}, {}
-    for rel in reversed(by_distance(count)):
-        for part in parts:
-            key = (rel, part)
-            if whole and len(bits_of(rel)) == 1:
-                waiting.setdefault(rel, []).append(key)
-            elif key in later:
-                waiting[key] = [key]
-            else:
-                groups.setdefault(key if whole else last_bit(*key), []).append(key)
-    return list(groups.values()), list(waiting.values())
-
-
-def row_of(keys, key, bounds):
-    before = keys[: keys.index(key)]
-    return sum(bounds[part][1] - bounds[part][0] for _, part in before)
-
-
-def scatter_blocks(terms, rows, whole, send_last, what, after=()):
-    count = lax.axis_size("seq")
-    bounds = part_bounds(rows, count)
-    groups, waiting = messages_of(rows, count, whole)
-    arrived, final, sums = {}, {}, []
-
-    def send(value, keys):
+    keys = [(rel, part) for rel in reversed(by_distance(count)) for part in parts]
+    groups = {}
+    for key in keys:
+        if key not in later:
+            groups.setdefault(last_bit(*key) if joined else key, []).append(key)
+    return list(groups.values()), [key for key in keys if key in later]
+
+
+class Scatter:
+
+    def __init__(self, terms, rows, joined, send_last, what):
+        count = lax.axis_size("seq")
+        self.bounds = part_bounds(rows, count)
+        self.groups, waiting = messages_of(rows, count, joined)
+        self.leaving = list(terms[: len(self.groups)])
+        self.waiting = dict(zip(waiting, terms[len(self.groups) :]))
+        self.send_last, self.what = send_last, what
+        self.arrived, self.final = {}, {}
+
+    def send(self, value, keys):
         bit = last_bit(*keys[0])
         targets = [(rel ^ (1 << bit), part) for rel, part in keys]
-        with jax.named_scope(f"scatter_{what}_block{keys[0][0]}_part{keys[0][1]}"):
-            moved = (across if any(rel for rel, _ in targets) else send_last)(value, bit)
+        onward = any(rel for rel, _ in targets)
+        with jax.named_scope(f"scatter_{self.what}_block{keys[0][0]}_part{keys[0][1]}"):
+            moved = (across if onward else self.send_last)(value, bit)
+        first = 0
         for key, target in zip(keys, targets):
-            piece = (moved, row_of(keys, key, bounds))
             if target[0]:
-                arrived.setdefault(target, []).append(piece)
+                self.arrived.setdefault(target, []).append((moved, first))
             else:
-                final[key] = piece
-
-    for value, keys in zip(terms, groups):
-        send(value, keys)
-    values = terms[len(groups) :]
-    for level in sorted({len(bits_of(keys[0][0])) for keys in waiting}, reverse=True):
-        found = [i for i, keys in enumerate(waiting) if len(bits_of(keys[0][0])) == level]
-        results = sum_rows(
-            [
-                (
-                    values[i],
-                    [
-                        (row_of(waiting[i], key, bounds), *piece)
-                        for key in waiting[i]
-                        for piece in arrived.get(key, [])
-                    ],
-                )
-                for i in found
-            ],
-            bounds,
-            after,
-        )
-        sums += results
-        for i, value in zip(found, results):
-            send(value, waiting[i])
-    return final, sums
+                self.final[key] = (moved, first)
+            first += self.bounds[key[1]][1] - self.bounds[key[1]][0]
+
+    def onward(self):
+        return [i for i, keys in enumerate(self.groups) if len(bits_of(keys[0][0])) > 1]
+
+    def send_groups(self, places):
+        for i in places:
+            self.send(self.leaving[i], self.groups[i])
+
+    def send_sums(self, handed_on=(), after=()):
+        for level in sorted({len(bits_of(rel)) for rel, _ in self.waiting}, reverse=True):
+            keys = [key for key in self.waiting if len(bits_of(key[0])) == level]
+            totals = [(self.waiting[key], self.arrived[key]) for key in keys]
+            results = sum_rows(totals, handed_on, after)
+            handed_on = results[len(keys) :]
+            for key, value in zip(keys, results):
+                self.send(value, [key])
+        return handed_on
 
 
 def call(kernel, out_shapes, operands, in_specs, scratch=(), flops=1, vmem=10, name=None):
@@ -214,9 +203,17 @@
     rows, width = inputs.shape
     n = len(pieces)
 
-    def kernel(x_ref, gain_ref, *refs):
-        refs = refs[:n] + refs[n + len(after) :]
+    def kernel(x_any, gain_any, *refs):
+        refs, (x_ref, gain_ref, sems) = refs[:n] + refs[n + len(after) : -3], refs[-3:]
         out_ref, inv_ref = refs[n : n + 2]
+        copies = [
+            pltpu.make_async_copy(source, held, sems.at[i])
+            for i, (source, held) in enumerate([(x_any, x_ref), (gain_any, gain_ref)])
+        ]
+        for copy in copies:
+            copy.start()
+        for copy in copies:
+            copy.wait()
         x = x_ref[...]
         inv = lax.rsqrt(jnp.mean(x * x, -1, keepdims=True) + 1e-05)
         out_ref[...] = (x * inv * gain_ref[...]).astype(jnp.bfloat16)
@@ -231,7 +228,12 @@
         ]
         + picked_shapes(pieces),
         [inputs, gain] + [value for value, _, _ in pieces] + list(after),
-        [VMEM] * (2 + n) + [ANY] * len(after),
+        [ANY] * 2 + [VMEM] * n + [ANY] * len(after),
+        [
+            pltpu.VMEM(inputs.shape, jnp.float32),
+            pltpu.VMEM(gain.shape, jnp.float32),
+            pltpu.SemaphoreType.DMA((2,)),
+        ],
         name="norm",
     )
 
@@ -264,27 +266,30 @@
     )[0]
 
 
-def sum_rows(totals, bounds, after=()):
-    height = bounds[0][1] - bounds[0][0]
+def sum_rows(totals, handed_on=(), after=()):
     pieces = [piece for _, pieces in totals for piece in pieces]
-    n, m = len(totals), len(pieces)
+    n, m, k = len(totals), len(pieces), len(handed_on)
 
     def kernel(*refs):
-        terms, arrivals, outs = refs[:n], list(refs[n : n + m]), refs[-n:]
-        for (term, moved), term_ref, out_ref in zip(totals, terms, outs):
-            found = [(row, first, arrivals.pop(0)) for row, _, first in moved]
-            for low in range(0, term.shape[0], height):
-                total = term_ref[low : low + height, :]
-                for row, first, ref in found:
-                    if row == low:
-                        total = total + ref[first : first + height, :].astype(jnp.float32)
-                out_ref[low : low + height, :] = total.astype(jnp.bfloat16)
-
-    return call(
-        kernel,
-        [jax.ShapeDtypeStruct(term.shape, jnp.bfloat16) for term, _ in totals],
-        [term for term, _ in totals] + [value for _, value, _ in pieces] + list(after),
-        [VMEM] * (n + m) + [ANY] * len(after),
+        arrivals, outs = list(refs[n : n + m]), refs[-n - k :]
+        for (term, moved), term_ref, out_ref in zip(totals, refs, outs):
+            total = term_ref[...]
+            for _, first in moved:
+                ref = arrivals.pop(0)
+                total = total + ref[first : first + term.shape[0], :].astype(jnp.float32)
+            out_ref[...] = total.astype(jnp.bfloat16)
+        for in_ref, out_ref in zip(refs[n + m : n + m + k], outs[n:]):
+            out_ref[...] = in_ref[...]
+
+    return call(
+        kernel,
+        [jax.ShapeDtypeStruct(term.shape, jnp.bfloat16) for term, _ in totals]
+        + [jax.ShapeDtypeStruct(value.shape, value.dtype) for value in handed_on],
+        [term for term, _ in totals]
+        + [value for value, _ in pieces]
+        + list(handed_on)
+        + list(after),
+        [VMEM] * (n + m + k) + [ANY] * len(after),
         name="sum_rows",
     )
 
@@ -348,23 +353,23 @@
     )
 
 
-def term_outs(rows, width, count, whole):
+def term_outs(rows, width, count, joined):
     bounds = part_bounds(rows, count)
-    groups, waiting = messages_of(rows, count, whole)
+    groups, waiting = messages_of(rows, count, joined)
 
     def shape(keys, dtype):
         height = sum(bounds[part][1] - bounds[part][0] for _, part in keys)
         return jax.ShapeDtypeStruct((height, width), dtype)
 
     return [shape(keys, jnp.bfloat16) for keys in groups] + [
-        shape(keys, jnp.float32) for keys in waiting
+        shape([key], jnp.float32) for key in waiting
     ]
 
 
-def store_terms(values, low, refs, rows, count, whole):
+def store_terms(values, low, refs, rows, count, joined):
     bounds = part_bounds(rows, count)
-    groups, waiting = messages_of(rows, count, whole)
-    for ref, keys in zip(refs, groups + waiting):
+    groups, waiting = messages_of(rows, count, joined)
+    for ref, keys in zip(refs, groups + [[key] for key in waiting]):
         at = 0
         for rel, part in keys:
             first, last = bounds[part]
@@ -435,10 +440,10 @@
     )
 
 
-def backward_terms(d_qkv, weights, rows, count, whole, after=()):
+def backward_terms(d_qkv, weights, rows, count, joined, after=()):
     length, features = d_qkv[0].shape
     width = weights[0].shape[0]
-    shapes = term_outs(rows, width, count, whole)
+    shapes = term_outs(rows, width, count, joined)
 
     def kernel(*refs):
         grads, weight_refs = refs[:3], refs[3:6]
@@ -453,7 +458,7 @@
                     preferred_element_type=jnp.float32,
                 )
             own_ref[:, low : low + CHUNK] = total[:rows]
-            store_terms(total, low, outs, rows, count, whole)
+            store_terms(total, low, outs, rows, count, joined)
 
     own, *terms = call(
         kernel,
@@ -467,10 +472,10 @@
     return own, terms
 
 
-def forward_terms(qkv, act_in, weight, rows, count, whole, after=()):
+def forward_terms(qkv, act_in, weight, rows, count, joined, after=()):
     length, features = qkv[0].shape
     width = weight.shape[0]
-    shapes = term_outs(rows, width, count, whole)
+    shapes = term_outs(rows, width, count, joined)
     step = min(length, 512)
 
     def kernel(*refs):
@@ -498,7 +503,7 @@
             )
             own = total[:rows] + act_ref[:, low : low + CHUNK]
             own_ref[:, low : low + CHUNK] = own.astype(jnp.bfloat16)
-            store_terms(total, low, outs, rows, count, whole)
+            store_terms(total, low, outs, rows, count, joined)
 
     own, *terms = call(
         kernel,
@@ -544,11 +549,11 @@
     )[0]
 
 
-def activation_sum(own, pieces, bounds):
+def activation_sum(own, pieces, bounds, after=()):
     keys = sorted(pieces)
 
     def kernel(own_ref, *refs):
-        out_ref = refs[len(keys)]
+        out_ref = refs[-1]
         for part, (low, high) in enumerate(bounds):
             total = own_ref[low:high, :].astype(jnp.float32)
             for ref, key in zip(refs, keys):
@@ -560,22 +565,22 @@
     return call(
         kernel,
         [jax.ShapeDtypeStruct((1, *own.shape), jnp.float32)],
-        [own] + [pieces[key][0] for key in keys],
-        [VMEM] * (1 + len(keys)),
+        [own] + [pieces[key][0] for key in keys] + list(after),
+        [VMEM] * (1 + len(keys)) + [ANY] * len(after),
         flops=LAST_SUM_WEIGHT,
         name="activation_sum",
     )[0]
 
 
-def widened(values, after=()):
-    def kernel(in_ref, *refs):
-        refs[len(after)][0] = in_ref[...].astype(jnp.float32)
+def widened(values):
+    def kernel(in_ref, out_ref):
+        out_ref[0] = in_ref[...].astype(jnp.float32)
 
     return call(
         kernel,
         [jax.ShapeDtypeStruct((1, *values.shape), jnp.float32)],
-        (values, *after),
-        [VMEM] + [ANY] * len(after),
+        (values,),
+        [VMEM],
         name="widen",
     )[0]
 
@@ -618,18 +623,27 @@
     d_qkv = backward_heads(all_grad, qkv, own_out, cosine, sine, rows)
     picked = picked_rows(second_hops(all_fwd, rows), d_qkv[:1])
     all_fwd = gather_rest(all_fwd, picked, "input")
-    d_own, d_terms = backward_terms(d_qkv, projections, rows, count, False, picked)
+    d_own, d_terms = backward_terms(d_qkv, projections, rows, count, True, picked)
     qkv = project(all_fwd, projections, cosine, sine, rows, FORWARD_WEIGHT)
-    own, terms = forward_terms(qkv, act_in, own_out, rows, count, True)
-
-    d_pieces, d_sums = scatter_blocks(d_terms, rows, False, across, "grad", [own])
-    pieces, sums = scatter_blocks(
-        terms, rows, True, lambda value, bit: across_and_on(value, 1 << bit), "branch", d_sums
-    )
+    own, terms = forward_terms(qkv, act_in, own_out, rows, count, False)
+
+    back = Scatter(d_terms, rows, True, across, "grad")
+    front = Scatter(
+        terms, rows, False, lambda value, bit: across_and_on(value, 1 << bit), "branch"
+    )
+    back.send_groups(range(len(back.groups)))
+    onward = front.onward()
+    front.send_groups([i for i in range(len(front.groups)) if i not in onward])
     own = across_and_on(own, 0)
-    d_input = input_grad(d_own, d_pieces, saved_in, grad, inv_bwd, gain, bounds, sums)
-    act_next = activation_sum(own, pieces, bounds)
-    return (act_next, widened(passed_along(d_input, "pipe", -1), [act_next]))
+    soon = [own] + [value for value, _ in front.final.values()]
+    held = back.send_sums([front.leaving[i] for i in onward], [terms[0]])
+    for i, value in zip(onward, held):
+        front.leaving[i] = value
+    front.send_groups(onward)
+    d_input = input_grad(d_own, back.final, saved_in, grad, inv_bwd, gain, bounds, soon)
+    front.send_sums(after=[d_input])
+    grad_prev = widened(passed_along(d_input, "pipe", -1))
+    return (activation_sum(own, front.final, bounds, [grad_prev]), grad_prev)
 
 
 def solution(mesh):

time: 108 us -> 106 us (0.981)
  waiting for transfers between devices: 50.8 us -> 46.8 us
  starting transfers between devices: 24.4 us -> 26.1 us
    ppermute x3 -> x5, waiting for transfers between devices: 19.4 us -> 16.1 us  [across_and_on(): return lax.ppermute(value, ('pipe', 'seq'), pairs)]
    ppermute x3 -> x5, starting transfers between devices: 2.36 us -> 4.54 us  [across_and_on(): return lax.ppermute(value, ('pipe', 'seq'), pairs)]
    ppermute x1, starting transfers between devices: 1.53 us -> 0.06 us  [passed_along(): return lax.ppermute(value, axis, pairs)]
  transfers between devices with their start and end apart: 22 -> 24, of which waited for: 13 -> 16; matrix products, arithmetic and copies ran while one was open for 1% -> 1% of each run, Pallas kernels for 23% -> 23%
where the time goes in v3:
time: 106 us; the launch traced here: 105 us
  waiting for transfers between devices  46.8 us (44%)
  starting transfers between devices  26.1 us (25%)
  Pallas kernels  25.8 us (24%)
  local copies, waits for them, and re-layouts  4.41 us (4%)
  other arithmetic  1.28 us (1%)
    ppermute x18, waiting for transfers between devices, across(): return lax.ppermute(value, 'seq', [(i, i ^ 1 << bit) for i in range(count)])  30.5 us
    pallas_call x16, Pallas kernels, call(): pl.pallas_call(kernel, out_shape=out_shapes, in_specs=in_specs, out_specs...  25.8 us
    ppermute x18, starting transfers between devices, across(): return lax.ppermute(value, 'seq', [(i, i ^ 1 << bit) for i in range(count)])  21.5 us
    ppermute x5, waiting for transfers between devices, across_and_on(): return lax.ppermute(value, ('pipe', 'seq'), pairs)  16.1 us
    ppermute x5, starting transfers between devices, across_and_on(): return lax.ppermute(value, ('pipe', 'seq'), pairs)  4.54 us
    unnamed x24, local copies, waits for them, and re-layouts  4.41 us
  transfers between devices with their start and end apart: 24, of which 16 were waited for; matrix products, arithmetic and copies ran while one was open for 1% of the time, Pallas kernels for 23%

profile of v3, /device:TPU:0, one launch (start us, length us, event | category | flops | bytes accessed | tf_op | source)
XLA Modules:
  0.0 105.2 jit_solution(3180003464481378873)
XLA Ops:
  0.6 1.2 %copy-done.7 = f32[1,128,2048]{2,1,0:T(8,128)S(1)} copy-done((f32[1,128,2048]{2,1,0:T(8,128)S(1)}, f32[1,128,2048]{2,1,0:T(8,128)}, u32[]{:S(2)}) %copy-start.7) | copy-done | bytes 1048600
  1.9 0.7 copy-done.9
  2.6 0.3 norm.2
  2.9 3.0 %collective-permute-start.2 = (bf16[128,2048]{1,0:T(8,128)(2,1)S(1)}, bf16[128,2048]{1,0:T(8,128)(2,1)S(1)}, u32[]{:S(2)}, u32[]{:S(2)}) collective-permute-start(bf16[128,2048]{1,0:T(8,128)(2,1)S(1)} %get-tuple-element.38.refs_0_), channel_id=1, source_target_pairs={{0,2},{1,3},{2,0},{3,1},{4,6},{5,7},{6,4},{7,5},{8,10},{9,11},{10,... | collective-permute-start | bytes 1572872 | tf_op jit(solution)/shard_map/gather_saved_block2/ppermute | solution.py:53
  5.9 1.5 %collective-permute-start.3 = (bf16[128,2048]{1,0:T(8,128)(2,1)S(1)}, bf16[128,2048]{1,0:T(8,128)(2,1)S(1)}, u32[]{:S(2)}, u32[]{:S(2)}) collective-permute-start(bf16[128,2048]{1,0:T(8,128)(2,1)S(1)} %get-tuple-element.38.refs_0_), channel_id=1, source_target_pairs={{0,1},{1,0},{2,3},{3,2},{4,5},{5,4},{6,7},{7,6},{8,9},{9,8},{10,11... | collective-permute-start | bytes 1572872 | tf_op jit(solution)/shard_map/gather_saved_block1/ppermute | solution.py:53
  7.4 1.2 %copy-done.5 = f32[1,128,2048]{2,1,0:T(8,128)S(1)} copy-done((f32[1,128,2048]{2,1,0:T(8,128)S(1)}, f32[1,128,2048]{2,1,0:T(8,128)}, u32[]{:S(2)}) %copy-start.5) | copy-done | bytes 1048600
  8.7 0.6 collective-permute-start
  9.4 9.2 %collective-permute-done.2.refs_0_.refs_2_ = bf16[128,2048]{1,0:T(8,128)(2,1)S(1)} collective-permute-done((bf16[128,2048]{1,0:T(8,128)(2,1)S(1)}, bf16[128,2048]{1,0:T(8,128)(2,1)S(1)}, u32[]{:S(2)}, u32[]{:S(2)}) %collective-permute-start.2) | collective-permute-done | bytes 524320 | tf_op jit(solution)/shard_map/gather_saved_block2/ppermute | solution.py:53
  18.6 2.1 %collective-permute-done.3.refs_1_ = bf16[128,2048]{1,0:T(8,128)(2,1)S(1)} collective-permute-done((bf16[128,2048]{1,0:T(8,128)(2,1)S(1)}, bf16[128,2048]{1,0:T(8,128)(2,1)S(1)}, u32[]{:S(2)}, u32[]{:S(2)}) %collective-permute-start.3) | collective-permute-done | bytes 524320 | tf_op jit(solution)/shard_map/gather_saved_block1/ppermute | solution.py:53
  20.8 1.6 %collective-permute-start.8 = (bf16[64,2048]{1,0:T(8,128)(2,1)S(1)}, bf16[64,2048]{1,0:T(8,128)(2,1)S(1)}, u32[]{:S(2)}, u32[]{:S(2)}) collective-permute-start(bf16[64,2048]{1,0:T(8,128)(2,1)S(1)} %get-tuple-element.39.refs_2_), channel_id=1, source_target_pairs={{0,1},{1,0},{2,3},{3,2},{4,5},{5,4},{6,7},{7,6},{8,9},{9,8},{10,11... | collective-permute-start | bytes 786440 | tf_op jit(solution)/shard_map/gather_saved_block3_row0/ppermute | solution.py:53
  22.4 0.5 collective-permute-start.9
  22.9 7.1 %collective-permute-done.refs_0_.refs_2_ = bf16[128,2048]{1,0:T(8,128)(2,1)} collective-permute-done((bf16[128,2048]{1,0:T(8,128)(2,1)S(1)}, bf16[128,2048]{1,0:T(8,128)(2,1)}, u32[]{:S(2)}, u32[]{:S(2)}) %collective-permute-start) | collective-permute-done | bytes 524320 | tf_op jit(solution)/shard_map/gather_grad_block2/ppermute | solution.py:53
  30.0 2.1 %collective-permute-done.1.refs_1_ = bf16[128,2048]{1,0:T(8,128)(2,1)} collective-permute-done((bf16[128,2048]{1,0:T(8,128)(2,1)S(1)}, bf16[128,2048]{1,0:T(8,128)(2,1)}, u32[]{:S(2)}, u32[]{:S(2)}) %collective-permute-start.1) | collective-permute-done | bytes 524320 | tf_op jit(solution)/shard_map/gather_grad_block1/ppermute | solution.py:53
  32.1 1.4 %pick.4 = (bf16[64,2048]{1,0:T(8,128)(2,1)S(1)}, bf16[64,2048]{1,0:T(8,128)(2,1)S(1)}) custom-call(bf16[128,2048]{1,0:T(8,128)(2,1)} %collective-permute-done.refs_0_.refs_2_, bf16[128,2048]{1,0:T(8,128)(2,1)} %collective-permute-done.1.refs_1_, bf16[64,2048]{1,0:T(8,128)(2,1)S(1)} %get-tuple-element.39.refs_2_, bf16[64,2048]{1,0:T(8,128)(2,1)S(1)} %get-tuple-element.40.refs_3_), custom_call_target="tpu_custom_call" | custom-call | flops 1 | bytes 1 | tf_op jit(solution)/shard_map/pick/pallas_call | solution.py:174
  33.5 1.6 %collective-permute-start.6 = (bf16[64,2048]{1,0:T(8,128)(2,1)S(1)}, bf16[64,2048]{1,0:T(8,128)(2,1)S(1)}, u32[]{:S(2)}, u32[]{:S(2)}) collective-permute-start(bf16[64,2048]{1,0:T(8,128)(2,1)S(1)} %get-tuple-element.41.refs_0_), channel_id=1, source_target_pairs={{0,1},{1,0},{2,3},{3,2},{4,5},{5,4},{6,7},{7,6},{8,9},{9,8},{10,11... | collective-permute-start | bytes 786440 | tf_op jit(solution)/shard_map/gather_grad_block3_row0/ppermute | solution.py:53
  35.0 0.5 collective-permute-start.7
  35.6 1.0 fusion
  36.8 0.9 norm.3
  37.9 2.0 %collective-permute-start.5 = (bf16[128,2048]{1,0:T(8,128)(2,1)S(1)}, bf16[128,2048]{1,0:T(8,128)(2,1)S(1)}, u32[]{:S(2)}, u32[]{:S(2)}) collective-permute-start(bf16[128,2048]{1,0:T(8,128)(2,1)S(1)} %get-tuple-element.43.refs_0_), channel_id=1, source_target_pairs={{0,2},{1,3},{2,0},{3,1},{4,6},{5,7},{6,4},{7,5},{8,10},{9,11},{10,... | collective-permute-start | bytes 1572872 | tf_op jit(solution)/shard_map/gather_input_block2/ppermute | solution.py:53
  39.9 3.6 %project.2 = (bf16[512,512]{1,0:T(8,128)(2,1)S(1)}, bf16[512,512]{1,0:T(8,128)(2,1)S(1)}, bf16[512,512]{1,0:T(8,128)(2,1)S(1)}) custom-call(bf16[128,2048]{1,0:T(8,128)(2,1)S(1)} %get-tuple-element.38.refs_0_, bf16[128,2048]{1,0:T(8,128)(2,1)S(1)} %collective-permute-done.3.refs_1_, bf16[128,2048]{1,0:T(8,128)(2,1)S(1)} %collective-permute-done.2.refs_0_.refs_2_, ...), custom_call_target="tpu_custom_call" | custom-call | flops 1 | bytes 1 | tf_op jit(solution)/shard_map/project/pallas_call | solution.py:174
  43.5 0.8 collective-permute-done.7.refs_4_
  44.3 6.6 %backward_heads.1 = (bf16[512,512]{1,0:T(8,128)(2,1)S(1)}, bf16[512,512]{1,0:T(8,128)(2,1)S(1)}, bf16[512,512]{1,0:T(8,128)(2,1)S(1)}) custom-call(bf16[128,2048]{1,0:T(8,128)(2,1)S(1)} %cast.1.refs_2_.refs_0_, bf16[128,2048]{1,0:T(8,128)(2,1)} %collective-permute-done.1.refs_1_, bf16[128,2048]{1,0:T(8,128)(2,1)} %collective-permute-done.refs_0_.refs_2_, ...), custom_call_target="tpu_custom_call" | custom-call | flops 8000000000 | bytes 1 | tf_op jit(solution)/shard_map/backward_heads/pallas_call | solution.py:174
  50.9 2.0 %collective-permute-done.4.refs_1_ = bf16[128,2048]{1,0:T(8,128)(2,1)S(1)} collective-permute-done((bf16[128,2048]{1,0:T(8,128)(2,1)S(1)}, bf16[128,2048]{1,0:T(8,128)(2,1)S(1)}, u32[]{:S(2)}, u32[]{:S(2)}) %collective-permute-start.4) | collective-permute-done | bytes 524320 | tf_op jit(solution)/shard_map/gather_input_block1/ppermute | solution.py:53
  53.0 1.6 %collective-permute-start.10 = (bf16[64,2048]{1,0:T(8,128)(2,1)S(1)}, bf16[64,2048]{1,0:T(8,128)(2,1)S(1)}, u32[]{:S(2)}, u32[]{:S(2)}) collective-permute-start(bf16[64,2048]{1,0:T(8,128)(2,1)S(1)} %get-tuple-element.48.refs_6_), channel_id=1, source_target_pairs={{0,1},{1,0},{2,3},{3,2},{4,5},{5,4},{6,7},{7,6},{8,9},{9,8},{10,11... | collective-permute-start | bytes 786440 | tf_op jit(solution)/shard_map/gather_input_block3_row0/ppermute | solution.py:53
  54.6 0.5 collective-permute-start.11
  55.1 3.4 %backward_terms.1 = (f32[128,2048]{1,0:T(8,128)S(1)}, bf16[128,2048]{1,0:T(8,128)(2,1)S(1)}, bf16[128,2048]{1,0:T(8,128)(2,1)S(1)}, f32[64,2048]{1,0:T(8,128)S(1)}, f32[64,2048]{1,0:T(8,128)S(1)}) custom-call(bf16[512,512]{1,0:T(8,128)(2,1)S(1)} %get-tuple-element.47.refs_2_.refs_0_, bf16[512,512]{1,0:T(8,128)(2,1)S(1)} %get-tuple-element.57.refs_1_, ...), custom_call_target="tpu_custom_call" | custom-call | flops 3000000000 | bytes 1 | tf_op jit(solution)/shard_map/backward_terms/pallas_call | solution.py:174
  58.5 0.5 collective-permute-start.14
  59.0 1.7 %collective-permute-start.15 = (bf16[128,2048]{1,0:T(8,128)(2,1)S(1)}, bf16[128,2048]{1,0:T(8,128)(2,1)S(1)}, u32[]{:S(2)}, u32[]{:S(2)}) collective-permute-start(bf16[128,2048]{1,0:T(8,128)(2,1)S(1)} %get-tuple-element.62), channel_id=1, source_target_pairs={{0,2},{1,3},{2,0},{3,1},{4,6},{5,7},{6,4},{7,5},{8,10},{9,11},{10,... | collective-permute-start | bytes 1572872 | tf_op jit(solution)/shard_map/scatter_grad_block3_part1/ppermute | solution.py:53
  60.7 1.9 %collective-permute-done.11.refs_4_ = bf16[64,2048]{1,0:T(8,128)(2,1)S(1)} collective-permute-done((bf16[64,2048]{1,0:T(8,128)(2,1)S(1)}, bf16[64,2048]{1,0:T(8,128)(2,1)S(1)}, u32[]{:S(2)}, u32[]{:S(2)}) %collective-permute-start.11) | collective-permute-done | bytes 262176 | tf_op jit(solution)/shard_map/gather_input_block3_row64/ppermute | solution.py:53
  62.5 3.6 %project.3 = (bf16[512,512]{1,0:T(8,128)(2,1)S(1)}, bf16[512,512]{1,0:T(8,128)(2,1)S(1)}, bf16[512,512]{1,0:T(8,128)(2,1)S(1)}) custom-call(bf16[128,2048]{1,0:T(8,128)(2,1)S(1)} %get-tuple-element.43.refs_0_, bf16[128,2048]{1,0:T(8,128)(2,1)S(1)} %collective-permute-done.4.refs_1_, bf16[128,2048]{1,0:T(8,128)(2,1)S(1)} %collective-permute-done.5.refs_0_.refs_2_, ...), custom_call_target="tpu_custom_call" | custom-call | flops 5000000000 | bytes 1 | tf_op jit(solution)/shard_map/project/pallas_call | solution.py:174
  66.2 2.8 %forward_terms.1 = (bf16[128,2048]{1,0:T(8,128)(2,1)S(1)}, bf16[64,2048]{1,0:T(8,128)(2,1)S(1)}, bf16[64,2048]{1,0:T(8,128)(2,1)S(1)}, bf16[64,2048]{1,0:T(8,128...) custom-call(bf16[512,512]{1,0:T(8,128)(2,1)S(1)} %get-tuple-element.50.refs_0_, ...), custom_call_target="tpu_custom_call" | custom-call | flops 5000000000 | bytes 1 | tf_op jit(solution)/shard_map/forward_terms/pallas_call | solution.py:174
  69.1 1.7 %collective-permute-start.13 = (bf16[64,2048]{1,0:T(8,128)(2,1)S(1)}, bf16[64,2048]{1,0:T(8,128)(2,1)S(1)}, u32[]{:S(2)}, u32[]{:S(2)}) collective-permute-start(bf16[64,2048]{1,0:T(8,128)(2,1)S(1)} %get-tuple-element.54), channel_id=1, source_target_pairs={{0,5},{1,4},{2,7},{3,6},{4,9},{5,8},{6,11},{7,10},{8,13},{9,12},{1... | collective-permute-start | bytes 786440 | tf_op jit(solution)/shard_map/scatter_branch_block1_part0/ppermute | solution.py:63
  70.8 0.4 collective-permute-done.14.refs_2_.refs_0_
  71.2 1.2 %collective-permute-done.15.refs_3_ = bf16[128,2048]{1,0:T(8,128)(2,1)S(1)} collective-permute-done((bf16[128,2048]{1,0:T(8,128)(2,1)S(1)}, bf16[128,2048]{1,0:T(8,128)(2,1)S(1)}, u32[]{:S(2)}, u32[]{:S(2)}) %collective-permute-start.15) | collective-permute-done | bytes 524320 | tf_op jit(solution)/shard_map/scatter_grad_block3_part1/ppermute | solution.py:53
  72.5 0.6 collective-permute-start.18
  73.1 1.2 %collective-permute-start.19 = (bf16[64,2048]{1,0:T(8,128)(2,1)S(1)}, bf16[64,2048]{1,0:T(8,128)(2,1)S(1)}, u32[]{:S(2)}, u32[]{:S(2)}) collective-permute-start(bf16[64,2048]{1,0:T(8,128)(2,1)S(1)} %get-tuple-element.70), channel_id=1, source_target_pairs={{0,2},{1,3},{2,0},{3,1},{4,6},{5,7},{6,4},{7,5},{8,10},{9,11},{10,... | collective-permute-start | bytes 786440 | tf_op jit(solution)/shard_map/scatter_grad_block2_part0/ppermute | solution.py:53
  74.3 7.8 %collective-permute-done.13.refs_6_.refs_0_ = bf16[64,2048]{1,0:T(8,128)(2,1)S(1)} collective-permute-done((bf16[64,2048]{1,0:T(8,128)(2,1)S(1)}, bf16[64,2048]{1,0:T(8,128)(2,1)S(1)}, u32[]{:S(2)}, u32[]{:S(2)}) %collective-permute-start.13) | collective-permute-done | bytes 262176 | tf_op jit(solution)/shard_map/scatter_branch_block1_part0/ppermute | solution.py:63
  82.1 1.7 %collective-permute-start.16 = (bf16[64,2048]{1,0:T(8,128)(2,1)S(1)}, bf16[64,2048]{1,0:T(8,128)(2,1)S(1)}, u32[]{:S(2)}, u32[]{:S(2)}) collective-permute-start(bf16[64,2048]{1,0:T(8,128)(2,1)S(1)} %get-tuple-element.65), channel_id=1, source_target_pairs={{0,1},{1,0},{2,3},{3,2},{4,5},{5,4},{6,7},{7,6},{8,9},{9,8},{10,11... | collective-permute-start | bytes 786440 | tf_op jit(solution)/shard_map/scatter_branch_block3_part0/ppermute | solution.py:53
  83.8 0.5 collective-permute-done.20.refs_5_.refs_3_
  84.3 2.4 %collective-permute-start.17 = (bf16[64,2048]{1,0:T(8,128)(2,1)S(1)}, bf16[64,2048]{1,0:T(8,128)(2,1)S(1)}, u32[]{:S(2)}, u32[]{:S(2)}) collective-permute-start(bf16[64,2048]{1,0:T(8,128)(2,1)S(1)} %get-tuple-element.66), channel_id=1, source_target_pairs={{0,2},{1,3},{2,0},{3,1},{4,6},{5,7},{6,4},{7,5},{8,10},{9,11},{10,... | collective-permute-start | bytes 786440 | tf_op jit(solution)/shard_map/scatter_branch_block3_part1/ppermute | solution.py:53
  86.7 0.6 input_grad.1.refs_4_
  87.3 3.6 %collective-permute-done.16.refs_2_ = bf16[64,2048]{1,0:T(8,128)(2,1)S(1)} collective-permute-done((bf16[64,2048]{1,0:T(8,128)(2,1)S(1)}, bf16[64,2048]{1,0:T(8,128)(2,1)S(1)}, u32[]{:S(2)}, u32[]{:S(2)}) %collective-permute-start.16) | collective-permute-done | bytes 262176 | tf_op jit(solution)/shard_map/scatter_branch_block3_part0/ppermute | solution.py:53
  91.2 2.7 %collective-permute-start.22 = (bf16[64,2048]{1,0:T(8,128)(2,1)S(1)}, bf16[64,2048]{1,0:T(8,128)(2,1)S(1)}, u32[]{:S(2)}, u32[]{:S(2)}) collective-permute-start(bf16[64,2048]{1,0:T(8,128)(2,1)S(1)} %get-tuple-element.73), channel_id=1, source_target_pairs={{0,6},{1,7},{2,4},{3,5},{4,10},{5,11},{6,8},{7,9},{8,14},{9,15},{1... | collective-permute-start | bytes 786440 | tf_op jit(solution)/shard_map/scatter_branch_block2_part0/ppermute | solution.py:63
  94.0 1.0 widen.1.refs_4_
  95.1 5.1 %collective-permute-done.21.refs_1_ = bf16[64,2048]{1,0:T(8,128)(2,1)S(1)} collective-permute-done((bf16[64,2048]{1,0:T(8,128)(2,1)S(1)}, bf16[64,2048]{1,0:T(8,128)(2,1)S(1)}, u32[]{:S(2)}, u32[]{:S(2)}) %collective-permute-start.21) | collective-permute-done | bytes 262176 | tf_op jit(solution)/shard_map/scatter_branch_block1_part1/ppermute | solution.py:63
  100.2 2.6 %collective-permute-done.22.refs_2_ = bf16[64,2048]{1,0:T(8,128)(2,1)S(1)} collective-permute-done((bf16[64,2048]{1,0:T(8,128)(2,1)S(1)}, bf16[64,2048]{1,0:T(8,128)(2,1)S(1)}, u32[]{:S(2)}, u32[]{:S(2)}) %collective-permute-start.22) | collective-permute-done | bytes 262176 | tf_op jit(solution)/shard_map/scatter_branch_block2_part0/ppermute | solution.py:63
  102.8 1.2 %copy-done.4 = f32[1,128,2048]{2,1,0:T(8,128)S(1)} copy-done((f32[1,128,2048]{2,1,0:T(8,128)S(1)}, f32[1,128,2048]{2,1,0:T(8,128)}, u32[]{:S(2)}) %copy-start.4) | copy-done | bytes 1048600
  104.1 1.1 %activation_sum.1 = f32[1,128,2048]{2,1,0:T(8,128)} custom-call(bf16[128,2048]{1,0:T(8,128)(2,1)S(1)} %collective-permute-done.12.refs_4_.own_ref, bf16[64,2048]{1,0:T(8,128)(2,1)S(1)} %collective-permute-done.13.refs_6_.refs_0_, bf16[64,2048]{1,0:T(8,128)(2,1)S(1)} %collective-permute-done.21.refs_1_, bf16[64,2048]{1,0:T(8,128)(2,1)S(1)} %collective-permute-done.22.refs_2_, ...), custom_call_target="tpu_custom_call" | custom-call | flops 8000000000 | bytes 1 | tf_op jit(solution)/shard_map/activation_sum/pallas_call | solution.py:174
  (45 shorter events, 1.4 us)
Async XLA Ops:
  0.6 1.2 %copy-start.7 = (f32[1,128,2048]{2,1,0:T(8,128)S(1)}, f32[1,128,2048]{2,1,0:T(8,128)}, u32[]{:S(2)}) copy-start(f32[1,128,2048]{2,1,0:T(8,128)} %param.9) | copy-start | bytes 3145732
  1.9 0.7 copy-start.9
  2.9 15.8 %collective-permute-start.2 = (bf16[128,2048]{1,0:T(8,128)(2,1)S(1)}, bf16[128,2048]{1,0:T(8,128)(2,1)S(1)}, u32[]{:S(2)}, u32[]{:S(2)}) collective-permute-start(bf16[128,2048]{1,0:T(8,128)(2,1)S(1)} %get-tuple-element.38.refs_0_), channel_id=1, source_target_pairs={{0,2},{1,3},{2,0},{3,1},{4,6},{5,7},{6,4},{7,5},{8,10},{9,11},{10,... | collective-permute-start | bytes 1572872 | tf_op jit(solution)/shard_map/gather_saved_block2/ppermute | solution.py:53
  5.9 14.8 %collective-permute-start.3 = (bf16[128,2048]{1,0:T(8,128)(2,1)S(1)}, bf16[128,2048]{1,0:T(8,128)(2,1)S(1)}, u32[]{:S(2)}, u32[]{:S(2)}) collective-permute-start(bf16[128,2048]{1,0:T(8,128)(2,1)S(1)} %get-tuple-element.38.refs_0_), channel_id=1, source_target_pairs={{0,1},{1,0},{2,3},{3,2},{4,5},{5,4},{6,7},{7,6},{8,9},{9,8},{10,11... | collective-permute-start | bytes 1572872 | tf_op jit(solution)/shard_map/gather_saved_block1/ppermute | solution.py:53
  7.4 1.2 %copy-start.5 = (f32[1,128,2048]{2,1,0:T(8,128)S(1)}, f32[1,128,2048]{2,1,0:T(8,128)}, u32[]{:S(2)}) copy-start(f32[1,128,2048]{2,1,0:T(8,128)} %param.10) | copy-start | bytes 3145732
  8.6 28.1 %copy-start.3 = (f32[1,128,2048]{2,1,0:T(8,128)S(1)}, f32[1,128,2048]{2,1,0:T(8,128)}, u32[]{:S(2)}) copy-start(f32[1,128,2048]{2,1,0:T(8,128)} %param.8) | copy-start | bytes 3145732
  8.7 21.3 %collective-permute-start = (bf16[128,2048]{1,0:T(8,128)(2,1)S(1)}, bf16[128,2048]{1,0:T(8,128)(2,1)}, u32[]{:S(2)}, u32[]{:S(2)}) collective-permute-start(bf16[128,2048]{1,0:T(8,128)(2,1)S(1)} %cast.1.refs_2_.refs_0_), channel_id=1, source_target_pairs={{0,2},{1,3},{2,0},{3,1},{4,6},{5,7},{6,4},{7,5},{8,10},{9,11},{10,... | collective-permute-start | bytes 1572872 | tf_op jit(solution)/shard_map/gather_grad_block2/ppermute | solution.py:53
  9.2 22.8 %collective-permute-start.1 = (bf16[128,2048]{1,0:T(8,128)(2,1)S(1)}, bf16[128,2048]{1,0:T(8,128)(2,1)}, u32[]{:S(2)}, u32[]{:S(2)}) collective-permute-start(bf16[128,2048]{1,0:T(8,128)(2,1)S(1)} %cast.1.refs_2_.refs_0_), channel_id=1, source_target_pairs={{0,1},{1,0},{2,3},{3,2},{4,5},{5,4},{6,7},{7,6},{8,9},{9,8},{10,11... | collective-permute-start | bytes 1572872 | tf_op jit(solution)/shard_map/gather_grad_block1/ppermute | solution.py:53
  20.7 19.1 %copy-start.2 = (bf16[1,2048,512]{2,1,0:T(8,128)(2,1)S(1)}, bf16[1,2048,512]{2,1,0:T(8,128)(2,1)}, u32[]{:S(2)}) copy-start(bf16[1,2048,512]{2,1,0:T(8,128)(2,1)} %param.14) | copy-start | bytes 6291460
  20.8 16.0 %copy-start.10 = (f32[1,2048]{1,0:T(1,128)S(1)}, f32[1,2048]{1,0:T(1,128)}, u32[]{:S(2)}) copy-start(f32[1,2048]{1,0:T(1,128)} %gain_ref.1) | copy-start | bytes 24580
  20.8 17.1 %collective-permute-start.8 = (bf16[64,2048]{1,0:T(8,128)(2,1)S(1)}, bf16[64,2048]{1,0:T(8,128)(2,1)S(1)}, u32[]{:S(2)}, u32[]{:S(2)}) collective-permute-start(bf16[64,2048]{1,0:T(8,128)(2,1)S(1)} %get-tuple-element.39.refs_2_), channel_id=1, source_target_pairs={{0,1},{1,0},{2,3},{3,2},{4,5},{5,4},{6,7},{7,6},{8,9},{9,8},{10,11... | collective-permute-start | bytes 786440 | tf_op jit(solution)/shard_map/gather_saved_block3_row0/ppermute | solution.py:53
  22.4 17.5 %collective-permute-start.9 = (bf16[64,2048]{1,0:T(8,128)(2,1)S(1)}, bf16[64,2048]{1,0:T(8,128)(2,1)S(1)}, u32[]{:S(2)}, u32[]{:S(2)}) collective-permute-start(bf16[64,2048]{1,0:T(8,128)(2,1)S(1)} %get-tuple-element.40.refs_3_), channel_id=1, source_target_pairs={{0,2},{1,3},{2,0},{3,1},{4,6},{5,7},{6,4},{7,5},{8,10},{9,11},{10,... | collective-permute-start | bytes 786440 | tf_op jit(solution)/shard_map/gather_saved_block3_row64/ppermute | solution.py:53
  32.1 7.8 %copy-start.1 = (bf16[1,2048,512]{2,1,0:T(8,128)(2,1)S(1)}, bf16[1,2048,512]{2,1,0:T(8,128)(2,1)}, u32[]{:S(2)}) copy-start(bf16[1,2048,512]{2,1,0:T(8,128)(2,1)} %param.13) | copy-start | bytes 6291460
  33.5 6.4 %copy-start = (bf16[1,2048,512]{2,1,0:T(8,128)(2,1)S(1)}, bf16[1,2048,512]{2,1,0:T(8,128)(2,1)}, u32[]{:S(2)}) copy-start(bf16[1,2048,512]{2,1,0:T(8,128)(2,1)} %param.12) | copy-start | bytes 6291460
  33.5 10.0 %collective-permute-start.6 = (bf16[64,2048]{1,0:T(8,128)(2,1)S(1)}, bf16[64,2048]{1,0:T(8,128)(2,1)S(1)}, u32[]{:S(2)}, u32[]{:S(2)}) collective-permute-start(bf16[64,2048]{1,0:T(8,128)(2,1)S(1)} %get-tuple-element.41.refs_0_), channel_id=1, source_target_pairs={{0,1},{1,0},{2,3},{3,2},{4,5},{5,4},{6,7},{7,6},{8,9},{9,8},{10,11... | collective-permute-start | bytes 786440 | tf_op jit(solution)/shard_map/gather_grad_block3_row0/ppermute | solution.py:53
  35.0 9.2 %collective-permute-start.7 = (bf16[64,2048]{1,0:T(8,128)(2,1)S(1)}, bf16[64,2048]{1,0:T(8,128)(2,1)S(1)}, u32[]{:S(2)}, u32[]{:S(2)}) collective-permute-start(bf16[64,2048]{1,0:T(8,128)(2,1)S(1)} %get-tuple-element.42.refs_1_), channel_id=1, source_target_pairs={{0,2},{1,3},{2,0},{3,1},{4,6},{5,7},{6,4},{7,5},{8,10},{9,11},{10,... | collective-permute-start | bytes 786440 | tf_op jit(solution)/shard_map/gather_grad_block3_row64/ppermute | solution.py:53
  37.7 15.3 %collective-permute-start.4 = (bf16[128,2048]{1,0:T(8,128)(2,1)S(1)}, bf16[128,2048]{1,0:T(8,128)(2,1)S(1)}, u32[]{:S(2)}, u32[]{:S(2)}) collective-permute-start(bf16[128,2048]{1,0:T(8,128)(2,1)S(1)} %get-tuple-element.43.refs_0_), channel_id=1, source_target_pairs={{0,1},{1,0},{2,3},{3,2},{4,5},{5,4},{6,7},{7,6},{8,9},{9,8},{10,11... | collective-permute-start | bytes 1572872 | tf_op jit(solution)/shard_map/gather_input_block1/ppermute | solution.py:53
  37.9 15.1 %collective-permute-start.5 = (bf16[128,2048]{1,0:T(8,128)(2,1)S(1)}, bf16[128,2048]{1,0:T(8,128)(2,1)S(1)}, u32[]{:S(2)}, u32[]{:S(2)}) collective-permute-start(bf16[128,2048]{1,0:T(8,128)(2,1)S(1)} %get-tuple-element.43.refs_0_), channel_id=1, source_target_pairs={{0,2},{1,3},{2,0},{3,1},{4,6},{5,7},{6,4},{7,5},{8,10},{9,11},{10,... | collective-permute-start | bytes 1572872 | tf_op jit(solution)/shard_map/gather_input_block2/ppermute | solution.py:53
  39.9 4.4 %copy-start.11 = (bf16[1,2048,512]{2,1,0:T(8,128)(2,1)S(1)}, bf16[1,2048,512]{2,1,0:T(8,128)(2,1)}, u32[]{:S(2)}) copy-start(bf16[1,2048,512]{2,1,0:T(8,128)(2,1)} %param.15) | copy-start | bytes 6291460
  53.0 7.6 %collective-permute-start.10 = (bf16[64,2048]{1,0:T(8,128)(2,1)S(1)}, bf16[64,2048]{1,0:T(8,128)(2,1)S(1)}, u32[]{:S(2)}, u32[]{:S(2)}) collective-permute-start(bf16[64,2048]{1,0:T(8,128)(2,1)S(1)} %get-tuple-element.48.refs_6_), channel_id=1, source_target_pairs={{0,1},{1,0},{2,3},{3,2},{4,5},{5,4},{6,7},{7,6},{8,9},{9,8},{10,11... | collective-permute-start | bytes 786440 | tf_op jit(solution)/shard_map/gather_input_block3_row0/ppermute | solution.py:53
  54.6 8.0 %collective-permute-start.11 = (bf16[64,2048]{1,0:T(8,128)(2,1)S(1)}, bf16[64,2048]{1,0:T(8,128)(2,1)S(1)}, u32[]{:S(2)}, u32[]{:S(2)}) collective-permute-start(bf16[64,2048]{1,0:T(8,128)(2,1)S(1)} %get-tuple-element.49.refs_7_), channel_id=1, source_target_pairs={{0,2},{1,3},{2,0},{3,1},{4,6},{5,7},{6,4},{7,5},{8,10},{9,11},{10,... | collective-permute-start | bytes 786440 | tf_op jit(solution)/shard_map/gather_input_block3_row64/ppermute | solution.py:53
  58.5 12.6 %collective-permute-start.14 = (bf16[128,2048]{1,0:T(8,128)(2,1)S(1)}, bf16[128,2048]{1,0:T(8,128)(2,1)S(1)}, u32[]{:S(2)}, u32[]{:S(2)}) collective-permute-start(bf16[128,2048]{1,0:T(8,128)(2,1)S(1)} %get-tuple-element.61), channel_id=1, source_target_pairs={{0,1},{1,0},{2,3},{3,2},{4,5},{5,4},{6,7},{7,6},{8,9},{9,8},{10,11... | collective-permute-start | bytes 1572872 | tf_op jit(solution)/shard_map/scatter_grad_block3_part0/ppermute | solution.py:53
  59.0 13.4 %collective-permute-start.15 = (bf16[128,2048]{1,0:T(8,128)(2,1)S(1)}, bf16[128,2048]{1,0:T(8,128)(2,1)S(1)}, u32[]{:S(2)}, u32[]{:S(2)}) collective-permute-start(bf16[128,2048]{1,0:T(8,128)(2,1)S(1)} %get-tuple-element.62), channel_id=1, source_target_pairs={{0,2},{1,3},{2,0},{3,1},{4,6},{5,7},{6,4},{7,5},{8,10},{9,11},{10,... | collective-permute-start | bytes 1572872 | tf_op jit(solution)/shard_map/scatter_grad_block3_part1/ppermute | solution.py:53
  69.0 17.7 %copy-start.6 = (f32[1,128,2048]{2,1,0:T(8,128)S(1)}, f32[1,128,2048]{2,1,0:T(8,128)}, u32[]{:S(2)}) copy-start(f32[1,128,2048]{2,1,0:T(8,128)} %param.10) | copy-start | bytes 3145732
  69.0 17.7 %copy-start.8 = (f32[1,128,2048]{2,1,0:T(8,128)S(1)}, f32[1,128,2048]{2,1,0:T(8,128)}, u32[]{:S(2)}) copy-start(f32[1,128,2048]{2,1,0:T(8,128)} %param.9) | copy-start | bytes 3145732
  69.0 17.7 %collective-permute-start.12 = (bf16[128,2048]{1,0:T(8,128)(2,1)S(1)}, bf16[128,2048]{1,0:T(8,128)(2,1)S(1)}, u32[]{:S(2)}, u32[]{:S(2)}) collective-permute-start(bf16[128,2048]{1,0:T(8,128)(2,1)S(1)} %get-tuple-element.53), channel_id=1, source_target_pairs={{0,4},{1,5},{2,6},{3,7},{4,8},{5,9},{6,10},{7,11},{8,12},{9,13},{1... | collective-permute-start | bytes 1572872 | tf_op jit(solution)/shard_map/ppermute | solution.py:63
  69.1 13.0 %collective-permute-start.13 = (bf16[64,2048]{1,0:T(8,128)(2,1)S(1)}, bf16[64,2048]{1,0:T(8,128)(2,1)S(1)}, u32[]{:S(2)}, u32[]{:S(2)}) collective-permute-start(bf16[64,2048]{1,0:T(8,128)(2,1)S(1)} %get-tuple-element.54), channel_id=1, source_target_pairs={{0,5},{1,4},{2,7},{3,6},{4,9},{5,8},{6,11},{7,10},{8,13},{9,12},{1... | collective-permute-start | bytes 786440 | tf_op jit(solution)/shard_map/scatter_branch_block1_part0/ppermute | solution.py:63
  70.8 13.5 %collective-permute-start.20 = (bf16[64,2048]{1,0:T(8,128)(2,1)S(1)}, bf16[64,2048]{1,0:T(8,128)(2,1)S(1)}, u32[]{:S(2)}, u32[]{:S(2)}) collective-permute-start(bf16[64,2048]{1,0:T(8,128)(2,1)S(1)} %get-tuple-element.71), channel_id=1, source_target_pairs={{0,6},{1,7},{2,4},{3,5},{4,10},{5,11},{6,8},{7,9},{8,14},{9,15},{1... | collective-permute-start | bytes 786440 | tf_op jit(solution)/shard_map/scatter_branch_block2_part1/ppermute | solution.py:63
  72.5 14.2 %collective-permute-start.18 = (bf16[64,2048]{1,0:T(8,128)(2,1)S(1)}, bf16[64,2048]{1,0:T(8,128)(2,1)S(1)}, u32[]{:S(2)}, u32[]{:S(2)}) collective-permute-start(bf16[64,2048]{1,0:T(8,128)(2,1)S(1)} %get-tuple-element.69), channel_id=1, source_target_pairs={{0,1},{1,0},{2,3},{3,2},{4,5},{5,4},{6,7},{7,6},{8,9},{9,8},{10,11... | collective-permute-start | bytes 786440 | tf_op jit(solution)/shard_map/scatter_grad_block1_part1/ppermute | solution.py:53
  73.1 13.6 %collective-permute-start.19 = (bf16[64,2048]{1,0:T(8,128)(2,1)S(1)}, bf16[64,2048]{1,0:T(8,128)(2,1)S(1)}, u32[]{:S(2)}, u32[]{:S(2)}) collective-permute-start(bf16[64,2048]{1,0:T(8,128)(2,1)S(1)} %get-tuple-element.70), channel_id=1, source_target_pairs={{0,2},{1,3},{2,0},{3,1},{4,6},{5,7},{6,4},{7,5},{8,10},{9,11},{10,... | collective-permute-start | bytes 786440 | tf_op jit(solution)/shard_map/scatter_grad_block2_part0/ppermute | solution.py:53
  82.1 8.9 %collective-permute-start.16 = (bf16[64,2048]{1,0:T(8,128)(2,1)S(1)}, bf16[64,2048]{1,0:T(8,128)(2,1)S(1)}, u32[]{:S(2)}, u32[]{:S(2)}) collective-permute-start(bf16[64,2048]{1,0:T(8,128)(2,1)S(1)} %get-tuple-element.65), channel_id=1, source_target_pairs={{0,1},{1,0},{2,3},{3,2},{4,5},{5,4},{6,7},{7,6},{8,9},{9,8},{10,11... | collective-permute-start | bytes 786440 | tf_op jit(solution)/shard_map/scatter_branch_block3_part0/ppermute | solution.py:53
  84.3 6.7 %collective-permute-start.17 = (bf16[64,2048]{1,0:T(8,128)(2,1)S(1)}, bf16[64,2048]{1,0:T(8,128)(2,1)S(1)}, u32[]{:S(2)}, u32[]{:S(2)}) collective-permute-start(bf16[64,2048]{1,0:T(8,128)(2,1)S(1)} %get-tuple-element.66), channel_id=1, source_target_pairs={{0,2},{1,3},{2,0},{3,1},{4,6},{5,7},{6,4},{7,5},{8,10},{9,11},{10,... | collective-permute-start | bytes 786440 | tf_op jit(solution)/shard_map/scatter_branch_block3_part1/ppermute | solution.py:53
  87.3 6.8 %collective-permute-start.23 = (bf16[128,2048]{1,0:T(8,128)(2,1)S(1)}, bf16[128,2048]{1,0:T(8,128)(2,1)S(1)}, u32[]{:S(2)}, u32[]{:S(2)}) collective-permute-start(bf16[128,2048]{1,0:T(8,128)(2,1)S(1)} %input_grad.1.refs_4_), channel_id=1, source_target_pairs={{0,28},{4,0},{8,4},{12,8},{16,12},{20,16},{24,20},{28,24},{1,29},{... | collective-permute-start | bytes 1572872 | tf_op jit(solution)/shard_map/ppermute | solution.py:69
  91.2 9.0 %collective-permute-start.21 = (bf16[64,2048]{1,0:T(8,128)(2,1)S(1)}, bf16[64,2048]{1,0:T(8,128)(2,1)S(1)}, u32[]{:S(2)}, u32[]{:S(2)}) collective-permute-start(bf16[64,2048]{1,0:T(8,128)(2,1)S(1)} %get-tuple-element.72), channel_id=1, source_target_pairs={{0,5},{1,4},{2,7},{3,6},{4,9},{5,8},{6,11},{7,10},{8,13},{9,12},{1... | collective-permute-start | bytes 786440 | tf_op jit(solution)/shard_map/scatter_branch_block1_part1/ppermute | solution.py:63
  91.2 11.6 %collective-permute-start.22 = (bf16[64,2048]{1,0:T(8,128)(2,1)S(1)}, bf16[64,2048]{1,0:T(8,128)(2,1)S(1)}, u32[]{:S(2)}, u32[]{:S(2)}) collective-permute-start(bf16[64,2048]{1,0:T(8,128)(2,1)S(1)} %get-tuple-element.73), channel_id=1, source_target_pairs={{0,6},{1,7},{2,4},{3,5},{4,10},{5,11},{6,8},{7,9},{8,14},{9,15},{1... | collective-permute-start | bytes 786440 | tf_op jit(solution)/shard_map/scatter_branch_block2_part0/ppermute | solution.py:63
  102.8 1.2 %copy-start.4 = (f32[1,128,2048]{2,1,0:T(8,128)S(1)}, f32[1,128,2048]{2,1,0:T(8,128)}, u32[]{:S(2)}) copy-start(f32[1,128,2048]{2,1,0:T(8,128)} %widen.1.refs_4_) | copy-start | bytes 3145732

commit v4 on v3

--- a/solution.py
+++ b/solution.py
@@ -77,6 +77,12 @@
     ]
 
 
+def goes_on(rel, low, count, bounds):
+    return any(
+        rel == at and first <= low < last for at, _, first, last in onward_rows(count, bounds)
+    )
+
+
 def gather_first(own, what):
     count = lax.axis_size("seq")
     blocks = {(0, 0): own}
@@ -87,20 +93,30 @@
     return blocks
 
 
-def second_hops(blocks, rows):
+def gather_parts(blocks, own_parts, bounds, early, what):
     count = lax.axis_size("seq")
-    return [
-        (blocks[rel, 0], low, high)
-        for rel, bit, low, high in onward_rows(count, part_bounds(rows, count))
-        if len(bits_of(rel)) == 1
-    ]
-
-
-def gather_rest(blocks, picked, what):
+    for rel in by_distance(count):
+        for value, (low, _) in zip(own_parts, bounds):
+            blocks.setdefault((0, low), value)
+            if len(bits_of(rel)) == 1 and goes_on(rel, low, count, bounds) == early:
+                with jax.named_scope(f"gather_{what}_block{rel}_first{low}"):
+                    blocks[rel, low] = across(value, bits_of(rel)[0])
+    return blocks
+
+
+def second_hops(blocks, bounds):
+    hops = []
+    for rel, _, low, high in onward_rows(lax.axis_size("seq"), bounds):
+        if len(bits_of(rel)) == 1:
+            first = low if (rel, low) in blocks else 0
+            hops.append((blocks[rel, first], low - first, high - first))
+    return hops
+
+
+def gather_rest(blocks, picked, bounds, what):
     count = lax.axis_size("seq")
-    rows = blocks[0, 0].shape[0]
     picked = list(picked)
-    for rel, bit, low, high in onward_rows(count, part_bounds(rows, count)):
+    for rel, bit, low, high in onward_rows(count, bounds):
         if rel == 0:
             continue
         value = picked.pop(0) if len(bits_of(rel)) == 1 else blocks[rel, low]
@@ -159,15 +175,16 @@
         for i in places:
             self.send(self.leaving[i], self.groups[i])
 
-    def send_sums(self, handed_on=(), after=()):
+    def send_sums(self, after=()):
+        sums = []
         for level in sorted({len(bits_of(rel)) for rel, _ in self.waiting}, reverse=True):
             keys = [key for key in self.waiting if len(bits_of(key[0])) == level]
             totals = [(self.waiting[key], self.arrived[key]) for key in keys]
-            results = sum_rows(totals, handed_on, after)
-            handed_on = results[len(keys) :]
+            results = sum_rows(totals, after)
+            sums += results
             for key, value in zip(keys, results):
                 self.send(value, [key])
-        return handed_on
+        return sums
 
 
 def call(kernel, out_shapes, operands, in_specs, scratch=(), flops=1, vmem=10, name=None):
@@ -184,28 +201,15 @@
 
 
 ANY = pl.BlockSpec(memory_space=pl.ANY)
+HBM = pl.BlockSpec(memory_space=pltpu.HBM)
 VMEM = pl.BlockSpec(memory_space=pltpu.VMEM)
 
 
-def picked_shapes(pieces):
-    return [
-        jax.ShapeDtypeStruct((high - low, value.shape[1]), value.dtype)
-        for value, low, high in pieces
-    ]
-
-
-def pick(pieces, in_refs, out_refs):
-    for (_, low, high), in_ref, out_ref in zip(pieces, in_refs, out_refs):
-        out_ref[...] = in_ref[low:high, :]
-
-
-def normed_rows(inputs, gain, pieces=(), after=()):
+def normed_rows(inputs, gain, bounds, after=()):
     rows, width = inputs.shape
-    n = len(pieces)
 
     def kernel(x_any, gain_any, *refs):
-        refs, (x_ref, gain_ref, sems) = refs[:n] + refs[n + len(after) : -3], refs[-3:]
-        out_ref, inv_ref = refs[n : n + 2]
+        *outs, inv_ref, x_ref, gain_ref, sems = refs[len(after) :]
         copies = [
             pltpu.make_async_copy(source, held, sems.at[i])
             for i, (source, held) in enumerate([(x_any, x_ref), (gain_any, gain_ref)])
@@ -214,21 +218,18 @@
             copy.start()
         for copy in copies:
             copy.wait()
-        x = x_ref[...]
-        inv = lax.rsqrt(jnp.mean(x * x, -1, keepdims=True) + 1e-05)
-        out_ref[...] = (x * inv * gain_ref[...]).astype(jnp.bfloat16)
-        inv_ref[...] = inv
-        pick(pieces, refs[:n], refs[n + 2 :])
-
-    return call(
-        kernel,
-        [
-            jax.ShapeDtypeStruct((rows, width), jnp.bfloat16),
-            jax.ShapeDtypeStruct((rows, 1), jnp.float32),
-        ]
-        + picked_shapes(pieces),
-        [inputs, gain] + [value for value, _, _ in pieces] + list(after),
-        [ANY] * 2 + [VMEM] * n + [ANY] * len(after),
+        for out_ref, (low, high) in zip(outs, bounds):
+            x = x_ref[low:high, :]
+            inv = lax.rsqrt(jnp.mean(x * x, -1, keepdims=True) + 1e-05)
+            out_ref[...] = (x * inv * gain_ref[...]).astype(jnp.bfloat16)
+            inv_ref[low:high, :] = inv
+
+    *parts, inv = call(
+        kernel,
+        [jax.ShapeDtypeStruct((high - low, width), jnp.bfloat16) for low, high in bounds]
+        + [jax.ShapeDtypeStruct((rows, 1), jnp.float32)],
+        [inputs, gain, *after],
+        [HBM] * 2 + [ANY] * len(after),
         [
             pltpu.VMEM(inputs.shape, jnp.float32),
             pltpu.VMEM(gain.shape, jnp.float32),
@@ -236,19 +237,32 @@
         ],
         name="norm",
     )
+    return parts, inv
 
 
 def picked_rows(pieces, after=()):
     n = len(pieces)
 
     def kernel(*refs):
-        pick(pieces, refs[:n], refs[n + len(after) :])
-
-    return call(
-        kernel,
-        picked_shapes(pieces),
+        outs, sems = refs[n + len(after) : -1], refs[-1]
+        copies = [
+            pltpu.make_async_copy(ref.at[pl.ds(low, high - low), :], out_ref, sems.at[i])
+            for i, (ref, out_ref, (_, low, high)) in enumerate(zip(refs, outs, pieces))
+        ]
+        for copy in copies:
+            copy.start()
+        for copy in copies:
+            copy.wait()
+
+    return call(
+        kernel,
+        [
+            jax.ShapeDtypeStruct((high - low, value.shape[1]), value.dtype)
+            for value, low, high in pieces
+        ],
         [value for value, _, _ in pieces] + list(after),
-        [VMEM] * n + [ANY] * len(after),
+        [ANY] * (n + len(after)),
+        [pltpu.SemaphoreType.DMA((n,))],
         name="pick",
     )
 
@@ -266,30 +280,24 @@
     )[0]
 
 
-def sum_rows(totals, handed_on=(), after=()):
+def sum_rows(totals, after=()):
     pieces = [piece for _, pieces in totals for piece in pieces]
-    n, m, k = len(totals), len(pieces), len(handed_on)
+    n, m = len(totals), len(pieces)
 
     def kernel(*refs):
-        arrivals, outs = list(refs[n : n + m]), refs[-n - k :]
+        arrivals, outs = list(refs[n : n + m]), refs[-n:]
         for (term, moved), term_ref, out_ref in zip(totals, refs, outs):
             total = term_ref[...]
             for _, first in moved:
                 ref = arrivals.pop(0)
                 total = total + ref[first : first + term.shape[0], :].astype(jnp.float32)
             out_ref[...] = total.astype(jnp.bfloat16)
-        for in_ref, out_ref in zip(refs[n + m : n + m + k], outs[n:]):
-            out_ref[...] = in_ref[...]
-
-    return call(
-        kernel,
-        [jax.ShapeDtypeStruct(term.shape, jnp.bfloat16) for term, _ in totals]
-        + [jax.ShapeDtypeStruct(value.shape, value.dtype) for value in handed_on],
-        [term for term, _ in totals]
-        + [value for value, _ in pieces]
-        + list(handed_on)
-        + list(after),
-        [VMEM] * (n + m + k) + [ANY] * len(after),
+
+    return call(
+        kernel,
+        [jax.ShapeDtypeStruct(term.shape, jnp.bfloat16) for term, _ in totals],
+        [term for term, _ in totals] + [value for value, _ in pieces] + list(after),
+        [VMEM] * (n + m) + [ANY] * len(after),
         name="sum_rows",
     )
 
@@ -549,40 +557,47 @@
     )[0]
 
 
-def activation_sum(own, pieces, bounds, after=()):
-    keys = sorted(pieces)
-
-    def kernel(own_ref, *refs):
-        out_ref = refs[-1]
+def added_pieces(total, pieces, refs, part, height):
+    for ref, (key, (_, first)) in zip(refs, pieces.items()):
+        if key[1] == part:
+            total = total + ref[first : first + height, :].astype(jnp.float32)
+    return total
+
+
+def activation_sum(base, pieces, bounds, after=()):
+    def kernel(base_ref, *refs):
         for part, (low, high) in enumerate(bounds):
-            total = own_ref[low:high, :].astype(jnp.float32)
-            for ref, key in zip(refs, keys):
-                if key[1] == part:
-                    first = pieces[key][1]
-                    total = total + ref[first : first + high - low, :].astype(jnp.float32)
-            out_ref[0, low:high, :] = total
-
-    return call(
-        kernel,
-        [jax.ShapeDtypeStruct((1, *own.shape), jnp.float32)],
-        [own] + [pieces[key][0] for key in keys] + list(after),
-        [VMEM] * (1 + len(keys)) + [ANY] * len(after),
+            total = base_ref[low:high, :].astype(jnp.float32)
+            refs[-1][0, low:high, :] = added_pieces(total, pieces, refs, part, high - low)
+
+    return call(
+        kernel,
+        [jax.ShapeDtypeStruct((1, *base.shape), jnp.float32)],
+        [base] + [value for value, _ in pieces.values()] + list(after),
+        [VMEM] * (1 + len(pieces)) + [ANY] * len(after),
         flops=LAST_SUM_WEIGHT,
         name="activation_sum",
     )[0]
 
 
-def widened(values):
-    def kernel(in_ref, out_ref):
+def widened(values, base, pieces, bounds):
+    def kernel(in_ref, base_ref, *refs):
+        out_ref, sum_ref = refs[-2:]
         out_ref[0] = in_ref[...].astype(jnp.float32)
-
-    return call(
-        kernel,
-        [jax.ShapeDtypeStruct((1, *values.shape), jnp.float32)],
-        (values,),
-        [VMEM],
+        for part, (low, high) in enumerate(bounds):
+            total = base_ref[low:high, :].astype(jnp.float32)
+            sum_ref[low:high, :] = added_pieces(total, pieces, refs, part, high - low)
+
+    return call(
+        kernel,
+        [
+            jax.ShapeDtypeStruct((1, *values.shape), jnp.float32),
+            jax.ShapeDtypeStruct(base.shape, jnp.float32),
+        ],
+        [values, base] + [value for value, _ in pieces.values()],
+        [VMEM] * (2 + len(pieces)),
         name="widen",
-    )[0]
+    )
 
 
 def rope_tables(positions):
@@ -604,25 +619,25 @@
     positions = (block_of[:, None] * rows + jnp.arange(rows)[None, :]).reshape(-1)
     cosine, sine = rope_tables(positions)
 
-    def last_arrivals(blocks):
-        return [value for (rel, _), value in blocks.items() if rel == count - 1]
-
+    whole = [(0, rows)]
     projections = (own_query, own_key, own_value)
-    normed_bwd, inv_bwd = normed_rows(saved_in, gain)
+    (normed_bwd,), inv_bwd = normed_rows(saved_in, gain, whole)
     grad_low = cast_rows(grad, [normed_bwd])
     all_bwd = gather_first(normed_bwd, "saved")
     all_grad = gather_first(grad_low, "grad")
-    picked = picked_rows(second_hops(all_bwd, rows), [grad_low])
-    all_bwd = gather_rest(all_bwd, picked, "saved")
-    picked = picked_rows(second_hops(all_grad, rows), picked)
-    all_grad = gather_rest(all_grad, picked, "grad")
-    normed_fwd, _ = normed_rows(act_in, gain, after=picked)
-    all_fwd = gather_first(normed_fwd, "input")
+    picked = picked_rows(second_hops(all_bwd, bounds), [grad_low])
+    all_bwd = gather_rest(all_bwd, picked, bounds, "saved")
+    picked = picked_rows(second_hops(all_grad, bounds), picked)
+    all_grad = gather_rest(all_grad, picked, bounds, "grad")
+    normed_fwd, _ = normed_rows(act_in, gain, bounds, picked)
+    all_fwd = gather_parts({}, normed_fwd, bounds, True, "input")
 
     qkv = project(all_bwd, projections, cosine, sine, rows)
+    handed_on = picked_rows([(value, 0, value.shape[0]) for value in normed_fwd], qkv[:1])
+    all_fwd = gather_parts(all_fwd, handed_on, bounds, False, "input")
     d_qkv = backward_heads(all_grad, qkv, own_out, cosine, sine, rows)
-    picked = picked_rows(second_hops(all_fwd, rows), d_qkv[:1])
-    all_fwd = gather_rest(all_fwd, picked, "input")
+    picked = picked_rows(second_hops(all_fwd, bounds), d_qkv[:1])
+    all_fwd = gather_rest(all_fwd, picked, bounds, "input")
     d_own, d_terms = backward_terms(d_qkv, projections, rows, count, True, picked)
     qkv = project(all_fwd, projections, cosine, sine, rows, FORWARD_WEIGHT)
     own, terms = forward_terms(qkv, act_in, own_out, rows, count, False)
@@ -635,15 +650,28 @@
     onward = front.onward()
     front.send_groups([i for i in range(len(front.groups)) if i not in onward])
     own = across_and_on(own, 0)
-    soon = [own] + [value for value, _ in front.final.values()]
-    held = back.send_sums([front.leaving[i] for i in onward], [terms[0]])
+    soon = dict(front.final)
+    sums = back.send_sums([terms[0]])
+    held = picked_rows(
+        [(front.leaving[i], 0, front.leaving[i].shape[0]) for i in onward], [own, *sums]
+    )
     for i, value in zip(onward, held):
         front.leaving[i] = value
     front.send_groups(onward)
-    d_input = input_grad(d_own, back.final, saved_in, grad, inv_bwd, gain, bounds, soon)
-    front.send_sums(after=[d_input])
-    grad_prev = widened(passed_along(d_input, "pipe", -1))
-    return (activation_sum(own, front.final, bounds, [grad_prev]), grad_prev)
+    d_input = input_grad(
+        d_own,
+        back.final,
+        saved_in,
+        grad,
+        inv_bwd,
+        gain,
+        bounds,
+        [value for value, _ in soon.values()],
+    )
+    front.send_sums([d_input])
+    grad_prev, base = widened(passed_along(d_input, "pipe", -1), own, soon, bounds)
+    last = {key: piece for key, piece in front.final.items() if key not in soon}
+    return (activation_sum(base, last, bounds), grad_prev)
 
 
 def solution(mesh):

time: 106 us -> 105 us (level)
  starting transfers between devices: 26.1 us -> 29.6 us
  waiting for transfers between devices: 46.8 us -> 44.2 us
  local copies, waits for them, and re-layouts: 4.41 us -> 3.18 us
    ppermute x18 -> x20, waiting for transfers between devices: 30.5 us -> 25.8 us  [across(): return lax.ppermute(value, 'seq', [(i, i ^ 1 << bit) for i in range(count)])]
    ppermute x5, starting transfers between devices: 4.54 us -> 7.37 us  [across_and_on(): return lax.ppermute(value, ('pipe', 'seq'), pairs)]
    ppermute x1, waiting for transfers between devices: 0.15 us -> 1.53 us  [passed_along(): return lax.ppermute(value, axis, pairs)]
    unnamed x24 -> x22, local copies, waits for them, and re-layouts: 4.41 us -> 3.18 us
    ppermute x1, starting transfers between devices: 0.06 us -> 1.18 us  [passed_along(): return lax.ppermute(value, axis, pairs)]
    ppermute x18 -> x20, starting transfers between devices: 21.5 us -> 21 us  [across(): return lax.ppermute(value, 'seq', [(i, i ^ 1 << bit) for i in range(count)])]
    pallas_call x16 -> x18, Pallas kernels: 25.8 us -> 25.9 us  [call(): pl.pallas_call(kernel, out_shape=out_shapes, in_specs=in_specs, out_specs...]
  transfers between devices with their start and end apart: 24 -> 26, of which waited for: 16 -> 12; matrix products, arithmetic and copies ran while one was open for 1% -> 1% of each run, Pallas kernels for 23% -> 23%
where the time goes in v4:
time: 105 us
  waiting for transfers between devices  44.2 us (42%)
  starting transfers between devices  29.6 us (28%)
  Pallas kernels  25.9 us (25%)
  local copies, waits for them, and re-layouts  3.18 us (3%)
  other arithmetic  1.28 us (1%)
    pallas_call x18, Pallas kernels, call(): pl.pallas_call(kernel, out_shape=out_shapes, in_specs=in_specs, out_specs...  25.9 us
    ppermute x20, waiting for transfers between devices, across(): return lax.ppermute(value, 'seq', [(i, i ^ 1 << bit) for i in range(count)])  25.8 us
    ppermute x20, starting transfers between devices, across(): return lax.ppermute(value, 'seq', [(i, i ^ 1 << bit) for i in range(count)])  21 us
    ppermute x5, waiting for transfers between devices, across_and_on(): return lax.ppermute(value, ('pipe', 'seq'), pairs)  16.9 us
    ppermute x5, starting transfers between devices, across_and_on(): return lax.ppermute(value, ('pipe', 'seq'), pairs)  7.37 us
    unnamed x22, local copies, waits for them, and re-layouts  3.18 us
  transfers between devices with their start and end apart: 26, of which 12 were waited for; matrix products, arithmetic and copies ran while one was open for 1% of the time, Pallas kernels for 23%

profile of v4, /device:TPU:0, one launch (start us, length us, event | category | flops | bytes accessed | tf_op | source)
XLA Modules:
  0.0 105.1 jit_solution(4259478145442656662)
XLA Ops:
  0.6 1.2 %copy-done.6 = f32[1,128,2048]{2,1,0:T(8,128)S(1)} copy-done((f32[1,128,2048]{2,1,0:T(8,128)S(1)}, f32[1,128,2048]{2,1,0:T(8,128)}, u32[]{:S(2)}) %copy-start.6) | copy-done | bytes 1048600
  1.9 0.7 copy-done.8
  2.6 0.3 norm.2
  2.9 3.0 %collective-permute-start.2 = (bf16[128,2048]{1,0:T(8,128)(2,1)S(1)}, bf16[128,2048]{1,0:T(8,128)(2,1)S(1)}, u32[]{:S(2)}, u32[]{:S(2)}) collective-permute-start(bf16[128,2048]{1,0:T(8,128)(2,1)S(1)} %get-tuple-element.43.refs_0_), channel_id=1, source_target_pairs={{0,2},{1,3},{2,0},{3,1},{4,6},{5,7},{6,4},{7,5},{8,10},{9,11},{10,... | collective-permute-start | bytes 1572872 | tf_op jit(solution)/shard_map/gather_saved_block2/ppermute | solution.py:53
  5.9 1.5 %collective-permute-start.3 = (bf16[128,2048]{1,0:T(8,128)(2,1)S(1)}, bf16[128,2048]{1,0:T(8,128)(2,1)S(1)}, u32[]{:S(2)}, u32[]{:S(2)}) collective-permute-start(bf16[128,2048]{1,0:T(8,128)(2,1)S(1)} %get-tuple-element.43.refs_0_), channel_id=1, source_target_pairs={{0,1},{1,0},{2,3},{3,2},{4,5},{5,4},{6,7},{7,6},{8,9},{9,8},{10,11... | collective-permute-start | bytes 1572872 | tf_op jit(solution)/shard_map/gather_saved_block1/ppermute | solution.py:53
  7.4 1.2 %copy-done.4 = f32[1,128,2048]{2,1,0:T(8,128)S(1)} copy-done((f32[1,128,2048]{2,1,0:T(8,128)S(1)}, f32[1,128,2048]{2,1,0:T(8,128)}, u32[]{:S(2)}) %copy-start.4) | copy-done | bytes 1048600
  8.7 0.6 collective-permute-start
  9.4 9.2 %collective-permute-done.2.refs_0_.refs_2_ = bf16[128,2048]{1,0:T(8,128)(2,1)S(1)} collective-permute-done((bf16[128,2048]{1,0:T(8,128)(2,1)S(1)}, bf16[128,2048]{1,0:T(8,128)(2,1)S(1)}, u32[]{:S(2)}, u32[]{:S(2)}) %collective-permute-start.2) | collective-permute-done | bytes 524320 | tf_op jit(solution)/shard_map/gather_saved_block2/ppermute | solution.py:53
  18.6 2.1 %collective-permute-done.3.refs_1_ = bf16[128,2048]{1,0:T(8,128)(2,1)S(1)} collective-permute-done((bf16[128,2048]{1,0:T(8,128)(2,1)S(1)}, bf16[128,2048]{1,0:T(8,128)(2,1)S(1)}, u32[]{:S(2)}, u32[]{:S(2)}) %collective-permute-start.3) | collective-permute-done | bytes 524320 | tf_op jit(solution)/shard_map/gather_saved_block1/ppermute | solution.py:53
  20.8 1.6 %collective-permute-start.6 = (bf16[64,2048]{1,0:T(8,128)(2,1)S(1)}, bf16[64,2048]{1,0:T(8,128)(2,1)S(1)}, u32[]{:S(2)}, u32[]{:S(2)}) collective-permute-start(bf16[64,2048]{1,0:T(8,128)(2,1)S(1)} %get-tuple-element.44.refs_2_), channel_id=1, source_target_pairs={{0,1},{1,0},{2,3},{3,2},{4,5},{5,4},{6,7},{7,6},{8,9},{9,8},{10,11... | collective-permute-start | bytes 786440 | tf_op jit(solution)/shard_map/gather_saved_block3_row0/ppermute | solution.py:53
  22.4 0.5 collective-permute-start.7
  22.9 9.2 %collective-permute-done.refs_1_ = bf16[128,2048]{1,0:T(8,128)(2,1)} collective-permute-done((bf16[128,2048]{1,0:T(8,128)(2,1)S(1)}, bf16[128,2048]{1,0:T(8,128)(2,1)}, u32[]{:S(2)}, u32[]{:S(2)}) %collective-permute-start) | collective-permute-done | bytes 524320 | tf_op jit(solution)/shard_map/gather_grad_block1/ppermute | solution.py:53
  32.1 1.2 %pick.6 = (bf16[64,2048]{1,0:T(8,128)(2,1)S(1)}, bf16[64,2048]{1,0:T(8,128)(2,1)S(1)}) custom-call(bf16[128,2048]{1,0:T(8,128)(2,1)} %collective-permute-done.1.refs_0_.refs_2_, bf16[128,2048]{1,0:T(8,128)(2,1)} %collective-permute-done.refs_1_, bf16[64,2048]{1,0:T(8,128)(2,1)S(1)} %get-tuple-element.44.refs_2_, bf16[64,2048]{1,0:T(8,128)(2,1)S(1)} %get-tuple-element.45.refs_3_), custom_call_target="tpu_custom_call" | custom-call | flops 1 | bytes 1 | tf_op jit(solution)/shard_map/pick/pallas_call | solution.py:191
  33.3 1.6 %collective-permute-start.4 = (bf16[64,2048]{1,0:T(8,128)(2,1)S(1)}, bf16[64,2048]{1,0:T(8,128)(2,1)S(1)}, u32[]{:S(2)}, u32[]{:S(2)}) collective-permute-start(bf16[64,2048]{1,0:T(8,128)(2,1)S(1)} %get-tuple-element.46.refs_0_), channel_id=1, source_target_pairs={{0,1},{1,0},{2,3},{3,2},{4,5},{5,4},{6,7},{7,6},{8,9},{9,8},{10,11... | collective-permute-start | bytes 786440 | tf_op jit(solution)/shard_map/gather_grad_block3_row0/ppermute | solution.py:53
  34.9 0.5 collective-permute-start.5
  35.4 1.0 fusion
  36.6 0.9 norm.3
  37.5 1.6 %collective-permute-start.8 = (bf16[64,2048]{1,0:T(8,128)(2,1)S(1)}, bf16[64,2048]{1,0:T(8,128)(2,1)S(1)}, u32[]{:S(2)}, u32[]{:S(2)}) collective-permute-start(bf16[64,2048]{1,0:T(8,128)(2,1)S(1)} %get-tuple-element.54.refs_0_), channel_id=1, source_target_pairs={{0,2},{1,3},{2,0},{3,1},{4,6},{5,7},{6,4},{7,5},{8,10},{9,11},{10,... | collective-permute-start | bytes 786440 | tf_op jit(solution)/shard_map/gather_input_block2_first0/ppermute | solution.py:53
  39.1 0.5 collective-permute-start.9
  39.7 3.6 %project.2 = (bf16[512,512]{1,0:T(8,128)(2,1)S(1)}, bf16[512,512]{1,0:T(8,128)(2,1)S(1)}, bf16[512,512]{1,0:T(8,128)(2,1)S(1)}) custom-call(bf16[128,2048]{1,0:T(8,128)(2,1)S(1)} %get-tuple-element.43.refs_0_, bf16[128,2048]{1,0:T(8,128)(2,1)S(1)} %collective-permute-done.3.refs_1_, bf16[128,2048]{1,0:T(8,128)(2,1)S(1)} %collective-permute-done.2.refs_0_.refs_2_, ...), custom_call_target="tpu_custom_call" | custom-call | flops 1 | bytes 1 | tf_op jit(solution)/shard_map/project/pallas_call | solution.py:191
  43.4 1.6 %collective-permute-start.12 = (bf16[64,2048]{1,0:T(8,128)(2,1)S(1)}, bf16[64,2048]{1,0:T(8,128)(2,1)S(1)}, u32[]{:S(2)}, u32[]{:S(2)}) collective-permute-start(bf16[64,2048]{1,0:T(8,128)(2,1)S(1)} %get-tuple-element.64), channel_id=1, source_target_pairs={{0,1},{1,0},{2,3},{3,2},{4,5},{5,4},{6,7},{7,6},{8,9},{9,8},{10,11... | collective-permute-start | bytes 786440 | tf_op jit(solution)/shard_map/gather_input_block1_first0/ppermute | solution.py:53
  44.9 0.5 collective-permute-start.13
  45.5 6.6 %backward_heads.1 = (bf16[512,512]{1,0:T(8,128)(2,1)S(1)}, bf16[512,512]{1,0:T(8,128)(2,1)S(1)}, bf16[512,512]{1,0:T(8,128)(2,1)S(1)}) custom-call(bf16[128,2048]{1,0:T(8,128)(2,1)S(1)} %cast.1.refs_2_.refs_0_, bf16[128,2048]{1,0:T(8,128)(2,1)} %collective-permute-done.refs_1_, bf16[128,2048]{1,0:T(8,128)(2,1)} %collective-permute-done.1.refs_0_.refs_2_, ...), custom_call_target="tpu_custom_call" | custom-call | flops 8000000000 | bytes 1 | tf_op jit(solution)/shard_map/backward_heads/pallas_call | solution.py:191
  52.5 1.9 %collective-permute-start.15 = (bf16[64,2048]{1,0:T(8,128)(2,1)S(1)}, bf16[64,2048]{1,0:T(8,128)(2,1)S(1)}, u32[]{:S(2)}, u32[]{:S(2)}) collective-permute-start(bf16[64,2048]{1,0:T(8,128)(2,1)S(1)} %get-tuple-element.57.refs_7_), channel_id=1, source_target_pairs={{0,2},{1,3},{2,0},{3,1},{4,6},{5,7},{6,4},{7,5},{8,10},{9,11},{10,... | collective-permute-start | bytes 786440 | tf_op jit(solution)/shard_map/gather_input_block3_row64/ppermute | solution.py:53
  54.5 3.4 %backward_terms.1 = (f32[128,2048]{1,0:T(8,128)S(1)}, bf16[128,2048]{1,0:T(8,128)(2,1)S(1)}, bf16[128,2048]{1,0:T(8,128)(2,1)S(1)}, f32[64,2048]{1,0:T(8,128)S(1)}, f32[64,2048]{1,0:T(8,128)S(1)}) custom-call(bf16[512,512]{1,0:T(8,128)(2,1)S(1)} %get-tuple-element.51.refs_2_.refs_0_, bf16[512,512]{1,0:T(8,128)(2,1)S(1)} %get-tuple-element.52.refs_1_, ...), custom_call_target="tpu_custom_call" | custom-call | flops 3000000000 | bytes 1 | tf_op jit(solution)/shard_map/backward_terms/pallas_call | solution.py:191
  57.9 1.6 %collective-permute-start.10 = (bf16[128,2048]{1,0:T(8,128)(2,1)S(1)}, bf16[128,2048]{1,0:T(8,128)(2,1)S(1)}, u32[]{:S(2)}, u32[]{:S(2)}) collective-permute-start(bf16[128,2048]{1,0:T(8,128)(2,1)S(1)} %get-tuple-element.60), channel_id=1, source_target_pairs={{0,1},{1,0},{2,3},{3,2},{4,5},{5,4},{6,7},{7,6},{8,9},{9,8},{10,11... | collective-permute-start | bytes 1572872 | tf_op jit(solution)/shard_map/scatter_grad_block3_part0/ppermute | solution.py:53
  59.5 0.5 collective-permute-start.11
  60.0 1.4 %collective-permute-done.14.refs_6_ = bf16[64,2048]{1,0:T(8,128)(2,1)S(1)} collective-permute-done((bf16[64,2048]{1,0:T(8,128)(2,1)S(1)}, bf16[64,2048]{1,0:T(8,128)(2,1)S(1)}, u32[]{:S(2)}, u32[]{:S(2)}) %collective-permute-start.14) | collective-permute-done | bytes 262176 | tf_op jit(solution)/shard_map/gather_input_block3_row0/ppermute | solution.py:53
  61.5 3.6 %project.3 = (bf16[512,512]{1,0:T(8,128)(2,1)S(1)}, bf16[512,512]{1,0:T(8,128)(2,1)S(1)}, bf16[512,512]{1,0:T(8,128)(2,1)S(1)}) custom-call(bf16[64,2048]{1,0:T(8,128)(2,1)S(1)} %get-tuple-element.54.refs_0_, bf16[64,2048]{1,0:T(8,128)(2,1)S(1)} %get-tuple-element.55.refs_1_, bf16[64,2048]{1,0:T(8,128)(2,1)S(1)} %collective-permute-done.12.refs_2_, ...), custom_call_target="tpu_custom_call" | custom-call | flops 5000000000 | bytes 1 | tf_op jit(solution)/shard_map/project/pallas_call | solution.py:191
  65.1 2.8 %forward_terms.1 = (bf16[128,2048]{1,0:T(8,128)(2,1)S(1)}, bf16[64,2048]{1,0:T(8,128)(2,1)S(1)}, bf16[64,2048]{1,0:T(8,128)(2,1)S(1)}, bf16[64,2048]{1,0:T(8,128...) custom-call(bf16[512,512]{1,0:T(8,128)(2,1)S(1)} %get-tuple-element.66.refs_0_, ...), custom_call_target="tpu_custom_call" | custom-call | flops 5000000000 | bytes 1 | tf_op jit(solution)/shard_map/forward_terms/pallas_call | solution.py:191
  68.0 3.4 %collective-permute-start.18 = (bf16[64,2048]{1,0:T(8,128)(2,1)S(1)}, bf16[64,2048]{1,0:T(8,128)(2,1)S(1)}, u32[]{:S(2)}, u32[]{:S(2)}) collective-permute-start(bf16[64,2048]{1,0:T(8,128)(2,1)S(1)} %get-tuple-element.72), channel_id=1, source_target_pairs={{0,6},{1,7},{2,4},{3,5},{4,10},{5,11},{6,8},{7,9},{8,14},{9,15},{1... | collective-permute-start | bytes 786440 | tf_op jit(solution)/shard_map/scatter_branch_block2_part1/ppermute | solution.py:63
  71.5 1.1 %collective-permute-start.19 = (bf16[64,2048]{1,0:T(8,128)(2,1)S(1)}, bf16[64,2048]{1,0:T(8,128)(2,1)S(1)}, u32[]{:S(2)}, u32[]{:S(2)}) collective-permute-start(bf16[64,2048]{1,0:T(8,128)(2,1)S(1)} %get-tuple-element.73), channel_id=1, source_target_pairs={{0,5},{1,4},{2,7},{3,6},{4,9},{5,8},{6,11},{7,10},{8,13},{9,12},{1... | collective-permute-start | bytes 786440 | tf_op jit(solution)/shard_map/scatter_branch_block1_part0/ppermute | solution.py:63
  72.6 0.6 collective-permute-start.16
  73.2 0.5 collective-permute-start.17
  73.7 4.7 %collective-permute-done.21.base_ref.refs_2_ = bf16[128,2048]{1,0:T(8,128)(2,1)S(1)} collective-permute-done((bf16[128,2048]{1,0:T(8,128)(2,1)S(1)}, bf16[128,2048]{1,0:T(8,128)(2,1)S(1)}, u32[]{:S(2)}, u32[]{:S(2)}) %collective-permute-start.21) | collective-permute-done | bytes 524320 | tf_op jit(solution)/shard_map/ppermute | solution.py:63
  78.5 2.3 %collective-permute-start.22 = (bf16[64,2048]{1,0:T(8,128)(2,1)S(1)}, bf16[64,2048]{1,0:T(8,128)(2,1)S(1)}, u32[]{:S(2)}, u32[]{:S(2)}) collective-permute-start(bf16[64,2048]{1,0:T(8,128)(2,1)S(1)} %get-tuple-element.79), channel_id=1, source_target_pairs={{0,1},{1,0},{2,3},{3,2},{4,5},{5,4},{6,7},{7,6},{8,9},{9,8},{10,11... | collective-permute-start | bytes 786440 | tf_op jit(solution)/shard_map/scatter_branch_block3_part0/ppermute | solution.py:53
  80.7 2.2 %collective-permute-done.18.refs_4_.refs_0_ = bf16[64,2048]{1,0:T(8,128)(2,1)S(1)} collective-permute-done((bf16[64,2048]{1,0:T(8,128)(2,1)S(1)}, bf16[64,2048]{1,0:T(8,128)(2,1)S(1)}, u32[]{:S(2)}, u32[]{:S(2)}) %collective-permute-start.18) | collective-permute-done | bytes 262176 | tf_op jit(solution)/shard_map/scatter_branch_block2_part1/ppermute | solution.py:63
  82.9 2.9 %collective-permute-done.19.refs_5_.refs_1_ = bf16[64,2048]{1,0:T(8,128)(2,1)S(1)} collective-permute-done((bf16[64,2048]{1,0:T(8,128)(2,1)S(1)}, bf16[64,2048]{1,0:T(8,128)(2,1)S(1)}, u32[]{:S(2)}, u32[]{:S(2)}) %collective-permute-start.19) | collective-permute-done | bytes 262176 | tf_op jit(solution)/shard_map/scatter_branch_block1_part0/ppermute | solution.py:63
  85.8 0.5 collective-permute-done.16.refs_1_
  86.3 0.6 input_grad.1.refs_4_
  86.9 1.2 %collective-permute-start.20 = (bf16[128,2048]{1,0:T(8,128)(2,1)S(1)}, bf16[128,2048]{1,0:T(8,128)(2,1)S(1)}, u32[]{:S(2)}, u32[]{:S(2)}) collective-permute-start(bf16[128,2048]{1,0:T(8,128)(2,1)S(1)} %input_grad.1.refs_4_), channel_id=1, source_target_pairs={{0,28},{4,0},{8,4},{12,8},{16,12},{20,16},{24,20},{28,24},{1,29},{... | collective-permute-start | bytes 1572872 | tf_op jit(solution)/shard_map/ppermute | solution.py:69
  88.1 3.3 %collective-permute-done.22.refs_2_ = bf16[64,2048]{1,0:T(8,128)(2,1)S(1)} collective-permute-done((bf16[64,2048]{1,0:T(8,128)(2,1)S(1)}, bf16[64,2048]{1,0:T(8,128)(2,1)S(1)}, u32[]{:S(2)}, u32[]{:S(2)}) %collective-permute-start.22) | collective-permute-done | bytes 262176 | tf_op jit(solution)/shard_map/scatter_branch_block3_part0/ppermute | solution.py:53
  91.6 2.8 %collective-permute-start.25 = (bf16[64,2048]{1,0:T(8,128)(2,1)S(1)}, bf16[64,2048]{1,0:T(8,128)(2,1)S(1)}, u32[]{:S(2)}, u32[]{:S(2)}) collective-permute-start(bf16[64,2048]{1,0:T(8,128)(2,1)S(1)} %get-tuple-element.82), channel_id=1, source_target_pairs={{0,5},{1,4},{2,7},{3,6},{4,9},{5,8},{6,11},{7,10},{8,13},{9,12},{1... | collective-permute-start | bytes 786440 | tf_op jit(solution)/shard_map/scatter_branch_block1_part1/ppermute | solution.py:63
  94.3 1.5 %collective-permute-done.20.in_ref = bf16[128,2048]{1,0:T(8,128)(2,1)S(1)} collective-permute-done((bf16[128,2048]{1,0:T(8,128)(2,1)S(1)}, bf16[128,2048]{1,0:T(8,128)(2,1)S(1)}, u32[]{:S(2)}, u32[]{:S(2)}) %collective-permute-start.20) | collective-permute-done | bytes 524320 | tf_op jit(solution)/shard_map/ppermute | solution.py:69
  95.9 1.1 %widen.1 = (f32[1,128,2048]{2,1,0:T(8,128)}, f32[128,2048]{1,0:T(8,128)S(1)}) custom-call(bf16[128,2048]{1,0:T(8,128)(2,1)S(1)} %collective-permute-done.20.in_ref, bf16[128,2048]{1,0:T(8,128)(2,1)S(1)} %collective-permute-done.21.base_ref.refs_2_, bf16[64,2048]{1,0:T(8,128)(2,1)S(1)} %collective-permute-done.18.refs_4_.refs_0_, ...), custom_call_target="tpu_custom_call" | custom-call | flops 1 | bytes 1 | tf_op jit(solution)/shard_map/widen/pallas_call | solution.py:191
  96.9 3.2 %collective-permute-done.24.refs_0_ = bf16[64,2048]{1,0:T(8,128)(2,1)S(1)} collective-permute-done((bf16[64,2048]{1,0:T(8,128)(2,1)S(1)}, bf16[64,2048]{1,0:T(8,128)(2,1)S(1)}, u32[]{:S(2)}, u32[]{:S(2)}) %collective-permute-start.24) | collective-permute-done | bytes 262176 | tf_op jit(solution)/shard_map/scatter_branch_block2_part0/ppermute | solution.py:63
  100.2 3.8 %collective-permute-done.25.refs_1_ = bf16[64,2048]{1,0:T(8,128)(2,1)S(1)} collective-permute-done((bf16[64,2048]{1,0:T(8,128)(2,1)S(1)}, bf16[64,2048]{1,0:T(8,128)(2,1)S(1)}, u32[]{:S(2)}, u32[]{:S(2)}) %collective-permute-start.25) | collective-permute-done | bytes 262176 | tf_op jit(solution)/shard_map/scatter_branch_block1_part1/ppermute | solution.py:63
  104.0 1.1 %activation_sum.1 = f32[1,128,2048]{2,1,0:T(8,128)} custom-call(f32[128,2048]{1,0:T(8,128)S(1)} %get-tuple-element.75.base_ref, bf16[64,2048]{1,0:T(8,128)(2,1)S(1)} %collective-permute-done.24.refs_0_, bf16[64,2048]{1,0:T(8,128)(2,1)S(1)} %collective-permute-done.25.refs_1_), custom_call_target="tpu_custom_call" | custom-call | flops 8000000000 | bytes 1 | tf_op jit(solution)/shard_map/activation_sum/pallas_call | solution.py:191
  (49 shorter events, 1.4 us)
Async XLA Ops:
  0.6 1.2 %copy-start.6 = (f32[1,128,2048]{2,1,0:T(8,128)S(1)}, f32[1,128,2048]{2,1,0:T(8,128)}, u32[]{:S(2)}) copy-start(f32[1,128,2048]{2,1,0:T(8,128)} %param.9) | copy-start | bytes 3145732
  1.9 0.7 copy-start.8
  2.9 15.8 %collective-permute-start.2 = (bf16[128,2048]{1,0:T(8,128)(2,1)S(1)}, bf16[128,2048]{1,0:T(8,128)(2,1)S(1)}, u32[]{:S(2)}, u32[]{:S(2)}) collective-permute-start(bf16[128,2048]{1,0:T(8,128)(2,1)S(1)} %get-tuple-element.43.refs_0_), channel_id=1, source_target_pairs={{0,2},{1,3},{2,0},{3,1},{4,6},{5,7},{6,4},{7,5},{8,10},{9,11},{10,... | collective-permute-start | bytes 1572872 | tf_op jit(solution)/shard_map/gather_saved_block2/ppermute | solution.py:53
  5.9 14.8 %collective-permute-start.3 = (bf16[128,2048]{1,0:T(8,128)(2,1)S(1)}, bf16[128,2048]{1,0:T(8,128)(2,1)S(1)}, u32[]{:S(2)}, u32[]{:S(2)}) collective-permute-start(bf16[128,2048]{1,0:T(8,128)(2,1)S(1)} %get-tuple-element.43.refs_0_), channel_id=1, source_target_pairs={{0,1},{1,0},{2,3},{3,2},{4,5},{5,4},{6,7},{7,6},{8,9},{9,8},{10,11... | collective-permute-start | bytes 1572872 | tf_op jit(solution)/shard_map/gather_saved_block1/ppermute | solution.py:53
  7.4 1.2 %copy-start.4 = (f32[1,128,2048]{2,1,0:T(8,128)S(1)}, f32[1,128,2048]{2,1,0:T(8,128)}, u32[]{:S(2)}) copy-start(f32[1,128,2048]{2,1,0:T(8,128)} %param.10) | copy-start | bytes 3145732
  8.6 28.0 %copy-start.3 = (f32[1,128,2048]{2,1,0:T(8,128)S(1)}, f32[1,128,2048]{2,1,0:T(8,128)}, u32[]{:S(2)}) copy-start(f32[1,128,2048]{2,1,0:T(8,128)} %param.8) | copy-start | bytes 3145732
  8.7 23.4 %collective-permute-start = (bf16[128,2048]{1,0:T(8,128)(2,1)S(1)}, bf16[128,2048]{1,0:T(8,128)(2,1)}, u32[]{:S(2)}, u32[]{:S(2)}) collective-permute-start(bf16[128,2048]{1,0:T(8,128)(2,1)S(1)} %cast.1.refs_2_.refs_0_), channel_id=1, source_target_pairs={{0,1},{1,0},{2,3},{3,2},{4,5},{5,4},{6,7},{7,6},{8,9},{9,8},{10,11... | collective-permute-start | bytes 1572872 | tf_op jit(solution)/shard_map/gather_grad_block1/ppermute | solution.py:53
  9.3 22.8 %collective-permute-start.1 = (bf16[128,2048]{1,0:T(8,128)(2,1)S(1)}, bf16[128,2048]{1,0:T(8,128)(2,1)}, u32[]{:S(2)}, u32[]{:S(2)}) collective-permute-start(bf16[128,2048]{1,0:T(8,128)(2,1)S(1)} %cast.1.refs_2_.refs_0_), channel_id=1, source_target_pairs={{0,2},{1,3},{2,0},{3,1},{4,6},{5,7},{6,4},{7,5},{8,10},{9,11},{10,... | collective-permute-start | bytes 1572872 | tf_op jit(solution)/shard_map/gather_grad_block2/ppermute | solution.py:53
  20.7 18.9 %copy-start.2 = (bf16[1,2048,512]{2,1,0:T(8,128)(2,1)S(1)}, bf16[1,2048,512]{2,1,0:T(8,128)(2,1)}, u32[]{:S(2)}) copy-start(bf16[1,2048,512]{2,1,0:T(8,128)(2,1)} %param.14) | copy-start | bytes 6291460
  20.8 15.8 %copy-start.9 = (f32[1,2048]{1,0:T(1,128)S(1)}, f32[1,2048]{1,0:T(1,128)}, u32[]{:S(2)}) copy-start(f32[1,2048]{1,0:T(1,128)} %gain_ref.1) | copy-start | bytes 24580
  20.8 18.3 %collective-permute-start.6 = (bf16[64,2048]{1,0:T(8,128)(2,1)S(1)}, bf16[64,2048]{1,0:T(8,128)(2,1)S(1)}, u32[]{:S(2)}, u32[]{:S(2)}) collective-permute-start(bf16[64,2048]{1,0:T(8,128)(2,1)S(1)} %get-tuple-element.44.refs_2_), channel_id=1, source_target_pairs={{0,1},{1,0},{2,3},{3,2},{4,5},{5,4},{6,7},{7,6},{8,9},{9,8},{10,11... | collective-permute-start | bytes 786440 | tf_op jit(solution)/shard_map/gather_saved_block3_row0/ppermute | solution.py:53
  22.4 17.3 %collective-permute-start.7 = (bf16[64,2048]{1,0:T(8,128)(2,1)S(1)}, bf16[64,2048]{1,0:T(8,128)(2,1)S(1)}, u32[]{:S(2)}, u32[]{:S(2)}) collective-permute-start(bf16[64,2048]{1,0:T(8,128)(2,1)S(1)} %get-tuple-element.45.refs_3_), channel_id=1, source_target_pairs={{0,2},{1,3},{2,0},{3,1},{4,6},{5,7},{6,4},{7,5},{8,10},{9,11},{10,... | collective-permute-start | bytes 786440 | tf_op jit(solution)/shard_map/gather_saved_block3_row64/ppermute | solution.py:53
  32.1 7.6 %copy-start.1 = (bf16[1,2048,512]{2,1,0:T(8,128)(2,1)S(1)}, bf16[1,2048,512]{2,1,0:T(8,128)(2,1)}, u32[]{:S(2)}) copy-start(bf16[1,2048,512]{2,1,0:T(8,128)(2,1)} %param.13) | copy-start | bytes 6291460
  33.3 6.4 %copy-start = (bf16[1,2048,512]{2,1,0:T(8,128)(2,1)S(1)}, bf16[1,2048,512]{2,1,0:T(8,128)(2,1)}, u32[]{:S(2)}) copy-start(bf16[1,2048,512]{2,1,0:T(8,128)(2,1)} %param.12) | copy-start | bytes 6291460
  33.3 11.6 %collective-permute-start.4 = (bf16[64,2048]{1,0:T(8,128)(2,1)S(1)}, bf16[64,2048]{1,0:T(8,128)(2,1)S(1)}, u32[]{:S(2)}, u32[]{:S(2)}) collective-permute-start(bf16[64,2048]{1,0:T(8,128)(2,1)S(1)} %get-tuple-element.46.refs_0_), channel_id=1, source_target_pairs={{0,1},{1,0},{2,3},{3,2},{4,5},{5,4},{6,7},{7,6},{8,9},{9,8},{10,11... | collective-permute-start | bytes 786440 | tf_op jit(solution)/shard_map/gather_grad_block3_row0/ppermute | solution.py:53
  34.9 10.6 %collective-permute-start.5 = (bf16[64,2048]{1,0:T(8,128)(2,1)S(1)}, bf16[64,2048]{1,0:T(8,128)(2,1)S(1)}, u32[]{:S(2)}, u32[]{:S(2)}) collective-permute-start(bf16[64,2048]{1,0:T(8,128)(2,1)S(1)} %get-tuple-element.47.refs_1_), channel_id=1, source_target_pairs={{0,2},{1,3},{2,0},{3,1},{4,6},{5,7},{6,4},{7,5},{8,10},{9,11},{10,... | collective-permute-start | bytes 786440 | tf_op jit(solution)/shard_map/gather_grad_block3_row64/ppermute | solution.py:53
  37.5 14.6 %collective-permute-start.8 = (bf16[64,2048]{1,0:T(8,128)(2,1)S(1)}, bf16[64,2048]{1,0:T(8,128)(2,1)S(1)}, u32[]{:S(2)}, u32[]{:S(2)}) collective-permute-start(bf16[64,2048]{1,0:T(8,128)(2,1)S(1)} %get-tuple-element.54.refs_0_), channel_id=1, source_target_pairs={{0,2},{1,3},{2,0},{3,1},{4,6},{5,7},{6,4},{7,5},{8,10},{9,11},{10,... | collective-permute-start | bytes 786440 | tf_op jit(solution)/shard_map/gather_input_block2_first0/ppermute | solution.py:53
  39.1 13.0 %collective-permute-start.9 = (bf16[64,2048]{1,0:T(8,128)(2,1)S(1)}, bf16[64,2048]{1,0:T(8,128)(2,1)S(1)}, u32[]{:S(2)}, u32[]{:S(2)}) collective-permute-start(bf16[64,2048]{1,0:T(8,128)(2,1)S(1)} %get-tuple-element.55.refs_1_), channel_id=1, source_target_pairs={{0,1},{1,0},{2,3},{3,2},{4,5},{5,4},{6,7},{7,6},{8,9},{9,8},{10,11... | collective-permute-start | bytes 786440 | tf_op jit(solution)/shard_map/gather_input_block1_first64/ppermute | solution.py:53
  39.7 5.8 %copy-start.10 = (bf16[1,2048,512]{2,1,0:T(8,128)(2,1)S(1)}, bf16[1,2048,512]{2,1,0:T(8,128)(2,1)}, u32[]{:S(2)}) copy-start(bf16[1,2048,512]{2,1,0:T(8,128)(2,1)} %param.15) | copy-start | bytes 6291460
  43.4 16.1 %collective-permute-start.12 = (bf16[64,2048]{1,0:T(8,128)(2,1)S(1)}, bf16[64,2048]{1,0:T(8,128)(2,1)S(1)}, u32[]{:S(2)}, u32[]{:S(2)}) collective-permute-start(bf16[64,2048]{1,0:T(8,128)(2,1)S(1)} %get-tuple-element.64), channel_id=1, source_target_pairs={{0,1},{1,0},{2,3},{3,2},{4,5},{5,4},{6,7},{7,6},{8,9},{9,8},{10,11... | collective-permute-start | bytes 786440 | tf_op jit(solution)/shard_map/gather_input_block1_first0/ppermute | solution.py:53
  44.9 15.1 %collective-permute-start.13 = (bf16[64,2048]{1,0:T(8,128)(2,1)S(1)}, bf16[64,2048]{1,0:T(8,128)(2,1)S(1)}, u32[]{:S(2)}, u32[]{:S(2)}) collective-permute-start(bf16[64,2048]{1,0:T(8,128)(2,1)S(1)} %get-tuple-element.65), channel_id=1, source_target_pairs={{0,2},{1,3},{2,0},{3,1},{4,6},{5,7},{6,4},{7,5},{8,10},{9,11},{10,... | collective-permute-start | bytes 786440 | tf_op jit(solution)/shard_map/gather_input_block2_first64/ppermute | solution.py:53
  52.4 9.1 %collective-permute-start.14 = (bf16[64,2048]{1,0:T(8,128)(2,1)S(1)}, bf16[64,2048]{1,0:T(8,128)(2,1)S(1)}, u32[]{:S(2)}, u32[]{:S(2)}) collective-permute-start(bf16[64,2048]{1,0:T(8,128)(2,1)S(1)} %get-tuple-element.56.refs_6_), channel_id=1, source_target_pairs={{0,1},{1,0},{2,3},{3,2},{4,5},{5,4},{6,7},{7,6},{8,9},{9,8},{10,11... | collective-permute-start | bytes 786440 | tf_op jit(solution)/shard_map/gather_input_block3_row0/ppermute | solution.py:53
  52.5 8.9 %collective-permute-start.15 = (bf16[64,2048]{1,0:T(8,128)(2,1)S(1)}, bf16[64,2048]{1,0:T(8,128)(2,1)S(1)}, u32[]{:S(2)}, u32[]{:S(2)}) collective-permute-start(bf16[64,2048]{1,0:T(8,128)(2,1)S(1)} %get-tuple-element.57.refs_7_), channel_id=1, source_target_pairs={{0,2},{1,3},{2,0},{3,1},{4,6},{5,7},{6,4},{7,5},{8,10},{9,11},{10,... | collective-permute-start | bytes 786440 | tf_op jit(solution)/shard_map/gather_input_block3_row64/ppermute | solution.py:53
  57.9 14.6 %collective-permute-start.10 = (bf16[128,2048]{1,0:T(8,128)(2,1)S(1)}, bf16[128,2048]{1,0:T(8,128)(2,1)S(1)}, u32[]{:S(2)}, u32[]{:S(2)}) collective-permute-start(bf16[128,2048]{1,0:T(8,128)(2,1)S(1)} %get-tuple-element.60), channel_id=1, source_target_pairs={{0,1},{1,0},{2,3},{3,2},{4,5},{5,4},{6,7},{7,6},{8,9},{9,8},{10,11... | collective-permute-start | bytes 1572872 | tf_op jit(solution)/shard_map/scatter_grad_block3_part0/ppermute | solution.py:53
  59.5 13.0 %collective-permute-start.11 = (bf16[128,2048]{1,0:T(8,128)(2,1)S(1)}, bf16[128,2048]{1,0:T(8,128)(2,1)S(1)}, u32[]{:S(2)}, u32[]{:S(2)}) collective-permute-start(bf16[128,2048]{1,0:T(8,128)(2,1)S(1)} %get-tuple-element.63), channel_id=1, source_target_pairs={{0,2},{1,3},{2,0},{3,1},{4,6},{5,7},{6,4},{7,5},{8,10},{9,11},{10,... | collective-permute-start | bytes 1572872 | tf_op jit(solution)/shard_map/scatter_grad_block3_part1/ppermute | solution.py:53
  67.9 18.4 %copy-start.5 = (f32[1,128,2048]{2,1,0:T(8,128)S(1)}, f32[1,128,2048]{2,1,0:T(8,128)}, u32[]{:S(2)}) copy-start(f32[1,128,2048]{2,1,0:T(8,128)} %param.10) | copy-start | bytes 3145732
  67.9 18.4 %copy-start.7 = (f32[1,128,2048]{2,1,0:T(8,128)S(1)}, f32[1,128,2048]{2,1,0:T(8,128)}, u32[]{:S(2)}) copy-start(f32[1,128,2048]{2,1,0:T(8,128)} %param.9) | copy-start | bytes 3145732
  67.9 10.5 %collective-permute-start.21 = (bf16[128,2048]{1,0:T(8,128)(2,1)S(1)}, bf16[128,2048]{1,0:T(8,128)(2,1)S(1)}, u32[]{:S(2)}, u32[]{:S(2)}) collective-permute-start(bf16[128,2048]{1,0:T(8,128)(2,1)S(1)} %get-tuple-element.74), channel_id=1, source_target_pairs={{0,4},{1,5},{2,6},{3,7},{4,8},{5,9},{6,10},{7,11},{8,12},{9,13},{1... | collective-permute-start | bytes 1572872 | tf_op jit(solution)/shard_map/ppermute | solution.py:63
  68.0 14.9 %collective-permute-start.18 = (bf16[64,2048]{1,0:T(8,128)(2,1)S(1)}, bf16[64,2048]{1,0:T(8,128)(2,1)S(1)}, u32[]{:S(2)}, u32[]{:S(2)}) collective-permute-start(bf16[64,2048]{1,0:T(8,128)(2,1)S(1)} %get-tuple-element.72), channel_id=1, source_target_pairs={{0,6},{1,7},{2,4},{3,5},{4,10},{5,11},{6,8},{7,9},{8,14},{9,15},{1... | collective-permute-start | bytes 786440 | tf_op jit(solution)/shard_map/scatter_branch_block2_part1/ppermute | solution.py:63
  71.5 14.3 %collective-permute-start.19 = (bf16[64,2048]{1,0:T(8,128)(2,1)S(1)}, bf16[64,2048]{1,0:T(8,128)(2,1)S(1)}, u32[]{:S(2)}, u32[]{:S(2)}) collective-permute-start(bf16[64,2048]{1,0:T(8,128)(2,1)S(1)} %get-tuple-element.73), channel_id=1, source_target_pairs={{0,5},{1,4},{2,7},{3,6},{4,9},{5,8},{6,11},{7,10},{8,13},{9,12},{1... | collective-permute-start | bytes 786440 | tf_op jit(solution)/shard_map/scatter_branch_block1_part0/ppermute | solution.py:63
  72.6 13.7 %collective-permute-start.16 = (bf16[64,2048]{1,0:T(8,128)(2,1)S(1)}, bf16[64,2048]{1,0:T(8,128)(2,1)S(1)}, u32[]{:S(2)}, u32[]{:S(2)}) collective-permute-start(bf16[64,2048]{1,0:T(8,128)(2,1)S(1)} %get-tuple-element.70.refs_4_), channel_id=1, source_target_pairs={{0,1},{1,0},{2,3},{3,2},{4,5},{5,4},{6,7},{7,6},{8,9},{9,8},{10,11... | collective-permute-start | bytes 786440 | tf_op jit(solution)/shard_map/scatter_grad_block1_part1/ppermute | solution.py:53
  73.2 13.1 %collective-permute-start.17 = (bf16[64,2048]{1,0:T(8,128)(2,1)S(1)}, bf16[64,2048]{1,0:T(8,128)(2,1)S(1)}, u32[]{:S(2)}, u32[]{:S(2)}) collective-permute-start(bf16[64,2048]{1,0:T(8,128)(2,1)S(1)} %get-tuple-element.71.refs_3_), channel_id=1, source_target_pairs={{0,2},{1,3},{2,0},{3,1},{4,6},{5,7},{6,4},{7,5},{8,10},{9,11},{10,... | collective-permute-start | bytes 786440 | tf_op jit(solution)/shard_map/scatter_grad_block2_part0/ppermute | solution.py:53
  78.5 12.9 %collective-permute-start.22 = (bf16[64,2048]{1,0:T(8,128)(2,1)S(1)}, bf16[64,2048]{1,0:T(8,128)(2,1)S(1)}, u32[]{:S(2)}, u32[]{:S(2)}) collective-permute-start(bf16[64,2048]{1,0:T(8,128)(2,1)S(1)} %get-tuple-element.79), channel_id=1, source_target_pairs={{0,1},{1,0},{2,3},{3,2},{4,5},{5,4},{6,7},{7,6},{8,9},{9,8},{10,11... | collective-permute-start | bytes 786440 | tf_op jit(solution)/shard_map/scatter_branch_block3_part0/ppermute | solution.py:53
  82.9 8.5 %collective-permute-start.23 = (bf16[64,2048]{1,0:T(8,128)(2,1)S(1)}, bf16[64,2048]{1,0:T(8,128)(2,1)S(1)}, u32[]{:S(2)}, u32[]{:S(2)}) collective-permute-start(bf16[64,2048]{1,0:T(8,128)(2,1)S(1)} %get-tuple-element.80), channel_id=1, source_target_pairs={{0,2},{1,3},{2,0},{3,1},{4,6},{5,7},{6,4},{7,5},{8,10},{9,11},{10,... | collective-permute-start | bytes 786440 | tf_op jit(solution)/shard_map/scatter_branch_block3_part1/ppermute | solution.py:53
  86.9 9.0 %collective-permute-start.20 = (bf16[128,2048]{1,0:T(8,128)(2,1)S(1)}, bf16[128,2048]{1,0:T(8,128)(2,1)S(1)}, u32[]{:S(2)}, u32[]{:S(2)}) collective-permute-start(bf16[128,2048]{1,0:T(8,128)(2,1)S(1)} %input_grad.1.refs_4_), channel_id=1, source_target_pairs={{0,28},{4,0},{8,4},{12,8},{16,12},{20,16},{24,20},{28,24},{1,29},{... | collective-permute-start | bytes 1572872 | tf_op jit(solution)/shard_map/ppermute | solution.py:69
  91.5 8.6 %collective-permute-start.24 = (bf16[64,2048]{1,0:T(8,128)(2,1)S(1)}, bf16[64,2048]{1,0:T(8,128)(2,1)S(1)}, u32[]{:S(2)}, u32[]{:S(2)}) collective-permute-start(bf16[64,2048]{1,0:T(8,128)(2,1)S(1)} %get-tuple-element.81), channel_id=1, source_target_pairs={{0,6},{1,7},{2,4},{3,5},{4,10},{5,11},{6,8},{7,9},{8,14},{9,15},{1... | collective-permute-start | bytes 786440 | tf_op jit(solution)/shard_map/scatter_branch_block2_part0/ppermute | solution.py:63
  91.6 12.4 %collective-permute-start.25 = (bf16[64,2048]{1,0:T(8,128)(2,1)S(1)}, bf16[64,2048]{1,0:T(8,128)(2,1)S(1)}, u32[]{:S(2)}, u32[]{:S(2)}) collective-permute-start(bf16[64,2048]{1,0:T(8,128)(2,1)S(1)} %get-tuple-element.82), channel_id=1, source_target_pairs={{0,5},{1,4},{2,7},{3,6},{4,9},{5,8},{6,11},{7,10},{8,13},{9,12},{1... | collective-permute-start | bytes 786440 | tf_op jit(solution)/shard_map/scatter_branch_block1_part1/ppermute | solution.py:63

commit v5 on v4

--- a/solution.py
+++ b/solution.py
@@ -205,7 +205,7 @@
 VMEM = pl.BlockSpec(memory_space=pltpu.VMEM)
 
 
-def normed_rows(inputs, gain, bounds, after=()):
+def normed_rows(inputs, gain, bounds, after=(), vmem=10):
     rows, width = inputs.shape
 
     def kernel(x_any, gain_any, *refs):
@@ -235,6 +235,7 @@
             pltpu.VMEM(gain.shape, jnp.float32),
             pltpu.SemaphoreType.DMA((2,)),
         ],
+        vmem=vmem,
         name="norm",
     )
     return parts, inv
@@ -621,20 +622,21 @@
 
     whole = [(0, rows)]
     projections = (own_query, own_key, own_value)
-    (normed_bwd,), inv_bwd = normed_rows(saved_in, gain, whole)
+    (normed_bwd,), inv_bwd = normed_rows(saved_in, gain, whole, vmem=62)
     grad_low = cast_rows(grad, [normed_bwd])
     all_bwd = gather_first(normed_bwd, "saved")
     all_grad = gather_first(grad_low, "grad")
+    normed_fwd, _ = normed_rows(act_in, gain, bounds)
     picked = picked_rows(second_hops(all_bwd, bounds), [grad_low])
     all_bwd = gather_rest(all_bwd, picked, bounds, "saved")
-    picked = picked_rows(second_hops(all_grad, bounds), picked)
-    all_grad = gather_rest(all_grad, picked, bounds, "grad")
-    normed_fwd, _ = normed_rows(act_in, gain, bounds, picked)
-    all_fwd = gather_parts({}, normed_fwd, bounds, True, "input")
+    n = len(bounds)
+    handed_on = [(value, 0, value.shape[0]) for value in normed_fwd]
+    picked = picked_rows(handed_on + second_hops(all_grad, bounds), picked)
+    all_fwd = gather_parts({}, picked[:n], bounds, True, "input")
+    all_grad = gather_rest(all_grad, picked[n:], bounds, "grad")
 
     qkv = project(all_bwd, projections, cosine, sine, rows)
-    handed_on = picked_rows([(value, 0, value.shape[0]) for value in normed_fwd], qkv[:1])
-    all_fwd = gather_parts(all_fwd, handed_on, bounds, False, "input")
+    all_fwd = gather_parts(all_fwd, picked_rows(handed_on, qkv[:1]), bounds, False, "input")
     d_qkv = backward_heads(all_grad, qkv, own_out, cosine, sine, rows)
     picked = picked_rows(second_hops(all_fwd, bounds), d_qkv[:1])
     all_fwd = gather_rest(all_fwd, picked, bounds, "input")
@@ -649,15 +651,15 @@
     back.send_groups(range(len(back.groups)))
     onward = front.onward()
     front.send_groups([i for i in range(len(front.groups)) if i not in onward])
-    own = across_and_on(own, 0)
     soon = dict(front.final)
+    ready = [value for value, _ in soon.values()]
     sums = back.send_sums([terms[0]])
-    held = picked_rows(
-        [(front.leaving[i], 0, front.leaving[i].shape[0]) for i in onward], [own, *sums]
-    )
+    held = picked_rows([(front.leaving[i], 0, front.leaving[i].shape[0]) for i in onward], sums)
     for i, value in zip(onward, held):
         front.leaving[i] = value
     front.send_groups(onward)
+    (own,) = picked_rows([(own, 0, rows)], [*ready, *held])
+    own = across_and_on(own, 0)
     d_input = input_grad(
         d_own,
         back.final,
@@ -666,7 +668,7 @@
         inv_bwd,
         gain,
         bounds,
-        [value for value, _ in soon.values()],
+        ready,
     )
     front.send_sums([d_input])
     grad_prev, base = widened(passed_along(d_input, "pipe", -1), own, soon, bounds)

time: 105 us -> 105 us (level)
  waiting for transfers between devices: 44.2 us -> 40.3 us
  Pallas kernels: 25.9 us -> 28.9 us
    ppermute x5, waiting for transfers between devices: 16.9 us -> 9.69 us  [across_and_on(): return lax.ppermute(value, ('pipe', 'seq'), pairs)]
    pallas_call x18 -> x19, Pallas kernels: 25.9 us -> 28.9 us  [call(): pl.pallas_call(kernel, out_shape=out_shapes, in_specs=in_specs, out_specs...]
    ppermute x20, waiting for transfers between devices: 25.8 us -> 27.7 us  [across(): return lax.ppermute(value, 'seq', [(i, i ^ 1 << bit) for i in range(count)])]
    ppermute x1, waiting for transfers between devices: 1.53 us -> 2.95 us  [passed_along(): return lax.ppermute(value, axis, pairs)]
    ppermute x1, starting transfers between devices: 1.18 us -> 0.06 us  [passed_along(): return lax.ppermute(value, axis, pairs)]
    unnamed x22 -> x32, local copies, waits for them, and re-layouts: 3.18 us -> 4.02 us
  transfers between devices with their start and end apart: 26 -> 26, of which waited for: 12 -> 12; matrix products, arithmetic and copies ran while one was open for 1% -> 1% of each run, Pallas kernels for 23% -> 24%
where the time goes in v5:
time: 105 us
  waiting for transfers between devices  40.3 us (38%)
  starting transfers between devices  29.8 us (28%)
  Pallas kernels  28.9 us (28%)
  local copies, waits for them, and re-layouts  4.02 us (4%)
  other arithmetic  1.28 us (1%)
    pallas_call x19, Pallas kernels, call(): pl.pallas_call(kernel, out_shape=out_shapes, in_specs=in_specs, out_specs...  28.9 us
    ppermute x20, waiting for transfers between devices, across(): return lax.ppermute(value, 'seq', [(i, i ^ 1 << bit) for i in range(count)])  27.7 us
    ppermute x20, starting transfers between devices, across(): return lax.ppermute(value, 'seq', [(i, i ^ 1 << bit) for i in range(count)])  22 us
    ppermute x5, waiting for transfers between devices, across_and_on(): return lax.ppermute(value, ('pipe', 'seq'), pairs)  9.69 us
    ppermute x5, starting transfers between devices, across_and_on(): return lax.ppermute(value, ('pipe', 'seq'), pairs)  7.7 us
    unnamed x32, local copies, waits for them, and re-layouts  4.02 us
    ppermute x1, waiting for transfers between devices, passed_along(): return lax.ppermute(value, axis, pairs)  2.95 us
  transfers between devices with their start and end apart: 26, of which 12 were waited for; matrix products, arithmetic and copies ran while one was open for 1% of the time, Pallas kernels for 24%

profile of v5, /device:TPU:0, one launch (start us, length us, event | category | flops | bytes accessed | tf_op | source)
XLA Modules:
  0.0 105.2 jit_solution(1469816122218170027)
XLA Ops:
  0.6 2.3 %norm.2 = (bf16[128,2048]{1,0:T(8,128)(2,1)}, f32[128,1]{1,0:T(8,128)}) custom-call(f32[128,2048]{1,0:T(8,128)} %bitcast.22, f32[1,2048]{1,0:T(1,128)} %gain_ref.1), custom_call_target="tpu_custom_call" | custom-call | flops 1 | bytes 1 | tf_op jit(solution)/shard_map/norm/pallas_call | solution.py:191
  2.9 3.0 %collective-permute-start.3 = (bf16[128,2048]{1,0:T(8,128)(2,1)}, bf16[128,2048]{1,0:T(8,128)(2,1)S(1)}, u32[]{:S(2)}, u32[]{:S(2)}) collective-permute-start(bf16[128,2048]{1,0:T(8,128)(2,1)} %get-tuple-element.45.refs_0_), channel_id=1, source_target_pairs={{0,1},{1,0},{2,3},{3,2},{4,5},{5,4},{6,7},{7,6},{8,9},{9,8},{10,11... | collective-permute-start | bytes 1572872 | tf_op jit(solution)/shard_map/gather_saved_block1/ppermute | solution.py:53
  5.9 1.5 %collective-permute-start.2 = (bf16[128,2048]{1,0:T(8,128)(2,1)}, bf16[128,2048]{1,0:T(8,128)(2,1)S(1)}, u32[]{:S(2)}, u32[]{:S(2)}) collective-permute-start(bf16[128,2048]{1,0:T(8,128)(2,1)} %get-tuple-element.45.refs_0_), channel_id=1, source_target_pairs={{0,2},{1,3},{2,0},{3,1},{4,6},{5,7},{6,4},{7,5},{8,10},{9,11},{10,... | collective-permute-start | bytes 1572872 | tf_op jit(solution)/shard_map/gather_saved_block2/ppermute | solution.py:53
  7.4 1.1 %copy-done.3 = bf16[128,2048]{1,0:T(8,128)(2,1)S(1)} copy-done((bf16[128,2048]{1,0:T(8,128)(2,1)S(1)}, bf16[128,2048]{1,0:T(8,128)(2,1)}, u32[]{:S(2)}) %copy-start.3) | copy-done | bytes 524312
  8.5 1.2 %copy-done.7 = f32[1,128,2048]{2,1,0:T(8,128)S(1)} copy-done((f32[1,128,2048]{2,1,0:T(8,128)S(1)}, f32[1,128,2048]{2,1,0:T(8,128)}, u32[]{:S(2)}) %copy-start.7) | copy-done | bytes 1048600
  9.7 0.8 cast.1.refs_2_.refs_0_
  10.6 0.5 collective-permute-start.1
  11.2 0.9 norm.3
  12.1 0.7 copy-done.10
  12.9 5.9 %collective-permute-done.3.refs_1_ = bf16[128,2048]{1,0:T(8,128)(2,1)S(1)} collective-permute-done((bf16[128,2048]{1,0:T(8,128)(2,1)}, bf16[128,2048]{1,0:T(8,128)(2,1)S(1)}, u32[]{:S(2)}, u32[]{:S(2)}) %collective-permute-start.3) | collective-permute-done | bytes 524320 | tf_op jit(solution)/shard_map/gather_saved_block1/ppermute | solution.py:53
  18.9 2.1 %collective-permute-done.2.refs_0_.refs_2_ = bf16[128,2048]{1,0:T(8,128)(2,1)S(1)} collective-permute-done((bf16[128,2048]{1,0:T(8,128)(2,1)}, bf16[128,2048]{1,0:T(8,128)(2,1)S(1)}, u32[]{:S(2)}, u32[]{:S(2)}) %collective-permute-start.2) | collective-permute-done | bytes 524320 | tf_op jit(solution)/shard_map/gather_saved_block2/ppermute | solution.py:53
  21.2 2.0 %collective-permute-start.7 = (bf16[64,2048]{1,0:T(8,128)(2,1)S(1)}, bf16[64,2048]{1,0:T(8,128)(2,1)S(1)}, u32[]{:S(2)}, u32[]{:S(2)}) collective-permute-start(bf16[64,2048]{1,0:T(8,128)(2,1)S(1)} %get-tuple-element.49.refs_5_), channel_id=1, source_target_pairs={{0,2},{1,3},{2,0},{3,1},{4,6},{5,7},{6,4},{7,5},{8,10},{9,11},{10,... | collective-permute-start | bytes 786440 | tf_op jit(solution)/shard_map/gather_saved_block3_row64/ppermute | solution.py:53
  23.2 9.2 %collective-permute-done.1.refs_2_ = bf16[128,2048]{1,0:T(8,128)(2,1)} collective-permute-done((bf16[128,2048]{1,0:T(8,128)(2,1)}, bf16[128,2048]{1,0:T(8,128)(2,1)}, u32[]{:S(2)}, u32[]{:S(2)}) %collective-permute-start.1) | collective-permute-done | bytes 524320 | tf_op jit(solution)/shard_map/gather_grad_block2/ppermute | solution.py:53
  32.3 0.9 copy-done.11
  33.3 1.2 %pick.7 = (bf16[64,2048]{1,0:T(8,128)(2,1)S(1)}, bf16[64,2048]{1,0:T(8,128)(2,1)S(1)}, bf16[64,2048]{1,0:T(8,128)(2,1)S(1)}, bf16[64,2048]{1,0:T(8,128)(2,1)S(1)}) custom-call(bf16[64,2048]{1,0:T(8,128)(2,1)S(1)} %get-tuple-element.46.refs_0_, bf16[64,2048]{1,0:T(8,128)(2,1)S(1)} %copy-done.11, bf16[128,2048]{1,0:T(8,128)(2,1)} %collective-permute-done.1.refs_2_, ...), custom_call_target="tpu_custom_call" | custom-call | flops 1 | bytes 1 | tf_op jit(solution)/shard_map/pick/pallas_call | solution.py:191
  34.7 2.0 %collective-permute-start.5 = (bf16[64,2048]{1,0:T(8,128)(2,1)S(1)}, bf16[64,2048]{1,0:T(8,128)(2,1)S(1)}, u32[]{:S(2)}, u32[]{:S(2)}) collective-permute-start(bf16[64,2048]{1,0:T(8,128)(2,1)S(1)} %get-tuple-element.51), channel_id=1, source_target_pairs={{0,2},{1,3},{2,0},{3,1},{4,6},{5,7},{6,4},{7,5},{8,10},{9,11},{10,... | collective-permute-start | bytes 786440 | tf_op jit(solution)/shard_map/gather_grad_block3_row64/ppermute | solution.py:53
  36.6 1.0 fusion
  37.6 0.2 pad_maximum_fusion
  38.0 1.9 %collective-permute-start.9 = (bf16[64,2048]{1,0:T(8,128)(2,1)S(1)}, bf16[64,2048]{1,0:T(8,128)(2,1)S(1)}, u32[]{:S(2)}, u32[]{:S(2)}) collective-permute-start(bf16[64,2048]{1,0:T(8,128)(2,1)S(1)} %get-tuple-element.59.refs_1_), channel_id=1, source_target_pairs={{0,1},{1,0},{2,3},{3,2},{4,5},{5,4},{6,7},{7,6},{8,9},{9,8},{10,11... | collective-permute-start | bytes 786440 | tf_op jit(solution)/shard_map/gather_input_block1_first64/ppermute | solution.py:53
  40.0 3.6 %project.2 = (bf16[512,512]{1,0:T(8,128)(2,1)S(1)}, bf16[512,512]{1,0:T(8,128)(2,1)S(1)}, bf16[512,512]{1,0:T(8,128)(2,1)S(1)}) custom-call(bf16[128,2048]{1,0:T(8,128)(2,1)S(1)} %copy-done.4, bf16[128,2048]{1,0:T(8,128)(2,1)S(1)} %collective-permute-done.3.refs_1_, bf16[128,2048]{1,0:T(8,128)(2,1)S(1)} %collective-permute-done.2.refs_0_.refs_2_, ...), custom_call_target="tpu_custom_call" | custom-call | flops 1 | bytes 1 | tf_op jit(solution)/shard_map/project/pallas_call | solution.py:191
  43.8 1.9 %collective-permute-start.13 = (bf16[64,2048]{1,0:T(8,128)(2,1)S(1)}, bf16[64,2048]{1,0:T(8,128)(2,1)S(1)}, u32[]{:S(2)}, u32[]{:S(2)}) collective-permute-start(bf16[64,2048]{1,0:T(8,128)(2,1)S(1)} %get-tuple-element.69), channel_id=1, source_target_pairs={{0,2},{1,3},{2,0},{3,1},{4,6},{5,7},{6,4},{7,5},{8,10},{9,11},{10,... | collective-permute-start | bytes 786440 | tf_op jit(solution)/shard_map/gather_input_block2_first64/ppermute | solution.py:53
  45.8 6.8 %backward_heads.1 = (bf16[512,512]{1,0:T(8,128)(2,1)S(1)}, bf16[512,512]{1,0:T(8,128)(2,1)S(1)}, bf16[512,512]{1,0:T(8,128)(2,1)S(1)}) custom-call(bf16[128,2048]{1,0:T(8,128)(2,1)} %cast.1.refs_2_.refs_0_, bf16[128,2048]{1,0:T(8,128)(2,1)} %collective-permute-done.refs_3_.refs_1_, bf16[128,2048]{1,0:T(8,128)(2,1)} %collective-permute-done.1.refs_2_, ...), custom_call_target="tpu_custom_call" | custom-call | flops 8000000000 | bytes 1 | tf_op jit(solution)/shard_map/backward_heads/pallas_call | solution.py:191
  52.7 1.6 %collective-permute-start.14 = (bf16[64,2048]{1,0:T(8,128)(2,1)S(1)}, bf16[64,2048]{1,0:T(8,128)(2,1)S(1)}, u32[]{:S(2)}, u32[]{:S(2)}) collective-permute-start(bf16[64,2048]{1,0:T(8,128)(2,1)S(1)} %get-tuple-element.60.refs_6_), channel_id=1, source_target_pairs={{0,1},{1,0},{2,3},{3,2},{4,5},{5,4},{6,7},{7,6},{8,9},{9,8},{10,11... | collective-permute-start | bytes 786440 | tf_op jit(solution)/shard_map/gather_input_block3_row0/ppermute | solution.py:53
  54.2 0.5 collective-permute-start.15
  54.7 3.4 %backward_terms.1 = (f32[128,2048]{1,0:T(8,128)S(1)}, bf16[128,2048]{1,0:T(8,128)(2,1)S(1)}, bf16[128,2048]{1,0:T(8,128)(2,1)S(1)}, f32[64,2048]{1,0:T(8,128)S(1)}, f32[64,2048]{1,0:T(8,128)S(1)}) custom-call(bf16[512,512]{1,0:T(8,128)(2,1)S(1)} %get-tuple-element.55.refs_2_.refs_0_, bf16[512,512]{1,0:T(8,128)(2,1)S(1)} %get-tuple-element.56.refs_1_, ...), custom_call_target="tpu_custom_call" | custom-call | flops 3000000000 | bytes 1 | tf_op jit(solution)/shard_map/backward_terms/pallas_call | solution.py:191
  58.2 0.2 collective-permute-start.10
  58.4 1.9 %collective-permute-start.11 = (bf16[128,2048]{1,0:T(8,128)(2,1)S(1)}, bf16[128,2048]{1,0:T(8,128)(2,1)S(1)}, u32[]{:S(2)}, u32[]{:S(2)}) collective-permute-start(bf16[128,2048]{1,0:T(8,128)(2,1)S(1)} %get-tuple-element.67), channel_id=1, source_target_pairs={{0,2},{1,3},{2,0},{3,1},{4,6},{5,7},{6,4},{7,5},{8,10},{9,11},{10,... | collective-permute-start | bytes 1572872 | tf_op jit(solution)/shard_map/scatter_grad_block3_part1/ppermute | solution.py:53
  60.3 1.5 %collective-permute-done.14.refs_6_ = bf16[64,2048]{1,0:T(8,128)(2,1)S(1)} collective-permute-done((bf16[64,2048]{1,0:T(8,128)(2,1)S(1)}, bf16[64,2048]{1,0:T(8,128)(2,1)S(1)}, u32[]{:S(2)}, u32[]{:S(2)}) %collective-permute-start.14) | collective-permute-done | bytes 262176 | tf_op jit(solution)/shard_map/gather_input_block3_row0/ppermute | solution.py:53
  61.8 1.6 %collective-permute-done.15.refs_7_ = bf16[64,2048]{1,0:T(8,128)(2,1)S(1)} collective-permute-done((bf16[64,2048]{1,0:T(8,128)(2,1)S(1)}, bf16[64,2048]{1,0:T(8,128)(2,1)S(1)}, u32[]{:S(2)}, u32[]{:S(2)}) %collective-permute-start.15) | collective-permute-done | bytes 262176 | tf_op jit(solution)/shard_map/gather_input_block3_row64/ppermute | solution.py:53
  63.5 3.8 %project.3 = (bf16[512,512]{1,0:T(8,128)(2,1)S(1)}, bf16[512,512]{1,0:T(8,128)(2,1)S(1)}, bf16[512,512]{1,0:T(8,128)(2,1)S(1)}) custom-call(bf16[64,2048]{1,0:T(8,128)(2,1)S(1)} %get-tuple-element.58.refs_0_, bf16[64,2048]{1,0:T(8,128)(2,1)S(1)} %get-tuple-element.59.refs_1_, bf16[64,2048]{1,0:T(8,128)(2,1)S(1)} %collective-permute-done.12.refs_2_, ...), custom_call_target="tpu_custom_call" | custom-call | flops 5000000000 | bytes 1 | tf_op jit(solution)/shard_map/project/pallas_call | solution.py:191
  67.3 2.8 %forward_terms.1 = (bf16[128,2048]{1,0:T(8,128)(2,1)S(1)}, bf16[64,2048]{1,0:T(8,128)(2,1)S(1)}, bf16[64,2048]{1,0:T(8,128)(2,1)S(1)}, bf16[64,2048]{1,0:T(8,128...) custom-call(bf16[512,512]{1,0:T(8,128)(2,1)S(1)} %get-tuple-element.70.refs_0_, ...), custom_call_target="tpu_custom_call" | custom-call | flops 5000000000 | bytes 1 | tf_op jit(solution)/shard_map/forward_terms/pallas_call | solution.py:191
  70.2 1.5 %collective-permute-start.19 = (bf16[64,2048]{1,0:T(8,128)(2,1)S(1)}, bf16[64,2048]{1,0:T(8,128)(2,1)S(1)}, u32[]{:S(2)}, u32[]{:S(2)}) collective-permute-start(bf16[64,2048]{1,0:T(8,128)(2,1)S(1)} %get-tuple-element.77), channel_id=1, source_target_pairs={{0,5},{1,4},{2,7},{3,6},{4,9},{5,8},{6,11},{7,10},{8,13},{9,12},{1... | collective-permute-start | bytes 786440 | tf_op jit(solution)/shard_map/scatter_branch_block1_part0/ppermute | solution.py:63
  71.8 1.7 %collective-permute-start.16 = (bf16[64,2048]{1,0:T(8,128)(2,1)S(1)}, bf16[64,2048]{1,0:T(8,128)(2,1)S(1)}, u32[]{:S(2)}, u32[]{:S(2)}) collective-permute-start(bf16[64,2048]{1,0:T(8,128)(2,1)S(1)} %get-tuple-element.74.refs_3_), channel_id=1, source_target_pairs={{0,1},{1,0},{2,3},{3,2},{4,5},{5,4},{6,7},{7,6},{8,9},{9,8},{10,11... | collective-permute-start | bytes 786440 | tf_op jit(solution)/shard_map/scatter_grad_block1_part1/ppermute | solution.py:53
  73.5 1.6 %collective-permute-start.17 = (bf16[64,2048]{1,0:T(8,128)(2,1)S(1)}, bf16[64,2048]{1,0:T(8,128)(2,1)S(1)}, u32[]{:S(2)}, u32[]{:S(2)}) collective-permute-start(bf16[64,2048]{1,0:T(8,128)(2,1)S(1)} %get-tuple-element.75.refs_2_), channel_id=1, source_target_pairs={{0,2},{1,3},{2,0},{3,1},{4,6},{5,7},{6,4},{7,5},{8,10},{9,11},{10,... | collective-permute-start | bytes 786440 | tf_op jit(solution)/shard_map/scatter_grad_block2_part0/ppermute | solution.py:53
  75.2 0.5 collective-permute-start.22
  75.7 3.0 %collective-permute-done.18.refs_4_.refs_1_.refs_0_ = bf16[64,2048]{1,0:T(8,128)(2,1)S(1)} collective-permute-done((bf16[64,2048]{1,0:T(8,128)(2,1)S(1)}, bf16[64,2048]{1,0:T(8,128)(2,1)S(1)}, u32[]{:S(2)}, u32[]{:S(2)}) %collective-permute-start.18) | collective-permute-done | bytes 262176 | tf_op jit(solution)/shard_map/scatter_branch_block2_part1/ppermute | solution.py:63
  78.8 0.4 collective-permute-start.23
  79.2 0.9 collective-permute-done.19.refs_5_.refs_2_.refs_1_
  80.1 3.4 %collective-permute-start.21 = (bf16[128,2048]{1,0:T(8,128)(2,1)S(1)}, bf16[128,2048]{1,0:T(8,128)(2,1)S(1)}, u32[]{:S(2)}, u32[]{:S(2)}) collective-permute-start(bf16[128,2048]{1,0:T(8,128)(2,1)S(1)} %pick.11), channel_id=1, source_target_pairs={{0,4},{1,5},{2,6},{3,7},{4,8},{5,9},{6,10},{7,11},{8,12},{9,13},{1... | collective-permute-start | bytes 1572872 | tf_op jit(solution)/shard_map/ppermute | solution.py:63
  83.5 5.1 %collective-permute-done.16.refs_1_ = bf16[64,2048]{1,0:T(8,128)(2,1)S(1)} collective-permute-done((bf16[64,2048]{1,0:T(8,128)(2,1)S(1)}, bf16[64,2048]{1,0:T(8,128)(2,1)S(1)}, u32[]{:S(2)}, u32[]{:S(2)}) %collective-permute-start.16) | collective-permute-done | bytes 262176 | tf_op jit(solution)/shard_map/scatter_grad_block1_part1/ppermute | solution.py:53
  88.7 0.6 input_grad.1.refs_4_
  89.3 2.2 %collective-permute-done.22.refs_2_ = bf16[64,2048]{1,0:T(8,128)(2,1)S(1)} collective-permute-done((bf16[64,2048]{1,0:T(8,128)(2,1)S(1)}, bf16[64,2048]{1,0:T(8,128)(2,1)S(1)}, u32[]{:S(2)}, u32[]{:S(2)}) %collective-permute-start.22) | collective-permute-done | bytes 262176 | tf_op jit(solution)/shard_map/scatter_branch_block3_part0/ppermute | solution.py:53
  91.6 2.7 %collective-permute-start.25 = (bf16[64,2048]{1,0:T(8,128)(2,1)S(1)}, bf16[64,2048]{1,0:T(8,128)(2,1)S(1)}, u32[]{:S(2)}, u32[]{:S(2)}) collective-permute-start(bf16[64,2048]{1,0:T(8,128)(2,1)S(1)} %get-tuple-element.86), channel_id=1, source_target_pairs={{0,5},{1,4},{2,7},{3,6},{4,9},{5,8},{6,11},{7,10},{8,13},{9,12},{1... | collective-permute-start | bytes 786440 | tf_op jit(solution)/shard_map/scatter_branch_block1_part1/ppermute | solution.py:63
  94.3 2.9 %collective-permute-done.20.in_ref = bf16[128,2048]{1,0:T(8,128)(2,1)S(1)} collective-permute-done((bf16[128,2048]{1,0:T(8,128)(2,1)S(1)}, bf16[128,2048]{1,0:T(8,128)(2,1)S(1)}, u32[]{:S(2)}, u32[]{:S(2)}) %collective-permute-start.20) | collective-permute-done | bytes 524320 | tf_op jit(solution)/shard_map/ppermute | solution.py:69
  97.3 1.1 %widen.1 = (f32[1,128,2048]{2,1,0:T(8,128)}, f32[128,2048]{1,0:T(8,128)S(1)}) custom-call(bf16[128,2048]{1,0:T(8,128)(2,1)S(1)} %collective-permute-done.20.in_ref, bf16[128,2048]{1,0:T(8,128)(2,1)S(1)} %collective-permute-done.21.base_ref, bf16[64,2048]{1,0:T(8,128)(2,1)S(1)} %collective-permute-done.18.refs_4_.refs_1_.refs_0_, ...), custom_call_target="tpu_custom_call" | custom-call | flops 1 | bytes 1 | tf_op jit(solution)/shard_map/widen/pallas_call | solution.py:191
  98.3 4.2 %collective-permute-done.24.refs_0_ = bf16[64,2048]{1,0:T(8,128)(2,1)S(1)} collective-permute-done((bf16[64,2048]{1,0:T(8,128)(2,1)S(1)}, bf16[64,2048]{1,0:T(8,128)(2,1)S(1)}, u32[]{:S(2)}, u32[]{:S(2)}) %collective-permute-start.24) | collective-permute-done | bytes 262176 | tf_op jit(solution)/shard_map/scatter_branch_block2_part0/ppermute | solution.py:63
  102.6 1.5 %collective-permute-done.25.refs_1_ = bf16[64,2048]{1,0:T(8,128)(2,1)S(1)} collective-permute-done((bf16[64,2048]{1,0:T(8,128)(2,1)S(1)}, bf16[64,2048]{1,0:T(8,128)(2,1)S(1)}, u32[]{:S(2)}, u32[]{:S(2)}) %collective-permute-start.25) | collective-permute-done | bytes 262176 | tf_op jit(solution)/shard_map/scatter_branch_block1_part1/ppermute | solution.py:63
  104.1 1.1 %activation_sum.1 = f32[1,128,2048]{2,1,0:T(8,128)} custom-call(f32[128,2048]{1,0:T(8,128)S(1)} %get-tuple-element.82.base_ref, bf16[64,2048]{1,0:T(8,128)(2,1)S(1)} %collective-permute-done.24.refs_0_, bf16[64,2048]{1,0:T(8,128)(2,1)S(1)} %collective-permute-done.25.refs_1_), custom_call_target="tpu_custom_call" | custom-call | flops 8000000000 | bytes 1 | tf_op jit(solution)/shard_map/activation_sum/pallas_call | solution.py:191
  (60 shorter events, 1.5 us)
Async XLA Ops:
  0.6 10.6 %copy-start.13 = (f32[1,2048]{1,0:T(1,128)S(1)}, f32[1,2048]{1,0:T(1,128)}, u32[]{:S(2)}) copy-start(f32[1,2048]{1,0:T(1,128)} %gain_ref.1) | copy-start | bytes 24580
  2.9 16.0 %collective-permute-start.3 = (bf16[128,2048]{1,0:T(8,128)(2,1)}, bf16[128,2048]{1,0:T(8,128)(2,1)S(1)}, u32[]{:S(2)}, u32[]{:S(2)}) collective-permute-start(bf16[128,2048]{1,0:T(8,128)(2,1)} %get-tuple-element.45.refs_0_), channel_id=1, source_target_pairs={{0,1},{1,0},{2,3},{3,2},{4,5},{5,4},{6,7},{7,6},{8,9},{9,8},{10,11... | collective-permute-start | bytes 1572872 | tf_op jit(solution)/shard_map/gather_saved_block1/ppermute | solution.py:53
  5.9 15.1 %collective-permute-start.2 = (bf16[128,2048]{1,0:T(8,128)(2,1)}, bf16[128,2048]{1,0:T(8,128)(2,1)S(1)}, u32[]{:S(2)}, u32[]{:S(2)}) collective-permute-start(bf16[128,2048]{1,0:T(8,128)(2,1)} %get-tuple-element.45.refs_0_), channel_id=1, source_target_pairs={{0,2},{1,3},{2,0},{3,1},{4,6},{5,7},{6,4},{7,5},{8,10},{9,11},{10,... | collective-permute-start | bytes 1572872 | tf_op jit(solution)/shard_map/gather_saved_block2/ppermute | solution.py:53
  7.4 1.1 %copy-start.3 = (bf16[128,2048]{1,0:T(8,128)(2,1)S(1)}, bf16[128,2048]{1,0:T(8,128)(2,1)}, u32[]{:S(2)}) copy-start(bf16[128,2048]{1,0:T(8,128)(2,1)} %get-tuple-element.45.refs_0_) | copy-start | bytes 1572868
  8.5 1.2 %copy-start.7 = (f32[1,128,2048]{2,1,0:T(8,128)S(1)}, f32[1,128,2048]{2,1,0:T(8,128)}, u32[]{:S(2)}) copy-start(f32[1,128,2048]{2,1,0:T(8,128)} %param.10) | copy-start | bytes 3145732
  9.7 1.5 %copy-start.5 = (f32[1,128,2048]{2,1,0:T(8,128)S(1)}, f32[1,128,2048]{2,1,0:T(8,128)}, u32[]{:S(2)}) copy-start(f32[1,128,2048]{2,1,0:T(8,128)} %param.8) | copy-start | bytes 3145732
  10.6 21.7 %collective-permute-start.1 = (bf16[128,2048]{1,0:T(8,128)(2,1)}, bf16[128,2048]{1,0:T(8,128)(2,1)}, u32[]{:S(2)}, u32[]{:S(2)}) collective-permute-start(bf16[128,2048]{1,0:T(8,128)(2,1)} %cast.1.refs_2_.refs_0_), channel_id=1, source_target_pairs={{0,2},{1,3},{2,0},{3,1},{4,6},{5,7},{6,4},{7,5},{8,10},{9,11},{10,... | collective-permute-start | bytes 1572872 | tf_op jit(solution)/shard_map/gather_grad_block2/ppermute | solution.py:53
  11.1 21.2 %collective-permute-start = (bf16[128,2048]{1,0:T(8,128)(2,1)}, bf16[128,2048]{1,0:T(8,128)(2,1)}, u32[]{:S(2)}, u32[]{:S(2)}) collective-permute-start(bf16[128,2048]{1,0:T(8,128)(2,1)} %cast.1.refs_2_.refs_0_), channel_id=1, source_target_pairs={{0,1},{1,0},{2,3},{3,2},{4,5},{5,4},{6,7},{7,6},{8,9},{9,8},{10,11... | collective-permute-start | bytes 1572872 | tf_op jit(solution)/shard_map/gather_grad_block1/ppermute | solution.py:53
  11.2 28.7 %copy-start.2 = (bf16[1,2048,512]{2,1,0:T(8,128)(2,1)S(1)}, bf16[1,2048,512]{2,1,0:T(8,128)(2,1)}, u32[]{:S(2)}) copy-start(bf16[1,2048,512]{2,1,0:T(8,128)(2,1)} %param.14) | copy-start | bytes 6291460
  12.1 0.7 copy-start.10
  21.0 19.0 %copy-start.4 = (bf16[128,2048]{1,0:T(8,128)(2,1)S(1)}, bf16[128,2048]{1,0:T(8,128)(2,1)}, u32[]{:S(2)}) copy-start(bf16[128,2048]{1,0:T(8,128)(2,1)} %get-tuple-element.45.refs_0_) | copy-start | bytes 1572868
  21.0 16.9 %collective-permute-start.6 = (bf16[64,2048]{1,0:T(8,128)(2,1)S(1)}, bf16[64,2048]{1,0:T(8,128)(2,1)S(1)}, u32[]{:S(2)}, u32[]{:S(2)}) collective-permute-start(bf16[64,2048]{1,0:T(8,128)(2,1)S(1)} %get-tuple-element.48.refs_4_), channel_id=1, source_target_pairs={{0,1},{1,0},{2,3},{3,2},{4,5},{5,4},{6,7},{7,6},{8,9},{9,8},{10,11... | collective-permute-start | bytes 786440 | tf_op jit(solution)/shard_map/gather_saved_block3_row0/ppermute | solution.py:53
  21.2 18.8 %collective-permute-start.7 = (bf16[64,2048]{1,0:T(8,128)(2,1)S(1)}, bf16[64,2048]{1,0:T(8,128)(2,1)S(1)}, u32[]{:S(2)}, u32[]{:S(2)}) collective-permute-start(bf16[64,2048]{1,0:T(8,128)(2,1)S(1)} %get-tuple-element.49.refs_5_), channel_id=1, source_target_pairs={{0,2},{1,3},{2,0},{3,1},{4,6},{5,7},{6,4},{7,5},{8,10},{9,11},{10,... | collective-permute-start | bytes 786440 | tf_op jit(solution)/shard_map/gather_saved_block3_row64/ppermute | solution.py:53
  32.3 1.0 copy-start.11
  33.3 6.7 %copy-start = (bf16[1,2048,512]{2,1,0:T(8,128)(2,1)S(1)}, bf16[1,2048,512]{2,1,0:T(8,128)(2,1)}, u32[]{:S(2)}) copy-start(bf16[1,2048,512]{2,1,0:T(8,128)(2,1)} %param.12) | copy-start | bytes 6291460
  33.3 6.7 %copy-start.1 = (bf16[1,2048,512]{2,1,0:T(8,128)(2,1)S(1)}, bf16[1,2048,512]{2,1,0:T(8,128)(2,1)}, u32[]{:S(2)}) copy-start(bf16[1,2048,512]{2,1,0:T(8,128)(2,1)} %param.13) | copy-start | bytes 6291460
  34.5 9.3 %collective-permute-start.4 = (bf16[64,2048]{1,0:T(8,128)(2,1)S(1)}, bf16[64,2048]{1,0:T(8,128)(2,1)S(1)}, u32[]{:S(2)}, u32[]{:S(2)}) collective-permute-start(bf16[64,2048]{1,0:T(8,128)(2,1)S(1)} %get-tuple-element.50), channel_id=1, source_target_pairs={{0,1},{1,0},{2,3},{3,2},{4,5},{5,4},{6,7},{7,6},{8,9},{9,8},{10,11... | collective-permute-start | bytes 786440 | tf_op jit(solution)/shard_map/gather_grad_block3_row0/ppermute | solution.py:53
  34.7 11.1 %collective-permute-start.5 = (bf16[64,2048]{1,0:T(8,128)(2,1)S(1)}, bf16[64,2048]{1,0:T(8,128)(2,1)S(1)}, u32[]{:S(2)}, u32[]{:S(2)}) collective-permute-start(bf16[64,2048]{1,0:T(8,128)(2,1)S(1)} %get-tuple-element.51), channel_id=1, source_target_pairs={{0,2},{1,3},{2,0},{3,1},{4,6},{5,7},{6,4},{7,5},{8,10},{9,11},{10,... | collective-permute-start | bytes 786440 | tf_op jit(solution)/shard_map/gather_grad_block3_row64/ppermute | solution.py:53
  37.8 14.7 %collective-permute-start.8 = (bf16[64,2048]{1,0:T(8,128)(2,1)S(1)}, bf16[64,2048]{1,0:T(8,128)(2,1)S(1)}, u32[]{:S(2)}, u32[]{:S(2)}) collective-permute-start(bf16[64,2048]{1,0:T(8,128)(2,1)S(1)} %get-tuple-element.58.refs_0_), channel_id=1, source_target_pairs={{0,2},{1,3},{2,0},{3,1},{4,6},{5,7},{6,4},{7,5},{8,10},{9,11},{10,... | collective-permute-start | bytes 786440 | tf_op jit(solution)/shard_map/gather_input_block2_first0/ppermute | solution.py:53
  38.0 14.6 %collective-permute-start.9 = (bf16[64,2048]{1,0:T(8,128)(2,1)S(1)}, bf16[64,2048]{1,0:T(8,128)(2,1)S(1)}, u32[]{:S(2)}, u32[]{:S(2)}) collective-permute-start(bf16[64,2048]{1,0:T(8,128)(2,1)S(1)} %get-tuple-element.59.refs_1_), channel_id=1, source_target_pairs={{0,1},{1,0},{2,3},{3,2},{4,5},{5,4},{6,7},{7,6},{8,9},{9,8},{10,11... | collective-permute-start | bytes 786440 | tf_op jit(solution)/shard_map/gather_input_block1_first64/ppermute | solution.py:53
  39.9 3.6 %copy-start.12 = (bf16[64,2048]{1,0:T(8,128)(2,1)S(1)}, bf16[64,2048]{1,0:T(8,128)(2,1)}, u32[]{:S(2)}) copy-start(bf16[64,2048]{1,0:T(8,128)(2,1)} %copy-done.10) | copy-start | bytes 786436
  40.0 5.8 %copy-start.14 = (bf16[1,2048,512]{2,1,0:T(8,128)(2,1)S(1)}, bf16[1,2048,512]{2,1,0:T(8,128)(2,1)}, u32[]{:S(2)}) copy-start(bf16[1,2048,512]{2,1,0:T(8,128)(2,1)} %param.15) | copy-start | bytes 6291460
  43.7 14.7 %collective-permute-start.12 = (bf16[64,2048]{1,0:T(8,128)(2,1)S(1)}, bf16[64,2048]{1,0:T(8,128)(2,1)S(1)}, u32[]{:S(2)}, u32[]{:S(2)}) collective-permute-start(bf16[64,2048]{1,0:T(8,128)(2,1)S(1)} %get-tuple-element.68), channel_id=1, source_target_pairs={{0,1},{1,0},{2,3},{3,2},{4,5},{5,4},{6,7},{7,6},{8,9},{9,8},{10,11... | collective-permute-start | bytes 786440 | tf_op jit(solution)/shard_map/gather_input_block1_first0/ppermute | solution.py:53
  43.8 16.5 %collective-permute-start.13 = (bf16[64,2048]{1,0:T(8,128)(2,1)S(1)}, bf16[64,2048]{1,0:T(8,128)(2,1)S(1)}, u32[]{:S(2)}, u32[]{:S(2)}) collective-permute-start(bf16[64,2048]{1,0:T(8,128)(2,1)S(1)} %get-tuple-element.69), channel_id=1, source_target_pairs={{0,2},{1,3},{2,0},{3,1},{4,6},{5,7},{6,4},{7,5},{8,10},{9,11},{10,... | collective-permute-start | bytes 786440 | tf_op jit(solution)/shard_map/gather_input_block2_first64/ppermute | solution.py:53
  52.7 9.2 %collective-permute-start.14 = (bf16[64,2048]{1,0:T(8,128)(2,1)S(1)}, bf16[64,2048]{1,0:T(8,128)(2,1)S(1)}, u32[]{:S(2)}, u32[]{:S(2)}) collective-permute-start(bf16[64,2048]{1,0:T(8,128)(2,1)S(1)} %get-tuple-element.60.refs_6_), channel_id=1, source_target_pairs={{0,1},{1,0},{2,3},{3,2},{4,5},{5,4},{6,7},{7,6},{8,9},{9,8},{10,11... | collective-permute-start | bytes 786440 | tf_op jit(solution)/shard_map/gather_input_block3_row0/ppermute | solution.py:53
  54.2 9.2 %collective-permute-start.15 = (bf16[64,2048]{1,0:T(8,128)(2,1)S(1)}, bf16[64,2048]{1,0:T(8,128)(2,1)S(1)}, u32[]{:S(2)}, u32[]{:S(2)}) collective-permute-start(bf16[64,2048]{1,0:T(8,128)(2,1)S(1)} %get-tuple-element.61.refs_7_), channel_id=1, source_target_pairs={{0,2},{1,3},{2,0},{3,1},{4,6},{5,7},{6,4},{7,5},{8,10},{9,11},{10,... | collective-permute-start | bytes 786440 | tf_op jit(solution)/shard_map/gather_input_block3_row64/ppermute | solution.py:53
  58.2 13.5 %collective-permute-start.10 = (bf16[128,2048]{1,0:T(8,128)(2,1)S(1)}, bf16[128,2048]{1,0:T(8,128)(2,1)S(1)}, u32[]{:S(2)}, u32[]{:S(2)}) collective-permute-start(bf16[128,2048]{1,0:T(8,128)(2,1)S(1)} %get-tuple-element.64), channel_id=1, source_target_pairs={{0,1},{1,0},{2,3},{3,2},{4,5},{5,4},{6,7},{7,6},{8,9},{9,8},{10,11... | collective-permute-start | bytes 1572872 | tf_op jit(solution)/shard_map/scatter_grad_block3_part0/ppermute | solution.py:53
  58.4 8.9 %copy-start.6 = (f32[1,128,2048]{2,1,0:T(8,128)S(1)}, f32[1,128,2048]{2,1,0:T(8,128)}, u32[]{:S(2)}) copy-start(f32[1,128,2048]{2,1,0:T(8,128)} %param.8) | copy-start | bytes 3145732
  58.4 13.3 %collective-permute-start.11 = (bf16[128,2048]{1,0:T(8,128)(2,1)S(1)}, bf16[128,2048]{1,0:T(8,128)(2,1)S(1)}, u32[]{:S(2)}, u32[]{:S(2)}) collective-permute-start(bf16[128,2048]{1,0:T(8,128)(2,1)S(1)} %get-tuple-element.67), channel_id=1, source_target_pairs={{0,2},{1,3},{2,0},{3,1},{4,6},{5,7},{6,4},{7,5},{8,10},{9,11},{10,... | collective-permute-start | bytes 1572872 | tf_op jit(solution)/shard_map/scatter_grad_block3_part1/ppermute | solution.py:53
  70.1 8.7 %collective-permute-start.18 = (bf16[64,2048]{1,0:T(8,128)(2,1)S(1)}, bf16[64,2048]{1,0:T(8,128)(2,1)S(1)}, u32[]{:S(2)}, u32[]{:S(2)}) collective-permute-start(bf16[64,2048]{1,0:T(8,128)(2,1)S(1)} %get-tuple-element.76), channel_id=1, source_target_pairs={{0,6},{1,7},{2,4},{3,5},{4,10},{5,11},{6,8},{7,9},{8,14},{9,15},{1... | collective-permute-start | bytes 786440 | tf_op jit(solution)/shard_map/scatter_branch_block2_part1/ppermute | solution.py:63
  70.2 9.8 %collective-permute-start.19 = (bf16[64,2048]{1,0:T(8,128)(2,1)S(1)}, bf16[64,2048]{1,0:T(8,128)(2,1)S(1)}, u32[]{:S(2)}, u32[]{:S(2)}) collective-permute-start(bf16[64,2048]{1,0:T(8,128)(2,1)S(1)} %get-tuple-element.77), channel_id=1, source_target_pairs={{0,5},{1,4},{2,7},{3,6},{4,9},{5,8},{6,11},{7,10},{8,13},{9,12},{1... | collective-permute-start | bytes 786440 | tf_op jit(solution)/shard_map/scatter_branch_block1_part0/ppermute | solution.py:63
  71.7 16.9 %copy-start.8 = (f32[1,128,2048]{2,1,0:T(8,128)S(1)}, f32[1,128,2048]{2,1,0:T(8,128)}, u32[]{:S(2)}) copy-start(f32[1,128,2048]{2,1,0:T(8,128)} %param.10) | copy-start | bytes 3145732
  71.7 16.9 %copy-start.9 = (f32[1,128,2048]{2,1,0:T(8,128)S(1)}, f32[1,128,2048]{2,1,0:T(8,128)}, u32[]{:S(2)}) copy-start(f32[1,128,2048]{2,1,0:T(8,128)} %param.9) | copy-start | bytes 3145732
  71.8 16.9 %copy-start.15 = (f32[128,1]{1,0:T(8,128)S(1)}, f32[128,1]{1,0:T(8,128)}, u32[]{:S(2)}) copy-start(f32[128,1]{1,0:T(8,128)} %get-tuple-element.63.inv_ref) | copy-start | bytes 1540
  71.8 16.9 %collective-permute-start.16 = (bf16[64,2048]{1,0:T(8,128)(2,1)S(1)}, bf16[64,2048]{1,0:T(8,128)(2,1)S(1)}, u32[]{:S(2)}, u32[]{:S(2)}) collective-permute-start(bf16[64,2048]{1,0:T(8,128)(2,1)S(1)} %get-tuple-element.74.refs_3_), channel_id=1, source_target_pairs={{0,1},{1,0},{2,3},{3,2},{4,5},{5,4},{6,7},{7,6},{8,9},{9,8},{10,11... | collective-permute-start | bytes 786440 | tf_op jit(solution)/shard_map/scatter_grad_block1_part1/ppermute | solution.py:53
  73.5 15.1 %collective-permute-start.17 = (bf16[64,2048]{1,0:T(8,128)(2,1)S(1)}, bf16[64,2048]{1,0:T(8,128)(2,1)S(1)}, u32[]{:S(2)}, u32[]{:S(2)}) collective-permute-start(bf16[64,2048]{1,0:T(8,128)(2,1)S(1)} %get-tuple-element.75.refs_2_), channel_id=1, source_target_pairs={{0,2},{1,3},{2,0},{3,1},{4,6},{5,7},{6,4},{7,5},{8,10},{9,11},{10,... | collective-permute-start | bytes 786440 | tf_op jit(solution)/shard_map/scatter_grad_block2_part0/ppermute | solution.py:53
  75.2 16.2 %collective-permute-start.22 = (bf16[64,2048]{1,0:T(8,128)(2,1)S(1)}, bf16[64,2048]{1,0:T(8,128)(2,1)S(1)}, u32[]{:S(2)}, u32[]{:S(2)}) collective-permute-start(bf16[64,2048]{1,0:T(8,128)(2,1)S(1)} %get-tuple-element.80.refs_3_), channel_id=1, source_target_pairs={{0,1},{1,0},{2,3},{3,2},{4,5},{5,4},{6,7},{7,6},{8,9},{9,8},{10,11... | collective-permute-start | bytes 786440 | tf_op jit(solution)/shard_map/scatter_branch_block3_part0/ppermute | solution.py:53
  78.8 12.7 %collective-permute-start.23 = (bf16[64,2048]{1,0:T(8,128)(2,1)S(1)}, bf16[64,2048]{1,0:T(8,128)(2,1)S(1)}, u32[]{:S(2)}, u32[]{:S(2)}) collective-permute-start(bf16[64,2048]{1,0:T(8,128)(2,1)S(1)} %get-tuple-element.81.refs_4_), channel_id=1, source_target_pairs={{0,2},{1,3},{2,0},{3,1},{4,6},{5,7},{6,4},{7,5},{8,10},{9,11},{10,... | collective-permute-start | bytes 786440 | tf_op jit(solution)/shard_map/scatter_branch_block3_part1/ppermute | solution.py:53
  80.1 14.2 %collective-permute-start.21 = (bf16[128,2048]{1,0:T(8,128)(2,1)S(1)}, bf16[128,2048]{1,0:T(8,128)(2,1)S(1)}, u32[]{:S(2)}, u32[]{:S(2)}) collective-permute-start(bf16[128,2048]{1,0:T(8,128)(2,1)S(1)} %pick.11), channel_id=1, source_target_pairs={{0,4},{1,5},{2,6},{3,7},{4,8},{5,9},{6,10},{7,11},{8,12},{9,13},{1... | collective-permute-start | bytes 1572872 | tf_op jit(solution)/shard_map/ppermute | solution.py:63
  89.2 8.0 %collective-permute-start.20 = (bf16[128,2048]{1,0:T(8,128)(2,1)S(1)}, bf16[128,2048]{1,0:T(8,128)(2,1)S(1)}, u32[]{:S(2)}, u32[]{:S(2)}) collective-permute-start(bf16[128,2048]{1,0:T(8,128)(2,1)S(1)} %input_grad.1.refs_4_), channel_id=1, source_target_pairs={{0,28},{4,0},{8,4},{12,8},{16,12},{20,16},{24,20},{28,24},{1,29},{... | collective-permute-start | bytes 1572872 | tf_op jit(solution)/shard_map/ppermute | solution.py:69
  91.5 11.0 %collective-permute-start.24 = (bf16[64,2048]{1,0:T(8,128)(2,1)S(1)}, bf16[64,2048]{1,0:T(8,128)(2,1)S(1)}, u32[]{:S(2)}, u32[]{:S(2)}) collective-permute-start(bf16[64,2048]{1,0:T(8,128)(2,1)S(1)} %get-tuple-element.85), channel_id=1, source_target_pairs={{0,6},{1,7},{2,4},{3,5},{4,10},{5,11},{6,8},{7,9},{8,14},{9,15},{1... | collective-permute-start | bytes 786440 | tf_op jit(solution)/shard_map/scatter_branch_block2_part0/ppermute | solution.py:63
  91.6 12.5 %collective-permute-start.25 = (bf16[64,2048]{1,0:T(8,128)(2,1)S(1)}, bf16[64,2048]{1,0:T(8,128)(2,1)S(1)}, u32[]{:S(2)}, u32[]{:S(2)}) collective-permute-start(bf16[64,2048]{1,0:T(8,128)(2,1)S(1)} %get-tuple-element.86), channel_id=1, source_target_pairs={{0,5},{1,4},{2,7},{3,6},{4,9},{5,8},{6,11},{7,10},{8,13},{9,12},{1... | collective-permute-start | bytes 786440 | tf_op jit(solution)/shard_map/scatter_branch_block1_part1/ppermute | solution.py:63

commit v6 on v5

--- a/solution.py
+++ b/solution.py
@@ -135,12 +135,17 @@
         for part in parts
         if len(bits_of(rel)) > 1
     }
-    keys = [(rel, part) for rel in reversed(by_distance(count)) for part in parts]
-    groups = {}
-    for key in keys:
-        if key not in later:
-            groups.setdefault(last_bit(*key) if joined else key, []).append(key)
-    return list(groups.values()), [key for key in keys if key in later]
+    groups, waiting = {}, {}
+    for rel in reversed(by_distance(count)):
+        for part in parts:
+            key = (rel, part)
+            if not joined and len(bits_of(rel)) == 1:
+                waiting.setdefault(rel, []).append(key)
+            elif key in later:
+                waiting[key] = [key]
+            else:
+                groups.setdefault(last_bit(*key) if joined else key, []).append(key)
+    return list(groups.values()), list(waiting.values())
 
 
 class Scatter:
@@ -150,7 +155,7 @@
         self.bounds = part_bounds(rows, count)
         self.groups, waiting = messages_of(rows, count, joined)
         self.leaving = list(terms[: len(self.groups)])
-        self.waiting = dict(zip(waiting, terms[len(self.groups) :]))
+        self.waiting = list(zip(waiting, terms[len(self.groups) :]))
         self.send_last, self.what = send_last, what
         self.arrived, self.final = {}, {}
 
@@ -168,22 +173,23 @@
                 self.final[key] = (moved, first)
             first += self.bounds[key[1]][1] - self.bounds[key[1]][0]
 
-    def onward(self):
-        return [i for i, keys in enumerate(self.groups) if len(bits_of(keys[0][0])) > 1]
-
-    def send_groups(self, places):
-        for i in places:
-            self.send(self.leaving[i], self.groups[i])
+    def send_groups(self):
+        for value, keys in zip(self.leaving, self.groups):
+            self.send(value, keys)
 
     def send_sums(self, after=()):
         sums = []
-        for level in sorted({len(bits_of(rel)) for rel, _ in self.waiting}, reverse=True):
-            keys = [key for key in self.waiting if len(bits_of(key[0])) == level]
-            totals = [(self.waiting[key], self.arrived[key]) for key in keys]
-            results = sum_rows(totals, after)
+        height = self.bounds[0][1] - self.bounds[0][0]
+        levels = {len(bits_of(keys[0][0])) for keys, _ in self.waiting}
+        for level in sorted(levels, reverse=True):
+            found = [pair for pair in self.waiting if len(bits_of(pair[0][0][0])) == level]
+            totals = [
+                (term, [self.arrived.get(key, []) for key in keys]) for keys, term in found
+            ]
+            results = sum_rows(totals, height, after)
             sums += results
-            for key, value in zip(keys, results):
-                self.send(value, [key])
+            for (keys, _), value in zip(found, results):
+                self.send(value, keys)
         return sums
 
 
@@ -281,18 +287,20 @@
     )[0]
 
 
-def sum_rows(totals, after=()):
-    pieces = [piece for _, pieces in totals for piece in pieces]
+def sum_rows(totals, height, after=()):
+    pieces = [piece for _, parts in totals for moved in parts for piece in moved]
     n, m = len(totals), len(pieces)
 
     def kernel(*refs):
         arrivals, outs = list(refs[n : n + m]), refs[-n:]
-        for (term, moved), term_ref, out_ref in zip(totals, refs, outs):
-            total = term_ref[...]
-            for _, first in moved:
-                ref = arrivals.pop(0)
-                total = total + ref[first : first + term.shape[0], :].astype(jnp.float32)
-            out_ref[...] = total.astype(jnp.bfloat16)
+        for (_, parts), term_ref, out_ref in zip(totals, refs, outs):
+            for i, moved in enumerate(parts):
+                here = slice(i * height, (i + 1) * height)
+                total = term_ref[here, :]
+                for _, first in moved:
+                    ref = arrivals.pop(0)
+                    total = total + ref[first : first + height, :].astype(jnp.float32)
+                out_ref[here, :] = total.astype(jnp.bfloat16)
 
     return call(
         kernel,
@@ -371,14 +379,14 @@
         return jax.ShapeDtypeStruct((height, width), dtype)
 
     return [shape(keys, jnp.bfloat16) for keys in groups] + [
-        shape([key], jnp.float32) for key in waiting
+        shape(keys, jnp.float32) for keys in waiting
     ]
 
 
 def store_terms(values, low, refs, rows, count, joined):
     bounds = part_bounds(rows, count)
     groups, waiting = messages_of(rows, count, joined)
-    for ref, keys in zip(refs, groups + [[key] for key in waiting]):
+    for ref, keys in zip(refs, groups + waiting):
         at = 0
         for rel, part in keys:
             first, last = bounds[part]
@@ -581,24 +589,17 @@
     )[0]
 
 
-def widened(values, base, pieces, bounds):
-    def kernel(in_ref, base_ref, *refs):
-        out_ref, sum_ref = refs[-2:]
-        out_ref[0] = in_ref[...].astype(jnp.float32)
-        for part, (low, high) in enumerate(bounds):
-            total = base_ref[low:high, :].astype(jnp.float32)
-            sum_ref[low:high, :] = added_pieces(total, pieces, refs, part, high - low)
-
-    return call(
-        kernel,
-        [
-            jax.ShapeDtypeStruct((1, *values.shape), jnp.float32),
-            jax.ShapeDtypeStruct(base.shape, jnp.float32),
-        ],
-        [values, base] + [value for value, _ in pieces.values()],
-        [VMEM] * (2 + len(pieces)),
+def widened(values, after=()):
+    def kernel(in_ref, *refs):
+        refs[-1][0] = in_ref[...].astype(jnp.float32)
+
+    return call(
+        kernel,
+        [jax.ShapeDtypeStruct((1, *values.shape), jnp.float32)],
+        [values, *after],
+        [VMEM] + [ANY] * len(after),
         name="widen",
-    )
+    )[0]
 
 
 def rope_tables(positions):
@@ -648,32 +649,16 @@
     front = Scatter(
         terms, rows, False, lambda value, bit: across_and_on(value, 1 << bit), "branch"
     )
-    back.send_groups(range(len(back.groups)))
-    onward = front.onward()
-    front.send_groups([i for i in range(len(front.groups)) if i not in onward])
-    soon = dict(front.final)
-    ready = [value for value, _ in soon.values()]
-    sums = back.send_sums([terms[0]])
-    held = picked_rows([(front.leaving[i], 0, front.leaving[i].shape[0]) for i in onward], sums)
-    for i, value in zip(onward, held):
-        front.leaving[i] = value
-    front.send_groups(onward)
-    (own,) = picked_rows([(own, 0, rows)], [*ready, *held])
+    back.send_groups()
+    front.send_groups()
     own = across_and_on(own, 0)
+    d_sums = back.send_sums([terms[0]])
+    sums = front.send_sums(d_sums)
     d_input = input_grad(
-        d_own,
-        back.final,
-        saved_in,
-        grad,
-        inv_bwd,
-        gain,
-        bounds,
-        ready,
-    )
-    front.send_sums([d_input])
-    grad_prev, base = widened(passed_along(d_input, "pipe", -1), own, soon, bounds)
-    last = {key: piece for key, piece in front.final.items() if key not in soon}
-    return (activation_sum(base, last, bounds), grad_prev)
+        d_own, back.final, saved_in, grad, inv_bwd, gain, bounds, [own, *sums]
+    )
+    act_next = activation_sum(own, front.final, bounds)
+    return (act_next, widened(passed_along(d_input, "pipe", -1), [act_next]))
 
 
 def solution(mesh):

time: 105 us -> 104 us (level)
  the two profiles are of different devices: /device:TPU:0 before, /device:TPU:1 now
where the time goes in v6:
time: 104 us
  waiting for transfers between devices  39.3 us (38%)
  Pallas kernels  28.8 us (28%)
  starting transfers between devices  28.3 us (27%)
  local copies, waits for them, and re-layouts  5.45 us (5%)
  other arithmetic  1.28 us (1%)
    ppermute x20, waiting for transfers between devices, across(): return lax.ppermute(value, 'seq', [(i, i ^ 1 << bit) for i in range(count)])  30.2 us
    pallas_call x17, Pallas kernels, call(): pl.pallas_call(kernel, out_shape=out_shapes, in_specs=in_specs, out_specs...  28.8 us
    ppermute x20, starting transfers between devices, across(): return lax.ppermute(value, 'seq', [(i, i ^ 1 << bit) for i in range(count)])  16.1 us
    ppermute x3, starting transfers between devices, across_and_on(): return lax.ppermute(value, ('pipe', 'seq'), pairs)  12.2 us
    ppermute x3, waiting for transfers between devices, across_and_on(): return lax.ppermute(value, ('pipe', 'seq'), pairs)  7.68 us
    unnamed x34, local copies, waits for them, and re-layouts  5.45 us
  transfers between devices with their start and end apart: 24, of which 11 were waited for; matrix products, arithmetic and copies ran while one was open for 1% of the time, Pallas kernels for 25%

profile of v6, /device:TPU:1, one launch (start us, length us, event | category | flops | bytes accessed | tf_op | source)
XLA Modules:
  0.0 104.1 jit_solution(11845932203845959115)
XLA Ops:
  0.6 2.3 %norm.3 = (bf16[128,2048]{1,0:T(8,128)(2,1)}, f32[128,1]{1,0:T(8,128)}) custom-call(f32[128,2048]{1,0:T(8,128)} %bitcast.22, f32[1,2048]{1,0:T(1,128)} %gain_ref.1), custom_call_target="tpu_custom_call" | custom-call | flops 1 | bytes 1 | tf_op jit(solution)/shard_map/norm/pallas_call | solution.py:197
  2.9 2.1 %collective-permute-start.3 = (bf16[128,2048]{1,0:T(8,128)(2,1)}, bf16[128,2048]{1,0:T(8,128)(2,1)S(1)}, u32[]{:S(2)}, u32[]{:S(2)}) collective-permute-start(bf16[128,2048]{1,0:T(8,128)(2,1)} %get-tuple-element.41.refs_0_), channel_id=1, source_target_pairs={{0,1},{1,0},{2,3},{3,2},{4,5},{5,4},{6,7},{7,6},{8,9},{9,8},{10,11... | collective-permute-start | bytes 1572872 | tf_op jit(solution)/shard_map/gather_saved_block1/ppermute | solution.py:53
  5.0 1.2 %collective-permute-start.2 = (bf16[128,2048]{1,0:T(8,128)(2,1)}, bf16[128,2048]{1,0:T(8,128)(2,1)S(1)}, u32[]{:S(2)}, u32[]{:S(2)}) collective-permute-start(bf16[128,2048]{1,0:T(8,128)(2,1)} %get-tuple-element.41.refs_0_), channel_id=1, source_target_pairs={{0,2},{1,3},{2,0},{3,1},{4,6},{5,7},{6,4},{7,5},{8,10},{9,11},{10,... | collective-permute-start | bytes 1572872 | tf_op jit(solution)/shard_map/gather_saved_block2/ppermute | solution.py:53
  6.3 1.1 %copy-done.3 = bf16[128,2048]{1,0:T(8,128)(2,1)S(1)} copy-done((bf16[128,2048]{1,0:T(8,128)(2,1)S(1)}, bf16[128,2048]{1,0:T(8,128)(2,1)}, u32[]{:S(2)}) %copy-start.3) | copy-done | bytes 524312
  7.3 1.2 %copy-done.7 = f32[1,128,2048]{2,1,0:T(8,128)S(1)} copy-done((f32[1,128,2048]{2,1,0:T(8,128)S(1)}, f32[1,128,2048]{2,1,0:T(8,128)}, u32[]{:S(2)}) %copy-start.7) | copy-done | bytes 1048600
  8.6 0.8 cast.1.refs_2_.refs_0_
  9.4 0.3 collective-permute-start.1
  9.7 0.2 copy-done.5
  10.0 0.9 norm.2
  10.9 0.7 copy-done.11
  11.7 5.2 %collective-permute-done.3.refs_1_ = bf16[128,2048]{1,0:T(8,128)(2,1)S(1)} collective-permute-done((bf16[128,2048]{1,0:T(8,128)(2,1)}, bf16[128,2048]{1,0:T(8,128)(2,1)S(1)}, u32[]{:S(2)}, u32[]{:S(2)}) %collective-permute-start.3) | collective-permute-done | bytes 524320 | tf_op jit(solution)/shard_map/gather_saved_block1/ppermute | solution.py:53
  16.9 0.8 collective-permute-done.2.refs_0_.refs_2_
  17.8 0.5 collective-permute-start.4
  18.2 1.1 %collective-permute-start.5 = (bf16[64,2048]{1,0:T(8,128)(2,1)S(1)}, bf16[64,2048]{1,0:T(8,128)(2,1)S(1)}, u32[]{:S(2)}, u32[]{:S(2)}) collective-permute-start(bf16[64,2048]{1,0:T(8,128)(2,1)S(1)} %get-tuple-element.43.refs_5_), channel_id=1, source_target_pairs={{0,2},{1,3},{2,0},{3,1},{4,6},{5,7},{6,4},{7,5},{8,10},{9,11},{10,... | collective-permute-start | bytes 786440 | tf_op jit(solution)/shard_map/gather_saved_block3_row64/ppermute | solution.py:53
  19.4 8.8 %collective-permute-done.1.refs_3_.refs_1_ = bf16[128,2048]{1,0:T(8,128)(2,1)} collective-permute-done((bf16[128,2048]{1,0:T(8,128)(2,1)}, bf16[128,2048]{1,0:T(8,128)(2,1)}, u32[]{:S(2)}, u32[]{:S(2)}) %collective-permute-start.1) | collective-permute-done | bytes 524320 | tf_op jit(solution)/shard_map/gather_grad_block1/ppermute | solution.py:53
  28.2 0.8 collective-permute-done.refs_2_
  29.0 0.9 copy-done.12
  30.0 1.2 %pick.5 = (bf16[64,2048]{1,0:T(8,128)(2,1)S(1)}, bf16[64,2048]{1,0:T(8,128)(2,1)S(1)}, bf16[64,2048]{1,0:T(8,128)(2,1)S(1)}, bf16[64,2048]{1,0:T(8,128)(2,1)S(1)}) custom-call(bf16[64,2048]{1,0:T(8,128)(2,1)S(1)} %get-tuple-element.39.refs_0_, bf16[64,2048]{1,0:T(8,128)(2,1)S(1)} %copy-done.12, bf16[128,2048]{1,0:T(8,128)(2,1)} %collective-permute-done.refs_2_, ...), custom_call_target="tpu_custom_call" | custom-call | flops 1 | bytes 1 | tf_op jit(solution)/shard_map/pick/pallas_call | solution.py:197
  31.2 0.5 collective-permute-start.10
  31.7 1.1 %collective-permute-start.11 = (bf16[64,2048]{1,0:T(8,128)(2,1)S(1)}, bf16[64,2048]{1,0:T(8,128)(2,1)S(1)}, u32[]{:S(2)}, u32[]{:S(2)}) collective-permute-start(bf16[64,2048]{1,0:T(8,128)(2,1)S(1)} %get-tuple-element.50), channel_id=1, source_target_pairs={{0,2},{1,3},{2,0},{3,1},{4,6},{5,7},{6,4},{7,5},{8,10},{9,11},{10,... | collective-permute-start | bytes 786440 | tf_op jit(solution)/shard_map/gather_grad_block3_row64/ppermute | solution.py:53
  32.9 1.0 fusion
  34.1 0.4 collective-permute-start.8
  34.5 1.0 %collective-permute-start.7 = (bf16[64,2048]{1,0:T(8,128)(2,1)S(1)}, bf16[64,2048]{1,0:T(8,128)(2,1)S(1)}, u32[]{:S(2)}, u32[]{:S(2)}) collective-permute-start(bf16[64,2048]{1,0:T(8,128)(2,1)S(1)} %get-tuple-element.45.refs_1_), channel_id=1, source_target_pairs={{0,1},{1,0},{2,3},{3,2},{4,5},{5,4},{6,7},{7,6},{8,9},{9,8},{10,11... | collective-permute-start | bytes 786440 | tf_op jit(solution)/shard_map/gather_input_block1_first64/ppermute | solution.py:53
  35.6 3.6 %project.2 = (bf16[512,512]{1,0:T(8,128)(2,1)S(1)}, bf16[512,512]{1,0:T(8,128)(2,1)S(1)}, bf16[512,512]{1,0:T(8,128)(2,1)S(1)}) custom-call(bf16[128,2048]{1,0:T(8,128)(2,1)S(1)} %copy-done.4, bf16[128,2048]{1,0:T(8,128)(2,1)S(1)} %collective-permute-done.3.refs_1_, bf16[128,2048]{1,0:T(8,128)(2,1)S(1)} %collective-permute-done.2.refs_0_.refs_2_, ...), custom_call_target="tpu_custom_call" | custom-call | flops 1 | bytes 1 | tf_op jit(solution)/shard_map/project/pallas_call | solution.py:197
  39.3 0.5 collective-permute-start.6
  39.8 1.1 %collective-permute-start.9 = (bf16[64,2048]{1,0:T(8,128)(2,1)S(1)}, bf16[64,2048]{1,0:T(8,128)(2,1)S(1)}, u32[]{:S(2)}, u32[]{:S(2)}) collective-permute-start(bf16[64,2048]{1,0:T(8,128)(2,1)S(1)} %get-tuple-element.48), channel_id=1, source_target_pairs={{0,2},{1,3},{2,0},{3,1},{4,6},{5,7},{6,4},{7,5},{8,10},{9,11},{10,... | collective-permute-start | bytes 786440 | tf_op jit(solution)/shard_map/gather_input_block2_first64/ppermute | solution.py:53
  40.9 6.8 %backward_heads.1 = (bf16[512,512]{1,0:T(8,128)(2,1)S(1)}, bf16[512,512]{1,0:T(8,128)(2,1)S(1)}, bf16[512,512]{1,0:T(8,128)(2,1)S(1)}) custom-call(bf16[128,2048]{1,0:T(8,128)(2,1)} %cast.1.refs_2_.refs_0_, bf16[128,2048]{1,0:T(8,128)(2,1)} %collective-permute-done.1.refs_3_.refs_1_, bf16[128,2048]{1,0:T(8,128)(2,1)} %collective-permute-done.refs_2_, ...), custom_call_target="tpu_custom_call" | custom-call | flops 8000000000 | bytes 1 | tf_op jit(solution)/shard_map/backward_heads/pallas_call | solution.py:197
  47.8 1.2 %collective-permute-start.12 = (bf16[64,2048]{1,0:T(8,128)(2,1)S(1)}, bf16[64,2048]{1,0:T(8,128)(2,1)S(1)}, u32[]{:S(2)}, u32[]{:S(2)}) collective-permute-start(bf16[64,2048]{1,0:T(8,128)(2,1)S(1)} %get-tuple-element.54.refs_6_), channel_id=1, source_target_pairs={{0,1},{1,0},{2,3},{3,2},{4,5},{5,4},{6,7},{7,6},{8,9},{9,8},{10,11... | collective-permute-start | bytes 786440 | tf_op jit(solution)/shard_map/gather_input_block3_row0/ppermute | solution.py:53
  49.2 3.4 %backward_terms.1 = (f32[128,2048]{1,0:T(8,128)S(1)}, bf16[128,2048]{1,0:T(8,128)(2,1)S(1)}, bf16[128,2048]{1,0:T(8,128)(2,1)S(1)}, f32[64,2048]{1,0:T(8,128)S(1)}, f32[64,2048]{1,0:T(8,128)S(1)}) custom-call(bf16[512,512]{1,0:T(8,128)(2,1)S(1)} %get-tuple-element.53.refs_2_.refs_0_, bf16[512,512]{1,0:T(8,128)(2,1)S(1)} %get-tuple-element.64.refs_1_, ...), custom_call_target="tpu_custom_call" | custom-call | flops 3000000000 | bytes 1 | tf_op jit(solution)/shard_map/backward_terms/pallas_call | solution.py:197
  52.6 0.5 collective-permute-start.17
  53.1 1.1 %collective-permute-start.18 = (bf16[128,2048]{1,0:T(8,128)(2,1)S(1)}, bf16[128,2048]{1,0:T(8,128)(2,1)S(1)}, u32[]{:S(2)}, u32[]{:S(2)}) collective-permute-start(bf16[128,2048]{1,0:T(8,128)(2,1)S(1)} %get-tuple-element.69), channel_id=1, source_target_pairs={{0,2},{1,3},{2,0},{3,1},{4,6},{5,7},{6,4},{7,5},{8,10},{9,11},{10,... | collective-permute-start | bytes 1572872 | tf_op jit(solution)/shard_map/scatter_grad_block3_part1/ppermute | solution.py:53
  54.3 1.1 %collective-permute-done.13.refs_7_ = bf16[64,2048]{1,0:T(8,128)(2,1)S(1)} collective-permute-done((bf16[64,2048]{1,0:T(8,128)(2,1)S(1)}, bf16[64,2048]{1,0:T(8,128)(2,1)S(1)}, u32[]{:S(2)}, u32[]{:S(2)}) %collective-permute-start.13) | collective-permute-done | bytes 262176 | tf_op jit(solution)/shard_map/gather_input_block3_row64/ppermute | solution.py:53
  55.4 3.8 %project.3 = (bf16[512,512]{1,0:T(8,128)(2,1)S(1)}, bf16[512,512]{1,0:T(8,128)(2,1)S(1)}, bf16[512,512]{1,0:T(8,128)(2,1)S(1)}) custom-call(bf16[64,2048]{1,0:T(8,128)(2,1)S(1)} %get-tuple-element.44.refs_0_, bf16[64,2048]{1,0:T(8,128)(2,1)S(1)} %get-tuple-element.45.refs_1_, bf16[64,2048]{1,0:T(8,128)(2,1)S(1)} %collective-permute-done.6.refs_2_, ...), custom_call_target="tpu_custom_call" | custom-call | flops 5000000000 | bytes 1 | tf_op jit(solution)/shard_map/project/pallas_call | solution.py:197
  59.2 2.8 %forward_terms.1 = (bf16[128,2048]{1,0:T(8,128)(2,1)S(1)}, bf16[64,2048]{1,0:T(8,128)(2,1)S(1)}, bf16[64,2048]{1,0:T(8,128)(2,1)S(1)}, f32[128,2048]{1,0:T(8,128)S(1)}, f32[128,2048]{1,0:T(8,128)S(1)}) custom-call(bf16[512,512]{1,0:T(8,128)(2,1)S(1)} %get-tuple-element.56.refs_0_, bf16[512,512]{1,0:T(8,128)(2,1)S(1)} %get-tuple-element.57.refs_1_, ...), custom_call_target="tpu_custom_call" | custom-call | flops 5000000000 | bytes 1 | tf_op jit(solution)/shard_map/forward_terms/pallas_call | solution.py:197
  62.0 9.4 %collective-permute-start.14 = (bf16[128,2048]{1,0:T(8,128)(2,1)S(1)}, bf16[128,2048]{1,0:T(8,128)(2,1)S(1)}, u32[]{:S(2)}, u32[]{:S(2)}) collective-permute-start(bf16[128,2048]{1,0:T(8,128)(2,1)S(1)} %get-tuple-element.59), channel_id=1, source_target_pairs={{0,4},{1,5},{2,6},{3,7},{4,8},{5,9},{6,10},{7,11},{8,12},{9,13},{1... | collective-permute-start | bytes 1572872 | tf_op jit(solution)/shard_map/ppermute | solution.py:63
  71.7 1.5 %collective-permute-start.22 = (bf16[64,2048]{1,0:T(8,128)(2,1)S(1)}, bf16[64,2048]{1,0:T(8,128)(2,1)S(1)}, u32[]{:S(2)}, u32[]{:S(2)}) collective-permute-start(bf16[64,2048]{1,0:T(8,128)(2,1)S(1)} %get-tuple-element.70.refs_4_), channel_id=1, source_target_pairs={{0,2},{1,3},{2,0},{3,1},{4,6},{5,7},{6,4},{7,5},{8,10},{9,11},{10,... | collective-permute-start | bytes 786440 | tf_op jit(solution)/shard_map/scatter_grad_block2_part0/ppermute | solution.py:53
  73.2 1.3 %collective-permute-start.21 = (bf16[64,2048]{1,0:T(8,128)(2,1)S(1)}, bf16[64,2048]{1,0:T(8,128)(2,1)S(1)}, u32[]{:S(2)}, u32[]{:S(2)}) collective-permute-start(bf16[64,2048]{1,0:T(8,128)(2,1)S(1)} %get-tuple-element.71.refs_5_), channel_id=1, source_target_pairs={{0,1},{1,0},{2,3},{3,2},{4,5},{5,4},{6,7},{7,6},{8,9},{9,8},{10,11... | collective-permute-start | bytes 786440 | tf_op jit(solution)/shard_map/scatter_grad_block1_part1/ppermute | solution.py:53
  74.5 5.1 %collective-permute-done.16.refs_3_ = bf16[64,2048]{1,0:T(8,128)(2,1)S(1)} collective-permute-done((bf16[64,2048]{1,0:T(8,128)(2,1)S(1)}, bf16[64,2048]{1,0:T(8,128)(2,1)S(1)}, u32[]{:S(2)}, u32[]{:S(2)}) %collective-permute-start.16) | collective-permute-done | bytes 262176 | tf_op jit(solution)/shard_map/scatter_branch_block3_part1/ppermute | solution.py:53
  79.9 2.2 %collective-permute-start.19 = (bf16[128,2048]{1,0:T(8,128)(2,1)S(1)}, bf16[128,2048]{1,0:T(8,128)(2,1)S(1)}, u32[]{:S(2)}, u32[]{:S(2)}) collective-permute-start(bf16[128,2048]{1,0:T(8,128)(2,1)S(1)} %get-tuple-element.72.refs_5_), channel_id=1, source_target_pairs={{0,6},{1,7},{2,4},{3,5},{4,10},{5,11},{6,8},{7,9},{8,14},{9,15},{1... | collective-permute-start | bytes 1572872 | tf_op jit(solution)/shard_map/scatter_branch_block2_part0/ppermute | solution.py:63
  82.0 0.7 collective-permute-start.20
  82.8 8.1 %collective-permute-done.22.refs_2_ = bf16[64,2048]{1,0:T(8,128)(2,1)S(1)} collective-permute-done((bf16[64,2048]{1,0:T(8,128)(2,1)S(1)}, bf16[64,2048]{1,0:T(8,128)(2,1)S(1)}, u32[]{:S(2)}, u32[]{:S(2)}) %collective-permute-start.22) | collective-permute-done | bytes 262176 | tf_op jit(solution)/shard_map/scatter_grad_block2_part0/ppermute | solution.py:53
  90.9 0.6 input_grad.1
  91.6 4.4 %collective-permute-done.19.refs_0_.refs_1_ = bf16[128,2048]{1,0:T(8,128)(2,1)S(1)} collective-permute-done((bf16[128,2048]{1,0:T(8,128)(2,1)S(1)}, bf16[128,2048]{1,0:T(8,128)(2,1)S(1)}, u32[]{:S(2)}, u32[]{:S(2)}) %collective-permute-start.19) | collective-permute-done | bytes 524320 | tf_op jit(solution)/shard_map/scatter_branch_block2_part0/ppermute | solution.py:63
  95.9 3.3 %collective-permute-done.20.refs_2_.refs_3_ = bf16[128,2048]{1,0:T(8,128)(2,1)S(1)} collective-permute-done((bf16[128,2048]{1,0:T(8,128)(2,1)S(1)}, bf16[128,2048]{1,0:T(8,128)(2,1)S(1)}, u32[]{:S(2)}, u32[]{:S(2)}) %collective-permute-start.20) | collective-permute-done | bytes 524320 | tf_op jit(solution)/shard_map/scatter_branch_block1_part0/ppermute | solution.py:63
  99.2 1.1 %activation_sum.1.refs_0_ = f32[1,128,2048]{2,1,0:T(8,128)} custom-call(bf16[128,2048]{1,0:T(8,128)(2,1)S(1)} %collective-permute-done.14.base_ref.refs_4_, bf16[128,2048]{1,0:T(8,128)(2,1)S(1)} %collective-permute-done.19.refs_0_.refs_1_, bf16[128,2048]{1,0:T(8,128)(2,1)S(1)} %collective-permute-done.19.refs_0_.refs_1_, ...), custom_call_target="tpu_custom_call" | custom-call | flops 8000000000 | bytes 1 | tf_op jit(solution)/shard_map/activation_sum/pallas_call | solution.py:197
  100.4 1.5 %collective-permute-done.23.in_ref = bf16[128,2048]{1,0:T(8,128)(2,1)S(1)} collective-permute-done((bf16[128,2048]{1,0:T(8,128)(2,1)S(1)}, bf16[128,2048]{1,0:T(8,128)(2,1)S(1)}, u32[]{:S(2)}, u32[]{:S(2)}) %collective-permute-start.23) | collective-permute-done | bytes 524320 | tf_op jit(solution)/shard_map/ppermute | solution.py:69
  101.9 1.2 %copy-done.10 = f32[1,128,2048]{2,1,0:T(8,128)S(1)} copy-done((f32[1,128,2048]{2,1,0:T(8,128)S(1)}, f32[1,128,2048]{2,1,0:T(8,128)}, u32[]{:S(2)}) %copy-start.10) | copy-done | bytes 1048600
  103.1 1.0 widen.1
  (56 shorter events, 1.4 us)
Async XLA Ops:
  0.6 9.1 %copy-start.14 = (f32[1,2048]{1,0:T(1,128)S(1)}, f32[1,2048]{1,0:T(1,128)}, u32[]{:S(2)}) copy-start(f32[1,2048]{1,0:T(1,128)} %gain_ref.1) | copy-start | bytes 24580
  2.9 14.0 %collective-permute-start.3 = (bf16[128,2048]{1,0:T(8,128)(2,1)}, bf16[128,2048]{1,0:T(8,128)(2,1)S(1)}, u32[]{:S(2)}, u32[]{:S(2)}) collective-permute-start(bf16[128,2048]{1,0:T(8,128)(2,1)} %get-tuple-element.41.refs_0_), channel_id=1, source_target_pairs={{0,1},{1,0},{2,3},{3,2},{4,5},{5,4},{6,7},{7,6},{8,9},{9,8},{10,11... | collective-permute-start | bytes 1572872 | tf_op jit(solution)/shard_map/gather_saved_block1/ppermute | solution.py:53
  5.0 12.7 %collective-permute-start.2 = (bf16[128,2048]{1,0:T(8,128)(2,1)}, bf16[128,2048]{1,0:T(8,128)(2,1)S(1)}, u32[]{:S(2)}, u32[]{:S(2)}) collective-permute-start(bf16[128,2048]{1,0:T(8,128)(2,1)} %get-tuple-element.41.refs_0_), channel_id=1, source_target_pairs={{0,2},{1,3},{2,0},{3,1},{4,6},{5,7},{6,4},{7,5},{8,10},{9,11},{10,... | collective-permute-start | bytes 1572872 | tf_op jit(solution)/shard_map/gather_saved_block2/ppermute | solution.py:53
  6.2 1.1 %copy-start.3 = (bf16[128,2048]{1,0:T(8,128)(2,1)S(1)}, bf16[128,2048]{1,0:T(8,128)(2,1)}, u32[]{:S(2)}) copy-start(bf16[128,2048]{1,0:T(8,128)(2,1)} %get-tuple-element.41.refs_0_) | copy-start | bytes 1572868
  7.3 1.2 %copy-start.7 = (f32[1,128,2048]{2,1,0:T(8,128)S(1)}, f32[1,128,2048]{2,1,0:T(8,128)}, u32[]{:S(2)}) copy-start(f32[1,128,2048]{2,1,0:T(8,128)} %param.10) | copy-start | bytes 3145732
  8.6 1.4 %copy-start.5 = (f32[1,128,2048]{2,1,0:T(8,128)S(1)}, f32[1,128,2048]{2,1,0:T(8,128)}, u32[]{:S(2)}) copy-start(f32[1,128,2048]{2,1,0:T(8,128)} %param.8) | copy-start | bytes 3145732
  9.4 18.8 %collective-permute-start.1 = (bf16[128,2048]{1,0:T(8,128)(2,1)}, bf16[128,2048]{1,0:T(8,128)(2,1)}, u32[]{:S(2)}, u32[]{:S(2)}) collective-permute-start(bf16[128,2048]{1,0:T(8,128)(2,1)} %cast.1.refs_2_.refs_0_), channel_id=1, source_target_pairs={{0,1},{1,0},{2,3},{3,2},{4,5},{5,4},{6,7},{7,6},{8,9},{9,8},{10,11... | collective-permute-start | bytes 1572872 | tf_op jit(solution)/shard_map/gather_grad_block1/ppermute | solution.py:53
  9.7 19.4 %collective-permute-start = (bf16[128,2048]{1,0:T(8,128)(2,1)}, bf16[128,2048]{1,0:T(8,128)(2,1)}, u32[]{:S(2)}, u32[]{:S(2)}) collective-permute-start(bf16[128,2048]{1,0:T(8,128)(2,1)} %cast.1.refs_2_.refs_0_), channel_id=1, source_target_pairs={{0,2},{1,3},{2,0},{3,1},{4,6},{5,7},{6,4},{7,5},{8,10},{9,11},{10,... | collective-permute-start | bytes 1572872 | tf_op jit(solution)/shard_map/gather_grad_block2/ppermute | solution.py:53
  10.0 25.6 %copy-start.2 = (bf16[1,2048,512]{2,1,0:T(8,128)(2,1)S(1)}, bf16[1,2048,512]{2,1,0:T(8,128)(2,1)}, u32[]{:S(2)}) copy-start(bf16[1,2048,512]{2,1,0:T(8,128)(2,1)} %param.14) | copy-start | bytes 6291460
  10.9 0.7 copy-start.11
  17.7 17.8 %copy-start.4 = (bf16[128,2048]{1,0:T(8,128)(2,1)S(1)}, bf16[128,2048]{1,0:T(8,128)(2,1)}, u32[]{:S(2)}) copy-start(bf16[128,2048]{1,0:T(8,128)(2,1)} %get-tuple-element.41.refs_0_) | copy-start | bytes 1572868
  17.8 16.7 %collective-permute-start.4 = (bf16[64,2048]{1,0:T(8,128)(2,1)S(1)}, bf16[64,2048]{1,0:T(8,128)(2,1)S(1)}, u32[]{:S(2)}, u32[]{:S(2)}) collective-permute-start(bf16[64,2048]{1,0:T(8,128)(2,1)S(1)} %get-tuple-element.42.refs_4_), channel_id=1, source_target_pairs={{0,1},{1,0},{2,3},{3,2},{4,5},{5,4},{6,7},{7,6},{8,9},{9,8},{10,11... | collective-permute-start | bytes 786440 | tf_op jit(solution)/shard_map/gather_saved_block3_row0/ppermute | solution.py:53
  18.2 17.3 %collective-permute-start.5 = (bf16[64,2048]{1,0:T(8,128)(2,1)S(1)}, bf16[64,2048]{1,0:T(8,128)(2,1)S(1)}, u32[]{:S(2)}, u32[]{:S(2)}) collective-permute-start(bf16[64,2048]{1,0:T(8,128)(2,1)S(1)} %get-tuple-element.43.refs_5_), channel_id=1, source_target_pairs={{0,2},{1,3},{2,0},{3,1},{4,6},{5,7},{6,4},{7,5},{8,10},{9,11},{10,... | collective-permute-start | bytes 786440 | tf_op jit(solution)/shard_map/gather_saved_block3_row64/ppermute | solution.py:53
  29.0 1.0 copy-start.12
  30.0 5.5 %copy-start = (bf16[1,2048,512]{2,1,0:T(8,128)(2,1)S(1)}, bf16[1,2048,512]{2,1,0:T(8,128)(2,1)}, u32[]{:S(2)}) copy-start(bf16[1,2048,512]{2,1,0:T(8,128)(2,1)} %param.12) | copy-start | bytes 6291460
  30.0 5.6 %copy-start.1 = (bf16[1,2048,512]{2,1,0:T(8,128)(2,1)S(1)}, bf16[1,2048,512]{2,1,0:T(8,128)(2,1)}, u32[]{:S(2)}) copy-start(bf16[1,2048,512]{2,1,0:T(8,128)(2,1)} %param.13) | copy-start | bytes 6291460
  31.2 8.5 %collective-permute-start.10 = (bf16[64,2048]{1,0:T(8,128)(2,1)S(1)}, bf16[64,2048]{1,0:T(8,128)(2,1)S(1)}, u32[]{:S(2)}, u32[]{:S(2)}) collective-permute-start(bf16[64,2048]{1,0:T(8,128)(2,1)S(1)} %get-tuple-element.49), channel_id=1, source_target_pairs={{0,1},{1,0},{2,3},{3,2},{4,5},{5,4},{6,7},{7,6},{8,9},{9,8},{10,11... | collective-permute-start | bytes 786440 | tf_op jit(solution)/shard_map/gather_grad_block3_row0/ppermute | solution.py:53
  31.7 9.2 %collective-permute-start.11 = (bf16[64,2048]{1,0:T(8,128)(2,1)S(1)}, bf16[64,2048]{1,0:T(8,128)(2,1)S(1)}, u32[]{:S(2)}, u32[]{:S(2)}) collective-permute-start(bf16[64,2048]{1,0:T(8,128)(2,1)S(1)} %get-tuple-element.50), channel_id=1, source_target_pairs={{0,2},{1,3},{2,0},{3,1},{4,6},{5,7},{6,4},{7,5},{8,10},{9,11},{10,... | collective-permute-start | bytes 786440 | tf_op jit(solution)/shard_map/gather_grad_block3_row64/ppermute | solution.py:53
  34.1 13.6 %collective-permute-start.8 = (bf16[64,2048]{1,0:T(8,128)(2,1)S(1)}, bf16[64,2048]{1,0:T(8,128)(2,1)S(1)}, u32[]{:S(2)}, u32[]{:S(2)}) collective-permute-start(bf16[64,2048]{1,0:T(8,128)(2,1)S(1)} %get-tuple-element.44.refs_0_), channel_id=1, source_target_pairs={{0,2},{1,3},{2,0},{3,1},{4,6},{5,7},{6,4},{7,5},{8,10},{9,11},{10,... | collective-permute-start | bytes 786440 | tf_op jit(solution)/shard_map/gather_input_block2_first0/ppermute | solution.py:53
  34.5 13.2 %collective-permute-start.7 = (bf16[64,2048]{1,0:T(8,128)(2,1)S(1)}, bf16[64,2048]{1,0:T(8,128)(2,1)S(1)}, u32[]{:S(2)}, u32[]{:S(2)}) collective-permute-start(bf16[64,2048]{1,0:T(8,128)(2,1)S(1)} %get-tuple-element.45.refs_1_), channel_id=1, source_target_pairs={{0,1},{1,0},{2,3},{3,2},{4,5},{5,4},{6,7},{7,6},{8,9},{9,8},{10,11... | collective-permute-start | bytes 786440 | tf_op jit(solution)/shard_map/gather_input_block1_first64/ppermute | solution.py:53
  35.5 3.6 %copy-start.13 = (bf16[64,2048]{1,0:T(8,128)(2,1)S(1)}, bf16[64,2048]{1,0:T(8,128)(2,1)}, u32[]{:S(2)}) copy-start(bf16[64,2048]{1,0:T(8,128)(2,1)} %copy-done.11) | copy-start | bytes 786436
  35.6 5.3 %copy-start.15 = (bf16[1,2048,512]{2,1,0:T(8,128)(2,1)S(1)}, bf16[1,2048,512]{2,1,0:T(8,128)(2,1)}, u32[]{:S(2)}) copy-start(bf16[1,2048,512]{2,1,0:T(8,128)(2,1)} %param.15) | copy-start | bytes 6291460
  39.3 13.9 %collective-permute-start.6 = (bf16[64,2048]{1,0:T(8,128)(2,1)S(1)}, bf16[64,2048]{1,0:T(8,128)(2,1)S(1)}, u32[]{:S(2)}, u32[]{:S(2)}) collective-permute-start(bf16[64,2048]{1,0:T(8,128)(2,1)S(1)} %get-tuple-element.47), channel_id=1, source_target_pairs={{0,1},{1,0},{2,3},{3,2},{4,5},{5,4},{6,7},{7,6},{8,9},{9,8},{10,11... | collective-permute-start | bytes 786440 | tf_op jit(solution)/shard_map/gather_input_block1_first0/ppermute | solution.py:53
  39.8 14.5 %collective-permute-start.9 = (bf16[64,2048]{1,0:T(8,128)(2,1)S(1)}, bf16[64,2048]{1,0:T(8,128)(2,1)S(1)}, u32[]{:S(2)}, u32[]{:S(2)}) collective-permute-start(bf16[64,2048]{1,0:T(8,128)(2,1)S(1)} %get-tuple-element.48), channel_id=1, source_target_pairs={{0,2},{1,3},{2,0},{3,1},{4,6},{5,7},{6,4},{7,5},{8,10},{9,11},{10,... | collective-permute-start | bytes 786440 | tf_op jit(solution)/shard_map/gather_input_block2_first64/ppermute | solution.py:53
  47.8 6.5 %collective-permute-start.12 = (bf16[64,2048]{1,0:T(8,128)(2,1)S(1)}, bf16[64,2048]{1,0:T(8,128)(2,1)S(1)}, u32[]{:S(2)}, u32[]{:S(2)}) collective-permute-start(bf16[64,2048]{1,0:T(8,128)(2,1)S(1)} %get-tuple-element.54.refs_6_), channel_id=1, source_target_pairs={{0,1},{1,0},{2,3},{3,2},{4,5},{5,4},{6,7},{7,6},{8,9},{9,8},{10,11... | collective-permute-start | bytes 786440 | tf_op jit(solution)/shard_map/gather_input_block3_row0/ppermute | solution.py:53
  49.0 6.4 %collective-permute-start.13 = (bf16[64,2048]{1,0:T(8,128)(2,1)S(1)}, bf16[64,2048]{1,0:T(8,128)(2,1)S(1)}, u32[]{:S(2)}, u32[]{:S(2)}) collective-permute-start(bf16[64,2048]{1,0:T(8,128)(2,1)S(1)} %get-tuple-element.55.refs_7_), channel_id=1, source_target_pairs={{0,2},{1,3},{2,0},{3,1},{4,6},{5,7},{6,4},{7,5},{8,10},{9,11},{10,... | collective-permute-start | bytes 786440 | tf_op jit(solution)/shard_map/gather_input_block3_row64/ppermute | solution.py:53
  52.6 19.0 %collective-permute-start.17 = (bf16[128,2048]{1,0:T(8,128)(2,1)S(1)}, bf16[128,2048]{1,0:T(8,128)(2,1)S(1)}, u32[]{:S(2)}, u32[]{:S(2)}) collective-permute-start(bf16[128,2048]{1,0:T(8,128)(2,1)S(1)} %get-tuple-element.68), channel_id=1, source_target_pairs={{0,1},{1,0},{2,3},{3,2},{4,5},{5,4},{6,7},{7,6},{8,9},{9,8},{10,11... | collective-permute-start | bytes 1572872 | tf_op jit(solution)/shard_map/scatter_grad_block3_part0/ppermute | solution.py:53
  53.1 6.1 %copy-start.6 = (f32[1,128,2048]{2,1,0:T(8,128)S(1)}, f32[1,128,2048]{2,1,0:T(8,128)}, u32[]{:S(2)}) copy-start(f32[1,128,2048]{2,1,0:T(8,128)} %param.8) | copy-start | bytes 3145732
  53.1 18.5 %collective-permute-start.18 = (bf16[128,2048]{1,0:T(8,128)(2,1)S(1)}, bf16[128,2048]{1,0:T(8,128)(2,1)S(1)}, u32[]{:S(2)}, u32[]{:S(2)}) collective-permute-start(bf16[128,2048]{1,0:T(8,128)(2,1)S(1)} %get-tuple-element.69), channel_id=1, source_target_pairs={{0,2},{1,3},{2,0},{3,1},{4,6},{5,7},{6,4},{7,5},{8,10},{9,11},{10,... | collective-permute-start | bytes 1572872 | tf_op jit(solution)/shard_map/scatter_grad_block3_part1/ppermute | solution.py:53
  62.0 20.7 %collective-permute-start.14 = (bf16[128,2048]{1,0:T(8,128)(2,1)S(1)}, bf16[128,2048]{1,0:T(8,128)(2,1)S(1)}, u32[]{:S(2)}, u32[]{:S(2)}) collective-permute-start(bf16[128,2048]{1,0:T(8,128)(2,1)S(1)} %get-tuple-element.59), channel_id=1, source_target_pairs={{0,4},{1,5},{2,6},{3,7},{4,8},{5,9},{6,10},{7,11},{8,12},{9,13},{1... | collective-permute-start | bytes 1572872 | tf_op jit(solution)/shard_map/ppermute | solution.py:63
  71.4 8.3 %collective-permute-start.16 = (bf16[64,2048]{1,0:T(8,128)(2,1)S(1)}, bf16[64,2048]{1,0:T(8,128)(2,1)S(1)}, u32[]{:S(2)}, u32[]{:S(2)}) collective-permute-start(bf16[64,2048]{1,0:T(8,128)(2,1)S(1)} %get-tuple-element.63), channel_id=1, source_target_pairs={{0,2},{1,3},{2,0},{3,1},{4,6},{5,7},{6,4},{7,5},{8,10},{9,11},{10,... | collective-permute-start | bytes 786440 | tf_op jit(solution)/shard_map/scatter_branch_block3_part1/ppermute | solution.py:53
  71.5 8.2 %collective-permute-start.15 = (bf16[64,2048]{1,0:T(8,128)(2,1)S(1)}, bf16[64,2048]{1,0:T(8,128)(2,1)S(1)}, u32[]{:S(2)}, u32[]{:S(2)}) collective-permute-start(bf16[64,2048]{1,0:T(8,128)(2,1)S(1)} %get-tuple-element.62.refs_4_), channel_id=1, source_target_pairs={{0,1},{1,0},{2,3},{3,2},{4,5},{5,4},{6,7},{7,6},{8,9},{9,8},{10,11... | collective-permute-start | bytes 786440 | tf_op jit(solution)/shard_map/scatter_branch_block3_part0/ppermute | solution.py:53
  71.7 19.2 %copy-start.8 = (f32[1,128,2048]{2,1,0:T(8,128)S(1)}, f32[1,128,2048]{2,1,0:T(8,128)}, u32[]{:S(2)}) copy-start(f32[1,128,2048]{2,1,0:T(8,128)} %param.10) | copy-start | bytes 3145732
  71.7 19.2 %copy-start.9 = (f32[1,128,2048]{2,1,0:T(8,128)S(1)}, f32[1,128,2048]{2,1,0:T(8,128)}, u32[]{:S(2)}) copy-start(f32[1,128,2048]{2,1,0:T(8,128)} %param.9) | copy-start | bytes 3145732
  71.7 19.2 %copy-start.16 = (f32[128,1]{1,0:T(8,128)S(1)}, f32[128,1]{1,0:T(8,128)}, u32[]{:S(2)}) copy-start(f32[128,1]{1,0:T(8,128)} %get-tuple-element.75.inv_ref) | copy-start | bytes 1540
  71.7 19.2 %collective-permute-start.22 = (bf16[64,2048]{1,0:T(8,128)(2,1)S(1)}, bf16[64,2048]{1,0:T(8,128)(2,1)S(1)}, u32[]{:S(2)}, u32[]{:S(2)}) collective-permute-start(bf16[64,2048]{1,0:T(8,128)(2,1)S(1)} %get-tuple-element.70.refs_4_), channel_id=1, source_target_pairs={{0,2},{1,3},{2,0},{3,1},{4,6},{5,7},{6,4},{7,5},{8,10},{9,11},{10,... | collective-permute-start | bytes 786440 | tf_op jit(solution)/shard_map/scatter_grad_block2_part0/ppermute | solution.py:53
  73.2 17.7 %collective-permute-start.21 = (bf16[64,2048]{1,0:T(8,128)(2,1)S(1)}, bf16[64,2048]{1,0:T(8,128)(2,1)S(1)}, u32[]{:S(2)}, u32[]{:S(2)}) collective-permute-start(bf16[64,2048]{1,0:T(8,128)(2,1)S(1)} %get-tuple-element.71.refs_5_), channel_id=1, source_target_pairs={{0,1},{1,0},{2,3},{3,2},{4,5},{5,4},{6,7},{7,6},{8,9},{9,8},{10,11... | collective-permute-start | bytes 786440 | tf_op jit(solution)/shard_map/scatter_grad_block1_part1/ppermute | solution.py:53
  79.9 16.0 %collective-permute-start.19 = (bf16[128,2048]{1,0:T(8,128)(2,1)S(1)}, bf16[128,2048]{1,0:T(8,128)(2,1)S(1)}, u32[]{:S(2)}, u32[]{:S(2)}) collective-permute-start(bf16[128,2048]{1,0:T(8,128)(2,1)S(1)} %get-tuple-element.72.refs_5_), channel_id=1, source_target_pairs={{0,6},{1,7},{2,4},{3,5},{4,10},{5,11},{6,8},{7,9},{8,14},{9,15},{1... | collective-permute-start | bytes 1572872 | tf_op jit(solution)/shard_map/scatter_branch_block2_part0/ppermute | solution.py:63
  82.0 17.2 %collective-permute-start.20 = (bf16[128,2048]{1,0:T(8,128)(2,1)S(1)}, bf16[128,2048]{1,0:T(8,128)(2,1)S(1)}, u32[]{:S(2)}, u32[]{:S(2)}) collective-permute-start(bf16[128,2048]{1,0:T(8,128)(2,1)S(1)} %get-tuple-element.73.refs_6_), channel_id=1, source_target_pairs={{0,5},{1,4},{2,7},{3,6},{4,9},{5,8},{6,11},{7,10},{8,13},{9,12},{1... | collective-permute-start | bytes 1572872 | tf_op jit(solution)/shard_map/scatter_branch_block1_part0/ppermute | solution.py:63
  91.5 10.4 %collective-permute-start.23 = (bf16[128,2048]{1,0:T(8,128)(2,1)S(1)}, bf16[128,2048]{1,0:T(8,128)(2,1)S(1)}, u32[]{:S(2)}, u32[]{:S(2)}) collective-permute-start(bf16[128,2048]{1,0:T(8,128)(2,1)S(1)} %input_grad.1), channel_id=1, source_target_pairs={{0,28},{4,0},{8,4},{12,8},{16,12},{20,16},{24,20},{28,24},{1,29},{... | collective-permute-start | bytes 1572872 | tf_op jit(solution)/shard_map/ppermute | solution.py:69
  101.9 1.2 %copy-start.10 = (f32[1,128,2048]{2,1,0:T(8,128)S(1)}, f32[1,128,2048]{2,1,0:T(8,128)}, u32[]{:S(2)}) copy-start(f32[1,128,2048]{2,1,0:T(8,128)} %activation_sum.1.refs_0_) | copy-start | bytes 3145732
